TPU v7x, 32 devices: a whole 2x2x4 slice. The times are simulated.
32 devices in a mesh: groups: 2 (over x), samples: 16 (over z, y, core).
Axes of the slice: x: 2, y: 2, z: 4, core: 2. Of those that a mesh axis runs over, the one named last changes fastest.
Arguments:
- acts: bfloat16 [12288, 1024], P(('groups', 'samples')), parts along dimension 0
- grads: bfloat16 [12288, 2048], P(('groups', 'samples')), parts along dimension 0
- counts: int32 [32], P(('groups', 'samples')), parts along dimension 0, may hold values from 1 to 384, 4608 in all
- basis_a: bfloat16 [1024, 1024], P('samples')
- basis_g: bfloat16 [2048, 2048], P('samples')
Outputs:
- precond: bfloat16 [2048, 2048], P(('groups', 'samples')), parts along dimension 0
There are 2 independent parts, one for each index of `groups`. A program takes and returns all parts, laid end to end along the dimension named above; an argument that names none is the same for every part. Nothing has to cross between parts.
Inputs may be any that keep to these rules, and one draw needn't show every extreme that they name: `counts`: one device of every draw holds 384 valid rows.
All inputs are finite; a program needn't handle non-finite values.
Results may differ from a plain program's by a relative error of at most 0.0061.
Values may be sent and summed in bfloat16 or wider, within the bound.
No kernel may reach another device: no remote copies, remote signals or barrier semaphores. Data moves between devices by JAX's collectives and lax.ppermute only.
A program may use at most 64 MiB of HBM per device.

v0:
```python
import jax
import jax.numpy as jnp
from jax import lax
from jax.sharding import PartitionSpec as P

damping = 0.01


def body(acts, grads, counts, basis_a, basis_g):
    rows = acts.shape[0]
    width_a = basis_a.shape[1]
    width_g = basis_g.shape[1]
    local_rows = basis_a.shape[0]
    full_a, full_g = (
        lax.all_gather(basis_a, "samples", axis=0, tiled=True),
        lax.all_gather(basis_g, "samples", axis=0, tiled=True),
    )
    valid = counts[0]
    block = min(128, rows)
    parts_a = []
    parts_g = []
    for first in range(0, rows, block):

        def busy(operand):
            left = jnp.dot(
                acts[first : first + block], full_a, preferred_element_type=jnp.float32
            ).astype(jnp.bfloat16)
            right = jnp.dot(
                grads[first : first + block], full_g, preferred_element_type=jnp.float32
            ).astype(jnp.bfloat16)
            return (left, right)

        def quiet(operand):
            return (
                jnp.zeros((block, width_a), jnp.bfloat16),
                jnp.zeros((block, width_g), jnp.bfloat16),
            )

        left, right = lax.cond(first < valid, busy, quiet, 0)
        keep = (first + jnp.arange(block, dtype=jnp.int32) < valid).astype(jnp.bfloat16)[:, None]
        parts_a.append(left * keep)
        parts_g.append(right * keep)
    rot_a = jnp.concatenate(parts_a, axis=0)
    rot_g = jnp.concatenate(parts_g, axis=0)
    square_a = jnp.sum(jnp.square(rot_a.astype(jnp.float32)), axis=0)
    square_g = jnp.sum(jnp.square(rot_g.astype(jnp.float32)), axis=0)
    square_a, square_g, total = lax.psum((square_a, square_g, valid.astype(jnp.float32)), "samples")
    lam_a = square_a / total
    lam_g = square_g / total
    summed = lax.psum_scatter(
        lax.dot_general(rot_a, rot_g, (((0,), (0,)), ((), ())), preferred_element_type=jnp.float32),
        "samples",
        scatter_dimension=0,
        tiled=True,
    )
    offset = lax.axis_index("samples") * local_rows
    lam_own = lax.dynamic_slice_in_dim(lam_a, offset, local_rows)
    scaled = (summed / total / (lam_own[:, None] * lam_g[None, :] + damping)).astype(jnp.bfloat16)
    scaled_all = lax.all_gather(scaled, "samples", axis=0, tiled=True)
    mid = jnp.dot(basis_a, scaled_all, preferred_element_type=jnp.float32).astype(jnp.bfloat16)
    return lax.dot_general(
        mid, full_g, (((1,), (1,)), ((), ())), preferred_element_type=jnp.float32
    ).astype(jnp.bfloat16)


def solution(mesh):
    in_specs = (
        P(("groups", "samples"), None),
        P(("groups", "samples"), None),
        P(("groups", "samples")),
        P("samples", None),
        P("samples", None),
    )
    out_specs = P(("groups", "samples"), None)
    return jax.shard_map(body, mesh=mesh, in_specs=in_specs, out_specs=out_specs, check_vma=False)
```

profile of v0, /device:TPU:0, one launch (start us, length us, event | category | flops | bytes accessed | tf_op | source)
XLA Modules:
  0.0 330.3 jit_solution(9561161617807678735)
XLA Ops:
  6.5 0.0 all-gather.4.cloned.1.call-start
  6.5 0.7 all-gather.4.cloned.1.call-update
  7.3 0.0 all-gather.6.cloned.1.call-start
  7.3 0.7 all-gather.6.cloned.1.call-update
  8.0 0.0 reduce-scatter.2.cloned.1.call-start
  8.7 44.9 %all-gather.4.cloned.1.call-done = bf16[1024,1024]{1,0:T(8,128)(2,1)} async-done(((bf16[64,1024]{1,0:T(8,128)(2,1)}), bf16[1024,1024]{1,0:T(8,128)(2,1)}) %all-gather.4.cloned.1.call-update) | async-done | bytes 2097168 | tf_op jit(solution)/shard_map/all_gather | solution.py:15
  53.7 75.9 %all-gather.6.cloned.1.call-done = bf16[2048,2048]{1,0:T(8,128)(2,1)} async-done(((bf16[128,2048]{1,0:T(8,128)(2,1)}), bf16[2048,2048]{1,0:T(8,128)(2,1)}) %all-gather.6.cloned.1.call-update) | async-done | bytes 8388624 | tf_op jit(solution)/shard_map/all_gather | solution.py:16
  129.5 6.9 %conditional.5 = (bf16[128,1024]{1,0:T(8,128)(2,1)S(1)}, bf16[128,2048]{1,0:T(8,128)(2,1)S(1)}) conditional(s32[]{:T(128)} %convert_element_type.71, () %tuple.32, (bf16[384,1024]{1,0:T(8,128)(2,1)}, bf16[1024,1024]{1,0:T(8,128)(2,1)}, bf16[384,2048]{1,0:T(8,128)(2,1)}, bf16[2048,2048]{1,0:T(8,128)(2,1)}) %tuple.30), branch_computations={%region_4.0_spmd, %region_5.0_spmd} | conditional | flops 1342570496 | bytes 18350124 | solution.py:39
  129.5 0.0 copy-start
  129.5 2.2 convolution_convert_fusion.5
  131.8 0.0 copy-done
  131.8 4.7 %convolution_convert_fusion.4 = bf16[128,2048]{1,0:T(8,128)(2,1)S(1)} fusion(bf16[2048,2048]{1,0:T(8,128)(2,1)} %get-tuple-element.40, bf16[384,2048]{1,0:T(8,128)(2,1)S(1)} %copy-done), kind=kOutput, calls=%fused_computation.8 | convolution fusion | flops 1074003968 | bytes 9437184 | tf_op jit(solution)/shard_map/cond/branch_1_fun/dot_general | solution.py:28
  136.4 0.1 broadcast_multiply_fusion.3
  136.5 0.1 broadcast_multiply_fusion
  136.6 7.0 %conditional.3 = (bf16[128,1024]{1,0:T(8,128)(2,1)S(1)}, bf16[128,2048]{1,0:T(8,128)(2,1)S(1)}) conditional(s32[]{:T(128)} %convert_element_type.67, () %tuple.29, (bf16[384,1024]{1,0:T(8,128)(2,1)}, bf16[1024,1024]{1,0:T(8,128)(2,1)}, bf16[384,2048]{1,0:T(8,128)(2,1)}, bf16[2048,2048]{1,0:T(8,128)(2,1)}) %tuple.30), branch_computations={%region_0.0_spmd, %region_1.0_spmd} | conditional | flops 1342570496 | bytes 18350124 | solution.py:39
  136.7 0.0 copy-start.1
  136.7 2.2 convolution_convert_fusion.1
  138.9 0.0 copy-done.1
  138.9 4.7 %convolution_convert_fusion = bf16[128,2048]{1,0:T(8,128)(2,1)S(1)} fusion(bf16[2048,2048]{1,0:T(8,128)(2,1)} %get-tuple-element.32, bf16[384,2048]{1,0:T(8,128)(2,1)S(1)} %copy-done.1), kind=kOutput, calls=%fused_computation | convolution fusion | flops 1074003968 | bytes 9437184 | tf_op jit(solution)/shard_map/cond/branch_1_fun/dot_general | solution.py:28
  143.6 0.1 broadcast_multiply_fusion.5
  143.7 0.1 broadcast_multiply_fusion.2
  143.8 7.0 %conditional.4 = (bf16[128,1024]{1,0:T(8,128)(2,1)S(1)}, bf16[128,2048]{1,0:T(8,128)(2,1)S(1)}) conditional(s32[]{:T(128)} %convert_element_type.69, () %tuple.31, (bf16[384,1024]{1,0:T(8,128)(2,1)}, bf16[1024,1024]{1,0:T(8,128)(2,1)}, bf16[384,2048]{1,0:T(8,128)(2,1)}, bf16[2048,2048]{1,0:T(8,128)(2,1)}) %tuple.30), branch_computations={%region_2.0_spmd, %region_3.0_spmd} | conditional | flops 1342570496 | bytes 18350124 | solution.py:39
  143.8 0.0 copy-start.2
  143.8 2.2 convolution_convert_fusion.3
  146.1 0.0 copy-done.2
  146.1 4.7 %convolution_convert_fusion.2 = bf16[128,2048]{1,0:T(8,128)(2,1)S(1)} fusion(bf16[2048,2048]{1,0:T(8,128)(2,1)} %get-tuple-element.36, bf16[384,2048]{1,0:T(8,128)(2,1)S(1)} %copy-done.2), kind=kOutput, calls=%fused_computation.4 | convolution fusion | flops 1074003968 | bytes 9437184 | tf_op jit(solution)/shard_map/cond/branch_1_fun/dot_general | solution.py:28
  150.8 0.1 broadcast_multiply_fusion.4
  150.9 0.1 broadcast_multiply_fusion.1
  151.0 5.6 %fusion.6 = f32[1024,2048]{1,0:T(8,128)} fusion(bf16[128,2048]{1,0:T(8,128)(2,1)S(1)} %broadcast_multiply_fusion, bf16[128,2048]{1,0:T(8,128)(2,1)S(1)} %broadcast_multiply_fusion.1, bf16[128,2048]{1,0:T(8,128)(2,1)S(1)} %broadcast_multiply_fusion.2, bf16[128,1024]{1,0:T(8,128)(2,1)S(1)} %broadcast_multiply_fusion.3, ...), kind=kOutput, calls=%fused_computation.18 | convolution fusion | flops 1617690624 | bytes 10747904 | tf_op jit(solution)/shard_map/dot_general | solution.py:51
  156.6 0.0 reduce-scatter.2.cloned.1.call-update
  156.6 0.0 copy-start.3
  156.6 0.0 all-gather.8.cloned.1.call-start
  156.7 0.2 multiply_reduce_fusion.1
  156.9 0.3 multiply_reduce_fusion
  157.2 60.9 %all-reduce = (f32[2048]{0:T(1024)S(1)}, f32[]{:T(128)}, f32[1024]{0:T(1024)S(1)}) all-reduce(f32[2048]{0:T(1024)S(1)} %multiply_reduce_fusion, f32[]{:T(128)S(6)} %convert_element_type.73, f32[1024]{0:T(1024)S(1)} %multiply_reduce_fusion.1), channel_id=1, replica_groups=mesh['groups'=2,'samples'=16] {'samples'}, use_global_device_ids=true, to_apply=%region_11.0 | all-reduce | flops 3073 | bytes 24584 | tf_op jit(solution)/shard_map/psum | solution.py:47
  218.1 0.6 broadcast_divide_fusion.1
  218.7 0.1 dynamic_slice.3
  218.8 0.6 broadcast_divide_fusion
  219.4 40.4 %reduce-scatter.2.cloned.1.call-done = f32[64,2048]{1,0:T(8,128)} async-done(((f32[1024,2048]{1,0:T(8,128)}), f32[64,2048]{1,0:T(8,128)}) %reduce-scatter.2.cloned.1.call-update) | async-done | bytes 524304 | tf_op jit(solution)/shard_map/reduce_scatter | solution.py:50
  259.8 2.5 divide_convert_fusion
  262.3 0.0 all-gather.8.cloned.1.call-update
  262.4 50.5 %all-gather.8.cloned.1.call-done = bf16[1024,2048]{1,0:T(8,128)(2,1)} async-done(((bf16[64,2048]{1,0:T(8,128)(2,1)}), bf16[1024,2048]{1,0:T(8,128)(2,1)}) %all-gather.8.cloned.1.call-update) | async-done | bytes 4194320 | tf_op jit(solution)/shard_map/all_gather | solution.py:59
  312.9 0.0 copy-done.3
  312.9 10.9 %convolution_convert_fusion.7 = bf16[64,2048]{1,0:T(8,128)(2,1)} fusion(bf16[2048,2048]{1,0:T(8,128)(2,1)} %all-gather.6.cloned.1.call-done, bf16[1024,2048]{1,0:T(8,128)(2,1)} %all-gather.8.cloned.1.call-done, bf16[64,1024]{1,0:T(8,128)(2,1)S(1)} %copy-done.3), kind=kOutput, calls=%fused_computation.14 | convolution fusion | flops 805568512 | bytes 12976128 | tf_op jit(solution)/shard_map/dot_general | solution.py:61
  (2 shorter events, 0.0 us)
Async XLA Ops:
  6.5 47.1 %all-gather.4.cloned.1.call-start = ((), (), s32[]{:S(2)}) async-start(), calls=%async_computation.1 | async-start | bytes 2228224 | tf_op jit(solution)/shard_map/all_gather | solution.py:15
  7.3 122.3 %all-gather.6.cloned.1.call-start = ((), (), s32[]{:S(2)}) async-start(), calls=%async_computation.2 | async-start | bytes 8912896 | tf_op jit(solution)/shard_map/all_gather | solution.py:16
  8.0 251.8 %reduce-scatter.2.cloned.1.call-start = ((), (), s32[]{:S(2)}) async-start(), calls=%async_computation.3 | async-start | bytes 8912896 | tf_op jit(solution)/shard_map/reduce_scatter | solution.py:50
  129.5 2.2 copy-start
  136.7 2.3 copy-start.1
  143.8 2.3 copy-start.2
  156.6 156.2 %copy-start.3 = (bf16[64,1024]{1,0:T(8,128)(2,1)S(1)}, bf16[64,1024]{1,0:T(8,128)(2,1)}, u32[]{:S(2)}) copy-start(bf16[64,1024]{1,0:T(8,128)(2,1)} %param.14) | copy-start | bytes 393220
  156.6 156.2 %all-gather.8.cloned.1.call-start = ((), (), s32[]{:S(2)}) async-start(), calls=%async_computation.4 | async-start | bytes 4456448 | tf_op jit(solution)/shard_map/all_gather | solution.py:59
Sparse Core Ops, SparseCore 0:
  9.5 44.0 all-gather.3
  55.8 73.6 all-gather.5
  156.7 103.0 reduce-scatter.1
  262.5 50.3 all-gather.7
where the time goes:
time: 331 us; the launch traced here: 330 us
  waiting for transfers between devices  213 us (64%)
  blocking collectives  60.9 us (18%)
  matrix products  37.2 us (11%)
  between operations  13.9 us (4%)
  other arithmetic  4.84 us (1%)
    all_gather x1, waiting for transfers between devices, body(): lax.all_gather(basis_g, 'samples', axis=0, tiled=True)  75.9 us
    psum x1, blocking collectives, body(): lax.psum((square_a, square_g, valid.astype(jnp.float32)), 'samples')  60.9 us
    all_gather x1, waiting for transfers between devices, body(): scaled_all = lax.all_gather(scaled, 'samples', axis=0, tiled=True)  50.5 us
    all_gather x1, waiting for transfers between devices, body(): lax.all_gather(basis_a, 'samples', axis=0, tiled=True)  44.9 us
    reduce_scatter x1, waiting for transfers between devices, body(): lax.psum_scatter(lax.dot_general(rot_a, rot_g, (((0,), (0,)), ((), ())),...  40.4 us
    dot_general x3, matrix products, busy(): jnp.dot(grads[first:first + block], full_g, preferred_element_type=jnp.fl...  14 us
    dot_general x1, matrix products, body(): lax.dot_general(mid, full_g, (((1,), (1,)), ((), ())), preferred_element_...  10.9 us
    dot_general x3, matrix products, busy(): jnp.dot(acts[first:first + block], full_a, preferred_element_type=jnp.flo...  6.7 us
  transfers between devices with their start and end apart: 4, of which 4 were waited for; matrix products, arithmetic and copies ran while one was open for 1% of the time, Pallas kernels for 0%

commit v1 on v0

v1 whole, which is shorter than its diff:
```python
import jax
import jax.numpy as jnp
from jax import lax
from jax.sharding import Mesh, PartitionSpec as P

damping = 0.01
bf16 = jnp.bfloat16
f32 = jnp.float32
SWAP = [(0, 1), (1, 0)]


def cut(x, first, size, axis=0):
    return lax.dynamic_slice_in_dim(x, first, size, axis)


def ordered(second, mine, other):
    return jnp.where(second == 0, jnp.concatenate([mine, other]), jnp.concatenate([other, mine]))


def two_parts(v):
    high = lax.reduce_precision(v, 8, 7)
    return high.astype(bf16), (v - high).astype(bf16)


def across(x, step, levels):
    return lax.ppermute(x, "level", [(i, i ^ step) for i in range(levels)])


def body(acts, grads, counts, basis_a, basis_g):
    group, level, chip, core = (lax.axis_index(n) for n in ("group", "level", "chip", "core"))
    levels = lax.axis_size("level")
    rows, width_a = acts.shape
    width_g = grads.shape[1]
    rows_a, rows_g = basis_a.shape[0], basis_g.shape[0]
    part_a, part_g = width_a // 4, width_g // 8

    def columns(c, chips):
        pieces = [cut(basis_g, ((y * 2 + c) * 2 + group) * part_g, part_g, 1) for y in chips]
        return jnp.concatenate(pieces + [cut(basis_a, (c * 2 + group) * part_a, part_a, 1)])

    mine = columns(core, (chip, 1 - chip))
    theirs = lax.ppermute(columns(1 - core, (chip, 1 - chip)), "core", SWAP)
    here_g = ordered(core, mine[:rows_g], theirs[:rows_g])
    there_g = ordered(core, mine[rows_g : 2 * rows_g], theirs[rows_g : 2 * rows_g])
    here_a = ordered(core, mine[2 * rows_g :], theirs[2 * rows_g :])
    passed = lax.ppermute(jnp.concatenate([there_g, here_a]), "chip", SWAP)
    level_g = 4 * rows_g
    level_a = 4 * rows_a
    unit = jnp.concatenate(
        [
            ordered(chip, here_g, passed[: 2 * rows_g]),
            ordered(chip, here_a, passed[2 * rows_g :]),
        ]
    )
    full_g = jnp.zeros((width_g, 2 * part_g), bf16)
    full_a = jnp.zeros((width_a, 2 * part_a), bf16)
    own_a = []
    for step in range(levels):
        slot = unit if step == 0 else across(unit, step, levels)
        other = lax.ppermute(slot, "group", SWAP)
        at = level ^ step
        for place, block in enumerate((slot, other)):
            full_g = lax.dynamic_update_slice(full_g, block[:level_g], (at * level_g, place * part_g))
            full_a = lax.dynamic_update_slice(full_a, block[level_g:], (at * level_a, place * part_a))
        if step == 0:
            own_a = [slot[level_g:], other[level_g:]]
    level_rows = jnp.concatenate(own_a, axis=1)
    level_rows = jnp.concatenate([level_rows, lax.ppermute(level_rows, "core", SWAP)], axis=1)

    valid = counts[0]
    keep = jnp.arange(rows, dtype=jnp.int32)[:, None] < valid
    marks = jnp.stack([valid // 16 * 16, valid % 16]).astype(bf16)
    marks = jnp.broadcast_to(jnp.pad(marks, (0, 14))[:, None], (16, width_a))
    acts = jnp.concatenate([jnp.where(keep, acts, 0), marks])
    grads = jnp.where(keep, grads, 0)
    half = rows // 2
    pieces_a = [acts, lax.ppermute(acts, "core", SWAP)]
    pieces_g = [grads, lax.ppermute(grads, "core", SWAP)]
    for piece, found in ((acts, pieces_a), (grads[:half], pieces_g), (grads[half:], pieces_g)):
        got = lax.ppermute(piece, "chip", SWAP)
        found += [got, lax.ppermute(got, "core", SWAP)]
    valid_here = sum(p[rows, 0].astype(f32) + p[rows + 1, 0].astype(f32) for p in pieces_a)

    def rotate(piece, basis):
        return jnp.dot(piece, basis, preferred_element_type=f32).astype(bf16)

    turned = [rotate(p[:rows], full_a) for p in pieces_a]
    turned_core = lax.ppermute(jnp.concatenate([turned[1], turned[0], turned[3], turned[2]]), "core", SWAP)
    rot_a = jnp.concatenate([jnp.concatenate(turned), turned_core], axis=1)
    r = [rotate(p, full_g) for p in pieces_g]
    rot_g = jnp.concatenate([r[0], r[1], r[2], r[4], r[3], r[5]])
    square_a = jnp.sum(jnp.square(rot_a.astype(f32)), axis=0)
    square_g = jnp.sum(jnp.square(rot_g.astype(f32)), axis=0)
    rotated = lax.dot_general(rot_a, rot_g, (((0,), (0,)), ((), ())), preferred_element_type=f32)

    chunk = width_a // levels
    cols = rot_g.shape[1]
    high_g, low_g = two_parts(square_g)
    high_a, low_a = two_parts(square_a)
    high_n, low_n = two_parts(valid_here)

    def message(to):
        def line(v):
            return jnp.pad(cut(v, to * chunk, chunk), (0, cols - chunk))

        extra = jnp.stack(
            [high_g, low_g, line(high_a), line(low_a), jnp.broadcast_to(high_n, cols), jnp.broadcast_to(low_n, cols)]
        )
        return jnp.concatenate([cut(rotated, to * chunk, chunk).astype(bf16), jnp.pad(extra, ((0, 10), (0, 0)))])

    got = [across(message(level ^ step), step, levels).astype(f32) for step in range(1, levels)]
    summed = cut(rotated, level * chunk, chunk)
    own_square_a = cut(square_a, level * chunk, chunk)
    total = valid_here
    for g in got:
        summed = summed + g[:chunk]
        square_g = square_g + (g[chunk] + g[chunk + 1])
        own_square_a = own_square_a + (g[chunk + 2, :chunk] + g[chunk + 3, :chunk])
        total = total + (g[chunk + 4, 0] + g[chunk + 5, 0])
    lam_a = own_square_a / total
    lam_g = square_g / total
    scaled = (summed / total / (lam_a[:, None] * lam_g[None, :] + damping)).astype(bf16)

    scaled_all = jnp.zeros((width_a, cols), bf16)
    for step in range(levels):
        slot = scaled if step == 0 else across(scaled, step, levels)
        scaled_all = lax.dynamic_update_slice(scaled_all, slot, ((level ^ step) * chunk, 0))

    def result(c):
        picked = jnp.concatenate(
            [cut(level_rows, ((1 - chip) * 2 + c) * rows_a, rows_a), cut(level_rows, (chip * 2 + c) * rows_a, rows_a)]
        )
        mid = jnp.dot(picked, scaled_all, preferred_element_type=f32).astype(bf16)
        return lax.dot_general(mid, full_g, (((1,), (1,)), ((), ())), preferred_element_type=f32)

    sent = lax.ppermute(result(1 - core).astype(bf16), "core", SWAP)
    both = result(core) + sent.astype(f32)
    last = lax.ppermute(both[:rows_a].astype(bf16), "chip", SWAP)
    return (both[rows_a:] + last.astype(f32)).astype(bf16)


def solution(mesh):
    groups, samples = mesh.shape["groups"], mesh.shape["samples"]
    grid = Mesh(mesh.devices.reshape(groups, samples // 4, 2, 2), ("group", "level", "chip", "core"))
    every = ("group", "level", "chip", "core")
    in_specs = (
        P(every, None),
        P(every, None),
        P(every),
        P(every[1:], None),
        P(every[1:], None),
    )
    return jax.shard_map(body, mesh=grid, in_specs=in_specs, out_specs=P(every, None), check_vma=False)
```

time: 331 us -> 227 us (0.69)
  waiting for transfers between devices: 213 us -> 102 us
  blocking collectives: 60.9 us -> 0 us
  starting transfers between devices: 0.12 us -> 33.6 us
  local copies, waits for them, and re-layouts: 0.1 us -> 32 us
  other arithmetic: 4.84 us -> 23.9 us
  matrix products: 37.2 us -> 21.9 us
    all_gather x3 -> x0, waiting for transfers between devices: 171 us -> none  [the longest x1 75.9 us: body(): lax.all_gather(basis_g, 'samples', axis=0, tiled=True)]
    ppermute x0 -> x27, waiting for transfers between devices: none -> 102 us  [the longest x9 56 us: across(): return lax.ppermute(x, 'level', [(i, i ^ step) for i in range(levels)])]
    psum x1 -> x0, blocking collectives: 60.9 us -> none  [body(): lax.psum((square_a, square_g, valid.astype(jnp.float32)), 'samples')]
    reduce_scatter x1 -> x0, waiting for transfers between devices: 40.4 us -> none  [body(): lax.psum_scatter(lax.dot_general(rot_a, rot_g, (((0,), (0,)), ((), ())),...]
    ppermute x0 -> x27, starting transfers between devices: none -> 33.6 us  [the longest x9 20.6 us: across(): return lax.ppermute(x, 'level', [(i, i ^ step) for i in range(levels)])]
    dynamic_update_slice x0 -> x16, local copies, waits for them, and re-layouts: none -> 13.6 us  [the longest x6 7.68 us: body(): lax.dynamic_update_slice(full_a, block[level_g:], (at * level_a, place *...]
    dot_general x7 -> x12, matrix products: 31.6 us -> 18.5 us  [the longest x10 12.7 us: rotate(): return jnp.dot(piece, basis, preferred_element_type=f32).astype(bf16)]
    slice x0 -> x13, local copies, waits for them, and re-layouts: none -> 10.4 us  [the longest x3 3.19 us: body(): p[rows + 1, 0].astype(f32)]
  transfers between devices with their start and end apart: 4 -> 27, of which waited for: 4 -> 13; matrix products, arithmetic and copies ran while one was open for 1% -> 23% of each run, Pallas kernels for 0% -> 0%
where the time goes in v1:
time: 227 us; the launch traced here: 224 us
  waiting for transfers between devices  102 us (45%)
  starting transfers between devices  33.6 us (15%)
  local copies, waits for them, and re-layouts  32 us (14%)
  other arithmetic  23.9 us (11%)
  matrix products  21.9 us (10%)
  between operations  10.7 us (5%)
    ppermute x9, waiting for transfers between devices, across(): return lax.ppermute(x, 'level', [(i, i ^ step) for i in range(levels)])  56 us
    ppermute x1, waiting for transfers between devices, body(): passed = lax.ppermute(jnp.concatenate([there_g, here_a]), 'chip', SWAP)  21.3 us
    ppermute x9, starting transfers between devices, across(): return lax.ppermute(x, 'level', [(i, i ^ step) for i in range(levels)])  20.6 us
    ppermute x4, waiting for transfers between devices, body(): other = lax.ppermute(slot, 'group', SWAP)  15.4 us
    dot_general x10, matrix products, rotate(): return jnp.dot(piece, basis, preferred_element_type=f32).astype(bf16)  12.7 us
    dynamic_update_slice x6, local copies, waits for them, and re-layouts, body(): lax.dynamic_update_slice(full_a, block[level_g:], (at * level_a, place *...  7.68 us
    ppermute x1, waiting for transfers between devices, body(): last = lax.ppermute(both[:rows_a].astype(bf16), 'chip', SWAP)  6.82 us
    reduce_sum x1, other arithmetic, body(): square_a = jnp.sum(jnp.square(rot_a.astype(f32)), axis=0)  5.92 us
  transfers between devices with their start and end apart: 27, of which 13 were waited for; matrix products, arithmetic and copies ran while one was open for 23% of the time, Pallas kernels for 0%

profile of v1, /device:TPU:0, one launch (start us, length us, event | category | flops | bytes accessed | tf_op | source)
XLA Modules:
  0.0 223.9 jit_solution(14066936701381820470)
XLA Ops:
  3.0 1.4 broadcast_select_fusion.1
  5.6 2.5 %collective-permute-start.11 = (bf16[400,1024]{1,0:T(8,128)(2,1)}, bf16[400,1024]{1,0:T(8,128)(2,1)}, u32[]{:S(2)}, u32[]{:S(2)}) collective-permute-start(bf16[400,1024]{1,0:T(8,128)(2,1)} %pad_maximum_fusion.2), channel_id=1, source_target_pairs={{0,2},{2,0},{1,3},{3,1},{4,6},{6,4},{5,7},{7,5},{8,10},{10,8},{9,1... | collective-permute-start | bytes 2457608 | tf_op jit(solution)/shard_map/ppermute | solution.py:80
  8.8 1.4 broadcast_select_fusion
  10.2 21.3 %collective-permute-done.1 = bf16[384,256]{1,0:T(8,128)(2,1)S(1)} collective-permute-done((bf16[384,256]{1,0:T(8,128)(2,1)S(1)}, bf16[384,256]{1,0:T(8,128)(2,1)S(1)}, u32[]{:S(2)}, u32[]{:S(2)}) %collective-permute-start.1) | collective-permute-done | bytes 196640 | tf_op jit(solution)/shard_map/ppermute | solution.py:46
  33.7 1.7 collective-permute-start.2
  35.4 1.3 fusion.43
  36.7 1.5 collective-permute-start.15
  38.7 6.2 %collective-permute-done.2 = bf16[768,256]{1,0:T(8,128)(2,1)} collective-permute-done((bf16[768,256]{1,0:T(8,128)(2,1)}, bf16[768,256]{1,0:T(8,128)(2,1)}, u32[]{:S(2)}, u32[]{:S(2)}) %collective-permute-start.2) | collective-permute-done | bytes 393248 | tf_op jit(solution)/shard_map/ppermute | solution.py:60
  44.9 1.6 collective-permute-start.4
  47.5 1.6 fusion.47
  49.1 6.2 %collective-permute-done.4 = bf16[768,256]{1,0:T(8,128)(2,1)} collective-permute-done((bf16[768,256]{1,0:T(8,128)(2,1)}, bf16[768,256]{1,0:T(8,128)(2,1)}, u32[]{:S(2)}, u32[]{:S(2)}) %collective-permute-start.4) | collective-permute-done | bytes 393248 | tf_op jit(solution)/shard_map/ppermute | solution.py:26
  55.3 2.4 %collective-permute-start.6 = (bf16[768,256]{1,0:T(8,128)(2,1)}, bf16[768,256]{1,0:T(8,128)(2,1)}, u32[]{:S(2)}, u32[]{:S(2)}) collective-permute-start(bf16[768,256]{1,0:T(8,128)(2,1)} %pad_maximum_fusion.4), channel_id=1, source_target_pairs={{0,8},{4,12},{8,0},{12,4},{1,9},{5,13},{9,1},{13,5},{2,10},{6,14},... | collective-permute-start | bytes 1179656 | tf_op jit(solution)/shard_map/ppermute | solution.py:26
  58.7 1.4 collective-permute-start.8
  60.1 1.5 collective-permute-start.5
  61.6 1.6 slice_dynamic-update-slice_fusion.12
  63.2 1.3 fusion.46
  65.7 1.3 fusion.45
  68.3 14.9 %collective-permute-done.6 = bf16[768,256]{1,0:T(8,128)(2,1)} collective-permute-done((bf16[768,256]{1,0:T(8,128)(2,1)}, bf16[768,256]{1,0:T(8,128)(2,1)}, u32[]{:S(2)}, u32[]{:S(2)}) %collective-permute-start.6) | collective-permute-done | bytes 393248 | tf_op jit(solution)/shard_map/ppermute | solution.py:26
  83.3 1.5 collective-permute-start.7
  86.8 1.6 slice_dynamic-update-slice_fusion.11
  89.3 6.1 %collective-permute-done.7 = bf16[768,256]{1,0:T(8,128)(2,1)S(1)} collective-permute-done((bf16[768,256]{1,0:T(8,128)(2,1)}, bf16[768,256]{1,0:T(8,128)(2,1)S(1)}, u32[]{:S(2)}, u32[]{:S(2)}) %collective-permute-start.7) | collective-permute-done | bytes 393248 | tf_op jit(solution)/shard_map/ppermute | solution.py:60
  95.4 1.6 slice_dynamic-update-slice_fusion.10
  97.7 1.6 slice_dynamic-update-slice_fusion.8
  100.3 3.2 %collective-permute-done.9 = bf16[768,256]{1,0:T(8,128)(2,1)S(1)} collective-permute-done((bf16[768,256]{1,0:T(8,128)(2,1)}, bf16[768,256]{1,0:T(8,128)(2,1)S(1)}, u32[]{:S(2)}, u32[]{:S(2)}) %collective-permute-start.9) | collective-permute-done | bytes 393248 | tf_op jit(solution)/shard_map/ppermute | solution.py:60
  104.1 1.9 convolution_convert_fusion.6
  106.0 1.8 convolution_convert_fusion.4
  107.9 1.8 convolution_convert_fusion.5
  113.6 1.7 fusion.5
  115.3 1.7 fusion.4
  123.6 5.9 %multiply_reduce_fusion = f32[1024]{0:T(1024)S(1)} fusion(bf16[1536,512]{1,0:T(8,128)(2,1)} %collective-permute-done.13, bf16[384,512]{1,0:T(8,128)(2,1)} %copy-done.8, bf16[384,512]{1,0:T(8,128)(2,1)S(1)} %convolution_convert_fusion.4, bf16[384,512]{1,0:T(8,128)(2,1)} %copy-done.7, bf16[384,512]{1,0:T(8,128)(2,1)S(1)} %copy-done.6), kind=kLoop, calls=%fused_computation | loop fusion | flops 18873344 | bytes 3149824 | tf_op jit(solution)/shard_map/reduce_sum | solution.py:92
  129.7 3.4 %fusion.41 = f32[1024,512]{1,0:T(8,128)S(1)} fusion(bf16[1536,512]{1,0:T(8,128)(2,1)S(1)} %copy-done.10, bf16[1536,512]{1,0:T(8,128)(2,1)} %collective-permute-done.13, bf16[384,512]{1,0:T(8,128)(2,1)} %copy-done.8, bf16[384,512]{1,0:T(8,128)(2,1)S(1)} %convolution_convert_fusion.4, bf16[384,512]{1,0:T(8,128)(2,1)} %copy-done.7, ...), kind=kOutput, calls=%fused_computation.117 | convolution fusion | flops 1626341376 | bytes 6815744 | tf_op jit(solution)/shard_map/dot_general | solution.py:94
  133.1 1.3 copy-done.14
  135.4 7.4 %collective-permute-start.19 = (bf16[272,512]{1,0:T(8,128)(2,1)}, bf16[272,512]{1,0:T(8,128)(2,1)S(1)}, u32[]{:S(2)}, u32[]{:S(2)}) collective-permute-start(bf16[272,512]{1,0:T(8,128)(2,1)} %fusion.15), channel_id=1, source_target_pairs={{0,4},{4,0},{8,12},{12,8},{1,5},{5,1},{9,13},{13,9},{2,6},{6,2},{1... | collective-permute-start | bytes 835592 | tf_op jit(solution)/shard_map/ppermute | solution.py:26
  143.6 3.4 %collective-permute-start.21 = (bf16[272,512]{1,0:T(8,128)(2,1)}, bf16[272,512]{1,0:T(8,128)(2,1)S(1)}, u32[]{:S(2)}, u32[]{:S(2)}) collective-permute-start(bf16[272,512]{1,0:T(8,128)(2,1)} %fusion.17), channel_id=1, source_target_pairs={{0,12},{4,8},{8,4},{12,0},{1,13},{5,9},{9,5},{13,1},{2,14},{6,10},... | collective-permute-start | bytes 835592 | tf_op jit(solution)/shard_map/ppermute | solution.py:26
  148.6 1.9 collective-permute-done.19
  152.2 7.8 %collective-permute-done.21 = bf16[272,512]{1,0:T(8,128)(2,1)S(1)} collective-permute-done((bf16[272,512]{1,0:T(8,128)(2,1)}, bf16[272,512]{1,0:T(8,128)(2,1)S(1)}, u32[]{:S(2)}, u32[]{:S(2)}) %collective-permute-start.21) | collective-permute-done | bytes 278560 | tf_op jit(solution)/shard_map/ppermute | solution.py:26
  160.7 10.4 %collective-permute-done.20 = bf16[272,512]{1,0:T(8,128)(2,1)} collective-permute-done((bf16[272,512]{1,0:T(8,128)(2,1)}, bf16[272,512]{1,0:T(8,128)(2,1)}, u32[]{:S(2)}, u32[]{:S(2)}) %collective-permute-start.20) | collective-permute-done | bytes 278560 | tf_op jit(solution)/shard_map/ppermute | solution.py:26
  174.2 1.3 fusion.49
  180.2 2.4 %constant_dynamic-update-slice_fusion.3 = (bf16[1024,512]{1,0:T(8,128)(2,1)S(1)}, bf16[256,512]{1,0:T(8,128)(2,1)}) fusion(bf16[1024,512]{1,0:T(8,128)(2,1)S(1)} %broadcast.35, s32[]{:T(128)S(6)} %select_n.148, f32[512]{0:T(512)S(1)} %bitcast.44, f32[256]{0:T(256)S(1)} %add_divide_fusion, f32[]{:T(128)S(6)} %add.317, f32[272,512]{1,0:T(8,128)} %copy-done.2, ...), kind=kLoop, calls=%fused_computation.82 | loop fusion | flops 1048576 | bytes 2624520 | tf_op jit(solution)/shard_map/dynamic_update_slice | solution.py:127
  182.6 3.2 %collective-permute-start.23 = (bf16[256,512]{1,0:T(8,128)(2,1)}, bf16[256,512]{1,0:T(8,128)(2,1)S(1)}, u32[]{:S(2)}, u32[]{:S(2)}) collective-permute-start(bf16[256,512]{1,0:T(8,128)(2,1)} %get-tuple-element.6), channel_id=1, source_target_pairs={{0,8},{4,12},{8,0},{12,4},{1,9},{5,13},{9,1},{13,5},{2,10},{6,14},... | collective-permute-start | bytes 786440 | tf_op jit(solution)/shard_map/ppermute | solution.py:26
  188.8 7.2 %collective-permute-done.22 = bf16[256,512]{1,0:T(8,128)(2,1)} collective-permute-done((bf16[256,512]{1,0:T(8,128)(2,1)}, bf16[256,512]{1,0:T(8,128)(2,1)}, u32[]{:S(2)}, u32[]{:S(2)}) %collective-permute-start.22) | collective-permute-done | bytes 262176 | tf_op jit(solution)/shard_map/ppermute | solution.py:26
  196.9 7.6 %collective-permute-done.23 = bf16[256,512]{1,0:T(8,128)(2,1)S(1)} collective-permute-done((bf16[256,512]{1,0:T(8,128)(2,1)}, bf16[256,512]{1,0:T(8,128)(2,1)S(1)}, u32[]{:S(2)}, u32[]{:S(2)}) %collective-permute-start.23) | collective-permute-done | bytes 262176 | tf_op jit(solution)/shard_map/ppermute | solution.py:26
  204.6 2.7 %convolution_convert_fusion = bf16[128,2048]{1,0:T(8,128)(2,1)} fusion(bf16[2048,512]{1,0:T(8,128)(2,1)S(1)} %slice_dynamic-update-slice_fusion, bf16[1024,512]{1,0:T(8,128)(2,1)S(1)} %constant_dynamic-update-slice_fusion, bf16[64,1024]{1,0:T(8,128)(2,1)S(1)} %get-tuple-element.23, bf16[64,1024]{1,0:T(8,128)(2,1)} %get-tuple-element.24), kind=kOutput, calls=%fused_computation.4 | convolution fusion | flops 403505152 | bytes 3932160 | tf_op jit(solution)/shard_map/dot_general | solution.py:134
  207.3 2.2 %collective-permute-done.25 = bf16[128,2048]{1,0:T(8,128)(2,1)} collective-permute-done((bf16[128,2048]{1,0:T(8,128)(2,1)}, bf16[128,2048]{1,0:T(8,128)(2,1)}, u32[]{:S(2)}, u32[]{:S(2)}) %collective-permute-start.25) | collective-permute-done | bytes 524320 | tf_op jit(solution)/shard_map/ppermute | solution.py:136
  209.5 3.1 %convolution_add_fusion = f32[128,2048]{1,0:T(8,128)} fusion(bf16[2048,512]{1,0:T(8,128)(2,1)S(1)} %slice_dynamic-update-slice_fusion, bf16[1024,512]{1,0:T(8,128)(2,1)S(1)} %constant_dynamic-update-slice_fusion, bf16[128,2048]{1,0:T(8,128)(2,1)} %collective-permute-done.25, bf16[64,1024]{1,0:T(8,128)(2,1)S(1)} %get-tuple-element.25, ...), kind=kOutput, calls=%fused_computation.3 | convolution fusion | flops 403767296 | bytes 4980736 | tf_op jit(solution)/shard_map/dot_general | solution.py:134
  213.7 1.6 collective-permute-start.26
  215.3 6.8 %collective-permute-done.26 = bf16[64,2048]{1,0:T(8,128)(2,1)S(1)} collective-permute-done((bf16[64,2048]{1,0:T(8,128)(2,1)S(1)}, bf16[64,2048]{1,0:T(8,128)(2,1)S(1)}, u32[]{:S(2)}, u32[]{:S(2)}) %collective-permute-start.26) | collective-permute-done | bytes 262176 | tf_op jit(solution)/shard_map/ppermute | solution.py:138
  222.1 1.8 fusion.12
  (141 shorter events, 36.1 us)
Async XLA Ops:
  1.8 6.6 %collective-permute-start = (bf16[320,256]{1,0:T(8,128)(2,1)S(1)}, bf16[320,256]{1,0:T(8,128)(2,1)S(1)}, u32[]{:S(2)}, u32[]{:S(2)}) collective-permute-start(bf16[320,256]{1,0:T(8,128)(2,1)S(1)} %pad_maximum_fusion.7), channel_id=1, source_target_pairs={{0,1},{1,0},{2,3},{3,2},{4,5},{5,4},{6,7},{7,6},{8,9},{9,8},{10,11... | collective-permute-start | bytes 491528 | tf_op jit(solution)/shard_map/ppermute | solution.py:42
  3.0 5.8 %copy-start.11 = (bf16[384,2048]{1,0:T(8,128)(2,1)S(1)}, bf16[384,2048]{1,0:T(8,128)(2,1)}, u32[]{:S(2)}) copy-start(bf16[384,2048]{1,0:T(8,128)(2,1)} %param.6) | copy-start | bytes 4718596
  5.6 53.1 %collective-permute-start.11 = (bf16[400,1024]{1,0:T(8,128)(2,1)}, bf16[400,1024]{1,0:T(8,128)(2,1)}, u32[]{:S(2)}, u32[]{:S(2)}) collective-permute-start(bf16[400,1024]{1,0:T(8,128)(2,1)} %pad_maximum_fusion.2), channel_id=1, source_target_pairs={{0,2},{2,0},{1,3},{3,1},{4,6},{6,4},{5,7},{7,5},{8,10},{10,8},{9,1... | collective-permute-start | bytes 2457608 | tf_op jit(solution)/shard_map/ppermute | solution.py:80
  8.1 52.0 %collective-permute-start.10 = (bf16[400,1024]{1,0:T(8,128)(2,1)}, bf16[400,1024]{1,0:T(8,128)(2,1)}, u32[]{:S(2)}, u32[]{:S(2)}) collective-permute-start(bf16[400,1024]{1,0:T(8,128)(2,1)} %pad_maximum_fusion.2), channel_id=1, source_target_pairs={{0,1},{1,0},{2,3},{3,2},{4,5},{5,4},{6,7},{7,6},{8,9},{9,8},{10,11... | collective-permute-start | bytes 2457608 | tf_op jit(solution)/shard_map/ppermute | solution.py:77
  8.5 23.0 %collective-permute-start.1 = (bf16[384,256]{1,0:T(8,128)(2,1)S(1)}, bf16[384,256]{1,0:T(8,128)(2,1)S(1)}, u32[]{:S(2)}, u32[]{:S(2)}) collective-permute-start(bf16[384,256]{1,0:T(8,128)(2,1)S(1)} %pad_maximum_fusion.6), channel_id=1, source_target_pairs={{0,2},{2,0},{1,3},{3,1},{4,6},{6,4},{5,7},{7,5},{8,10},{10,8},{9,1... | collective-permute-start | bytes 589832 | tf_op jit(solution)/shard_map/ppermute | solution.py:46
  31.5 3.8 %copy-start = (bf16[384,2048]{1,0:T(8,128)(2,1)S(1)}, bf16[384,2048]{1,0:T(8,128)(2,1)}, u32[]{:S(2)}) copy-start(bf16[384,2048]{1,0:T(8,128)(2,1)} %broadcast_select_fusion) | copy-start | bytes 4718596
  31.6 1.0 copy-start.12
  33.7 11.3 %collective-permute-start.2 = (bf16[768,256]{1,0:T(8,128)(2,1)}, bf16[768,256]{1,0:T(8,128)(2,1)}, u32[]{:S(2)}, u32[]{:S(2)}) collective-permute-start(bf16[768,256]{1,0:T(8,128)(2,1)} %pad_maximum_fusion.4), channel_id=1, source_target_pairs={{0,16},{16,0},{1,17},{17,1},{2,18},{18,2},{3,19},{19,3},{4,20},{20... | collective-permute-start | bytes 1179656 | tf_op jit(solution)/shard_map/ppermute | solution.py:60
  36.7 48.1 %collective-permute-start.15 = (bf16[192,2048]{1,0:T(8,128)(2,1)}, bf16[192,2048]{1,0:T(8,128)(2,1)}, u32[]{:S(2)}, u32[]{:S(2)}) collective-permute-start(bf16[192,2048]{1,0:T(8,128)(2,1)} %get-tuple-element.15), channel_id=1, source_target_pairs={{0,2},{2,0},{1,3},{3,1},{4,6},{6,4},{5,7},{7,5},{8,10},{10,8},{9,1... | collective-permute-start | bytes 2359304 | tf_op jit(solution)/shard_map/ppermute | solution.py:80
  38.2 47.1 %collective-permute-start.16 = (bf16[192,2048]{1,0:T(8,128)(2,1)}, bf16[192,2048]{1,0:T(8,128)(2,1)}, u32[]{:S(2)}, u32[]{:S(2)}) collective-permute-start(bf16[192,2048]{1,0:T(8,128)(2,1)} %get-tuple-element.14), channel_id=1, source_target_pairs={{0,2},{2,0},{1,3},{3,1},{4,6},{6,4},{5,7},{7,5},{8,10},{10,8},{9,1... | collective-permute-start | bytes 2359304 | tf_op jit(solution)/shard_map/ppermute | solution.py:80
  44.9 10.4 %collective-permute-start.4 = (bf16[768,256]{1,0:T(8,128)(2,1)}, bf16[768,256]{1,0:T(8,128)(2,1)}, u32[]{:S(2)}, u32[]{:S(2)}) collective-permute-start(bf16[768,256]{1,0:T(8,128)(2,1)} %pad_maximum_fusion.4), channel_id=1, source_target_pairs={{0,4},{4,0},{8,12},{12,8},{1,5},{5,1},{9,13},{13,9},{2,6},{6,2},{1... | collective-permute-start | bytes 1179656 | tf_op jit(solution)/shard_map/ppermute | solution.py:26
  55.3 28.0 %collective-permute-start.6 = (bf16[768,256]{1,0:T(8,128)(2,1)}, bf16[768,256]{1,0:T(8,128)(2,1)}, u32[]{:S(2)}, u32[]{:S(2)}) collective-permute-start(bf16[768,256]{1,0:T(8,128)(2,1)} %pad_maximum_fusion.4), channel_id=1, source_target_pairs={{0,8},{4,12},{8,0},{12,4},{1,9},{5,13},{9,1},{13,5},{2,10},{6,14},... | collective-permute-start | bytes 1179656 | tf_op jit(solution)/shard_map/ppermute | solution.py:26
  58.7 24.6 %collective-permute-start.8 = (bf16[768,256]{1,0:T(8,128)(2,1)}, bf16[768,256]{1,0:T(8,128)(2,1)}, u32[]{:S(2)}, u32[]{:S(2)}) collective-permute-start(bf16[768,256]{1,0:T(8,128)(2,1)} %pad_maximum_fusion.4), channel_id=1, source_target_pairs={{0,12},{4,8},{8,4},{12,0},{1,13},{5,9},{9,5},{13,1},{2,14},{6,10},... | collective-permute-start | bytes 1179656 | tf_op jit(solution)/shard_map/ppermute | solution.py:26
  60.1 25.2 %collective-permute-start.5 = (bf16[768,256]{1,0:T(8,128)(2,1)}, bf16[768,256]{1,0:T(8,128)(2,1)}, u32[]{:S(2)}, u32[]{:S(2)}) collective-permute-start(bf16[768,256]{1,0:T(8,128)(2,1)} %collective-permute-done.4), channel_id=1, source_target_pairs={{0,16},{16,0},{1,17},{17,1},{2,18},{18,2},{3,19},{19,3},{4,20},{20... | collective-permute-start | bytes 1179656 | tf_op jit(solution)/shard_map/ppermute | solution.py:60
  83.3 27.5 %collective-permute-start.14 = (bf16[384,2048]{1,0:T(8,128)(2,1)}, bf16[384,2048]{1,0:T(8,128)(2,1)S(1)}, u32[]{:S(2)}, u32[]{:S(2)}) collective-permute-start(bf16[384,2048]{1,0:T(8,128)(2,1)} %broadcast_select_fusion), channel_id=1, source_target_pairs={{0,1},{1,0},{2,3},{3,2},{4,5},{5,4},{6,7},{7,6},{8,9},{9,8},{10,11... | collective-permute-start | bytes 4718600 | tf_op jit(solution)/shard_map/ppermute | solution.py:78
  83.3 12.1 %collective-permute-start.7 = (bf16[768,256]{1,0:T(8,128)(2,1)}, bf16[768,256]{1,0:T(8,128)(2,1)S(1)}, u32[]{:S(2)}, u32[]{:S(2)}) collective-permute-start(bf16[768,256]{1,0:T(8,128)(2,1)} %collective-permute-done.6), channel_id=1, source_target_pairs={{0,16},{16,0},{1,17},{17,1},{2,18},{18,2},{3,19},{19,3},{4,20},{20... | collective-permute-start | bytes 1179656 | tf_op jit(solution)/shard_map/ppermute | solution.py:60
  84.8 18.7 %collective-permute-start.9 = (bf16[768,256]{1,0:T(8,128)(2,1)}, bf16[768,256]{1,0:T(8,128)(2,1)S(1)}, u32[]{:S(2)}, u32[]{:S(2)}) collective-permute-start(bf16[768,256]{1,0:T(8,128)(2,1)} %collective-permute-done.8), channel_id=1, source_target_pairs={{0,16},{16,0},{1,17},{17,1},{2,18},{18,2},{3,19},{19,3},{4,20},{20... | collective-permute-start | bytes 1179656 | tf_op jit(solution)/shard_map/ppermute | solution.py:60
  85.3 31.7 %collective-permute-start.17 = (bf16[192,2048]{1,0:T(8,128)(2,1)}, bf16[192,2048]{1,0:T(8,128)(2,1)S(1)}, u32[]{:S(2)}, u32[]{:S(2)}) collective-permute-start(bf16[192,2048]{1,0:T(8,128)(2,1)} %collective-permute-done.15), channel_id=1, source_target_pairs={{0,1},{1,0},{2,3},{3,2},{4,5},{5,4},{6,7},{7,6},{8,9},{9,8},{10,11... | collective-permute-start | bytes 2359304 | tf_op jit(solution)/shard_map/ppermute | solution.py:81
  85.3 32.3 %collective-permute-start.18 = (bf16[192,2048]{1,0:T(8,128)(2,1)}, bf16[192,2048]{1,0:T(8,128)(2,1)S(1)}, u32[]{:S(2)}, u32[]{:S(2)}) collective-permute-start(bf16[192,2048]{1,0:T(8,128)(2,1)} %collective-permute-done.16), channel_id=1, source_target_pairs={{0,1},{1,0},{2,3},{3,2},{4,5},{5,4},{6,7},{7,6},{8,9},{9,8},{10,11... | collective-permute-start | bytes 2359304 | tf_op jit(solution)/shard_map/ppermute | solution.py:81
  95.4 16.3 %collective-permute-start.12 = (bf16[400,1024]{1,0:T(8,128)(2,1)}, bf16[400,1024]{1,0:T(8,128)(2,1)S(1)}, u32[]{:S(2)}, u32[]{:S(2)}) collective-permute-start(bf16[400,1024]{1,0:T(8,128)(2,1)} %collective-permute-done.11), channel_id=1, source_target_pairs={{0,1},{1,0},{2,3},{3,2},{4,5},{5,4},{6,7},{7,6},{8,9},{9,8},{10,11... | collective-permute-start | bytes 2457608 | tf_op jit(solution)/shard_map/ppermute | solution.py:81
  104.1 1.9 copy-start.13
  106.0 6.3 %copy-start.5 = (bf16[384,512]{1,0:T(8,128)(2,1)}, bf16[384,512]{1,0:T(8,128)(2,1)S(1)}, u32[]{:S(2)}) copy-start(bf16[384,512]{1,0:T(8,128)(2,1)S(1)} %convolution_convert_fusion.6) | copy-start | bytes 1179652
  107.9 1.9 copy-start.1
  109.7 2.6 %copy-start.7 = (bf16[384,512]{1,0:T(8,128)(2,1)}, bf16[384,512]{1,0:T(8,128)(2,1)S(1)}, u32[]{:S(2)}) copy-start(bf16[384,512]{1,0:T(8,128)(2,1)S(1)} %convolution_convert_fusion.5) | copy-start | bytes 1179652
  112.3 3.0 %copy-start.8 = (bf16[384,512]{1,0:T(8,128)(2,1)}, bf16[384,512]{1,0:T(8,128)(2,1)S(1)}, u32[]{:S(2)}) copy-start(bf16[384,512]{1,0:T(8,128)(2,1)S(1)} %convolution_convert_fusion.3) | copy-start | bytes 1179652
  113.6 10.0 %collective-permute-start.13 = (bf16[1536,512]{1,0:T(8,128)(2,1)}, bf16[1536,512]{1,0:T(8,128)(2,1)}, u32[]{:S(2)}, u32[]{:S(2)}) collective-permute-start(bf16[1536,512]{1,0:T(8,128)(2,1)} %pad_maximum_fusion.1), channel_id=1, source_target_pairs={{0,1},{1,0},{2,3},{3,2},{4,5},{5,4},{6,7},{7,6},{8,9},{9,8},{10,11... | collective-permute-start | bytes 4718600 | tf_op jit(solution)/shard_map/ppermute | solution.py:88
  117.7 6.0 %copy-start.6 = (bf16[384,512]{1,0:T(8,128)(2,1)S(1)}, bf16[384,512]{1,0:T(8,128)(2,1)}, u32[]{:S(2)}) copy-start(bf16[384,512]{1,0:T(8,128)(2,1)} %copy-done.5) | copy-start | bytes 1179652
  118.3 1.2 copy-start.9
  123.6 6.1 %copy-start.10 = (bf16[1536,512]{1,0:T(8,128)(2,1)S(1)}, bf16[1536,512]{1,0:T(8,128)(2,1)}, u32[]{:S(2)}) copy-start(bf16[1536,512]{1,0:T(8,128)(2,1)} %copy-done.9) | copy-start | bytes 4718596
  133.1 1.3 copy-start.14
  135.4 15.0 %collective-permute-start.19 = (bf16[272,512]{1,0:T(8,128)(2,1)}, bf16[272,512]{1,0:T(8,128)(2,1)S(1)}, u32[]{:S(2)}, u32[]{:S(2)}) collective-permute-start(bf16[272,512]{1,0:T(8,128)(2,1)} %fusion.15), channel_id=1, source_target_pairs={{0,4},{4,0},{8,12},{12,8},{1,5},{5,1},{9,13},{13,9},{2,6},{6,2},{1... | collective-permute-start | bytes 835592 | tf_op jit(solution)/shard_map/ppermute | solution.py:26
  143.6 16.3 %collective-permute-start.21 = (bf16[272,512]{1,0:T(8,128)(2,1)}, bf16[272,512]{1,0:T(8,128)(2,1)S(1)}, u32[]{:S(2)}, u32[]{:S(2)}) collective-permute-start(bf16[272,512]{1,0:T(8,128)(2,1)} %fusion.17), channel_id=1, source_target_pairs={{0,12},{4,8},{8,4},{12,0},{1,13},{5,9},{9,5},{13,1},{2,14},{6,10},... | collective-permute-start | bytes 835592 | tf_op jit(solution)/shard_map/ppermute | solution.py:26
  147.7 38.1 %collective-permute-start.3 = (bf16[256,512]{1,0:T(8,128)(2,1)}, bf16[256,512]{1,0:T(8,128)(2,1)}, u32[]{:S(2)}, u32[]{:S(2)}) collective-permute-start(bf16[256,512]{1,0:T(8,128)(2,1)} %pad_maximum_fusion.5), channel_id=1, source_target_pairs={{0,1},{1,0},{2,3},{3,2},{4,5},{5,4},{6,7},{7,6},{8,9},{9,8},{10,11... | collective-permute-start | bytes 786440 | tf_op jit(solution)/shard_map/ppermute | solution.py:68
  148.6 22.5 %collective-permute-start.20 = (bf16[272,512]{1,0:T(8,128)(2,1)}, bf16[272,512]{1,0:T(8,128)(2,1)}, u32[]{:S(2)}, u32[]{:S(2)}) collective-permute-start(bf16[272,512]{1,0:T(8,128)(2,1)} %fusion.16), channel_id=1, source_target_pairs={{0,8},{4,12},{8,0},{12,4},{1,9},{5,13},{9,1},{13,5},{2,10},{6,14},... | collective-permute-start | bytes 835592 | tf_op jit(solution)/shard_map/ppermute | solution.py:26
  150.4 9.6 %copy-start.16 = (bf16[272,512]{1,0:T(8,128)(2,1)}, bf16[272,512]{1,0:T(8,128)(2,1)S(1)}, u32[]{:S(2)}) copy-start(bf16[272,512]{1,0:T(8,128)(2,1)S(1)} %collective-permute-done.19) | copy-start | bytes 835588
  159.9 0.7 copy-start.15
  160.0 20.1 %copy-start.2 = (f32[272,512]{1,0:T(8,128)}, f32[272,512]{1,0:T(8,128)S(1)}, u32[]{:S(2)}) copy-start(f32[272,512]{1,0:T(8,128)S(1)} %convert_element_type.189) | copy-start | bytes 1671172
  172.1 8.0 %copy-start.3 = (f32[272,512]{1,0:T(8,128)}, f32[272,512]{1,0:T(8,128)S(1)}, u32[]{:S(2)}) copy-start(f32[272,512]{1,0:T(8,128)S(1)} %convert_element_type.187) | copy-start | bytes 1671172
  173.4 0.8 copy-start.4
  182.6 13.3 %collective-permute-start.22 = (bf16[256,512]{1,0:T(8,128)(2,1)}, bf16[256,512]{1,0:T(8,128)(2,1)}, u32[]{:S(2)}, u32[]{:S(2)}) collective-permute-start(bf16[256,512]{1,0:T(8,128)(2,1)} %get-tuple-element.6), channel_id=1, source_target_pairs={{0,4},{4,0},{8,12},{12,8},{1,5},{5,1},{9,13},{13,9},{2,6},{6,2},{1... | collective-permute-start | bytes 786440 | tf_op jit(solution)/shard_map/ppermute | solution.py:26
  182.6 21.9 %collective-permute-start.23 = (bf16[256,512]{1,0:T(8,128)(2,1)}, bf16[256,512]{1,0:T(8,128)(2,1)S(1)}, u32[]{:S(2)}, u32[]{:S(2)}) collective-permute-start(bf16[256,512]{1,0:T(8,128)(2,1)} %get-tuple-element.6), channel_id=1, source_target_pairs={{0,8},{4,12},{8,0},{12,4},{1,9},{5,13},{9,1},{13,5},{2,10},{6,14},... | collective-permute-start | bytes 786440 | tf_op jit(solution)/shard_map/ppermute | solution.py:26
  186.8 17.7 %collective-permute-start.24 = (bf16[256,512]{1,0:T(8,128)(2,1)}, bf16[256,512]{1,0:T(8,128)(2,1)S(1)}, u32[]{:S(2)}, u32[]{:S(2)}) collective-permute-start(bf16[256,512]{1,0:T(8,128)(2,1)} %get-tuple-element.6), channel_id=1, source_target_pairs={{0,12},{4,8},{8,4},{12,0},{1,13},{5,9},{9,5},{13,1},{2,14},{6,10},... | collective-permute-start | bytes 786440 | tf_op jit(solution)/shard_map/ppermute | solution.py:26
  207.3 2.3 %collective-permute-start.25 = (bf16[128,2048]{1,0:T(8,128)(2,1)}, bf16[128,2048]{1,0:T(8,128)(2,1)}, u32[]{:S(2)}, u32[]{:S(2)}) collective-permute-start(bf16[128,2048]{1,0:T(8,128)(2,1)} %convolution_convert_fusion), channel_id=1, source_target_pairs={{0,1},{1,0},{2,3},{3,2},{4,5},{5,4},{6,7},{7,6},{8,9},{9,8},{10,11... | collective-permute-start | bytes 1572872 | tf_op jit(solution)/shard_map/ppermute | solution.py:136
  213.7 8.4 %collective-permute-start.26 = (bf16[64,2048]{1,0:T(8,128)(2,1)S(1)}, bf16[64,2048]{1,0:T(8,128)(2,1)S(1)}, u32[]{:S(2)}, u32[]{:S(2)}) collective-permute-start(bf16[64,2048]{1,0:T(8,128)(2,1)S(1)} %slice.342), channel_id=1, source_target_pairs={{0,2},{2,0},{1,3},{3,1},{4,6},{6,4},{5,7},{7,5},{8,10},{10,8},{9,1... | collective-permute-start | bytes 786440 | tf_op jit(solution)/shard_map/ppermute | solution.py:138

commit v2 on v0

v2 whole, which is shorter than its diff:
```python
import functools

import jax
import jax.numpy as jnp
from jax import lax
from jax.experimental import pallas as pl
from jax.experimental.pallas import tpu as pltpu
from jax.sharding import Mesh, PartitionSpec as P

damping = 0.01
bf16 = jnp.bfloat16
f32 = jnp.float32
SWAP = [(0, 1), (1, 0)]
ANY = pl.BlockSpec(memory_space=pl.ANY)
VMEM = pl.BlockSpec(memory_space=pltpu.VMEM)
SMEM = pl.BlockSpec(memory_space=pltpu.SMEM)
LIMIT = 40 * 2**20


def params():
    return pltpu.CompilerParams(vmem_limit_bytes=LIMIT)


def cost(flops, moved):
    return pl.CostEstimate(flops=flops, bytes_accessed=moved, transcendentals=0)


def shape(dims, dtype):
    return jax.ShapeDtypeStruct(dims, dtype)


def cut(x, first, size, axis=0):
    return lax.dynamic_slice_in_dim(x, first, size, axis)


def across(x, step, levels):
    return lax.ppermute(x, "level", [(i, i ^ step) for i in range(levels)])


def spread(slots, level, levels, source, height, target, sems):
    copies = []
    for i, slot in enumerate(slots):
        step, place = i // 2, i % 2
        width = slot.shape[1]
        row = pl.multiple_of((level ^ step) * height, height)
        copy = pltpu.make_async_copy(
            slot.at[pl.ds(source, height)],
            target.at[pl.ds(row, height), pl.ds(place * width, width)],
            sems.at[i],
        )
        copy.start()
        copies.append(copy)
    return copies


def turn_acts_kernel(levels, level_g, level_a, rows, where, *refs):
    slots, pieces = refs[: 2 * levels], refs[2 * levels : 2 * levels + 4]
    out, basis, held, sems, piece_sems = refs[2 * levels + 4 :]
    copies = spread(slots, where[0], levels, level_g, level_a, basis, sems)
    moves = []
    for i, piece in enumerate(pieces):
        move = pltpu.make_async_copy(piece.at[pl.ds(0, rows)], held.at[i], piece_sems.at[i])
        move.start()
        moves.append(move)
    for copy in copies:
        copy.wait()
    for i, move in enumerate(moves):
        move.wait()
        out[pl.ds(i * rows, rows)] = jnp.dot(held[i], basis[...], preferred_element_type=f32).astype(bf16)


def turn_acts(where, slots, pieces, rows, level_g, level_a):
    levels = len(slots) // 2
    width = levels * level_a
    cols = 2 * slots[0].shape[1]
    return pl.pallas_call(
        functools.partial(turn_acts_kernel, levels, level_g, level_a, rows),
        out_shape=shape((4 * rows, cols), bf16),
        in_specs=[SMEM] + [ANY] * (2 * levels + 4),
        out_specs=VMEM,
        scratch_shapes=[
            pltpu.VMEM((width, cols), bf16),
            pltpu.VMEM((4, rows, width), bf16),
            pltpu.SemaphoreType.DMA((2 * levels,)),
            pltpu.SemaphoreType.DMA((4,)),
        ],
        compiler_params=params(),
        cost_estimate=cost(8 * rows * width * cols, 8 * rows * width + 2 * width * cols),
    )(where, *slots, *pieces)


def turn_grads_kernel(levels, level_g, where, *refs):
    slots, pieces = refs[: 2 * levels], refs[2 * levels : 2 * levels + 8]
    out, basis, held, sems, piece_sems = refs[2 * levels + 8 :]
    half = pieces[0].shape[0]
    copies = spread(slots, where[0], levels, 0, level_g, basis, sems)
    moves = []
    for i, piece in enumerate(pieces):
        move = pltpu.make_async_copy(piece, held.at[pl.ds(i * half, half)], piece_sems.at[i])
        move.start()
        moves.append(move)
    for copy in copies:
        copy.wait()
    for i in range(0, 8, 2):
        moves[i].wait()
        moves[i + 1].wait()
        block = pl.ds(i * half, 2 * half)
        out[block] = jnp.dot(held[block], basis[...], preferred_element_type=f32).astype(bf16)


def turn_grads(where, slots, pieces, level_g):
    levels = len(slots) // 2
    half, width = pieces[0].shape
    cols = 2 * slots[0].shape[1]
    return pl.pallas_call(
        functools.partial(turn_grads_kernel, levels, level_g),
        out_shape=(shape((8 * half, cols), bf16), shape((width, cols), bf16)),
        in_specs=[SMEM] + [ANY] * (2 * levels + 8),
        out_specs=(VMEM, VMEM),
        scratch_shapes=[
            pltpu.VMEM((8 * half, width), bf16),
            pltpu.SemaphoreType.DMA((2 * levels,)),
            pltpu.SemaphoreType.DMA((8,)),
        ],
        compiler_params=params(),
        cost_estimate=cost(16 * half * width * cols, 16 * half * width + 4 * width * cols),
    )(where, *slots, *pieces)


def high_low(v):
    high = v.astype(bf16)
    return high, (v - high.astype(f32)).astype(bf16)


def cross_kernel(levels, rows, where, valid, mine, theirs, right, *refs):
    own, own_extra, messages = refs[0], refs[1], refs[2 : 1 + levels]
    whole, extra, swapped = refs[1 + levels :]
    level = where[0]
    width = whole.shape[0]
    chunk = width // levels
    cols = right.shape[1]
    for i, j in enumerate((1, 0, 3, 2)):
        swapped[pl.ds(i * rows, rows)] = theirs[pl.ds(j * rows, rows)]
    extra[...] = jnp.zeros_like(extra)
    turned = right[...]
    extra[0:1] = jnp.sum(jnp.square(turned.astype(f32)), axis=0, keepdims=True)
    for i, source in enumerate((mine, swapped)):
        extra[1 + i : 2 + i] = jnp.sum(jnp.square(source[...].astype(f32)), axis=0, keepdims=True)
        for j in range(2):
            part = cols // 2
            whole[pl.ds(i * cols + j * part, part)] = lax.dot_general(
                source[:, j * part : (j + 1) * part], turned, (((0,), (0,)), ((), ())), preferred_element_type=f32
            )
    extra[3:4] = jnp.full((1, cols), valid[0], f32)
    high, low = high_low(extra[...])
    own_extra[...] = extra[...]
    own[...] = whole[pl.ds(pl.multiple_of(level * chunk, chunk), chunk)]
    for step in range(1, levels):
        to = pl.multiple_of((level ^ step) * chunk, chunk)
        message = messages[step - 1]
        message[pl.ds(0, chunk)] = whole[pl.ds(to, chunk)].astype(bf16)
        message[pl.ds(chunk, 16)] = jnp.concatenate([high, low])


def cross(where, valid, mine, theirs, right, levels):
    samples, cols = right.shape
    width = 2 * mine.shape[1]
    chunk = width // levels
    return pl.pallas_call(
        functools.partial(cross_kernel, levels, samples // 4),
        out_shape=[shape((chunk, cols), f32), shape((8, cols), f32)] + [shape((chunk + 16, cols), bf16)] * (levels - 1),
        in_specs=[SMEM, SMEM, VMEM, VMEM, VMEM],
        out_specs=[VMEM] * (1 + levels),
        scratch_shapes=[
            pltpu.VMEM((width, cols), f32),
            pltpu.VMEM((8, cols), f32),
            pltpu.VMEM((samples, cols), bf16),
        ],
        compiler_params=params(),
        cost_estimate=cost(2 * samples * width * cols, 6 * samples * cols + 2 * width * cols),
    )(where, valid, mine, theirs, right)


def scale_kernel(levels, where, own, own_extra, *refs):
    messages, (out, turned) = refs[: levels - 1], refs[levels - 1 :]
    chunk, cols = own.shape
    total = own[...]
    extra = own_extra[...]
    for message in messages:
        total = total + message[pl.ds(0, chunk)].astype(f32)
        more = message[pl.ds(chunk, 16)].astype(f32)
        extra = extra + (more[0:8] + more[8:16])
    count = extra[3:4]
    lam_g = extra[0:1] / count
    turned[...] = jnp.transpose(extra / count)
    first = where[0] * chunk
    inside = pl.multiple_of(lax.rem(first, cols), chunk)
    picked = turned[pl.ds(inside, chunk)]
    lam_a = jnp.where(first < cols, picked[:, 1:2], picked[:, 2:3])
    out[...] = (total / count / (lam_a * lam_g + damping)).astype(bf16)


def scale(where, own, own_extra, messages):
    levels = len(messages) + 1
    chunk, cols = own.shape
    return pl.pallas_call(
        functools.partial(scale_kernel, levels),
        out_shape=shape((chunk, cols), bf16),
        in_specs=[SMEM] + [VMEM] * (1 + levels),
        out_specs=VMEM,
        scratch_shapes=[pltpu.VMEM((cols, 8), f32)],
        compiler_params=params(),
        cost_estimate=cost(8 * chunk * cols, 2 * levels * chunk * cols),
    )(where, own, own_extra, *messages)


def result_kernel(levels, where, *refs):
    slots = refs[:levels]
    picked, basis, sent, kept, scaled, sems = refs[levels:]
    chunk = slots[0].shape[0]
    copies = []
    for step, slot in enumerate(slots):
        row = pl.multiple_of((where[0] ^ step) * chunk, chunk)
        copy = pltpu.make_async_copy(slot, scaled.at[pl.ds(row, chunk)], sems.at[step])
        copy.start()
        copies.append(copy)
    for copy in copies:
        copy.wait()
    mid = jnp.dot(picked[...], scaled[...], preferred_element_type=f32).astype(bf16)
    half = mid.shape[0] // 2
    width = basis.shape[0]
    part = width // 4
    for j in range(4):
        columns = pl.ds(j * part, part)
        block = lax.dot_general(mid, basis[columns], (((1,), (1,)), ((), ())), preferred_element_type=f32)
        sent[:, columns] = block[:half].astype(bf16)
        kept[:, columns] = block[half:]


def result(where, slots, picked, basis):
    levels = len(slots)
    height, width = picked.shape
    wide, cols = basis.shape
    return pl.pallas_call(
        functools.partial(result_kernel, levels),
        out_shape=(shape((height // 2, wide), bf16), shape((height // 2, wide), f32)),
        in_specs=[SMEM] + [ANY] * levels + [VMEM, VMEM],
        out_specs=(VMEM, VMEM),
        scratch_shapes=[pltpu.VMEM((width, cols), bf16), pltpu.SemaphoreType.DMA((levels,))],
        compiler_params=params(),
        cost_estimate=cost(2 * height * cols * (width + wide), 2 * wide * cols + 2 * width * cols),
    )(where, *slots, picked, basis)


def gather_levels(unit, level, levels):
    if levels != 4:
        return [unit] + [across(unit, step, levels) for step in range(1, levels)]
    middle = (level == 1) | (level == 2)
    inner, outward = [(1, 2), (2, 1)], [(1, 0), (2, 3)]
    first = across(unit, 1, levels)
    third = lax.ppermute(unit, "level", inner)
    second_in = lax.ppermute(first, "level", inner)
    second_out = lax.ppermute(third, "level", outward)
    second = jnp.where(middle, second_in, second_out)
    third_out = lax.ppermute(second_in, "level", outward)
    third = jnp.where(middle, third, third_out)
    return [unit, first, second, third]


def body(acts, grads, counts, basis_a, basis_g):
    group, level, chip, core = (lax.axis_index(n) for n in ("group", "level", "chip", "core"))
    levels = lax.axis_size("level")
    rows, width_a = acts.shape
    width_g = grads.shape[1]
    rows_a, rows_g = basis_a.shape[0], basis_g.shape[0]
    part_a, part_g = width_a // 4, width_g // 8
    where = jnp.reshape(level, (1,)).astype(jnp.int32)

    def columns(y, c):
        return jnp.concatenate(
            [
                cut(basis_g, ((y * 2 + c) * 2 + group) * part_g, part_g, 1),
                cut(basis_a, (c * 2 + group) * part_a, part_a, 1),
            ]
        )

    def diagonal(x):
        return lax.ppermute(x, ("chip", "core"), [(i, 3 - i) for i in range(4)])

    blocks = jnp.stack(
        [
            columns(chip, core),
            lax.ppermute(columns(chip, 1 - core), "core", SWAP),
            lax.ppermute(columns(1 - chip, core), "chip", SWAP),
            diagonal(columns(1 - chip, 1 - core)),
        ]
    )
    blocks = [lax.dynamic_index_in_dim(blocks, j ^ (chip * 2 + core), 0, False) for j in range(4)]
    unit = jnp.concatenate([b[:rows_g] for b in blocks] + [b[rows_g:] for b in blocks])
    level_g, level_a = 4 * rows_g, 4 * rows_a

    slots = []
    for slot in gather_levels(unit, level, levels):
        slots += [slot, lax.ppermute(slot, "group", SWAP)]
    own_a = jnp.concatenate([slots[0][level_g:], slots[1][level_g:]], axis=1)
    own_a = jnp.concatenate([own_a, lax.ppermute(own_a, "core", SWAP)], axis=1)
    me = chip * 2 + core
    picked = jnp.concatenate([cut(own_a, (me ^ j) * rows_a, rows_a) for j in (3, 1, 2, 0)])

    valid = counts[0]
    keep = jnp.arange(rows, dtype=jnp.int32)[:, None] < valid
    marks = jnp.stack([valid // 16 * 16, valid % 16]).astype(bf16)
    marks = jnp.broadcast_to(jnp.pad(marks, (0, 14))[:, None], (16, width_a))
    acts = jnp.concatenate([jnp.where(keep, acts, 0), marks])
    half = rows // 2
    grads = [jnp.where(keep[:half], grads[:half], 0), jnp.where(keep[half:], grads[half:], 0)]
    ready, _ = lax.optimization_barrier(((acts, grads[0], grads[1]), unit))

    pieces_a = [acts, lax.ppermute(acts, "core", SWAP)]
    got = lax.ppermute(ready[0], "chip", SWAP)
    pieces_a += [got, lax.ppermute(got, "core", SWAP)]
    pieces_g = list(grads) + [lax.ppermute(g, "core", SWAP) for g in grads]
    far = [lax.ppermute(g, "chip", SWAP) for g in ready[1:]]
    pieces_g += far + [lax.ppermute(g, "core", SWAP) for g in far]
    valid_here = sum(p[rows, 0].astype(f32) + p[rows + 1, 0].astype(f32) for p in pieces_a)

    turned_a = turn_acts(where, slots, pieces_a, rows, level_g, level_a)
    their_a = lax.ppermute(turned_a, "core", SWAP)
    turned_g, full_g = turn_grads(where, slots, pieces_g, level_g)
    own, own_extra, *messages = cross(where, jnp.reshape(valid_here, (1,)), turned_a, their_a, turned_g, levels)

    got = [across(m, step + 1, levels) for step, m in enumerate(messages)]
    scaled = scale(where, own, own_extra, got)
    scaled_all = [scaled] + [across(scaled, step, levels) for step in range(1, levels)]

    sent, kept = result(where, scaled_all, picked, full_g)
    sent = lax.ppermute(sent, "core", SWAP).astype(f32)
    last = lax.ppermute((kept[:rows_a] + sent[:rows_a]).astype(bf16), "chip", SWAP)
    return (kept[rows_a:] + sent[rows_a:] + last.astype(f32)).astype(bf16)


def solution(mesh):
    groups, samples = mesh.shape["groups"], mesh.shape["samples"]
    grid = Mesh(mesh.devices.reshape(groups, samples // 4, 2, 2), ("group", "level", "chip", "core"))
    every = ("group", "level", "chip", "core")
    in_specs = (
        P(every, None),
        P(every, None),
        P(every),
        P(every[1:], None),
        P(every[1:], None),
    )
    return jax.shard_map(body, mesh=grid, in_specs=in_specs, out_specs=P(every, None), check_vma=False)
```

time: 331 us -> 177 us (0.53)
  waiting for transfers between devices: 213 us -> 98.6 us
  blocking collectives: 60.9 us -> 0 us
  matrix products: 37.2 us -> 0 us
  starting transfers between devices: 0.12 us -> 32.2 us
  Pallas kernels: 0 us -> 16.5 us
  local copies, waits for them, and re-layouts: 0.1 us -> 15.8 us
  between operations: 13.9 us -> 4.96 us
    all_gather x3 -> x0, waiting for transfers between devices: 171 us -> none  [the longest x1 75.9 us: body(): lax.all_gather(basis_g, 'samples', axis=0, tiled=True)]
    ppermute x0 -> x31, waiting for transfers between devices: none -> 98.6 us  [the longest x7 42.2 us: across(): return lax.ppermute(x, 'level', [(i, i ^ step) for i in range(levels)])]
    psum x1 -> x0, blocking collectives: 60.9 us -> none  [body(): lax.psum((square_a, square_g, valid.astype(jnp.float32)), 'samples')]
    reduce_scatter x1 -> x0, waiting for transfers between devices: 40.4 us -> none  [body(): lax.psum_scatter(lax.dot_general(rot_a, rot_g, (((0,), (0,)), ((), ())),...]
    dot_general x8 -> x0, matrix products: 37.2 us -> none  [the longest x3 14 us: busy(): jnp.dot(grads[first:first + block], full_g, preferred_element_type=jnp.fl...]
    ppermute x0 -> x31, starting transfers between devices: none -> 32.2 us  [the longest x7 14.8 us: across(): return lax.ppermute(x, 'level', [(i, i ^ step) for i in range(levels)])]
    pallas_call x0 -> x5, Pallas kernels: none -> 16.5 us  [the longest x1 5.59 us: turn_grads(): pl.pallas_call(functools.partial(turn_grads_kernel, levels, level_g), out...]
    unnamed x2 -> x51, local copies, waits for them, and re-layouts: 0.01 us -> 9.39 us
  transfers between devices with their start and end apart: 4 -> 31, of which waited for: 4 -> 15; matrix products, arithmetic and copies ran while one was open for 1% -> 5% of each run, Pallas kernels for 0% -> 6%
where the time goes in v2:
time: 177 us; the launch traced here: 175 us
  waiting for transfers between devices  98.6 us (56%)
  starting transfers between devices  32.2 us (18%)
  Pallas kernels  16.5 us (9%)
  local copies, waits for them, and re-layouts  15.8 us (9%)
  other arithmetic  6.62 us (4%)
  between operations  4.96 us (3%)
    ppermute x7, waiting for transfers between devices, across(): return lax.ppermute(x, 'level', [(i, i ^ step) for i in range(levels)])  42.2 us
    ppermute x7, starting transfers between devices, across(): return lax.ppermute(x, 'level', [(i, i ^ step) for i in range(levels)])  14.8 us
    ppermute x2, waiting for transfers between devices, body(): far = [lax.ppermute(g, 'chip', SWAP) for g in ready[1:]]  14.4 us
    ppermute x4, waiting for transfers between devices, body(): slots += [slot, lax.ppermute(slot, 'group', SWAP)]  12.7 us
    ppermute x1, waiting for transfers between devices, gather_levels(): second_out = lax.ppermute(third, 'level', outward)  11 us
    unnamed x51, local copies, waits for them, and re-layouts  9.39 us
    ppermute x1, waiting for transfers between devices, body(): lax.ppermute((kept[:rows_a] + sent[:rows_a]).astype(bf16), 'chip', SWAP)  7.9 us
    ppermute x1, waiting for transfers between devices, gather_levels(): third_out = lax.ppermute(second_in, 'level', outward)  5.66 us
  transfers between devices with their start and end apart: 31, of which 15 were waited for; matrix products, arithmetic and copies ran while one was open for 5% of the time, Pallas kernels for 6%

profile of v2, /device:TPU:0, one launch (start us, length us, event | category | flops | bytes accessed | tf_op | source)
XLA Modules:
  0.0 174.8 jit_solution(1387778239052281194)
XLA Ops:
  0.0 0.9 constant_dynamic-slice_fusion.8
  0.9 1.0 constant_dynamic-slice_fusion.9
  2.5 2.6 %collective-permute-start.2 = (bf16[192,256]{1,0:T(8,128)(2,1)S(1)}, bf16[192,256]{1,0:T(8,128)(2,1)S(1)}, u32[]{:S(2)}, u32[]{:S(2)}) collective-permute-start(bf16[192,256]{1,0:T(8,128)(2,1)S(1)} %get-tuple-element.58), channel_id=1, source_target_pairs={{0,2},{2,0},{1,3},{3,1},{4,6},{6,4},{5,7},{7,5},{8,10},{10,8},{9,1... | collective-permute-start | bytes 294920 | tf_op jit(solution)/shard_map/ppermute | solution.py:294
  6.2 1.4 slice_select_fusion
  7.7 1.0 collective-permute-done.2
  8.7 1.7 collective-permute-done.3
  11.9 1.6 collective-permute-start.7
  13.7 1.6 collective-permute-start.4
  15.9 7.2 %collective-permute-done.7.refs_2_ = bf16[768,256]{1,0:T(8,128)(2,1)} collective-permute-done((bf16[768,256]{1,0:T(8,128)(2,1)S(1)}, bf16[768,256]{1,0:T(8,128)(2,1)}, u32[]{:S(2)}, u32[]{:S(2)}) %collective-permute-start.7) | collective-permute-done | bytes 393248 | tf_op jit(solution)/shard_map/ppermute | solution.py:37
  23.8 1.3 collective-permute-start.11
  25.2 1.3 collective-permute-start.13
  26.5 1.7 collective-permute-start.6
  28.2 11.0 %collective-permute-done.11 = bf16[768,256]{1,0:T(8,128)(2,1)} collective-permute-done((bf16[768,256]{1,0:T(8,128)(2,1)S(1)}, bf16[768,256]{1,0:T(8,128)(2,1)}, u32[]{:S(2)}, u32[]{:S(2)}) %collective-permute-start.11) | collective-permute-done | bytes 393248 | tf_op jit(solution)/shard_map/ppermute | solution.py:263
  39.2 1.5 collective-permute-start.8
  40.7 1.0 broadcast_select_fusion.2.refs_4_
  41.7 5.7 %collective-permute-done.13 = bf16[768,256]{1,0:T(8,128)(2,1)} collective-permute-done((bf16[768,256]{1,0:T(8,128)(2,1)S(1)}, bf16[768,256]{1,0:T(8,128)(2,1)}, u32[]{:S(2)}, u32[]{:S(2)}) %collective-permute-start.13) | collective-permute-done | bytes 393248 | tf_op jit(solution)/shard_map/ppermute | solution.py:265
  47.4 1.5 collective-permute-start.12
  48.9 1.0 broadcast_select_fusion.1.refs_6_
  51.2 1.4 collective-permute-start.19
  52.6 6.9 %collective-permute-done.12.refs_5_ = bf16[768,256]{1,0:T(8,128)(2,1)S(1)} collective-permute-done((bf16[768,256]{1,0:T(8,128)(2,1)S(1)}, bf16[768,256]{1,0:T(8,128)(2,1)S(1)}, u32[]{:S(2)}, u32[]{:S(2)}) %collective-permute-start.12) | collective-permute-done | bytes 393248 | tf_op jit(solution)/shard_map/ppermute | solution.py:304
  59.4 5.8 %collective-permute-done.14.refs_7_ = bf16[768,256]{1,0:T(8,128)(2,1)S(1)} collective-permute-done((bf16[768,256]{1,0:T(8,128)(2,1)S(1)}, bf16[768,256]{1,0:T(8,128)(2,1)S(1)}, u32[]{:S(2)}, u32[]{:S(2)}) %collective-permute-start.14) | collective-permute-done | bytes 393248 | tf_op jit(solution)/shard_map/ppermute | solution.py:304
  65.3 4.6 %shard_map.55.mine = bf16[1536,512]{1,0:T(8,128)(2,1)} custom-call(s32[1]{0:T(128)} %bitcast.where, bf16[768,256]{1,0:T(8,128)(2,1)S(1)} %get-tuple-element.31.refs_0_, bf16[768,256]{1,0:T(8,128)(2,1)S(1)} %collective-permute-done.6.refs_1_, bf16[768,256]{1,0:T(8,128)(2,1)} %collective-permute-done.7.refs_2_, ...), custom_call_target="tpu_custom_call" | custom-call | flops 1610612736 | bytes 4194304 | tf_op jit(solution)/shard_map/pallas_call | solution.py:76
  71.3 13.7 %collective-permute-done.19.refs_13_ = bf16[192,2048]{1,0:T(8,128)(2,1)} collective-permute-done((bf16[192,2048]{1,0:T(8,128)(2,1)}, bf16[192,2048]{1,0:T(8,128)(2,1)}, u32[]{:S(2)}, u32[]{:S(2)}) %collective-permute-start.19) | collective-permute-done | bytes 786464 | tf_op jit(solution)/shard_map/ppermute | solution.py:323
  85.7 1.3 fusion.11
  90.0 0.9 copy-done.9
  91.0 1.0 copy-done.2
  92.0 1.0 copy-done.4
  92.9 1.0 copy-done.6
  93.9 1.0 copy-done.8
  94.9 1.1 copy-done.10
  96.1 5.6 %shard_map.56 = (bf16[1536,512]{1,0:T(8,128)(2,1)S(1)}, bf16[2048,512]{1,0:T(8,128)(2,1)S(1)}) custom-call(s32[1]{0:T(128)} %bitcast.where, bf16[768,256]{1,0:T(8,128)(2,1)S(1)} %copy-done.2, bf16[768,256]{1,0:T(8,128)(2,1)S(1)} %collective-permute-done.6.refs_1_, bf16[768,256]{1,0:T(8,128)(2,1)} %collective-permute-done.7.refs_2_, ...), custom_call_target="tpu_custom_call" | custom-call | flops 3221225472 | bytes 10485760 | tf_op jit(solution)/shard_map/pallas_call | solution.py:115
  101.7 1.2 copy-done.11
  102.9 1.3 fusion.9
  105.5 1.4 copy-done.12
  107.0 4.7 %shard_map.57 = (f32[256,512]{1,0:T(8,128)S(1)}, f32[8,512]{1,0:T(8,128)S(1)}, bf16[272,512]{1,0:T(8,128)(2,1)}, bf16[272,512]{1,0:T(8,128)(2,1)}, bf16[272,512]{1,0:T(8,128)(2,1)}) custom-call(s32[1]{0:T(128)} %bitcast.where, f32[1]{0:T(128)} %bitcast.20.valid, bf16[1536,512]{1,0:T(8,128)(2,1)} %shard_map.55.mine, ...), custom_call_target="tpu_custom_call" | custom-call | flops 1610612736 | bytes 5767168 | tf_op jit(solution)/shard_map/pallas_call | solution.py:169
  111.8 2.7 %collective-permute-start.23 = (bf16[272,512]{1,0:T(8,128)(2,1)}, bf16[272,512]{1,0:T(8,128)(2,1)S(1)}, u32[]{:S(2)}, u32[]{:S(2)}) collective-permute-start(bf16[272,512]{1,0:T(8,128)(2,1)} %get-tuple-element.24), channel_id=1, source_target_pairs={{0,8},{4,12},{8,0},{12,4},{1,9},{5,13},{9,1},{13,5},{2,10},{6,14},... | collective-permute-start | bytes 835592 | tf_op jit(solution)/shard_map/ppermute | solution.py:37
  114.6 1.4 collective-permute-start.24
  116.8 9.9 %collective-permute-done.22.refs_0_ = bf16[272,512]{1,0:T(8,128)(2,1)S(1)} collective-permute-done((bf16[272,512]{1,0:T(8,128)(2,1)}, bf16[272,512]{1,0:T(8,128)(2,1)S(1)}, u32[]{:S(2)}, u32[]{:S(2)}) %collective-permute-start.22) | collective-permute-done | bytes 278560 | tf_op jit(solution)/shard_map/ppermute | solution.py:37
  126.7 7.7 %collective-permute-done.23.refs_1_ = bf16[272,512]{1,0:T(8,128)(2,1)S(1)} collective-permute-done((bf16[272,512]{1,0:T(8,128)(2,1)}, bf16[272,512]{1,0:T(8,128)(2,1)S(1)}, u32[]{:S(2)}, u32[]{:S(2)}) %collective-permute-start.23) | collective-permute-done | bytes 278560 | tf_op jit(solution)/shard_map/ppermute | solution.py:37
  134.9 6.0 %collective-permute-start.25 = (bf16[256,512]{1,0:T(8,128)(2,1)S(1)}, bf16[256,512]{1,0:T(8,128)(2,1)S(1)}, u32[]{:S(2)}, u32[]{:S(2)}) collective-permute-start(bf16[256,512]{1,0:T(8,128)(2,1)S(1)} %shard_map.58.refs_0_), channel_id=1, source_target_pairs={{0,4},{4,0},{8,12},{12,8},{1,5},{5,1},{9,13},{13,9},{2,6},{6,2},{1... | collective-permute-start | bytes 786440 | tf_op jit(solution)/shard_map/ppermute | solution.py:37
  140.9 1.5 collective-permute-start.26
  142.3 1.4 collective-permute-start.27
  143.7 1.0 pad_maximum_fusion.1
  144.8 6.8 %collective-permute-done.25.refs_1_ = bf16[256,512]{1,0:T(8,128)(2,1)S(1)} collective-permute-done((bf16[256,512]{1,0:T(8,128)(2,1)S(1)}, bf16[256,512]{1,0:T(8,128)(2,1)S(1)}, u32[]{:S(2)}, u32[]{:S(2)}) %collective-permute-start.25) | collective-permute-done | bytes 262176 | tf_op jit(solution)/shard_map/ppermute | solution.py:37
  151.7 10.6 %collective-permute-done.26.refs_2_ = bf16[256,512]{1,0:T(8,128)(2,1)S(1)} collective-permute-done((bf16[256,512]{1,0:T(8,128)(2,1)S(1)}, bf16[256,512]{1,0:T(8,128)(2,1)S(1)}, u32[]{:S(2)}, u32[]{:S(2)}) %collective-permute-start.26) | collective-permute-done | bytes 262176 | tf_op jit(solution)/shard_map/ppermute | solution.py:37
  162.2 1.2 shard_map.59
  163.5 1.9 %collective-permute-done.29 = bf16[128,2048]{1,0:T(8,128)(2,1)S(1)} collective-permute-done((bf16[128,2048]{1,0:T(8,128)(2,1)S(1)}, bf16[128,2048]{1,0:T(8,128)(2,1)S(1)}, u32[]{:S(2)}, u32[]{:S(2)}) %collective-permute-start.29) | collective-permute-done | bytes 524320 | tf_op jit(solution)/shard_map/ppermute | solution.py:337
  166.1 7.9 %collective-permute-done.30 = bf16[64,2048]{1,0:T(8,128)(2,1)S(1)} collective-permute-done((bf16[64,2048]{1,0:T(8,128)(2,1)S(1)}, bf16[64,2048]{1,0:T(8,128)(2,1)S(1)}, u32[]{:S(2)}, u32[]{:S(2)}) %collective-permute-start.30) | collective-permute-done | bytes 262176 | tf_op jit(solution)/shard_map/ppermute | solution.py:338
  (97 shorter events, 10.9 us)
Async XLA Ops:
  0.0 6.1 %copy-start.16 = (bf16[384,1024]{1,0:T(8,128)(2,1)S(1)}, bf16[384,1024]{1,0:T(8,128)(2,1)}, u32[]{:S(2)}) copy-start(bf16[384,1024]{1,0:T(8,128)(2,1)} %param.5) | copy-start | bytes 2359300
  0.0 6.2 %copy-start.13 = (bf16[384,2048]{1,0:T(8,128)(2,1)S(1)}, bf16[384,2048]{1,0:T(8,128)(2,1)}, u32[]{:S(2)}) copy-start(bf16[384,2048]{1,0:T(8,128)(2,1)} %param.6) | copy-start | bytes 4718596
  1.9 5.7 %collective-permute-start.1 = (bf16[192,256]{1,0:T(8,128)(2,1)S(1)}, bf16[192,256]{1,0:T(8,128)(2,1)S(1)}, u32[]{:S(2)}, u32[]{:S(2)}) collective-permute-start(bf16[192,256]{1,0:T(8,128)(2,1)S(1)} %get-tuple-element.59), channel_id=1, source_target_pairs={{0,1},{1,0},{2,3},{3,2},{4,5},{5,4},{6,7},{7,6},{8,9},{9,8},{10,11... | collective-permute-start | bytes 294920 | tf_op jit(solution)/shard_map/ppermute | solution.py:293
  2.5 6.2 %collective-permute-start.2 = (bf16[192,256]{1,0:T(8,128)(2,1)S(1)}, bf16[192,256]{1,0:T(8,128)(2,1)S(1)}, u32[]{:S(2)}, u32[]{:S(2)}) collective-permute-start(bf16[192,256]{1,0:T(8,128)(2,1)S(1)} %get-tuple-element.58), channel_id=1, source_target_pairs={{0,2},{2,0},{1,3},{3,1},{4,6},{6,4},{5,7},{7,5},{8,10},{10,8},{9,1... | collective-permute-start | bytes 294920 | tf_op jit(solution)/shard_map/ppermute | solution.py:294
  5.1 5.4 %collective-permute-start.3 = (bf16[192,256]{1,0:T(8,128)(2,1)S(1)}, bf16[192,256]{1,0:T(8,128)(2,1)S(1)}, u32[]{:S(2)}, u32[]{:S(2)}) collective-permute-start(bf16[192,256]{1,0:T(8,128)(2,1)S(1)} %get-tuple-element.60), channel_id=1, source_target_pairs={{0,3},{1,2},{2,1},{3,0},{4,7},{5,6},{6,5},{7,4},{8,11},{9,10},{10,... | collective-permute-start | bytes 294920 | tf_op jit(solution)/shard_map/ppermute | solution.py:288
  11.9 53.4 %copy-start.1 = (bf16[768,256]{1,0:T(8,128)(2,1)}, bf16[768,256]{1,0:T(8,128)(2,1)S(1)}, u32[]{:S(2)}) copy-start(bf16[768,256]{1,0:T(8,128)(2,1)S(1)} %get-tuple-element.31.refs_0_) | copy-start | bytes 1179652
  11.9 11.2 %collective-permute-start.7 = (bf16[768,256]{1,0:T(8,128)(2,1)S(1)}, bf16[768,256]{1,0:T(8,128)(2,1)}, u32[]{:S(2)}, u32[]{:S(2)}) collective-permute-start(bf16[768,256]{1,0:T(8,128)(2,1)S(1)} %get-tuple-element.31.refs_0_), channel_id=1, source_target_pairs={{0,4},{4,0},{8,12},{12,8},{1,5},{5,1},{9,13},{13,9},{2,6},{6,2},{1... | collective-permute-start | bytes 1179656 | tf_op jit(solution)/shard_map/ppermute | solution.py:37
  13.7 27.0 %collective-permute-start.4 = (bf16[400,1024]{1,0:T(8,128)(2,1)S(1)}, bf16[400,1024]{1,0:T(8,128)(2,1)S(1)}, u32[]{:S(2)}, u32[]{:S(2)}) collective-permute-start(bf16[400,1024]{1,0:T(8,128)(2,1)S(1)} %pad_maximum_fusion.refs_8_), channel_id=1, source_target_pairs={{0,2},{2,0},{1,3},{3,1},{4,6},{6,4},{5,7},{7,5},{8,10},{10,8},{9,1... | collective-permute-start | bytes 2457608 | tf_op jit(solution)/shard_map/ppermute | solution.py:320
  15.2 8.5 %collective-permute-start.10 = (bf16[768,256]{1,0:T(8,128)(2,1)S(1)}, bf16[768,256]{1,0:T(8,128)(2,1)S(1)}, u32[]{:S(2)}, u32[]{:S(2)}) collective-permute-start(bf16[768,256]{1,0:T(8,128)(2,1)S(1)} %get-tuple-element.31.refs_0_), channel_id=1, source_target_pairs={{4,8},{8,4},{5,9},{9,5},{6,10},{10,6},{7,11},{11,7},{20,24},{24,20... | collective-permute-start | bytes 1179656 | tf_op jit(solution)/shard_map/ppermute | solution.py:261
  23.1 2.1 %collective-permute-start.9 = (bf16[768,256]{1,0:T(8,128)(2,1)}, bf16[768,256]{1,0:T(8,128)(2,1)S(1)}, u32[]{:S(2)}, u32[]{:S(2)}) collective-permute-start(bf16[768,256]{1,0:T(8,128)(2,1)} %collective-permute-done.7.refs_2_), channel_id=1, source_target_pairs={{4,8},{8,4},{5,9},{9,5},{6,10},{10,6},{7,11},{11,7},{20,24},{24,20... | collective-permute-start | bytes 1179656 | tf_op jit(solution)/shard_map/ppermute | solution.py:262
  23.8 16.9 %copy-start.17 = (bf16[768,256]{1,0:T(8,128)(2,1)}, bf16[768,256]{1,0:T(8,128)(2,1)S(1)}, u32[]{:S(2)}) copy-start(bf16[768,256]{1,0:T(8,128)(2,1)S(1)} %collective-permute-done.10) | copy-start | bytes 1179652
  23.8 15.4 %collective-permute-start.11 = (bf16[768,256]{1,0:T(8,128)(2,1)S(1)}, bf16[768,256]{1,0:T(8,128)(2,1)}, u32[]{:S(2)}, u32[]{:S(2)}) collective-permute-start(bf16[768,256]{1,0:T(8,128)(2,1)S(1)} %collective-permute-done.10), channel_id=1, source_target_pairs={{4,0},{8,12},{5,1},{9,13},{6,2},{10,14},{7,3},{11,15},{20,16},{24,... | collective-permute-start | bytes 1179656 | tf_op jit(solution)/shard_map/ppermute | solution.py:263
  25.1 25.4 %collective-permute-start = (bf16[400,1024]{1,0:T(8,128)(2,1)S(1)}, bf16[400,1024]{1,0:T(8,128)(2,1)}, u32[]{:S(2)}, u32[]{:S(2)}) collective-permute-start(bf16[400,1024]{1,0:T(8,128)(2,1)S(1)} %pad_maximum_fusion.refs_8_), channel_id=1, source_target_pairs={{0,1},{1,0},{2,3},{3,2},{4,5},{5,4},{6,7},{7,6},{8,9},{9,8},{10,11... | collective-permute-start | bytes 2457608 | tf_op jit(solution)/shard_map/ppermute | solution.py:319
  25.2 22.2 %collective-permute-start.13 = (bf16[768,256]{1,0:T(8,128)(2,1)S(1)}, bf16[768,256]{1,0:T(8,128)(2,1)}, u32[]{:S(2)}, u32[]{:S(2)}) collective-permute-start(bf16[768,256]{1,0:T(8,128)(2,1)S(1)} %collective-permute-done.9), channel_id=1, source_target_pairs={{4,0},{8,12},{5,1},{9,13},{6,2},{10,14},{7,3},{11,15},{20,16},{24,... | collective-permute-start | bytes 1179656 | tf_op jit(solution)/shard_map/ppermute | solution.py:265
  26.5 23.4 %collective-permute-start.6 = (bf16[768,256]{1,0:T(8,128)(2,1)S(1)}, bf16[768,256]{1,0:T(8,128)(2,1)S(1)}, u32[]{:S(2)}, u32[]{:S(2)}) collective-permute-start(bf16[768,256]{1,0:T(8,128)(2,1)S(1)} %get-tuple-element.31.refs_0_), channel_id=1, source_target_pairs={{0,16},{16,0},{1,17},{17,1},{2,18},{18,2},{3,19},{19,3},{4,20},{20... | collective-permute-start | bytes 1179656 | tf_op jit(solution)/shard_map/ppermute | solution.py:304
  39.2 12.0 %collective-permute-start.8 = (bf16[768,256]{1,0:T(8,128)(2,1)}, bf16[768,256]{1,0:T(8,128)(2,1)S(1)}, u32[]{:S(2)}, u32[]{:S(2)}) collective-permute-start(bf16[768,256]{1,0:T(8,128)(2,1)} %collective-permute-done.7.refs_2_), channel_id=1, source_target_pairs={{0,16},{16,0},{1,17},{17,1},{2,18},{18,2},{3,19},{19,3},{4,20},{20... | collective-permute-start | bytes 1179656 | tf_op jit(solution)/shard_map/ppermute | solution.py:304
  40.7 24.6 %collective-permute-start.5 = (bf16[400,1024]{1,0:T(8,128)(2,1)S(1)}, bf16[400,1024]{1,0:T(8,128)(2,1)S(1)}, u32[]{:S(2)}, u32[]{:S(2)}) collective-permute-start(bf16[400,1024]{1,0:T(8,128)(2,1)S(1)} %collective-permute-done.4.refs_10_), channel_id=1, source_target_pairs={{0,1},{1,0},{2,3},{3,2},{4,5},{5,4},{6,7},{7,6},{8,9},{9,8},{10,11... | collective-permute-start | bytes 2457608 | tf_op jit(solution)/shard_map/ppermute | solution.py:321
  47.4 12.1 %collective-permute-start.12 = (bf16[768,256]{1,0:T(8,128)(2,1)S(1)}, bf16[768,256]{1,0:T(8,128)(2,1)S(1)}, u32[]{:S(2)}, u32[]{:S(2)}) collective-permute-start(bf16[768,256]{1,0:T(8,128)(2,1)S(1)} %broadcast_select_fusion.2.refs_4_), channel_id=1, source_target_pairs={{0,16},{16,0},{1,17},{17,1},{2,18},{18,2},{3,19},{19,3},{4,20},{20... | collective-permute-start | bytes 1179656 | tf_op jit(solution)/shard_map/ppermute | solution.py:304
  49.9 15.3 %collective-permute-start.14 = (bf16[768,256]{1,0:T(8,128)(2,1)S(1)}, bf16[768,256]{1,0:T(8,128)(2,1)S(1)}, u32[]{:S(2)}, u32[]{:S(2)}) collective-permute-start(bf16[768,256]{1,0:T(8,128)(2,1)S(1)} %broadcast_select_fusion.1.refs_6_), channel_id=1, source_target_pairs={{0,16},{16,0},{1,17},{17,1},{2,18},{18,2},{3,19},{19,3},{4,20},{20... | collective-permute-start | bytes 1179656 | tf_op jit(solution)/shard_map/ppermute | solution.py:304
  50.5 20.8 %collective-permute-start.18 = (bf16[192,2048]{1,0:T(8,128)(2,1)}, bf16[192,2048]{1,0:T(8,128)(2,1)}, u32[]{:S(2)}, u32[]{:S(2)}) collective-permute-start(bf16[192,2048]{1,0:T(8,128)(2,1)} %get-tuple-element.18.refs_8_), channel_id=1, source_target_pairs={{0,2},{2,0},{1,3},{3,1},{4,6},{6,4},{5,7},{7,5},{8,10},{10,8},{9,1... | collective-permute-start | bytes 2359304 | tf_op jit(solution)/shard_map/ppermute | solution.py:323
  51.2 18.8 %copy-start.3 = (bf16[768,256]{1,0:T(8,128)(2,1)}, bf16[768,256]{1,0:T(8,128)(2,1)S(1)}, u32[]{:S(2)}) copy-start(bf16[768,256]{1,0:T(8,128)(2,1)S(1)} %collective-permute-done.8.refs_3_) | copy-start | bytes 1179652
  51.2 33.9 %collective-permute-start.19 = (bf16[192,2048]{1,0:T(8,128)(2,1)}, bf16[192,2048]{1,0:T(8,128)(2,1)}, u32[]{:S(2)}, u32[]{:S(2)}) collective-permute-start(bf16[192,2048]{1,0:T(8,128)(2,1)} %get-tuple-element.19.refs_9_), channel_id=1, source_target_pairs={{0,2},{2,0},{1,3},{3,1},{4,6},{6,4},{5,7},{7,5},{8,10},{10,8},{9,1... | collective-permute-start | bytes 2359304 | tf_op jit(solution)/shard_map/ppermute | solution.py:323
  59.4 10.5 %copy-start.5 = (bf16[768,256]{1,0:T(8,128)(2,1)}, bf16[768,256]{1,0:T(8,128)(2,1)S(1)}, u32[]{:S(2)}) copy-start(bf16[768,256]{1,0:T(8,128)(2,1)S(1)} %collective-permute-done.12.refs_5_) | copy-start | bytes 1179652
  65.3 4.7 %copy-start.7 = (bf16[768,256]{1,0:T(8,128)(2,1)}, bf16[768,256]{1,0:T(8,128)(2,1)S(1)}, u32[]{:S(2)}) copy-start(bf16[768,256]{1,0:T(8,128)(2,1)S(1)} %collective-permute-done.14.refs_7_) | copy-start | bytes 1179652
  65.3 4.7 %copy-start = (bf16[400,1024]{1,0:T(8,128)(2,1)}, bf16[400,1024]{1,0:T(8,128)(2,1)S(1)}, u32[]{:S(2)}) copy-start(bf16[400,1024]{1,0:T(8,128)(2,1)S(1)} %collective-permute-done.5.refs_11_) | copy-start | bytes 2457604
  70.0 35.5 %collective-permute-start.15 = (bf16[1536,512]{1,0:T(8,128)(2,1)}, bf16[1536,512]{1,0:T(8,128)(2,1)}, u32[]{:S(2)}, u32[]{:S(2)}) collective-permute-start(bf16[1536,512]{1,0:T(8,128)(2,1)} %shard_map.55.mine), channel_id=1, source_target_pairs={{0,1},{1,0},{2,3},{3,2},{4,5},{5,4},{6,7},{7,6},{8,9},{9,8},{10,11... | collective-permute-start | bytes 4718600 | tf_op jit(solution)/shard_map/ppermute | solution.py:328
  70.1 19.9 %collective-permute-start.16 = (bf16[192,2048]{1,0:T(8,128)(2,1)}, bf16[192,2048]{1,0:T(8,128)(2,1)S(1)}, u32[]{:S(2)}, u32[]{:S(2)}) collective-permute-start(bf16[192,2048]{1,0:T(8,128)(2,1)} %get-tuple-element.18.refs_8_), channel_id=1, source_target_pairs={{0,1},{1,0},{2,3},{3,2},{4,5},{5,4},{6,7},{7,6},{8,9},{9,8},{10,11... | collective-permute-start | bytes 2359304 | tf_op jit(solution)/shard_map/ppermute | solution.py:322
  70.6 20.4 %collective-permute-start.17 = (bf16[192,2048]{1,0:T(8,128)(2,1)}, bf16[192,2048]{1,0:T(8,128)(2,1)}, u32[]{:S(2)}, u32[]{:S(2)}) collective-permute-start(bf16[192,2048]{1,0:T(8,128)(2,1)} %get-tuple-element.19.refs_9_), channel_id=1, source_target_pairs={{0,1},{1,0},{2,3},{3,2},{4,5},{5,4},{6,7},{7,6},{8,9},{9,8},{10,11... | collective-permute-start | bytes 2359304 | tf_op jit(solution)/shard_map/ppermute | solution.py:322
  71.3 19.6 %collective-permute-start.20 = (bf16[192,2048]{1,0:T(8,128)(2,1)}, bf16[192,2048]{1,0:T(8,128)(2,1)}, u32[]{:S(2)}, u32[]{:S(2)}) collective-permute-start(bf16[192,2048]{1,0:T(8,128)(2,1)} %collective-permute-done.18.refs_12_), channel_id=1, source_target_pairs={{0,1},{1,0},{2,3},{3,2},{4,5},{5,4},{6,7},{7,6},{8,9},{9,8},{10,11... | collective-permute-start | bytes 2359304 | tf_op jit(solution)/shard_map/ppermute | solution.py:324
  85.0 5.9 %collective-permute-start.21 = (bf16[192,2048]{1,0:T(8,128)(2,1)}, bf16[192,2048]{1,0:T(8,128)(2,1)}, u32[]{:S(2)}, u32[]{:S(2)}) collective-permute-start(bf16[192,2048]{1,0:T(8,128)(2,1)} %collective-permute-done.19.refs_13_), channel_id=1, source_target_pairs={{0,1},{1,0},{2,3},{3,2},{4,5},{5,4},{6,7},{7,6},{8,9},{9,8},{10,11... | collective-permute-start | bytes 2359304 | tf_op jit(solution)/shard_map/ppermute | solution.py:324
  94.9 1.1 copy-start.10
  101.7 1.2 copy-start.11
  105.5 1.4 copy-start.12
  106.9 9.1 %copy-start.14 = (bf16[256,256]{1,0:T(8,128)(2,1)S(1)}, bf16[256,256]{1,0:T(8,128)(2,1)}, u32[]{:S(2)}) copy-start(bf16[256,256]{1,0:T(8,128)(2,1)} %slice.141) | copy-start | bytes 393220
  106.9 9.1 %copy-start.18 = (bf16[64,256]{1,0:T(8,128)(2,1)S(1)}, bf16[64,256]{1,0:T(8,128)(2,1)}, u32[]{:S(2)}) copy-start(bf16[64,256]{1,0:T(8,128)(2,1)} %get-tuple-element.34) | copy-start | bytes 98308
  107.0 9.1 %copy-start.20 = (bf16[64,256]{1,0:T(8,128)(2,1)S(1)}, bf16[64,256]{1,0:T(8,128)(2,1)}, u32[]{:S(2)}) copy-start(bf16[64,256]{1,0:T(8,128)(2,1)} %get-tuple-element.32) | copy-start | bytes 98308
  111.6 15.1 %collective-permute-start.22 = (bf16[272,512]{1,0:T(8,128)(2,1)}, bf16[272,512]{1,0:T(8,128)(2,1)S(1)}, u32[]{:S(2)}, u32[]{:S(2)}) collective-permute-start(bf16[272,512]{1,0:T(8,128)(2,1)} %get-tuple-element.23), channel_id=1, source_target_pairs={{0,4},{4,0},{8,12},{12,8},{1,5},{5,1},{9,13},{13,9},{2,6},{6,2},{1... | collective-permute-start | bytes 835592 | tf_op jit(solution)/shard_map/ppermute | solution.py:37
  111.8 22.6 %collective-permute-start.23 = (bf16[272,512]{1,0:T(8,128)(2,1)}, bf16[272,512]{1,0:T(8,128)(2,1)S(1)}, u32[]{:S(2)}, u32[]{:S(2)}) collective-permute-start(bf16[272,512]{1,0:T(8,128)(2,1)} %get-tuple-element.24), channel_id=1, source_target_pairs={{0,8},{4,12},{8,0},{12,4},{1,9},{5,13},{9,1},{13,5},{2,10},{6,14},... | collective-permute-start | bytes 835592 | tf_op jit(solution)/shard_map/ppermute | solution.py:37
  114.6 19.8 %collective-permute-start.24 = (bf16[272,512]{1,0:T(8,128)(2,1)}, bf16[272,512]{1,0:T(8,128)(2,1)S(1)}, u32[]{:S(2)}, u32[]{:S(2)}) collective-permute-start(bf16[272,512]{1,0:T(8,128)(2,1)} %get-tuple-element.25), channel_id=1, source_target_pairs={{0,12},{4,8},{8,4},{12,0},{1,13},{5,9},{9,5},{13,1},{2,14},{6,10},... | collective-permute-start | bytes 835592 | tf_op jit(solution)/shard_map/ppermute | solution.py:37
  116.8 27.0 %collective-permute-start.28 = (bf16[256,512]{1,0:T(8,128)(2,1)}, bf16[256,512]{1,0:T(8,128)(2,1)}, u32[]{:S(2)}, u32[]{:S(2)}) collective-permute-start(bf16[256,512]{1,0:T(8,128)(2,1)} %pad_maximum_fusion.4), channel_id=1, source_target_pairs={{0,1},{1,0},{2,3},{3,2},{4,5},{5,4},{6,7},{7,6},{8,9},{9,8},{10,11... | collective-permute-start | bytes 786440 | tf_op jit(solution)/shard_map/ppermute | solution.py:306
  116.8 27.0 %copy-start.15 = (bf16[256,256]{1,0:T(8,128)(2,1)S(1)}, bf16[256,256]{1,0:T(8,128)(2,1)}, u32[]{:S(2)}) copy-start(bf16[256,256]{1,0:T(8,128)(2,1)} %slice.141) | copy-start | bytes 393220
  116.8 27.0 %copy-start.19 = (bf16[64,256]{1,0:T(8,128)(2,1)S(1)}, bf16[64,256]{1,0:T(8,128)(2,1)}, u32[]{:S(2)}) copy-start(bf16[64,256]{1,0:T(8,128)(2,1)} %get-tuple-element.34) | copy-start | bytes 98308
  116.8 27.0 %copy-start.21 = (bf16[64,256]{1,0:T(8,128)(2,1)S(1)}, bf16[64,256]{1,0:T(8,128)(2,1)}, u32[]{:S(2)}) copy-start(bf16[64,256]{1,0:T(8,128)(2,1)} %get-tuple-element.32) | copy-start | bytes 98308
  134.9 16.8 %collective-permute-start.25 = (bf16[256,512]{1,0:T(8,128)(2,1)S(1)}, bf16[256,512]{1,0:T(8,128)(2,1)S(1)}, u32[]{:S(2)}, u32[]{:S(2)}) collective-permute-start(bf16[256,512]{1,0:T(8,128)(2,1)S(1)} %shard_map.58.refs_0_), channel_id=1, source_target_pairs={{0,4},{4,0},{8,12},{12,8},{1,5},{5,1},{9,13},{13,9},{2,6},{6,2},{1... | collective-permute-start | bytes 786440 | tf_op jit(solution)/shard_map/ppermute | solution.py:37
  140.9 21.4 %collective-permute-start.26 = (bf16[256,512]{1,0:T(8,128)(2,1)S(1)}, bf16[256,512]{1,0:T(8,128)(2,1)S(1)}, u32[]{:S(2)}, u32[]{:S(2)}) collective-permute-start(bf16[256,512]{1,0:T(8,128)(2,1)S(1)} %shard_map.58.refs_0_), channel_id=1, source_target_pairs={{0,8},{4,12},{8,0},{12,4},{1,9},{5,13},{9,1},{13,5},{2,10},{6,14},... | collective-permute-start | bytes 786440 | tf_op jit(solution)/shard_map/ppermute | solution.py:37
  142.3 19.9 %collective-permute-start.27 = (bf16[256,512]{1,0:T(8,128)(2,1)S(1)}, bf16[256,512]{1,0:T(8,128)(2,1)S(1)}, u32[]{:S(2)}, u32[]{:S(2)}) collective-permute-start(bf16[256,512]{1,0:T(8,128)(2,1)S(1)} %shard_map.58.refs_0_), channel_id=1, source_target_pairs={{0,12},{4,8},{8,4},{12,0},{1,13},{5,9},{9,5},{13,1},{2,14},{6,10},... | collective-permute-start | bytes 786440 | tf_op jit(solution)/shard_map/ppermute | solution.py:37
  163.4 2.0 %collective-permute-start.29 = (bf16[128,2048]{1,0:T(8,128)(2,1)S(1)}, bf16[128,2048]{1,0:T(8,128)(2,1)S(1)}, u32[]{:S(2)}, u32[]{:S(2)}) collective-permute-start(bf16[128,2048]{1,0:T(8,128)(2,1)S(1)} %get-tuple-element.28), channel_id=1, source_target_pairs={{0,1},{1,0},{2,3},{3,2},{4,5},{5,4},{6,7},{7,6},{8,9},{9,8},{10,11... | collective-permute-start | bytes 1572872 | tf_op jit(solution)/shard_map/ppermute | solution.py:337
  165.6 8.4 %collective-permute-start.30 = (bf16[64,2048]{1,0:T(8,128)(2,1)S(1)}, bf16[64,2048]{1,0:T(8,128)(2,1)S(1)}, u32[]{:S(2)}, u32[]{:S(2)}) collective-permute-start(bf16[64,2048]{1,0:T(8,128)(2,1)S(1)} %fusion), channel_id=1, source_target_pairs={{0,2},{2,0},{1,3},{3,1},{4,6},{6,4},{5,7},{7,5},{8,10},{10,8},{9,1... | collective-permute-start | bytes 786440 | tf_op jit(solution)/shard_map/ppermute | solution.py:338
  (5 other events, 4.9 us)

commit v3 on v2

v3 whole, which is shorter than its diff:
```python
import functools

import jax
import jax.numpy as jnp
from jax import lax
from jax.experimental import pallas as pl
from jax.experimental.pallas import tpu as pltpu
from jax.sharding import Mesh, PartitionSpec as P

damping = 0.01
bf16 = jnp.bfloat16
f32 = jnp.float32
SWAP = [(0, 1), (1, 0)]
ANY = pl.BlockSpec(memory_space=pl.ANY)
VMEM = pl.BlockSpec(memory_space=pltpu.VMEM)
SMEM = pl.BlockSpec(memory_space=pltpu.SMEM)
LARGE = 60 * 2**20
MIDDLE = 26 * 2**20
SMALL = 20 * 2**20


def params(limit):
    return pltpu.CompilerParams(vmem_limit_bytes=limit)


def cost(flops, moved):
    return pl.CostEstimate(flops=flops, bytes_accessed=moved, transcendentals=0)


def shape(dims, dtype):
    return jax.ShapeDtypeStruct(dims, dtype)


def cut(x, first, size, axis=0):
    return lax.dynamic_slice_in_dim(x, first, size, axis)


def across(x, step, levels):
    return lax.ppermute(x, "level", [(i, i ^ step) for i in range(levels)])


def turn_kernel(levels, level_g, level_a, rows, where, *refs):
    slots, pieces = refs[:levels], refs[levels : levels + 4]
    out_a, out_g, basis_g, sums, basis_a, held_a, held_g, sems, piece_sems = refs[levels + 4 :]
    half, width = rows // 2, held_a.shape[2]
    part = basis_a.shape[1]
    copies = []
    for step, slot in enumerate(slots):
        at = where[0] ^ step
        for i, (first, height, target) in enumerate(((level_g, level_a, basis_a), (0, level_g, basis_g))):
            row = pl.multiple_of(at * height, height)
            copies.append(
                pltpu.make_async_copy(
                    slot.at[pl.ds(first, height)], target.at[pl.ds(row, height)], sems.at[2 * step + i]
                )
            )
    moves = []
    for i, piece in enumerate(pieces):
        moves.append(pltpu.make_async_copy(piece.at[pl.ds(0, rows + 16)], held_a.at[i], piece_sems.at[3 * i]))
        for j in range(2):
            moves.append(
                pltpu.make_async_copy(
                    piece.at[pl.ds(rows + 16 + j * half, half)],
                    held_g.at[pl.ds(i * half, half), pl.ds(j * width, width)],
                    piece_sems.at[3 * i + 1 + j],
                )
            )
    for copy in copies + moves:
        copy.start()
    for copy in copies:
        copy.wait()
    total_a = jnp.zeros((1, part), f32)
    total_g = jnp.zeros((1, part), f32)
    for i in range(4):
        moves[3 * i].wait()
        block = jnp.dot(held_a[i, :rows], basis_a[...], preferred_element_type=f32).astype(bf16).astype(f32)
        total_a = total_a + jnp.sum(jnp.square(block), axis=0, keepdims=True)
        out_a[:part, i * rows : (i + 1) * rows] = jnp.transpose(block).astype(bf16)
    for i in range(0, 4, 2):
        for j in (1, 2, 4, 5):
            moves[3 * i + j].wait()
        block = pl.ds(i * half, 2 * half)
        turned = jnp.dot(held_g[block], basis_g[...], preferred_element_type=f32).astype(bf16)
        out_g[block] = turned
        total_g = total_g + jnp.sum(jnp.square(turned.astype(f32)), axis=0, keepdims=True)
    high, low = high_low(jnp.broadcast_to(total_a, (8, part)))
    out_a[part:, :part] = jnp.concatenate([high, low])
    out_a[part:, part:] = jnp.zeros((16, 4 * rows - part), bf16)
    marks = sum(held_a[i, rows : rows + 16, :part].astype(f32) for i in range(4))
    sums[0:1] = total_g
    sums[1:2] = marks[0:1] + marks[1:2]
    sums[2:8] = jnp.zeros((6, part), f32)


def turn(where, slots, pieces, rows, level_g, level_a):
    levels = len(slots)
    width_a, width_g = levels * level_a, levels * level_g
    part = slots[0].shape[1]
    half = rows // 2
    return pl.pallas_call(
        functools.partial(turn_kernel, levels, level_g, level_a, rows),
        out_shape=(
            shape((part + 16, 4 * rows), bf16),
            shape((4 * half, part), bf16),
            shape((width_g, part), bf16),
            shape((8, part), f32),
        ),
        in_specs=[SMEM] + [ANY] * (levels + 4),
        out_specs=(VMEM,) * 4,
        scratch_shapes=[
            pltpu.VMEM((width_a, part), bf16),
            pltpu.VMEM((4, rows + 16, width_a), bf16),
            pltpu.VMEM((4 * half, width_g), bf16),
            pltpu.SemaphoreType.DMA((2 * levels,)),
            pltpu.SemaphoreType.DMA((12,)),
        ],
        compiler_params=params(MIDDLE),
        cost_estimate=cost(8 * rows * part * (width_a + width_g // 2), 8 * rows * (width_a + width_g // 2)),
    )(where, *slots, *pieces)


def high_low(v):
    high = v.astype(bf16)
    return high, (v - high.astype(f32)).astype(bf16)


def cross_kernel(levels, rows, where, *refs):
    turned_a, early, bases, pieces, sums = refs[:4], refs[4:6], refs[6:8], refs[8:12], refs[12:14]
    own, own_extra, messages = refs[14], refs[15], refs[16 : 15 + levels]
    left, right, basis, held, whole, extra, sems = refs[15 + levels :]
    half = rows // 2
    part = bases[0].shape[1]
    cols = 2 * part
    width = whole.shape[0]
    chunk = width // levels
    level = where[0]
    count = 0

    def copy(source, target):
        nonlocal count
        made = pltpu.make_async_copy(source, target, sems.at[count])
        made.start()
        count += 1
        return made

    first = [copy(b, basis.at[:, pl.ds(i * part, part)]) for i, b in enumerate(bases)]
    moves = [copy(p, held.at[pl.ds(i * half, half)]) for i, p in enumerate(pieces)]
    rest = [copy(turned_a[i], left.at[i]) for i in range(2)]
    for i in range(2):
        for j, k in enumerate((1, 0, 3, 2)):
            rest.append(
                copy(turned_a[2 + i].at[:, pl.ds(k * rows, rows)], left.at[2 + i, :, pl.ds(j * rows, rows)])
            )
    for i in range(2):
        for j in range(4):
            rest.append(
                copy(early[i].at[pl.ds(j * half, half)], right.at[pl.ds(j * rows, half), pl.ds(i * part, part)])
            )
    for made in first:
        made.wait()
    total = jnp.concatenate([sums[0][0:1], sums[1][0:1]], axis=1)
    for i in range(0, 4, 2):
        moves[i].wait()
        moves[i + 1].wait()
        block = jnp.dot(held[pl.ds(i * half, rows)], basis[...], preferred_element_type=f32).astype(bf16)
        right[pl.ds(i * rows + half, half)] = block[:half]
        right[pl.ds(i * rows + rows + half, half)] = block[half:]
        total = total + jnp.sum(jnp.square(block.astype(f32)), axis=0, keepdims=True)
    for made in rest:
        made.wait()
    extra[...] = jnp.zeros_like(extra)
    extra[0:1] = total
    for i in range(4):
        moved = rows * (i // 2)
        tail = left[i, part:, moved : moved + part].astype(f32)
        at = pl.ds((i % 2) * part, part)
        extra[1 + i // 2 : 2 + i // 2, at] = tail[0:1] + tail[8:9]
        whole[pl.ds(i * part, part)] = jnp.dot(left[i, :part], right[...], preferred_element_type=f32)
        if i < 2:
            extra[3:4, at] = sums[i][1:2]
    high, low = high_low(extra[...])
    own_extra[...] = extra[...]
    own[...] = whole[pl.ds(pl.multiple_of(level * chunk, chunk), chunk)]
    for step in range(1, levels):
        to = pl.multiple_of((level ^ step) * chunk, chunk)
        message = messages[step - 1]
        message[pl.ds(0, chunk)] = whole[pl.ds(to, chunk)].astype(bf16)
        message[pl.ds(chunk, 16)] = jnp.concatenate([high, low])


def cross(where, turned_a, early, bases, pieces, sums, rows, levels):
    width_g, part = bases[0].shape
    width = 4 * part
    cols = 2 * part
    chunk = width // levels
    return pl.pallas_call(
        functools.partial(cross_kernel, levels, rows),
        out_shape=[shape((chunk, cols), f32), shape((8, cols), f32)] + [shape((chunk + 16, cols), bf16)] * (levels - 1),
        in_specs=[SMEM] + [ANY] * 12 + [VMEM] * 2,
        out_specs=[VMEM] * (1 + levels),
        scratch_shapes=[
            pltpu.VMEM((4, part + 16, 4 * rows), bf16),
            pltpu.VMEM((4 * rows, cols), bf16),
            pltpu.VMEM((width_g, cols), bf16),
            pltpu.VMEM((2 * rows, width_g), bf16),
            pltpu.VMEM((width, cols), f32),
            pltpu.VMEM((8, cols), f32),
            pltpu.SemaphoreType.DMA((24,)),
        ],
        compiler_params=params(LARGE),
        cost_estimate=cost(4 * rows * cols * (width_g + 2 * width), 16 * rows * width),
    )(where, *turned_a, *early, *bases, *pieces, *sums)


def scale_kernel(levels, where, own, own_extra, *refs):
    messages, (out, turned) = refs[: levels - 1], refs[levels - 1 :]
    chunk, cols = own.shape
    total = own[...]
    extra = own_extra[...]
    for message in messages:
        total = total + message[pl.ds(0, chunk)].astype(f32)
        more = message[pl.ds(chunk, 16)].astype(f32)
        extra = extra + (more[0:8] + more[8:16])
    count = extra[3:4]
    lam_g = extra[0:1] / count
    turned[...] = jnp.transpose(extra / count)
    first = where[0] * chunk
    inside = pl.multiple_of(lax.rem(first, cols), chunk)
    picked = turned[pl.ds(inside, chunk)]
    lam_a = jnp.where(first < cols, picked[:, 1:2], picked[:, 2:3])
    out[...] = (total / count / (lam_a * lam_g + damping)).astype(bf16)


def scale(where, own, own_extra, messages):
    levels = len(messages) + 1
    chunk, cols = own.shape
    return pl.pallas_call(
        functools.partial(scale_kernel, levels),
        out_shape=shape((chunk, cols), bf16),
        in_specs=[SMEM] + [VMEM] * (1 + levels),
        out_specs=VMEM,
        scratch_shapes=[pltpu.VMEM((cols, 8), f32)],
        compiler_params=params(SMALL),
        cost_estimate=cost(8 * chunk * cols, 2 * levels * chunk * cols),
    )(where, own, own_extra, *messages)


def result_kernel(levels, where, *refs):
    slots = refs[:levels]
    picked, one, two, sent, kept, scaled, sems = refs[levels:]
    chunk = slots[0].shape[0]
    copies = []
    for step, slot in enumerate(slots):
        row = pl.multiple_of((where[0] ^ step) * chunk, chunk)
        copy = pltpu.make_async_copy(slot, scaled.at[pl.ds(row, chunk)], sems.at[step])
        copy.start()
        copies.append(copy)
    for copy in copies:
        copy.wait()
    mid = jnp.dot(picked[...], scaled[...], preferred_element_type=f32).astype(bf16)
    half = mid.shape[0] // 2
    wide, side = one.shape
    part = wide // 4
    for j in range(4):
        columns = pl.ds(j * part, part)
        block = sum(
            lax.dot_general(m, b[columns], (((1,), (1,)), ((), ())), preferred_element_type=f32)
            for m, b in ((mid[:, :side], one), (mid[:, side:], two))
        )
        sent[:, columns] = block[:half].astype(bf16)
        kept[:, columns] = block[half:]


def result(where, slots, picked, bases):
    levels = len(slots)
    height, width = picked.shape
    wide, cols = bases[0].shape[0], 2 * bases[0].shape[1]
    return pl.pallas_call(
        functools.partial(result_kernel, levels),
        out_shape=(shape((height // 2, wide), bf16), shape((height // 2, wide), f32)),
        in_specs=[SMEM] + [ANY] * levels + [VMEM] * 3,
        out_specs=(VMEM, VMEM),
        scratch_shapes=[pltpu.VMEM((width, cols), bf16), pltpu.SemaphoreType.DMA((levels,))],
        compiler_params=params(SMALL),
        cost_estimate=cost(2 * height * cols * (width + wide), 2 * wide * cols + 2 * width * cols),
    )(where, *slots, picked, *bases)


def gather_levels(unit, level, levels):
    def over(slot):
        return lax.ppermute(slot, "group", SWAP)

    if levels != 4:
        slots = [unit] + [across(unit, step, levels) for step in range(1, levels)]
        return slots, [over(slot) for slot in slots]
    middle = (level == 1) | (level == 2)
    inner, outward = [(1, 2), (2, 1)], [(1, 0), (2, 3)]
    together = lax.optimization_barrier
    first, third, other0 = together((across(unit, 1, levels), lax.ppermute(unit, "level", inner), over(unit)))
    inside, outside, other1 = together(
        (lax.ppermute(first, "level", inner), lax.ppermute(third, "level", outward), over(first))
    )
    second = jnp.where(middle, inside, outside)
    outside, other2 = together((lax.ppermute(inside, "level", outward), over(second)))
    third = jnp.where(middle, third, outside)
    return [unit, first, second, third], [other0, other1, other2, over(third)]


def body(acts, grads, counts, basis_a, basis_g):
    group, level, chip, core = (lax.axis_index(n) for n in ("group", "level", "chip", "core"))
    levels = lax.axis_size("level")
    rows, width_a = acts.shape
    width_g = grads.shape[1]
    rows_a, rows_g = basis_a.shape[0], basis_g.shape[0]
    part_a, part_g = width_a // 4, width_g // 8
    where = jnp.reshape(level, (1,)).astype(jnp.int32)

    def columns(y, c):
        return jnp.concatenate(
            [
                cut(basis_g, ((y * 2 + c) * 2 + group) * part_g, part_g, 1),
                cut(basis_a, (c * 2 + group) * part_a, part_a, 1),
            ]
        )

    def diagonal(x):
        return lax.ppermute(x, ("chip", "core"), [(i, 3 - i) for i in range(4)])

    blocks = jnp.stack(
        [
            columns(chip, core),
            lax.ppermute(columns(chip, 1 - core), "core", SWAP),
            lax.ppermute(columns(1 - chip, core), "chip", SWAP),
            diagonal(columns(1 - chip, 1 - core)),
        ]
    )
    blocks = [lax.dynamic_index_in_dim(blocks, j ^ (chip * 2 + core), 0, False) for j in range(4)]
    unit = jnp.concatenate([b[:rows_g] for b in blocks] + [b[rows_g:] for b in blocks])
    level_g, level_a = 4 * rows_g, 4 * rows_a

    slots, others = gather_levels(unit, level, levels)
    own_a = jnp.concatenate([slots[0][level_g:], others[0][level_g:]], axis=1)
    own_a = jnp.concatenate([own_a, lax.ppermute(own_a, "core", SWAP)], axis=1)
    me = chip * 2 + core
    picked = jnp.concatenate([cut(own_a, (me ^ j) * rows_a, rows_a) for j in (3, 1, 2, 0)])

    valid = counts[0]
    keep = jnp.arange(rows, dtype=jnp.int32)[:, None] < valid
    marks = jnp.stack([valid // 16 * 16, valid % 16]).astype(bf16)
    marks = jnp.broadcast_to(jnp.pad(marks, (0, 14))[:, None], (16, width_a))
    half = rows // 2
    early = jnp.where(keep[:half], grads[:half], 0)
    early = jnp.concatenate([jnp.where(keep, acts, 0), marks, early[:, :width_a], early[:, width_a:]])
    late = jnp.where(keep[half:], grads[half:], 0)
    (early_out, late_out), _ = lax.optimization_barrier(((early, late), unit))

    def four(mine, out, after=None):
        far = lax.ppermute(out, "chip", SWAP)
        if after is not None:
            far, _ = lax.optimization_barrier((far, after))
        return [mine, lax.ppermute(mine, "core", SWAP), far, lax.ppermute(far, "core", SWAP)]

    early, late = four(early, early_out, slots[-1]), four(late, late_out)
    turned_a, turned_g, bases, sums = zip(
        turn(where, slots, early, rows, level_g, level_a), turn(where, others, early, rows, level_g, level_a)
    )
    turned_a += tuple(lax.ppermute(t, "core", SWAP) for t in turned_a)
    own, own_extra, *messages = cross(where, turned_a, turned_g, bases, late, sums, rows, levels)

    got = [across(m, step + 1, levels) for step, m in enumerate(messages)]
    scaled = scale(where, own, own_extra, got)
    scaled_all = [scaled] + [across(scaled, step, levels) for step in range(1, levels)]

    sent, kept = result(where, scaled_all, picked, bases)
    sent = lax.ppermute(sent, "core", SWAP).astype(f32)
    last = lax.ppermute((kept[:rows_a] + sent[:rows_a]).astype(bf16), "chip", SWAP)
    return (kept[rows_a:] + sent[rows_a:] + last.astype(f32)).astype(bf16)


def solution(mesh):
    groups, samples = mesh.shape["groups"], mesh.shape["samples"]
    grid = Mesh(mesh.devices.reshape(groups, samples // 4, 2, 2), ("group", "level", "chip", "core"))
    every = ("group", "level", "chip", "core")
    in_specs = (
        P(every, None),
        P(every, None),
        P(every),
        P(every[1:], None),
        P(every[1:], None),
    )
    return jax.shard_map(body, mesh=grid, in_specs=in_specs, out_specs=P(every, None), check_vma=False)
```

time: 177 us -> 156 us (0.88)
  waiting for transfers between devices: 98.6 us -> 81.7 us
  local copies, waits for them, and re-layouts: 15.8 us -> 9.52 us
  Pallas kernels: 16.5 us -> 21.2 us
  between operations: 4.96 us -> 1.16 us
  starting transfers between devices: 32.2 us -> 35.7 us
    ppermute x18 -> x16, waiting for transfers between devices: 43.8 us -> 27.4 us  [the longest x1 10.9 us: gather_levels(): lax.ppermute(third, 'level', outward)]
    pallas_call x3, Pallas kernels: 14.9 us -> 19.6 us  [the longest x2 11.8 us: turn(): pl.pallas_call(functools.partial(turn_kernel, levels, level_g, level_a, r...]
    slice x5 -> x3, local copies, waits for them, and re-layouts: 3.88 us -> 0.15 us  [the longest x1 0.09 us: body(): late = jnp.where(keep[half:], grads[half:], 0)]
    ppermute x1, starting transfers between devices: 0.17 us -> 2.47 us  [diagonal(): return lax.ppermute(x, ('chip', 'core'), [(i, 3 - i) for i in range(4)])]
    ppermute x18 -> x16, starting transfers between devices: 13.5 us -> 15.6 us  [the longest x4 6.09 us: over(): return lax.ppermute(slot, 'group', SWAP)]
    ppermute x1, starting transfers between devices: 2.6 us -> 0.65 us  [body(): lax.ppermute(columns(1 - chip, core), 'chip', SWAP)]
    unnamed x51 -> x53, local copies, waits for them, and re-layouts: 9.39 us -> 7.56 us
  transfers between devices with their start and end apart: 31 -> 29, of which waited for: 15 -> 17; matrix products, arithmetic and copies ran while one was open for 5% -> 3% of each run, Pallas kernels for 6% -> 8%
where the time goes in v3:
time: 156 us; the launch traced here: 155 us
  waiting for transfers between devices  81.7 us (52%)
  starting transfers between devices  35.7 us (23%)
  Pallas kernels  21.2 us (14%)
  local copies, waits for them, and re-layouts  9.52 us (6%)
  other arithmetic  5.32 us (3%)
    ppermute x7, waiting for transfers between devices, across(): return lax.ppermute(x, 'level', [(i, i ^ step) for i in range(levels)])  43.4 us
    ppermute x7, starting transfers between devices, across(): return lax.ppermute(x, 'level', [(i, i ^ step) for i in range(levels)])  16.3 us
    pallas_call x2, Pallas kernels, turn(): pl.pallas_call(functools.partial(turn_kernel, levels, level_g, level_a, r...  11.8 us
    ppermute x1, waiting for transfers between devices, gather_levels(): lax.ppermute(third, 'level', outward)  10.9 us
    ppermute x1, waiting for transfers between devices, body(): lax.ppermute((kept[:rows_a] + sent[:rows_a]).astype(bf16), 'chip', SWAP)  8.03 us
    pallas_call x1, Pallas kernels, cross(): pl.pallas_call(functools.partial(cross_kernel, levels, rows), out_shape=[...  7.81 us
    unnamed x53, local copies, waits for them, and re-layouts  7.56 us
    ppermute x1, waiting for transfers between devices, gather_levels(): lax.ppermute(inside, 'level', outward)  7.25 us
  transfers between devices with their start and end apart: 29, of which 17 were waited for; matrix products, arithmetic and copies ran while one was open for 3% of the time, Pallas kernels for 8%

profile of v3, /device:TPU:0, one launch (start us, length us, event | category | flops | bytes accessed | tf_op | source)
XLA Modules:
  0.0 154.5 jit_solution(14765507032434520427)
XLA Ops:
  0.0 0.8 constant_dynamic-slice_fusion.8
  0.8 1.0 constant_dynamic-slice_fusion.9
  1.8 2.5 %collective-permute-start.2 = (bf16[192,256]{1,0:T(8,128)(2,1)S(1)}, bf16[192,256]{1,0:T(8,128)(2,1)S(1)}, u32[]{:S(2)}, u32[]{:S(2)}) collective-permute-start(bf16[192,256]{1,0:T(8,128)(2,1)S(1)} %get-tuple-element.84), channel_id=1, source_target_pairs={{0,3},{1,2},{2,1},{3,0},{4,7},{5,6},{6,5},{7,4},{8,11},{9,10},{10,... | collective-permute-start | bytes 294920 | tf_op jit(solution)/shard_map/ppermute | solution.py:327
  4.3 0.6 collective-permute-start.1
  5.9 2.5 %slice_select_fusion = (bf16[192,2048]{1,0:T(8,128)(2,1)}, bf16[192,2048]{1,0:T(8,128)(2,1)S(1)}) fusion(bf16[384,2048]{1,0:T(8,128)(2,1)} %param.6, pred[192]{0:T(512)(128)(4,1)S(1)} %get-tuple-element.57, pred[192]{0:T(512)(128)(4,1)S(1)} %get-tuple-element.58), kind=kLoop, calls=%fused_computation.1 | loop fusion | flops 786432 | bytes 3146112 | tf_op jit(solution)/shard_map/jit(_where)/select_n | solution.py:354
  8.8 0.9 collective-permute-done.1
  10.0 2.4 %collective-permute-start.3 = (bf16[768,256]{1,0:T(8,128)(2,1)S(1)}, bf16[768,256]{1,0:T(8,128)(2,1)}, u32[]{:S(2)}, u32[]{:S(2)}) collective-permute-start(bf16[768,256]{1,0:T(8,128)(2,1)S(1)} %get-tuple-element.59.refs_0_), channel_id=1, source_target_pairs={{0,4},{4,0},{8,12},{12,8},{1,5},{5,1},{9,13},{13,9},{2,6},{6,2},{1... | collective-permute-start | bytes 1179656 | tf_op jit(solution)/shard_map/ppermute | solution.py:39
  12.4 1.4 collective-permute-start.4
  13.8 1.5 collective-permute-start.5
  15.6 1.6 %collective-permute-start.12 = (bf16[784,1024]{1,0:T(8,128)(2,1)S(1)}, bf16[784,1024]{1,0:T(8,128)(2,1)S(1)}, u32[]{:S(2)}, u32[]{:S(2)}) collective-permute-start(bf16[784,1024]{1,0:T(8,128)(2,1)S(1)} %pad_maximum_fusion.refs_4_), channel_id=1, source_target_pairs={{0,2},{2,0},{1,3},{3,1},{4,6},{6,4},{5,7},{7,5},{8,10},{10,8},{9,1... | collective-permute-start | bytes 4816904 | tf_op jit(solution)/shard_map/ppermute | solution.py:358
  17.2 4.6 %collective-permute-done.3.refs_1_ = bf16[768,256]{1,0:T(8,128)(2,1)} collective-permute-done((bf16[768,256]{1,0:T(8,128)(2,1)S(1)}, bf16[768,256]{1,0:T(8,128)(2,1)}, u32[]{:S(2)}, u32[]{:S(2)}) %collective-permute-start.3) | collective-permute-done | bytes 393248 | tf_op jit(solution)/shard_map/ppermute | solution.py:39
  21.8 2.8 %collective-permute-done.5.refs_0_ = bf16[768,256]{1,0:T(8,128)(2,1)S(1)} collective-permute-done((bf16[768,256]{1,0:T(8,128)(2,1)S(1)}, bf16[768,256]{1,0:T(8,128)(2,1)S(1)}, u32[]{:S(2)}, u32[]{:S(2)}) %collective-permute-start.5) | collective-permute-done | bytes 393248 | tf_op jit(solution)/shard_map/ppermute | solution.py:291
  24.6 0.8 copy-done.4
  25.4 1.4 collective-permute-start.6
  26.8 1.3 collective-permute-start.7
  28.0 1.6 %collective-permute-start.8 = (bf16[768,256]{1,0:T(8,128)(2,1)}, bf16[768,256]{1,0:T(8,128)(2,1)}, u32[]{:S(2)}, u32[]{:S(2)}) collective-permute-start(bf16[768,256]{1,0:T(8,128)(2,1)} %collective-permute-done.3.refs_1_), channel_id=1, source_target_pairs={{0,16},{16,0},{1,17},{17,1},{2,18},{18,2},{3,19},{19,3},{4,20},{20... | collective-permute-start | bytes 1179656 | tf_op jit(solution)/shard_map/ppermute | solution.py:291
  29.6 10.9 %collective-permute-done.7 = bf16[768,256]{1,0:T(8,128)(2,1)} collective-permute-done((bf16[768,256]{1,0:T(8,128)(2,1)}, bf16[768,256]{1,0:T(8,128)(2,1)}, u32[]{:S(2)}, u32[]{:S(2)}) %collective-permute-start.7) | collective-permute-done | bytes 393248 | tf_op jit(solution)/shard_map/ppermute | solution.py:301
  40.5 1.3 collective-permute-start.9
  41.8 1.1 broadcast_select_fusion.2.refs_2_
  42.9 1.6 %collective-permute-start.10 = (bf16[768,256]{1,0:T(8,128)(2,1)S(1)}, bf16[768,256]{1,0:T(8,128)(2,1)S(1)}, u32[]{:S(2)}, u32[]{:S(2)}) collective-permute-start(bf16[768,256]{1,0:T(8,128)(2,1)S(1)} %broadcast_select_fusion.2.refs_2_), channel_id=1, source_target_pairs={{0,16},{16,0},{1,17},{17,1},{2,18},{18,2},{3,19},{19,3},{4,20},{20... | collective-permute-start | bytes 1179656 | tf_op jit(solution)/shard_map/ppermute | solution.py:291
  44.5 7.3 %collective-permute-done.9 = bf16[768,256]{1,0:T(8,128)(2,1)S(1)} collective-permute-done((bf16[768,256]{1,0:T(8,128)(2,1)}, bf16[768,256]{1,0:T(8,128)(2,1)S(1)}, u32[]{:S(2)}, u32[]{:S(2)}) %collective-permute-start.9) | collective-permute-done | bytes 393248 | tf_op jit(solution)/shard_map/ppermute | solution.py:304
  52.2 1.8 %collective-permute-start.18 = (bf16[192,2048]{1,0:T(8,128)(2,1)S(1)}, bf16[192,2048]{1,0:T(8,128)(2,1)S(1)}, u32[]{:S(2)}, u32[]{:S(2)}) collective-permute-start(bf16[192,2048]{1,0:T(8,128)(2,1)S(1)} %copy-done.17), channel_id=1, source_target_pairs={{0,2},{2,0},{1,3},{3,1},{4,6},{6,4},{5,7},{7,5},{8,10},{10,8},{9,1... | collective-permute-start | bytes 2359304 | tf_op jit(solution)/shard_map/ppermute | solution.py:358
  54.0 1.5 collective-permute-start.14
  55.6 5.9 %shard_map.55 = (bf16[272,1536]{1,0:T(8,128)(2,1)S(1)}, bf16[768,256]{1,0:T(8,128)(2,1)S(1)}, bf16[2048,256]{1,0:T(8,128)(2,1)S(1)}, f32[8,256]{1,0:T(8,128)S(1)}) custom-call(s32[1]{0:T(128)} %bitcast.where, bf16[768,256]{1,0:T(8,128)(2,1)S(1)} %copy-done.7, bf16[768,256]{1,0:T(8,128)(2,1)} %collective-permute-done.3.refs_1_, ...), custom_call_target="tpu_custom_call" | custom-call | flops 1610612736 | bytes 6291456 | tf_op jit(solution)/shard_map/pallas_call | solution.py:100
  61.5 1.0 copy-done
  62.6 0.6 copy-done.14
  63.3 1.9 %collective-permute-done.14.refs_3_ = bf16[768,256]{1,0:T(8,128)(2,1)S(1)} collective-permute-done((bf16[768,256]{1,0:T(8,128)(2,1)S(1)}, bf16[768,256]{1,0:T(8,128)(2,1)S(1)}, u32[]{:S(2)}, u32[]{:S(2)}) %collective-permute-start.14) | collective-permute-done | bytes 393248 | tf_op jit(solution)/shard_map/ppermute | solution.py:291
  65.2 5.9 %shard_map.56 = (bf16[272,1536]{1,0:T(8,128)(2,1)S(1)}, bf16[768,256]{1,0:T(8,128)(2,1)S(1)}, bf16[2048,256]{1,0:T(8,128)(2,1)S(1)}, f32[8,256]{1,0:T(8,128)S(1)}) custom-call(s32[1]{0:T(128)} %bitcast.where, bf16[768,256]{1,0:T(8,128)(2,1)S(1)} %copy-done.5, bf16[768,256]{1,0:T(8,128)(2,1)} %collective-permute-done.8.refs_1_, ...), custom_call_target="tpu_custom_call" | custom-call | flops 1610612736 | bytes 6291456 | tf_op jit(solution)/shard_map/pallas_call | solution.py:100
  71.1 1.0 copy-done.2
  72.1 0.8 copy-done.13
  73.4 2.9 %collective-permute-done.17.refs_9_ = bf16[192,2048]{1,0:T(8,128)(2,1)S(1)} collective-permute-done((bf16[192,2048]{1,0:T(8,128)(2,1)S(1)}, bf16[192,2048]{1,0:T(8,128)(2,1)S(1)}, u32[]{:S(2)}, u32[]{:S(2)}) %collective-permute-start.17) | collective-permute-done | bytes 786464 | tf_op jit(solution)/shard_map/ppermute | solution.py:361
  76.3 1.1 collective-permute-done.19.refs_11_
  77.5 0.9 copy-done.18
  79.0 7.8 %shard_map.57 = (f32[256,512]{1,0:T(8,128)}, f32[8,512]{1,0:T(8,128)}, bf16[272,512]{1,0:T(8,128)(2,1)}, bf16[272,512]{1,0:T(8,128)(2,1)}, bf16[272,512]{1,0:T(8,128)(2,1)}) custom-call(s32[1]{0:T(128)} %bitcast.where, bf16[272,1536]{1,0:T(8,128)(2,1)} %copy-done.10, bf16[272,1536]{1,0:T(8,128)(2,1)} %copy-done.11, bf16[272,1536]{1,0:T(8,128)(2,1)} %copy-done.18, ...), custom_call_target="tpu_custom_call" | custom-call | flops 3221225472 | bytes 6291456 | tf_op jit(solution)/shard_map/pallas_call | solution.py:196
  86.8 3.5 %collective-permute-start.20 = (bf16[272,512]{1,0:T(8,128)(2,1)}, bf16[272,512]{1,0:T(8,128)(2,1)S(1)}, u32[]{:S(2)}, u32[]{:S(2)}) collective-permute-start(bf16[272,512]{1,0:T(8,128)(2,1)} %get-tuple-element.52), channel_id=1, source_target_pairs={{0,4},{4,0},{8,12},{12,8},{1,5},{5,1},{9,13},{13,9},{2,6},{6,2},{1... | collective-permute-start | bytes 835592 | tf_op jit(solution)/shard_map/ppermute | solution.py:39
  90.8 1.9 %collective-permute-start.22 = (bf16[272,512]{1,0:T(8,128)(2,1)}, bf16[272,512]{1,0:T(8,128)(2,1)S(1)}, u32[]{:S(2)}, u32[]{:S(2)}) collective-permute-start(bf16[272,512]{1,0:T(8,128)(2,1)} %get-tuple-element.54), channel_id=1, source_target_pairs={{0,12},{4,8},{8,4},{12,0},{1,13},{5,9},{9,5},{13,1},{2,14},{6,10},... | collective-permute-start | bytes 835592 | tf_op jit(solution)/shard_map/ppermute | solution.py:39
  92.8 9.7 %collective-permute-done.20.refs_0_ = bf16[272,512]{1,0:T(8,128)(2,1)S(1)} collective-permute-done((bf16[272,512]{1,0:T(8,128)(2,1)}, bf16[272,512]{1,0:T(8,128)(2,1)S(1)}, u32[]{:S(2)}, u32[]{:S(2)}) %collective-permute-start.20) | collective-permute-done | bytes 278560 | tf_op jit(solution)/shard_map/ppermute | solution.py:39
  102.5 10.3 %collective-permute-done.21.refs_1_ = bf16[272,512]{1,0:T(8,128)(2,1)S(1)} collective-permute-done((bf16[272,512]{1,0:T(8,128)(2,1)}, bf16[272,512]{1,0:T(8,128)(2,1)S(1)}, u32[]{:S(2)}, u32[]{:S(2)}) %collective-permute-start.21) | collective-permute-done | bytes 278560 | tf_op jit(solution)/shard_map/ppermute | solution.py:39
  112.8 1.0 copy-done.8
  113.9 0.7 copy-done.9
  115.1 5.5 %collective-permute-start.23 = (bf16[256,512]{1,0:T(8,128)(2,1)S(1)}, bf16[256,512]{1,0:T(8,128)(2,1)S(1)}, u32[]{:S(2)}, u32[]{:S(2)}) collective-permute-start(bf16[256,512]{1,0:T(8,128)(2,1)S(1)} %shard_map.58.refs_0_), channel_id=1, source_target_pairs={{0,4},{4,0},{8,12},{12,8},{1,5},{5,1},{9,13},{13,9},{2,6},{6,2},{1... | collective-permute-start | bytes 786440 | tf_op jit(solution)/shard_map/ppermute | solution.py:39
  121.1 1.9 %collective-permute-start.25 = (bf16[256,512]{1,0:T(8,128)(2,1)S(1)}, bf16[256,512]{1,0:T(8,128)(2,1)S(1)}, u32[]{:S(2)}, u32[]{:S(2)}) collective-permute-start(bf16[256,512]{1,0:T(8,128)(2,1)S(1)} %shard_map.58.refs_0_), channel_id=1, source_target_pairs={{0,12},{4,8},{8,4},{12,0},{1,13},{5,9},{9,5},{13,1},{2,14},{6,10},... | collective-permute-start | bytes 786440 | tf_op jit(solution)/shard_map/ppermute | solution.py:39
  123.2 7.1 %collective-permute-done.23.refs_1_ = bf16[256,512]{1,0:T(8,128)(2,1)S(1)} collective-permute-done((bf16[256,512]{1,0:T(8,128)(2,1)S(1)}, bf16[256,512]{1,0:T(8,128)(2,1)S(1)}, u32[]{:S(2)}, u32[]{:S(2)}) %collective-permute-start.23) | collective-permute-done | bytes 262176 | tf_op jit(solution)/shard_map/ppermute | solution.py:39
  130.2 11.7 %collective-permute-done.24.refs_2_ = bf16[256,512]{1,0:T(8,128)(2,1)S(1)} collective-permute-done((bf16[256,512]{1,0:T(8,128)(2,1)S(1)}, bf16[256,512]{1,0:T(8,128)(2,1)S(1)}, u32[]{:S(2)}, u32[]{:S(2)}) %collective-permute-start.24) | collective-permute-done | bytes 262176 | tf_op jit(solution)/shard_map/ppermute | solution.py:39
  142.0 1.2 shard_map.59
  143.3 1.9 %collective-permute-done.27 = bf16[128,2048]{1,0:T(8,128)(2,1)S(1)} collective-permute-done((bf16[128,2048]{1,0:T(8,128)(2,1)S(1)}, bf16[128,2048]{1,0:T(8,128)(2,1)S(1)}, u32[]{:S(2)}, u32[]{:S(2)}) %collective-permute-start.27) | collective-permute-done | bytes 524320 | tf_op jit(solution)/shard_map/ppermute | solution.py:375
  145.7 8.0 %collective-permute-done.28 = bf16[64,2048]{1,0:T(8,128)(2,1)S(1)} collective-permute-done((bf16[64,2048]{1,0:T(8,128)(2,1)S(1)}, bf16[64,2048]{1,0:T(8,128)(2,1)S(1)}, u32[]{:S(2)}, u32[]{:S(2)}) %collective-permute-start.28) | collective-permute-done | bytes 262176 | tf_op jit(solution)/shard_map/ppermute | solution.py:376
  153.7 0.8 fusion.2
  (93 shorter events, 5.3 us)
Async XLA Ops:
  1.8 7.0 %collective-permute-start.2 = (bf16[192,256]{1,0:T(8,128)(2,1)S(1)}, bf16[192,256]{1,0:T(8,128)(2,1)S(1)}, u32[]{:S(2)}, u32[]{:S(2)}) collective-permute-start(bf16[192,256]{1,0:T(8,128)(2,1)S(1)} %get-tuple-element.84), channel_id=1, source_target_pairs={{0,3},{1,2},{2,1},{3,0},{4,7},{5,6},{6,5},{7,4},{8,11},{9,10},{10,... | collective-permute-start | bytes 294920 | tf_op jit(solution)/shard_map/ppermute | solution.py:327
  4.3 5.4 %collective-permute-start.1 = (bf16[192,256]{1,0:T(8,128)(2,1)S(1)}, bf16[192,256]{1,0:T(8,128)(2,1)S(1)}, u32[]{:S(2)}, u32[]{:S(2)}) collective-permute-start(bf16[192,256]{1,0:T(8,128)(2,1)S(1)} %get-tuple-element.82), channel_id=1, source_target_pairs={{0,2},{2,0},{1,3},{3,1},{4,6},{6,4},{5,7},{7,5},{8,10},{10,8},{9,1... | collective-permute-start | bytes 294920 | tf_op jit(solution)/shard_map/ppermute | solution.py:333
  4.9 4.8 %collective-permute-start = (bf16[192,256]{1,0:T(8,128)(2,1)S(1)}, bf16[192,256]{1,0:T(8,128)(2,1)S(1)}, u32[]{:S(2)}, u32[]{:S(2)}) collective-permute-start(bf16[192,256]{1,0:T(8,128)(2,1)S(1)} %get-tuple-element.83), channel_id=1, source_target_pairs={{0,1},{1,0},{2,3},{3,2},{4,5},{5,4},{6,7},{7,6},{8,9},{9,8},{10,11... | collective-permute-start | bytes 294920 | tf_op jit(solution)/shard_map/ppermute | solution.py:332
  5.8 2.7 %copy-start.16 = (bf16[384,1024]{1,0:T(8,128)(2,1)S(1)}, bf16[384,1024]{1,0:T(8,128)(2,1)}, u32[]{:S(2)}) copy-start(bf16[384,1024]{1,0:T(8,128)(2,1)} %param.5) | copy-start | bytes 2359300
  9.9 14.6 %copy-start.6 = (bf16[768,256]{1,0:T(8,128)(2,1)}, bf16[768,256]{1,0:T(8,128)(2,1)S(1)}, u32[]{:S(2)}) copy-start(bf16[768,256]{1,0:T(8,128)(2,1)S(1)} %get-tuple-element.59.refs_0_) | copy-start | bytes 1179652
  10.0 11.8 %collective-permute-start.3 = (bf16[768,256]{1,0:T(8,128)(2,1)S(1)}, bf16[768,256]{1,0:T(8,128)(2,1)}, u32[]{:S(2)}, u32[]{:S(2)}) collective-permute-start(bf16[768,256]{1,0:T(8,128)(2,1)S(1)} %get-tuple-element.59.refs_0_), channel_id=1, source_target_pairs={{0,4},{4,0},{8,12},{12,8},{1,5},{5,1},{9,13},{13,9},{2,6},{6,2},{1... | collective-permute-start | bytes 1179656 | tf_op jit(solution)/shard_map/ppermute | solution.py:39
  12.4 9.4 %collective-permute-start.4 = (bf16[768,256]{1,0:T(8,128)(2,1)S(1)}, bf16[768,256]{1,0:T(8,128)(2,1)}, u32[]{:S(2)}, u32[]{:S(2)}) collective-permute-start(bf16[768,256]{1,0:T(8,128)(2,1)S(1)} %get-tuple-element.59.refs_0_), channel_id=1, source_target_pairs={{4,8},{8,4},{5,9},{9,5},{6,10},{10,6},{7,11},{11,7},{20,24},{24,20... | collective-permute-start | bytes 1179656 | tf_op jit(solution)/shard_map/ppermute | solution.py:299
  13.8 10.8 %collective-permute-start.5 = (bf16[768,256]{1,0:T(8,128)(2,1)S(1)}, bf16[768,256]{1,0:T(8,128)(2,1)S(1)}, u32[]{:S(2)}, u32[]{:S(2)}) collective-permute-start(bf16[768,256]{1,0:T(8,128)(2,1)S(1)} %get-tuple-element.59.refs_0_), channel_id=1, source_target_pairs={{0,16},{16,0},{1,17},{17,1},{2,18},{18,2},{3,19},{19,3},{4,20},{20... | collective-permute-start | bytes 1179656 | tf_op jit(solution)/shard_map/ppermute | solution.py:291
  15.6 36.5 %collective-permute-start.12 = (bf16[784,1024]{1,0:T(8,128)(2,1)S(1)}, bf16[784,1024]{1,0:T(8,128)(2,1)S(1)}, u32[]{:S(2)}, u32[]{:S(2)}) collective-permute-start(bf16[784,1024]{1,0:T(8,128)(2,1)S(1)} %pad_maximum_fusion.refs_4_), channel_id=1, source_target_pairs={{0,2},{2,0},{1,3},{3,1},{4,6},{6,4},{5,7},{7,5},{8,10},{10,8},{9,1... | collective-permute-start | bytes 4816904 | tf_op jit(solution)/shard_map/ppermute | solution.py:358
  25.4 4.2 %collective-permute-start.6 = (bf16[768,256]{1,0:T(8,128)(2,1)}, bf16[768,256]{1,0:T(8,128)(2,1)}, u32[]{:S(2)}, u32[]{:S(2)}) collective-permute-start(bf16[768,256]{1,0:T(8,128)(2,1)} %collective-permute-done.3.refs_1_), channel_id=1, source_target_pairs={{4,8},{8,4},{5,9},{9,5},{6,10},{10,6},{7,11},{11,7},{20,24},{24,20... | collective-permute-start | bytes 1179656 | tf_op jit(solution)/shard_map/ppermute | solution.py:301
  26.8 13.8 %collective-permute-start.7 = (bf16[768,256]{1,0:T(8,128)(2,1)}, bf16[768,256]{1,0:T(8,128)(2,1)}, u32[]{:S(2)}, u32[]{:S(2)}) collective-permute-start(bf16[768,256]{1,0:T(8,128)(2,1)} %collective-permute-done.4), channel_id=1, source_target_pairs={{4,0},{8,12},{5,1},{9,13},{6,2},{10,14},{7,3},{11,15},{20,16},{24,... | collective-permute-start | bytes 1179656 | tf_op jit(solution)/shard_map/ppermute | solution.py:301
  28.0 12.5 %collective-permute-start.8 = (bf16[768,256]{1,0:T(8,128)(2,1)}, bf16[768,256]{1,0:T(8,128)(2,1)}, u32[]{:S(2)}, u32[]{:S(2)}) collective-permute-start(bf16[768,256]{1,0:T(8,128)(2,1)} %collective-permute-done.3.refs_1_), channel_id=1, source_target_pairs={{0,16},{16,0},{1,17},{17,1},{2,18},{18,2},{3,19},{19,3},{4,20},{20... | collective-permute-start | bytes 1179656 | tf_op jit(solution)/shard_map/ppermute | solution.py:291
  29.6 22.6 %copy-start.17 = (bf16[192,2048]{1,0:T(8,128)(2,1)S(1)}, bf16[192,2048]{1,0:T(8,128)(2,1)}, u32[]{:S(2)}) copy-start(bf16[192,2048]{1,0:T(8,128)(2,1)} %get-tuple-element.47.refs_8_) | copy-start | bytes 2359300
  29.6 26.0 %copy-start.7 = (bf16[768,256]{1,0:T(8,128)(2,1)S(1)}, bf16[768,256]{1,0:T(8,128)(2,1)}, u32[]{:S(2)}) copy-start(bf16[768,256]{1,0:T(8,128)(2,1)} %copy-done.6) | copy-start | bytes 1179652
  40.5 11.2 %collective-permute-start.9 = (bf16[768,256]{1,0:T(8,128)(2,1)}, bf16[768,256]{1,0:T(8,128)(2,1)S(1)}, u32[]{:S(2)}, u32[]{:S(2)}) collective-permute-start(bf16[768,256]{1,0:T(8,128)(2,1)} %collective-permute-done.6), channel_id=1, source_target_pairs={{4,0},{8,12},{5,1},{9,13},{6,2},{10,14},{7,3},{11,15},{20,16},{24,... | collective-permute-start | bytes 1179656 | tf_op jit(solution)/shard_map/ppermute | solution.py:304
  42.9 9.1 %collective-permute-start.10 = (bf16[768,256]{1,0:T(8,128)(2,1)S(1)}, bf16[768,256]{1,0:T(8,128)(2,1)S(1)}, u32[]{:S(2)}, u32[]{:S(2)}) collective-permute-start(bf16[768,256]{1,0:T(8,128)(2,1)S(1)} %broadcast_select_fusion.2.refs_2_), channel_id=1, source_target_pairs={{0,16},{16,0},{1,17},{17,1},{2,18},{18,2},{3,19},{19,3},{4,20},{20... | collective-permute-start | bytes 1179656 | tf_op jit(solution)/shard_map/ppermute | solution.py:291
  44.5 11.0 %collective-permute-start.11 = (bf16[784,1024]{1,0:T(8,128)(2,1)S(1)}, bf16[784,1024]{1,0:T(8,128)(2,1)S(1)}, u32[]{:S(2)}, u32[]{:S(2)}) collective-permute-start(bf16[784,1024]{1,0:T(8,128)(2,1)S(1)} %pad_maximum_fusion.refs_4_), channel_id=1, source_target_pairs={{0,1},{1,0},{2,3},{3,2},{4,5},{5,4},{6,7},{7,6},{8,9},{9,8},{10,11... | collective-permute-start | bytes 4816904 | tf_op jit(solution)/shard_map/ppermute | solution.py:361
  52.2 3.5 %collective-permute-start.13 = (bf16[784,1024]{1,0:T(8,128)(2,1)S(1)}, bf16[784,1024]{1,0:T(8,128)(2,1)S(1)}, u32[]{:S(2)}, u32[]{:S(2)}) collective-permute-start(bf16[784,1024]{1,0:T(8,128)(2,1)S(1)} %collective-permute-done.12.refs_6_), channel_id=1, source_target_pairs={{0,1},{1,0},{2,3},{3,2},{4,5},{5,4},{6,7},{7,6},{8,9},{9,8},{10,11... | collective-permute-start | bytes 4816904 | tf_op jit(solution)/shard_map/ppermute | solution.py:361
  52.2 21.2 %collective-permute-start.18 = (bf16[192,2048]{1,0:T(8,128)(2,1)S(1)}, bf16[192,2048]{1,0:T(8,128)(2,1)S(1)}, u32[]{:S(2)}, u32[]{:S(2)}) collective-permute-start(bf16[192,2048]{1,0:T(8,128)(2,1)S(1)} %copy-done.17), channel_id=1, source_target_pairs={{0,2},{2,0},{1,3},{3,1},{4,6},{6,4},{5,7},{7,5},{8,10},{10,8},{9,1... | collective-permute-start | bytes 2359304 | tf_op jit(solution)/shard_map/ppermute | solution.py:358
  54.0 11.2 %collective-permute-start.14 = (bf16[768,256]{1,0:T(8,128)(2,1)S(1)}, bf16[768,256]{1,0:T(8,128)(2,1)S(1)}, u32[]{:S(2)}, u32[]{:S(2)}) collective-permute-start(bf16[768,256]{1,0:T(8,128)(2,1)S(1)} %broadcast_select_fusion.1.refs_3_), channel_id=1, source_target_pairs={{0,16},{16,0},{1,17},{17,1},{2,18},{18,2},{3,19},{19,3},{4,20},{20... | collective-permute-start | bytes 1179656 | tf_op jit(solution)/shard_map/ppermute | solution.py:291
  55.6 9.5 %copy-start.5 = (bf16[768,256]{1,0:T(8,128)(2,1)S(1)}, bf16[768,256]{1,0:T(8,128)(2,1)}, u32[]{:S(2)}) copy-start(bf16[768,256]{1,0:T(8,128)(2,1)} %copy-done.4) | copy-start | bytes 1179652
  61.5 1.0 copy-start
  63.2 7.9 %copy-start.10 = (bf16[272,1536]{1,0:T(8,128)(2,1)}, bf16[272,1536]{1,0:T(8,128)(2,1)S(1)}, u32[]{:S(2)}) copy-start(bf16[272,1536]{1,0:T(8,128)(2,1)S(1)} %get-tuple-element.38.refs_0_) | copy-start | bytes 2506756
  63.2 7.9 %copy-start.12 = (bf16[768,256]{1,0:T(8,128)(2,1)}, bf16[768,256]{1,0:T(8,128)(2,1)S(1)}, u32[]{:S(2)}) copy-start(bf16[768,256]{1,0:T(8,128)(2,1)S(1)} %get-tuple-element.43.refs_4_) | copy-start | bytes 1179652
  63.2 14.3 %collective-permute-start.15 = (bf16[272,1536]{1,0:T(8,128)(2,1)S(1)}, bf16[272,1536]{1,0:T(8,128)(2,1)S(1)}, u32[]{:S(2)}, u32[]{:S(2)}) collective-permute-start(bf16[272,1536]{1,0:T(8,128)(2,1)S(1)} %get-tuple-element.38.refs_0_), channel_id=1, source_target_pairs={{0,1},{1,0},{2,3},{3,2},{4,5},{5,4},{6,7},{7,6},{8,9},{9,8},{10,11... | collective-permute-start | bytes 2506760 | tf_op jit(solution)/shard_map/ppermute | solution.py:367
  71.1 1.0 copy-start.2
  72.8 4.6 %copy-start.11 = (bf16[272,1536]{1,0:T(8,128)(2,1)}, bf16[272,1536]{1,0:T(8,128)(2,1)S(1)}, u32[]{:S(2)}) copy-start(bf16[272,1536]{1,0:T(8,128)(2,1)S(1)} %get-tuple-element.42.refs_1_) | copy-start | bytes 2506756
  72.8 4.6 %copy-start.15 = (f32[8,256]{1,0:T(8,128)}, f32[8,256]{1,0:T(8,128)S(1)}, u32[]{:S(2)}) copy-start(f32[8,256]{1,0:T(8,128)S(1)} %get-tuple-element.49.refs_13_) | copy-start | bytes 24580
  72.8 4.6 %collective-permute-start.16 = (bf16[272,1536]{1,0:T(8,128)(2,1)S(1)}, bf16[272,1536]{1,0:T(8,128)(2,1)S(1)}, u32[]{:S(2)}, u32[]{:S(2)}) collective-permute-start(bf16[272,1536]{1,0:T(8,128)(2,1)S(1)} %get-tuple-element.42.refs_1_), channel_id=1, source_target_pairs={{0,1},{1,0},{2,3},{3,2},{4,5},{5,4},{6,7},{7,6},{8,9},{9,8},{10,11... | collective-permute-start | bytes 2506760 | tf_op jit(solution)/shard_map/ppermute | solution.py:367
  72.8 3.5 %collective-permute-start.17 = (bf16[192,2048]{1,0:T(8,128)(2,1)S(1)}, bf16[192,2048]{1,0:T(8,128)(2,1)S(1)}, u32[]{:S(2)}, u32[]{:S(2)}) collective-permute-start(bf16[192,2048]{1,0:T(8,128)(2,1)S(1)} %copy-done.17), channel_id=1, source_target_pairs={{0,1},{1,0},{2,3},{3,2},{4,5},{5,4},{6,7},{7,6},{8,9},{9,8},{10,11... | collective-permute-start | bytes 2359304 | tf_op jit(solution)/shard_map/ppermute | solution.py:361
  73.3 5.1 %copy-start.20 = (bf16[192,2048]{1,0:T(8,128)(2,1)}, bf16[192,2048]{1,0:T(8,128)(2,1)S(1)}, u32[]{:S(2)}) copy-start(bf16[192,2048]{1,0:T(8,128)(2,1)S(1)} %collective-permute-done.18.refs_10_) | copy-start | bytes 2359300
  73.4 4.1 %collective-permute-start.19 = (bf16[192,2048]{1,0:T(8,128)(2,1)S(1)}, bf16[192,2048]{1,0:T(8,128)(2,1)S(1)}, u32[]{:S(2)}, u32[]{:S(2)}) collective-permute-start(bf16[192,2048]{1,0:T(8,128)(2,1)S(1)} %collective-permute-done.18.refs_10_), channel_id=1, source_target_pairs={{0,1},{1,0},{2,3},{3,2},{4,5},{5,4},{6,7},{7,6},{8,9},{9,8},{10,11... | collective-permute-start | bytes 2359304 | tf_op jit(solution)/shard_map/ppermute | solution.py:361
  76.3 2.1 %copy-start.21 = (bf16[192,2048]{1,0:T(8,128)(2,1)}, bf16[192,2048]{1,0:T(8,128)(2,1)S(1)}, u32[]{:S(2)}) copy-start(bf16[192,2048]{1,0:T(8,128)(2,1)S(1)} %collective-permute-done.17.refs_9_) | copy-start | bytes 2359300
  77.4 1.3 copy-start.22
  77.5 1.0 copy-start.18
  77.5 1.5 copy-start.19
  86.8 15.7 %collective-permute-start.20 = (bf16[272,512]{1,0:T(8,128)(2,1)}, bf16[272,512]{1,0:T(8,128)(2,1)S(1)}, u32[]{:S(2)}, u32[]{:S(2)}) collective-permute-start(bf16[272,512]{1,0:T(8,128)(2,1)} %get-tuple-element.52), channel_id=1, source_target_pairs={{0,4},{4,0},{8,12},{12,8},{1,5},{5,1},{9,13},{13,9},{2,6},{6,2},{1... | collective-permute-start | bytes 835592 | tf_op jit(solution)/shard_map/ppermute | solution.py:39
  90.2 22.6 %collective-permute-start.21 = (bf16[272,512]{1,0:T(8,128)(2,1)}, bf16[272,512]{1,0:T(8,128)(2,1)S(1)}, u32[]{:S(2)}, u32[]{:S(2)}) collective-permute-start(bf16[272,512]{1,0:T(8,128)(2,1)} %get-tuple-element.53), channel_id=1, source_target_pairs={{0,8},{4,12},{8,0},{12,4},{1,9},{5,13},{9,1},{13,5},{2,10},{6,14},... | collective-permute-start | bytes 835592 | tf_op jit(solution)/shard_map/ppermute | solution.py:39
  90.8 22.1 %collective-permute-start.22 = (bf16[272,512]{1,0:T(8,128)(2,1)}, bf16[272,512]{1,0:T(8,128)(2,1)S(1)}, u32[]{:S(2)}, u32[]{:S(2)}) collective-permute-start(bf16[272,512]{1,0:T(8,128)(2,1)} %get-tuple-element.54), channel_id=1, source_target_pairs={{0,12},{4,8},{8,4},{12,0},{1,13},{5,9},{9,5},{13,1},{2,14},{6,10},... | collective-permute-start | bytes 835592 | tf_op jit(solution)/shard_map/ppermute | solution.py:39
  92.7 30.3 %collective-permute-start.26 = (bf16[256,512]{1,0:T(8,128)(2,1)S(1)}, bf16[256,512]{1,0:T(8,128)(2,1)S(1)}, u32[]{:S(2)}, u32[]{:S(2)}) collective-permute-start(bf16[256,512]{1,0:T(8,128)(2,1)S(1)} %pad_maximum_fusion.4), channel_id=1, source_target_pairs={{0,1},{1,0},{2,3},{3,2},{4,5},{5,4},{6,7},{7,6},{8,9},{9,8},{10,11... | collective-permute-start | bytes 786440 | tf_op jit(solution)/shard_map/ppermute | solution.py:343
  112.8 1.0 copy-start.8
  115.0 26.9 %copy-start.1 = (bf16[2048,256]{1,0:T(8,128)(2,1)S(1)}, bf16[2048,256]{1,0:T(8,128)(2,1)}, u32[]{:S(2)}) copy-start(bf16[2048,256]{1,0:T(8,128)(2,1)} %copy-done) | copy-start | bytes 3145732
  115.1 26.9 %copy-start.3 = (bf16[2048,256]{1,0:T(8,128)(2,1)S(1)}, bf16[2048,256]{1,0:T(8,128)(2,1)}, u32[]{:S(2)}) copy-start(bf16[2048,256]{1,0:T(8,128)(2,1)} %copy-done.2) | copy-start | bytes 3145732
  115.1 15.2 %collective-permute-start.23 = (bf16[256,512]{1,0:T(8,128)(2,1)S(1)}, bf16[256,512]{1,0:T(8,128)(2,1)S(1)}, u32[]{:S(2)}, u32[]{:S(2)}) collective-permute-start(bf16[256,512]{1,0:T(8,128)(2,1)S(1)} %shard_map.58.refs_0_), channel_id=1, source_target_pairs={{0,4},{4,0},{8,12},{12,8},{1,5},{5,1},{9,13},{13,9},{2,6},{6,2},{1... | collective-permute-start | bytes 786440 | tf_op jit(solution)/shard_map/ppermute | solution.py:39
  120.6 21.4 %collective-permute-start.24 = (bf16[256,512]{1,0:T(8,128)(2,1)S(1)}, bf16[256,512]{1,0:T(8,128)(2,1)S(1)}, u32[]{:S(2)}, u32[]{:S(2)}) collective-permute-start(bf16[256,512]{1,0:T(8,128)(2,1)S(1)} %shard_map.58.refs_0_), channel_id=1, source_target_pairs={{0,8},{4,12},{8,0},{12,4},{1,9},{5,13},{9,1},{13,5},{2,10},{6,14},... | collective-permute-start | bytes 786440 | tf_op jit(solution)/shard_map/ppermute | solution.py:39
  121.1 20.9 %collective-permute-start.25 = (bf16[256,512]{1,0:T(8,128)(2,1)S(1)}, bf16[256,512]{1,0:T(8,128)(2,1)S(1)}, u32[]{:S(2)}, u32[]{:S(2)}) collective-permute-start(bf16[256,512]{1,0:T(8,128)(2,1)S(1)} %shard_map.58.refs_0_), channel_id=1, source_target_pairs={{0,12},{4,8},{8,4},{12,0},{1,13},{5,9},{9,5},{13,1},{2,14},{6,10},... | collective-permute-start | bytes 786440 | tf_op jit(solution)/shard_map/ppermute | solution.py:39
  143.2 2.0 %collective-permute-start.27 = (bf16[128,2048]{1,0:T(8,128)(2,1)S(1)}, bf16[128,2048]{1,0:T(8,128)(2,1)S(1)}, u32[]{:S(2)}, u32[]{:S(2)}) collective-permute-start(bf16[128,2048]{1,0:T(8,128)(2,1)S(1)} %get-tuple-element.56), channel_id=1, source_target_pairs={{0,1},{1,0},{2,3},{3,2},{4,5},{5,4},{6,7},{7,6},{8,9},{9,8},{10,11... | collective-permute-start | bytes 1572872 | tf_op jit(solution)/shard_map/ppermute | solution.py:375
  145.3 8.4 %collective-permute-start.28 = (bf16[64,2048]{1,0:T(8,128)(2,1)S(1)}, bf16[64,2048]{1,0:T(8,128)(2,1)S(1)}, u32[]{:S(2)}, u32[]{:S(2)}) collective-permute-start(bf16[64,2048]{1,0:T(8,128)(2,1)S(1)} %fusion), channel_id=1, source_target_pairs={{0,2},{2,0},{1,3},{3,1},{4,6},{6,4},{5,7},{7,5},{8,10},{10,8},{9,1... | collective-permute-start | bytes 786440 | tf_op jit(solution)/shard_map/ppermute | solution.py:376
  (4 other events, 2.9 us)

commit v4 on v3

v4 whole, which is shorter than its diff:
```python
import functools

import jax
import jax.numpy as jnp
from jax import lax
from jax.experimental import pallas as pl
from jax.experimental.pallas import tpu as pltpu
from jax.sharding import Mesh, PartitionSpec as P

damping = 0.01
bf16 = jnp.bfloat16
f32 = jnp.float32
SWAP = [(0, 1), (1, 0)]
ANY = pl.BlockSpec(memory_space=pl.ANY)
VMEM = pl.BlockSpec(memory_space=pltpu.VMEM)
SMEM = pl.BlockSpec(memory_space=pltpu.SMEM)
LARGE = 18 * 2**20
MIDDLE = 16 * 2**20
SMALL = 12 * 2**20


def params(limit):
    return pltpu.CompilerParams(vmem_limit_bytes=limit)


def cost(flops, moved):
    return pl.CostEstimate(flops=flops, bytes_accessed=moved, transcendentals=0)


def shape(dims, dtype):
    return jax.ShapeDtypeStruct(dims, dtype)


def cut(x, first, size, axis=0):
    return lax.dynamic_slice_in_dim(x, first, size, axis)


def across(x, step, levels):
    return lax.ppermute(x, "level", [(i, i ^ step) for i in range(levels)])


def split(rows):
    return rows * 2 // 3, rows - rows * 2 // 3


def turn_kernel(levels, level_g, level_a, rows, where, *refs):
    slots, pieces = refs[:levels], refs[levels : levels + 4]
    basis_a, out_g, basis_g, sums, sems = refs[levels + 4 :]
    half, width = split(rows)[0], basis_a.shape[0]
    part = basis_a.shape[1]
    copies = []
    for i, (first, height, target) in enumerate(((level_g, level_a, basis_a), (0, level_g, basis_g))):
        for step, slot in enumerate(slots):
            row = pl.multiple_of((where[0] ^ step) * height, height)
            copy = pltpu.make_async_copy(
                slot.at[pl.ds(first, height)], target.at[pl.ds(row, height)], sems.at[i * levels + step]
            )
            copy.start()
            copies.append(copy)
    for copy in copies[:levels]:
        copy.wait()
    total_a = jnp.zeros((1, part), f32)
    total_g = jnp.zeros((1, part), f32)
    for piece in pieces:
        block = jnp.dot(piece[:rows], basis_a[...], preferred_element_type=f32).astype(bf16)
        total_a = total_a + jnp.sum(jnp.square(block.astype(f32)), axis=0, keepdims=True)
    for copy in copies[levels:]:
        copy.wait()
    for i, piece in enumerate(pieces):
        turned = sum(
            jnp.dot(
                piece[pl.ds(rows + 16 + j * half, half)],
                basis_g[pl.ds(j * width, width)],
                preferred_element_type=f32,
            )
            for j in range(2)
        ).astype(bf16)
        out_g[pl.ds(i * half, half)] = turned
        total_g = total_g + jnp.sum(jnp.square(turned.astype(f32)), axis=0, keepdims=True)
    marks = sum(piece[rows : rows + 16, :part].astype(f32) for piece in pieces)
    sums[0:1] = total_g
    sums[1:2] = marks[0:1] + marks[1:2]
    sums[2:3] = total_a
    sums[3:8] = jnp.zeros((5, part), f32)


def turn(where, slots, pieces, rows, level_g, level_a):
    levels = len(slots)
    width_a, width_g = levels * level_a, levels * level_g
    part = slots[0].shape[1]
    half = split(rows)[0]
    return pl.pallas_call(
        functools.partial(turn_kernel, levels, level_g, level_a, rows),
        out_shape=(
            shape((width_a, part), bf16),
            shape((4 * half, part), bf16),
            shape((width_g, part), bf16),
            shape((8, part), f32),
        ),
        in_specs=[SMEM] + [ANY] * levels + [VMEM] * 4,
        out_specs=(VMEM,) * 4,
        scratch_shapes=[pltpu.SemaphoreType.DMA((2 * levels,))],
        compiler_params=params(MIDDLE),
        cost_estimate=cost(8 * rows * part * (width_a + width_g // 2), 8 * rows * (width_a + width_g // 2)),
    )(where, *slots, *pieces)


def high_low(v):
    high = v.astype(bf16)
    return high, (v - high.astype(f32)).astype(bf16)


def cross_kernel(levels, rows, where, *refs):
    acts, early, bases, pieces, sums = refs[:4], refs[4:6], refs[6:8], refs[8:12], refs[12:16]
    own, own_extra, messages = refs[16], refs[17], refs[18 : 17 + levels]
    left, right, basis, held, whole, extra, sems = refs[17 + levels :]
    half, late = split(rows)
    part = bases[0].shape[1]
    cols = 2 * part
    chunk = cols // levels
    level = where[0]
    count = 0

    def copy(source, target):
        nonlocal count
        made = pltpu.make_async_copy(source, target, sems.at[count])
        made.start()
        count += 1
        return made

    first = [copy(b, basis.at[:, pl.ds(i * part, part)]) for i, b in enumerate(bases)]
    moves = [copy(p, held.at[pl.ds(i * late, late)]) for i, p in enumerate(pieces)]
    rest = [copy(a.at[pl.ds(0, rows)], left.at[pl.ds(i * rows, rows)]) for i, a in enumerate(acts)]
    for i in range(2):
        for j in range(4):
            rest.append(
                copy(early[i].at[pl.ds(j * half, half)], right.at[pl.ds(j * rows, half), pl.ds(i * part, part)])
            )
    for made in first:
        made.wait()
    total = jnp.concatenate([sums[0][0:1], sums[1][0:1]], axis=1)
    for i in range(0, 4, 2):
        moves[i].wait()
        moves[i + 1].wait()
        block = jnp.dot(held[pl.ds(i * late, 2 * late)], basis[...], preferred_element_type=f32).astype(bf16)
        right[pl.ds(i * rows + half, late)] = block[:late]
        right[pl.ds(i * rows + rows + half, late)] = block[late:]
        total = total + jnp.sum(jnp.square(block.astype(f32)), axis=0, keepdims=True)
    for made in rest:
        made.wait()
    extra[...] = jnp.zeros_like(extra)
    extra[0:1, :cols] = total
    for i in range(4):
        extra[1:2, pl.ds(i * part, part)] = sums[i][2:3]
        extra[2:3, pl.ds(i * part, part)] = sums[i][1:2]
    for i in range(2):
        block = pl.ds(i * part, part)
        whole[block] = lax.dot_general(
            right[:, block], left[...], (((0,), (0,)), ((), ())), preferred_element_type=f32
        )
    high, low = high_low(extra[...])
    own_extra[...] = extra[...]
    own[...] = whole[pl.ds(pl.multiple_of(level * chunk, chunk), chunk)]
    for step in range(1, levels):
        to = pl.multiple_of((level ^ step) * chunk, chunk)
        message = messages[step - 1]
        message[pl.ds(0, chunk)] = whole[pl.ds(to, chunk)].astype(bf16)
        message[pl.ds(chunk, 16)] = jnp.concatenate([high, low])


def cross(where, acts, early, bases, pieces, sums, rows, levels):
    width_g, part = bases[0].shape
    width = acts[0].shape[1]
    cols = 2 * part
    chunk = cols // levels
    return pl.pallas_call(
        functools.partial(cross_kernel, levels, rows),
        out_shape=[shape((chunk, width), f32), shape((8, width), f32)]
        + [shape((chunk + 16, width), bf16)] * (levels - 1),
        in_specs=[SMEM] + [ANY] * 12 + [VMEM] * 4,
        out_specs=[VMEM] * (1 + levels),
        scratch_shapes=[
            pltpu.VMEM((4 * rows, width), bf16),
            pltpu.VMEM((4 * rows, cols), bf16),
            pltpu.VMEM((width_g, cols), bf16),
            pltpu.VMEM((4 * split(rows)[1], width_g), bf16),
            pltpu.VMEM((cols, width), f32),
            pltpu.VMEM((8, width), f32),
            pltpu.SemaphoreType.DMA((18,)),
        ],
        compiler_params=params(LARGE),
        cost_estimate=cost(4 * rows * cols * (width_g + 2 * width), 16 * rows * width),
    )(where, *acts, *early, *bases, *pieces, *sums)


def middle_kernel(levels, where, own, own_extra, *refs):
    messages, bases, outs = refs[: levels - 1], refs[levels - 1 : levels + 3], refs[levels + 3 : 2 * levels + 3]
    basis, turned = refs[2 * levels + 3 :]
    chunk, width = own.shape
    cols = chunk * levels
    part = bases[0].shape[1]
    for i, b in enumerate(bases):
        basis[:, pl.ds(i * part, part)] = b[...]
    total = own[...]
    extra = own_extra[...]
    for message in messages:
        total = total + message[pl.ds(0, chunk)].astype(f32)
        more = message[pl.ds(chunk, 16)].astype(f32)
        extra = extra + (more[0:8] + more[8:16])
    count = extra[2:3]
    extra = extra / count
    lam_a = extra[1:2]
    turned[...] = jnp.transpose(extra[:, :cols])
    lam_g = turned[pl.ds(pl.multiple_of(where[0] * chunk, chunk), chunk)][:, 0:1]
    both = jnp.dot(jnp.concatenate(high_low(total)), basis[...], preferred_element_type=f32)
    rotated = (both[:chunk] + both[chunk:]) / count
    scaled = (rotated / (lam_g * lam_a + damping)).astype(bf16)
    height = width // levels
    for step, out in enumerate(outs):
        rows = pl.ds(pl.multiple_of((where[0] ^ step) * height, height), height)
        out[...] = lax.dot_general(
            scaled, basis[rows], (((1,), (1,)), ((), ())), preferred_element_type=f32
        ).astype(bf16)


def middle(where, own, own_extra, messages, bases):
    levels = len(messages) + 1
    chunk, width = own.shape
    return pl.pallas_call(
        functools.partial(middle_kernel, levels),
        out_shape=[shape((chunk, width // levels), bf16)] * levels,
        in_specs=[SMEM] + [VMEM] * (levels + 5),
        out_specs=[VMEM] * levels,
        scratch_shapes=[pltpu.VMEM((width, width), bf16), pltpu.VMEM((chunk * levels, 8), f32)],
        compiler_params=params(SMALL),
        cost_estimate=cost(6 * chunk * width * width, 2 * width * width),
    )(where, own, own_extra, *messages, *bases)


def result_kernel(levels, where, *refs):
    slots = refs[:levels]
    one, two, sent, kept, mid, whole, sems = refs[levels:]
    chunk, height = slots[0].shape
    wide, part = one.shape
    copies = []
    for step, slot in enumerate(slots):
        row = pl.multiple_of((where[0] ^ step) * chunk, chunk)
        copy = pltpu.make_async_copy(slot, mid.at[pl.ds(row, chunk)], sems.at[step])
        copy.start()
        copies.append(copy)
    for copy in copies:
        copy.wait()
    quarter = wide // 4
    for j in range(4):
        columns = pl.ds(j * quarter, quarter)
        whole[:, columns] = sum(
            lax.dot_general(
                mid[pl.ds(i * part, part)], b[columns], (((0,), (1,)), ((), ())), preferred_element_type=f32
            )
            for i, b in enumerate((one, two))
        )
    rows = height // 4
    for i, (other, target) in enumerate(((3, sent), (1, sent), (2, kept), (0, kept))):
        block = whole[pl.ds(pl.multiple_of((where[1] ^ other) * rows, rows), rows)]
        target[pl.ds((i % 2) * rows, rows)] = block.astype(target.dtype)


def result(where, slots, bases):
    levels = len(slots)
    chunk, height = slots[0].shape
    wide, part = bases[0].shape
    return pl.pallas_call(
        functools.partial(result_kernel, levels),
        out_shape=(shape((height // 2, wide), f32), shape((height // 2, wide), f32)),
        in_specs=[SMEM] + [ANY] * levels + [VMEM] * 2,
        out_specs=(VMEM, VMEM),
        scratch_shapes=[
            pltpu.VMEM((2 * part, height), bf16),
            pltpu.VMEM((height, wide), f32),
            pltpu.SemaphoreType.DMA((levels,)),
        ],
        compiler_params=params(SMALL),
        cost_estimate=cost(4 * height * part * wide, 4 * wide * part),
    )(where, *slots, *bases)


def gather_levels(unit, level, levels):
    def over(slot):
        return lax.ppermute(slot, "group", SWAP)

    if levels != 4:
        slots = [unit] + [across(unit, step, levels) for step in range(1, levels)]
        return slots, [over(slot) for slot in slots]
    middle = (level == 1) | (level == 2)
    inner, outward = [(1, 2), (2, 1)], [(1, 0), (2, 3)]
    together = lax.optimization_barrier
    first, third, other0 = together((across(unit, 1, levels), lax.ppermute(unit, "level", inner), over(unit)))
    inside, outside, other1 = together(
        (lax.ppermute(first, "level", inner), lax.ppermute(third, "level", outward), over(first))
    )
    second = jnp.where(middle, inside, outside)
    outside, other2 = together((lax.ppermute(inside, "level", outward), over(second)))
    third = jnp.where(middle, third, outside)
    return [unit, first, second, third], [other0, other1, other2, over(third)]


def body(acts, grads, counts, basis_a, basis_g):
    group, level, chip, core = (lax.axis_index(n) for n in ("group", "level", "chip", "core"))
    levels = lax.axis_size("level")
    rows, width_a = acts.shape
    width_g = grads.shape[1]
    rows_a, rows_g = basis_a.shape[0], basis_g.shape[0]
    part_a, part_g = width_a // 4, width_g // 8
    where = jnp.stack([level, chip * 2 + core]).astype(jnp.int32)

    def columns(y, c):
        return jnp.concatenate(
            [
                cut(basis_g, ((y * 2 + c) * 2 + group) * part_g, part_g, 1),
                cut(basis_a, (c * 2 + group) * part_a, part_a, 1),
            ]
        )

    def diagonal(x):
        return lax.ppermute(x, ("chip", "core"), [(i, 3 - i) for i in range(4)])

    beside = lax.ppermute(columns(chip, 1 - core), "core", SWAP)
    blocks = jnp.stack(
        [
            columns(chip, core),
            beside,
            lax.ppermute(columns(1 - chip, core), "chip", SWAP),
            diagonal(columns(1 - chip, 1 - core)),
        ]
    )
    blocks = [lax.dynamic_index_in_dim(blocks, j ^ (chip * 2 + core), 0, False) for j in range(4)]
    unit = jnp.concatenate([b[:rows_g] for b in blocks] + [b[rows_g:] for b in blocks])
    level_g, level_a = 4 * rows_g, 4 * rows_a

    slots, others = gather_levels(unit, level, levels)
    valid = counts[0]
    keep = jnp.arange(rows, dtype=jnp.int32)[:, None] < valid
    marks = jnp.stack([valid // 16 * 16, valid % 16]).astype(bf16)
    marks = jnp.broadcast_to(jnp.pad(marks, (0, 14))[:, None], (16, width_a))
    half = split(rows)[0]
    early = jnp.where(keep[:half], grads[:half], 0)
    early = jnp.concatenate([jnp.where(keep, acts, 0), marks, early[:, :width_a], early[:, width_a:]])
    late = jnp.where(keep[half:], grads[half:], 0)
    (early_out, late_out), _ = lax.optimization_barrier(((early, late), beside))

    def four(mine, out, after):
        far = lax.ppermute(out, "chip", SWAP)
        if after is not None:
            far, after = lax.optimization_barrier((far, after))
        return [mine, lax.ppermute(mine, "core", SWAP), far, lax.ppermute(far, "core", SWAP)], after

    early, slots[-1] = four(early, early_out, slots[-1])
    late, _ = four(late, late_out, None)
    bases_a, turned_g, bases_g, sums = zip(
        turn(where, slots, early, rows, level_g, level_a), turn(where, others, early, rows, level_g, level_a)
    )
    sums += tuple(lax.ppermute(t, "core", SWAP) for t in sums)
    bases_a += tuple(lax.ppermute(t, "core", SWAP) for t in bases_a)
    own, own_extra, *messages = cross(where, early, turned_g, bases_g, late, sums, rows, levels)

    got = [across(m, step + 1, levels) for step, m in enumerate(messages)]
    mids = middle(where, own, own_extra, got, bases_a)
    mids = [m if step == 0 else across(m, step, levels) for step, m in enumerate(mids)]

    sent, kept = result(where, mids, bases_g)
    sent = lax.ppermute(sent.astype(bf16), "core", SWAP).astype(f32)
    last = lax.ppermute((kept[:rows_a] + sent[:rows_a]).astype(bf16), "chip", SWAP)
    return (kept[rows_a:] + sent[rows_a:] + last.astype(f32)).astype(bf16)


def solution(mesh):
    groups, samples = mesh.shape["groups"], mesh.shape["samples"]
    grid = Mesh(mesh.devices.reshape(groups, samples // 4, 2, 2), ("group", "level", "chip", "core"))
    every = ("group", "level", "chip", "core")
    in_specs = (
        P(every, None),
        P(every, None),
        P(every),
        P(every[1:], None),
        P(every[1:], None),
    )
    return jax.shard_map(body, mesh=grid, in_specs=in_specs, out_specs=P(every, None), check_vma=False)
```

time: 156 us -> 139 us (0.89)
  local copies, waits for them, and re-layouts: 9.52 us -> 2.69 us
  waiting for transfers between devices: 81.7 us -> 78.1 us
  Pallas kernels: 21.2 us -> 18.1 us
  starting transfers between devices: 35.7 us -> 32.7 us
    ppermute x7, waiting for transfers between devices: 43.4 us -> 30.9 us  [across(): return lax.ppermute(x, 'level', [(i, i ^ step) for i in range(levels)])]
    ppermute x2, waiting for transfers between devices: 0.08 us -> 12.2 us  [four(): far = lax.ppermute(out, 'chip', SWAP)]
    ppermute x4, waiting for transfers between devices: 4.97 us -> 15.3 us  [over(): return lax.ppermute(slot, 'group', SWAP)]
    unnamed x53 -> x13, local copies, waits for them, and re-layouts: 7.56 us -> 0.85 us
    ppermute x1, waiting for transfers between devices: 7.25 us -> 2.35 us  [gather_levels(): lax.ppermute(inside, 'level', outward)]
    ppermute x1, waiting for transfers between devices: 10.9 us -> 6.3 us  [gather_levels(): lax.ppermute(third, 'level', outward)]
    pallas_call x1, Pallas kernels: 7.81 us -> 4.67 us  [cross(): pl.pallas_call(functools.partial(cross_kernel, levels, rows), out_shape=[...]
    ppermute x2, waiting for transfers between devices: 2.88 us -> 0.01 us  [four(): lax.ppermute(mine, 'core', SWAP)]
  transfers between devices with their start and end apart: 29 -> 30, of which waited for: 17 -> 14; matrix products, arithmetic and copies ran while one was open for 3% -> 3% of each run, Pallas kernels for 8% -> 10%
where the time goes in v4:
time: 139 us; the launch traced here: 138 us
  waiting for transfers between devices  78.1 us (56%)
  starting transfers between devices  32.7 us (24%)
  Pallas kernels  18.1 us (13%)
  other arithmetic  5.44 us (4%)
  local copies, waits for them, and re-layouts  2.69 us (2%)
    ppermute x7, waiting for transfers between devices, across(): return lax.ppermute(x, 'level', [(i, i ^ step) for i in range(levels)])  30.9 us
    ppermute x4, waiting for transfers between devices, over(): return lax.ppermute(slot, 'group', SWAP)  15.3 us
    ppermute x7, starting transfers between devices, across(): return lax.ppermute(x, 'level', [(i, i ^ step) for i in range(levels)])  14.3 us
    ppermute x2, waiting for transfers between devices, four(): far = lax.ppermute(out, 'chip', SWAP)  12.2 us
    pallas_call x2, Pallas kernels, turn(): pl.pallas_call(functools.partial(turn_kernel, levels, level_g, level_a, r...  9.68 us
    ppermute x1, waiting for transfers between devices, body(): lax.ppermute((kept[:rows_a] + sent[:rows_a]).astype(bf16), 'chip', SWAP)  7.49 us
    ppermute x1, waiting for transfers between devices, gather_levels(): lax.ppermute(third, 'level', outward)  6.3 us
    ppermute x4, starting transfers between devices, over(): return lax.ppermute(slot, 'group', SWAP)  5.07 us
  transfers between devices with their start and end apart: 30, of which 14 were waited for; matrix products, arithmetic and copies ran while one was open for 3% of the time, Pallas kernels for 10%

profile of v4, /device:TPU:0, one launch (start us, length us, event | category | flops | bytes accessed | tf_op | source)
XLA Modules:
  0.0 138.1 jit_solution(1823459045707968768)
XLA Ops:
  0.0 0.8 constant_dynamic-slice_fusion.2
  0.8 1.0 constant_dynamic-slice_fusion.3
  1.8 0.5 collective-permute-start.1
  2.3 2.6 %collective-permute-start.3 = (bf16[192,256]{1,0:T(8,128)(2,1)S(1)}, bf16[192,256]{1,0:T(8,128)(2,1)S(1)}, u32[]{:S(2)}, u32[]{:S(2)}) collective-permute-start(bf16[192,256]{1,0:T(8,128)(2,1)S(1)} %get-tuple-element.76), channel_id=1, source_target_pairs={{0,2},{2,0},{1,3},{3,1},{4,6},{6,4},{5,7},{7,5},{8,10},{10,8},{9,1... | collective-permute-start | bytes 294920 | tf_op jit(solution)/shard_map/ppermute | solution.py:332
  5.8 1.4 slice_select_fusion
  7.3 1.2 slice_select_fusion.1.refs_8_
  9.2 1.1 collective-permute-done.4
  10.4 1.6 %collective-permute-start.2 = (bf16[912,1024]{1,0:T(8,128)(2,1)S(1)}, bf16[912,1024]{1,0:T(8,128)(2,1)}, u32[]{:S(2)}, u32[]{:S(2)}) collective-permute-start(bf16[912,1024]{1,0:T(8,128)(2,1)S(1)} %pad_maximum_fusion.refs_4_.refs_0_), channel_id=1, source_target_pairs={{0,2},{2,0},{1,3},{3,1},{4,6},{6,4},{5,7},{7,5},{8,10},{10,8},{9,1... | collective-permute-start | bytes 5603336 | tf_op jit(solution)/shard_map/ppermute | solution.py:352
  12.1 1.5 %collective-permute-start.5 = (bf16[768,256]{1,0:T(8,128)(2,1)S(1)}, bf16[768,256]{1,0:T(8,128)(2,1)S(1)}, u32[]{:S(2)}, u32[]{:S(2)}) collective-permute-start(bf16[768,256]{1,0:T(8,128)(2,1)S(1)} %fusion.8.refs_0_), channel_id=1, source_target_pairs={{0,4},{4,0},{8,12},{12,8},{1,5},{5,1},{9,13},{13,9},{2,6},{6,2},{1... | collective-permute-start | bytes 1179656 | tf_op jit(solution)/shard_map/ppermute | solution.py:39
  13.6 1.4 %collective-permute-start.6 = (bf16[768,256]{1,0:T(8,128)(2,1)S(1)}, bf16[768,256]{1,0:T(8,128)(2,1)}, u32[]{:S(2)}, u32[]{:S(2)}) collective-permute-start(bf16[768,256]{1,0:T(8,128)(2,1)S(1)} %fusion.8.refs_0_), channel_id=1, source_target_pairs={{4,8},{8,4},{5,9},{9,5},{6,10},{10,6},{7,11},{11,7},{20,24},{24,20... | collective-permute-start | bytes 1179656 | tf_op jit(solution)/shard_map/ppermute | solution.py:297
  15.0 1.5 %collective-permute-start.7 = (bf16[768,256]{1,0:T(8,128)(2,1)S(1)}, bf16[768,256]{1,0:T(8,128)(2,1)S(1)}, u32[]{:S(2)}, u32[]{:S(2)}) collective-permute-start(bf16[768,256]{1,0:T(8,128)(2,1)S(1)} %fusion.8.refs_0_), channel_id=1, source_target_pairs={{0,16},{16,0},{1,17},{17,1},{2,18},{18,2},{3,19},{19,3},{4,20},{20... | collective-permute-start | bytes 1179656 | tf_op jit(solution)/shard_map/ppermute | solution.py:289
  16.5 6.5 %collective-permute-done.5.refs_1_ = bf16[768,256]{1,0:T(8,128)(2,1)S(1)} collective-permute-done((bf16[768,256]{1,0:T(8,128)(2,1)S(1)}, bf16[768,256]{1,0:T(8,128)(2,1)S(1)}, u32[]{:S(2)}, u32[]{:S(2)}) %collective-permute-start.5) | collective-permute-done | bytes 393248 | tf_op jit(solution)/shard_map/ppermute | solution.py:39
  23.0 2.7 %collective-permute-done.7.refs_0_ = bf16[768,256]{1,0:T(8,128)(2,1)S(1)} collective-permute-done((bf16[768,256]{1,0:T(8,128)(2,1)S(1)}, bf16[768,256]{1,0:T(8,128)(2,1)S(1)}, u32[]{:S(2)}, u32[]{:S(2)}) %collective-permute-start.7) | collective-permute-done | bytes 393248 | tf_op jit(solution)/shard_map/ppermute | solution.py:289
  25.7 0.7 copy-done
  26.5 1.5 %collective-permute-start.10 = (bf16[768,256]{1,0:T(8,128)(2,1)S(1)}, bf16[768,256]{1,0:T(8,128)(2,1)}, u32[]{:S(2)}, u32[]{:S(2)}) collective-permute-start(bf16[768,256]{1,0:T(8,128)(2,1)S(1)} %collective-permute-done.5.refs_1_), channel_id=1, source_target_pairs={{0,16},{16,0},{1,17},{17,1},{2,18},{18,2},{3,19},{19,3},{4,20},{20... | collective-permute-start | bytes 1179656 | tf_op jit(solution)/shard_map/ppermute | solution.py:289
  28.0 1.4 %collective-permute-start.8 = (bf16[768,256]{1,0:T(8,128)(2,1)S(1)}, bf16[768,256]{1,0:T(8,128)(2,1)}, u32[]{:S(2)}, u32[]{:S(2)}) collective-permute-start(bf16[768,256]{1,0:T(8,128)(2,1)S(1)} %collective-permute-done.5.refs_1_), channel_id=1, source_target_pairs={{4,8},{8,4},{5,9},{9,5},{6,10},{10,6},{7,11},{11,7},{20,24},{24,20... | collective-permute-start | bytes 1179656 | tf_op jit(solution)/shard_map/ppermute | solution.py:299
  29.4 1.3 collective-permute-start.9
  30.7 5.8 %collective-permute-done.10.refs_1_ = bf16[768,256]{1,0:T(8,128)(2,1)} collective-permute-done((bf16[768,256]{1,0:T(8,128)(2,1)S(1)}, bf16[768,256]{1,0:T(8,128)(2,1)}, u32[]{:S(2)}, u32[]{:S(2)}) %collective-permute-start.10) | collective-permute-done | bytes 393248 | tf_op jit(solution)/shard_map/ppermute | solution.py:289
  36.5 6.3 %collective-permute-done.9 = bf16[768,256]{1,0:T(8,128)(2,1)} collective-permute-done((bf16[768,256]{1,0:T(8,128)(2,1)}, bf16[768,256]{1,0:T(8,128)(2,1)}, u32[]{:S(2)}, u32[]{:S(2)}) %collective-permute-start.9) | collective-permute-done | bytes 393248 | tf_op jit(solution)/shard_map/ppermute | solution.py:299
  42.8 1.0 broadcast_select_fusion.2.refs_2_
  43.8 0.6 collective-permute-start.12
  44.4 1.3 collective-permute-start.11
  45.8 6.8 %collective-permute-done.12.refs_2_ = bf16[768,256]{1,0:T(8,128)(2,1)S(1)} collective-permute-done((bf16[768,256]{1,0:T(8,128)(2,1)S(1)}, bf16[768,256]{1,0:T(8,128)(2,1)S(1)}, u32[]{:S(2)}, u32[]{:S(2)}) %collective-permute-start.12) | collective-permute-done | bytes 393248 | tf_op jit(solution)/shard_map/ppermute | solution.py:289
  52.6 2.3 %collective-permute-done.11 = bf16[768,256]{1,0:T(8,128)(2,1)S(1)} collective-permute-done((bf16[768,256]{1,0:T(8,128)(2,1)}, bf16[768,256]{1,0:T(8,128)(2,1)S(1)}, u32[]{:S(2)}, u32[]{:S(2)}) %collective-permute-start.11) | collective-permute-done | bytes 393248 | tf_op jit(solution)/shard_map/ppermute | solution.py:302
  55.1 0.6 collective-permute-start.16
  55.7 1.5 %collective-permute-start.14 = (bf16[768,256]{1,0:T(8,128)(2,1)S(1)}, bf16[768,256]{1,0:T(8,128)(2,1)S(1)}, u32[]{:S(2)}, u32[]{:S(2)}) collective-permute-start(bf16[768,256]{1,0:T(8,128)(2,1)S(1)} %broadcast_select_fusion.1.refs_3_), channel_id=1, source_target_pairs={{0,16},{16,0},{1,17},{17,1},{2,18},{18,2},{3,19},{19,3},{4,20},{20... | collective-permute-start | bytes 1179656 | tf_op jit(solution)/shard_map/ppermute | solution.py:289
  57.2 12.2 %collective-permute-done.16.refs_10_ = bf16[128,2048]{1,0:T(8,128)(2,1)S(1)} collective-permute-done((bf16[128,2048]{1,0:T(8,128)(2,1)S(1)}, bf16[128,2048]{1,0:T(8,128)(2,1)S(1)}, u32[]{:S(2)}, u32[]{:S(2)}) %collective-permute-start.16) | collective-permute-done | bytes 524320 | tf_op jit(solution)/shard_map/ppermute | solution.py:352
  69.5 5.0 %shard_map.56 = (bf16[1024,256]{1,0:T(8,128)(2,1)S(1)}, bf16[1024,256]{1,0:T(8,128)(2,1)S(1)}, bf16[2048,256]{1,0:T(8,128)(2,1)S(1)}, f32[8,256]{1,0:T(8,128)S(1)}) custom-call(s32[2]{0:T(128)S(1)} %pad_add_fusion.where, bf16[768,256]{1,0:T(8,128)(2,1)S(1)} %copy-done.1, bf16[768,256]{1,0:T(8,128)(2,1)} %collective-permute-done.10.refs_1_, ...), custom_call_target="tpu_custom_call" | custom-call | flops 1610612736 | bytes 6291456 | tf_op jit(solution)/shard_map/pallas_call | solution.py:92
  74.5 0.6 collective-permute-start.19
  75.1 4.7 %shard_map.55 = (bf16[1024,256]{1,0:T(8,128)(2,1)S(1)}, bf16[1024,256]{1,0:T(8,128)(2,1)S(1)}, bf16[2048,256]{1,0:T(8,128)(2,1)S(1)}, f32[8,256]{1,0:T(8,128)S(1)}) custom-call(s32[2]{0:T(128)S(1)} %pad_add_fusion.where, bf16[768,256]{1,0:T(8,128)(2,1)S(1)} %fusion.8.refs_0_, bf16[768,256]{1,0:T(8,128)(2,1)S(1)} %collective-permute-done.5.refs_1_, ...), custom_call_target="tpu_custom_call" | custom-call | flops 1610612736 | bytes 6291456 | tf_op jit(solution)/shard_map/pallas_call | solution.py:92
  79.9 0.5 collective-permute-start.24
  80.4 0.6 collective-permute-done.18.refs_14_
  81.0 4.7 %shard_map.57 = (f32[128,1024]{1,0:T(8,128)S(1)}, f32[8,1024]{1,0:T(8,128)S(1)}, bf16[144,1024]{1,0:T(8,128)(2,1)S(1)}, bf16[144,1024]{1,0:T(8,128)(2,1)S(1)}, bf16[144,1024]{1,0:T(8,128)(2,1)S(1)}) custom-call(s32[2]{0:T(128)S(1)} %pad_add_fusion.where, bf16[912,1024]{1,0:T(8,128)(2,1)S(1)} %pad_maximum_fusion.refs_4_.refs_0_, ...), custom_call_target="tpu_custom_call" | custom-call | flops 3221225472 | bytes 6291456 | tf_op jit(solution)/shard_map/pallas_call | solution.py:176
  85.7 0.7 collective-permute-start.20
  86.4 2.0 %collective-permute-start.21 = (bf16[144,1024]{1,0:T(8,128)(2,1)S(1)}, bf16[144,1024]{1,0:T(8,128)(2,1)S(1)}, u32[]{:S(2)}, u32[]{:S(2)}) collective-permute-start(bf16[144,1024]{1,0:T(8,128)(2,1)S(1)} %get-tuple-element.57), channel_id=1, source_target_pairs={{0,8},{4,12},{8,0},{12,4},{1,9},{5,13},{9,1},{13,5},{2,10},{6,14},... | collective-permute-start | bytes 884744 | tf_op jit(solution)/shard_map/ppermute | solution.py:39
  88.4 1.8 %collective-permute-start.22 = (bf16[144,1024]{1,0:T(8,128)(2,1)S(1)}, bf16[144,1024]{1,0:T(8,128)(2,1)S(1)}, u32[]{:S(2)}, u32[]{:S(2)}) collective-permute-start(bf16[144,1024]{1,0:T(8,128)(2,1)S(1)} %get-tuple-element.58), channel_id=1, source_target_pairs={{0,12},{4,8},{8,4},{12,0},{1,13},{5,9},{9,5},{13,1},{2,14},{6,10},... | collective-permute-start | bytes 884744 | tf_op jit(solution)/shard_map/ppermute | solution.py:39
  90.2 10.2 %collective-permute-done.20.refs_0_ = bf16[144,1024]{1,0:T(8,128)(2,1)S(1)} collective-permute-done((bf16[144,1024]{1,0:T(8,128)(2,1)S(1)}, bf16[144,1024]{1,0:T(8,128)(2,1)S(1)}, u32[]{:S(2)}, u32[]{:S(2)}) %collective-permute-start.20) | collective-permute-done | bytes 294944 | tf_op jit(solution)/shard_map/ppermute | solution.py:39
  100.4 9.5 %collective-permute-done.21.refs_1_ = bf16[144,1024]{1,0:T(8,128)(2,1)S(1)} collective-permute-done((bf16[144,1024]{1,0:T(8,128)(2,1)S(1)}, bf16[144,1024]{1,0:T(8,128)(2,1)S(1)}, u32[]{:S(2)}, u32[]{:S(2)}) %collective-permute-start.21) | collective-permute-done | bytes 294944 | tf_op jit(solution)/shard_map/ppermute | solution.py:39
  109.8 1.9 %shard_map.58 = (bf16[128,256]{1,0:T(8,128)(2,1)S(1)}, bf16[128,256]{1,0:T(8,128)(2,1)S(1)}, bf16[128,256]{1,0:T(8,128)(2,1)S(1)}, bf16[128,256]{1,0:T(8,128)(2,1)S(1)}) custom-call(s32[2]{0:T(128)S(1)} %pad_add_fusion.where, f32[128,1024]{1,0:T(8,128)S(1)} %get-tuple-element.54.own, f32[8,1024]{1,0:T(8,128)S(1)} %get-tuple-element.55.own_extra, ...), custom_call_target="tpu_custom_call" | custom-call | flops 805306368 | bytes 2097152 | tf_op jit(solution)/shard_map/pallas_call | solution.py:229
  111.8 5.9 %collective-permute-start.25 = (bf16[128,256]{1,0:T(8,128)(2,1)S(1)}, bf16[128,256]{1,0:T(8,128)(2,1)S(1)}, u32[]{:S(2)}, u32[]{:S(2)}) collective-permute-start(bf16[128,256]{1,0:T(8,128)(2,1)S(1)} %get-tuple-element.62), channel_id=1, source_target_pairs={{0,4},{4,0},{8,12},{12,8},{1,5},{5,1},{9,13},{13,9},{2,6},{6,2},{1... | collective-permute-start | bytes 196616 | tf_op jit(solution)/shard_map/ppermute | solution.py:39
  117.7 0.7 collective-permute-start.26
  118.3 1.8 %collective-permute-start.27 = (bf16[128,256]{1,0:T(8,128)(2,1)S(1)}, bf16[128,256]{1,0:T(8,128)(2,1)S(1)}, u32[]{:S(2)}, u32[]{:S(2)}) collective-permute-start(bf16[128,256]{1,0:T(8,128)(2,1)S(1)} %get-tuple-element.64), channel_id=1, source_target_pairs={{0,12},{4,8},{8,4},{12,0},{1,13},{5,9},{9,5},{13,1},{2,14},{6,10},... | collective-permute-start | bytes 196616 | tf_op jit(solution)/shard_map/ppermute | solution.py:39
  120.1 4.7 %collective-permute-done.26.refs_2_ = bf16[128,256]{1,0:T(8,128)(2,1)S(1)} collective-permute-done((bf16[128,256]{1,0:T(8,128)(2,1)S(1)}, bf16[128,256]{1,0:T(8,128)(2,1)S(1)}, u32[]{:S(2)}, u32[]{:S(2)}) %collective-permute-start.26) | collective-permute-done | bytes 65568 | tf_op jit(solution)/shard_map/ppermute | solution.py:39
  124.9 1.8 %shard_map.59 = (f32[128,2048]{1,0:T(8,128)S(1)}, f32[128,2048]{1,0:T(8,128)S(1)}) custom-call(s32[2]{0:T(128)S(1)} %pad_add_fusion.where, bf16[128,256]{1,0:T(8,128)(2,1)S(1)} %get-tuple-element.61.refs_0_, bf16[128,256]{1,0:T(8,128)(2,1)S(1)} %collective-permute-done.25.refs_1_, bf16[128,256]{1,0:T(8,128)(2,1)S(1)} %collective-permute-done.26.refs_2_, ...), custom_call_target="tpu_custom_call" | custom-call | flops 536870912 | bytes 2097152 | tf_op jit(solution)/shard_map/pallas_call | solution.py:272
  126.9 1.9 %collective-permute-done.28 = bf16[128,2048]{1,0:T(8,128)(2,1)S(1)} collective-permute-done((bf16[128,2048]{1,0:T(8,128)(2,1)S(1)}, bf16[128,2048]{1,0:T(8,128)(2,1)S(1)}, u32[]{:S(2)}, u32[]{:S(2)}) %collective-permute-start.28) | collective-permute-done | bytes 524320 | tf_op jit(solution)/shard_map/ppermute | solution.py:371
  128.9 0.9 collective-permute-start.29
  129.9 7.5 %collective-permute-done.29 = bf16[64,2048]{1,0:T(8,128)(2,1)S(1)} collective-permute-done((bf16[64,2048]{1,0:T(8,128)(2,1)S(1)}, bf16[64,2048]{1,0:T(8,128)(2,1)S(1)}, u32[]{:S(2)}, u32[]{:S(2)}) %collective-permute-start.29) | collective-permute-done | bytes 262176 | tf_op jit(solution)/shard_map/ppermute | solution.py:372
  137.3 0.8 fusion.2
  (54 shorter events, 1.8 us)
Async XLA Ops:
  1.8 7.4 %collective-permute-start.1 = (bf16[192,256]{1,0:T(8,128)(2,1)S(1)}, bf16[192,256]{1,0:T(8,128)(2,1)S(1)}, u32[]{:S(2)}, u32[]{:S(2)}) collective-permute-start(bf16[192,256]{1,0:T(8,128)(2,1)S(1)} %get-tuple-element.78), channel_id=1, source_target_pairs={{0,1},{1,0},{2,3},{3,2},{4,5},{5,4},{6,7},{7,6},{8,9},{9,8},{10,11... | collective-permute-start | bytes 294920 | tf_op jit(solution)/shard_map/ppermute | solution.py:327
  2.3 6.9 %collective-permute-start.3 = (bf16[192,256]{1,0:T(8,128)(2,1)S(1)}, bf16[192,256]{1,0:T(8,128)(2,1)S(1)}, u32[]{:S(2)}, u32[]{:S(2)}) collective-permute-start(bf16[192,256]{1,0:T(8,128)(2,1)S(1)} %get-tuple-element.76), channel_id=1, source_target_pairs={{0,2},{2,0},{1,3},{3,1},{4,6},{6,4},{5,7},{7,5},{8,10},{10,8},{9,1... | collective-permute-start | bytes 294920 | tf_op jit(solution)/shard_map/ppermute | solution.py:332
  4.9 5.4 %collective-permute-start.4 = (bf16[192,256]{1,0:T(8,128)(2,1)S(1)}, bf16[192,256]{1,0:T(8,128)(2,1)S(1)}, u32[]{:S(2)}, u32[]{:S(2)}) collective-permute-start(bf16[192,256]{1,0:T(8,128)(2,1)S(1)} %get-tuple-element.77), channel_id=1, source_target_pairs={{0,3},{1,2},{2,1},{3,0},{4,7},{5,6},{6,5},{7,4},{8,11},{9,10},{10,... | collective-permute-start | bytes 294920 | tf_op jit(solution)/shard_map/ppermute | solution.py:325
  7.2 1.4 %copy-start.2 = (bf16[384,1024]{1,0:T(8,128)(2,1)S(1)}, bf16[384,1024]{1,0:T(8,128)(2,1)}, u32[]{:S(2)}) copy-start(bf16[384,1024]{1,0:T(8,128)(2,1)} %param.5) | copy-start | bytes 2359300
  10.4 44.5 %collective-permute-start.2 = (bf16[912,1024]{1,0:T(8,128)(2,1)S(1)}, bf16[912,1024]{1,0:T(8,128)(2,1)}, u32[]{:S(2)}, u32[]{:S(2)}) collective-permute-start(bf16[912,1024]{1,0:T(8,128)(2,1)S(1)} %pad_maximum_fusion.refs_4_.refs_0_), channel_id=1, source_target_pairs={{0,2},{2,0},{1,3},{3,1},{4,6},{6,4},{5,7},{7,5},{8,10},{10,8},{9,1... | collective-permute-start | bytes 5603336 | tf_op jit(solution)/shard_map/ppermute | solution.py:352
  12.1 10.9 %collective-permute-start.5 = (bf16[768,256]{1,0:T(8,128)(2,1)S(1)}, bf16[768,256]{1,0:T(8,128)(2,1)S(1)}, u32[]{:S(2)}, u32[]{:S(2)}) collective-permute-start(bf16[768,256]{1,0:T(8,128)(2,1)S(1)} %fusion.8.refs_0_), channel_id=1, source_target_pairs={{0,4},{4,0},{8,12},{12,8},{1,5},{5,1},{9,13},{13,9},{2,6},{6,2},{1... | collective-permute-start | bytes 1179656 | tf_op jit(solution)/shard_map/ppermute | solution.py:39
  13.6 9.4 %collective-permute-start.6 = (bf16[768,256]{1,0:T(8,128)(2,1)S(1)}, bf16[768,256]{1,0:T(8,128)(2,1)}, u32[]{:S(2)}, u32[]{:S(2)}) collective-permute-start(bf16[768,256]{1,0:T(8,128)(2,1)S(1)} %fusion.8.refs_0_), channel_id=1, source_target_pairs={{4,8},{8,4},{5,9},{9,5},{6,10},{10,6},{7,11},{11,7},{20,24},{24,20... | collective-permute-start | bytes 1179656 | tf_op jit(solution)/shard_map/ppermute | solution.py:297
  15.0 10.7 %collective-permute-start.7 = (bf16[768,256]{1,0:T(8,128)(2,1)S(1)}, bf16[768,256]{1,0:T(8,128)(2,1)S(1)}, u32[]{:S(2)}, u32[]{:S(2)}) collective-permute-start(bf16[768,256]{1,0:T(8,128)(2,1)S(1)} %fusion.8.refs_0_), channel_id=1, source_target_pairs={{0,16},{16,0},{1,17},{17,1},{2,18},{18,2},{3,19},{19,3},{4,20},{20... | collective-permute-start | bytes 1179656 | tf_op jit(solution)/shard_map/ppermute | solution.py:289
  25.7 0.7 copy-start
  26.5 10.0 %collective-permute-start.10 = (bf16[768,256]{1,0:T(8,128)(2,1)S(1)}, bf16[768,256]{1,0:T(8,128)(2,1)}, u32[]{:S(2)}, u32[]{:S(2)}) collective-permute-start(bf16[768,256]{1,0:T(8,128)(2,1)S(1)} %collective-permute-done.5.refs_1_), channel_id=1, source_target_pairs={{0,16},{16,0},{1,17},{17,1},{2,18},{18,2},{3,19},{19,3},{4,20},{20... | collective-permute-start | bytes 1179656 | tf_op jit(solution)/shard_map/ppermute | solution.py:289
  28.0 8.5 %collective-permute-start.8 = (bf16[768,256]{1,0:T(8,128)(2,1)S(1)}, bf16[768,256]{1,0:T(8,128)(2,1)}, u32[]{:S(2)}, u32[]{:S(2)}) collective-permute-start(bf16[768,256]{1,0:T(8,128)(2,1)S(1)} %collective-permute-done.5.refs_1_), channel_id=1, source_target_pairs={{4,8},{8,4},{5,9},{9,5},{6,10},{10,6},{7,11},{11,7},{20,24},{24,20... | collective-permute-start | bytes 1179656 | tf_op jit(solution)/shard_map/ppermute | solution.py:299
  29.4 13.4 %collective-permute-start.9 = (bf16[768,256]{1,0:T(8,128)(2,1)}, bf16[768,256]{1,0:T(8,128)(2,1)}, u32[]{:S(2)}, u32[]{:S(2)}) collective-permute-start(bf16[768,256]{1,0:T(8,128)(2,1)} %collective-permute-done.6), channel_id=1, source_target_pairs={{4,0},{8,12},{5,1},{9,13},{6,2},{10,14},{7,3},{11,15},{20,16},{24,... | collective-permute-start | bytes 1179656 | tf_op jit(solution)/shard_map/ppermute | solution.py:299
  30.7 38.8 %copy-start.1 = (bf16[768,256]{1,0:T(8,128)(2,1)S(1)}, bf16[768,256]{1,0:T(8,128)(2,1)}, u32[]{:S(2)}) copy-start(bf16[768,256]{1,0:T(8,128)(2,1)} %copy-done) | copy-start | bytes 1179652
  43.8 8.7 %collective-permute-start.12 = (bf16[768,256]{1,0:T(8,128)(2,1)S(1)}, bf16[768,256]{1,0:T(8,128)(2,1)S(1)}, u32[]{:S(2)}, u32[]{:S(2)}) collective-permute-start(bf16[768,256]{1,0:T(8,128)(2,1)S(1)} %broadcast_select_fusion.2.refs_2_), channel_id=1, source_target_pairs={{0,16},{16,0},{1,17},{17,1},{2,18},{18,2},{3,19},{19,3},{4,20},{20... | collective-permute-start | bytes 1179656 | tf_op jit(solution)/shard_map/ppermute | solution.py:289
  44.4 10.5 %collective-permute-start.11 = (bf16[768,256]{1,0:T(8,128)(2,1)}, bf16[768,256]{1,0:T(8,128)(2,1)S(1)}, u32[]{:S(2)}, u32[]{:S(2)}) collective-permute-start(bf16[768,256]{1,0:T(8,128)(2,1)} %collective-permute-done.8), channel_id=1, source_target_pairs={{4,0},{8,12},{5,1},{9,13},{6,2},{10,14},{7,3},{11,15},{20,16},{24,... | collective-permute-start | bytes 1179656 | tf_op jit(solution)/shard_map/ppermute | solution.py:302
  45.7 23.8 %collective-permute-start = (bf16[912,1024]{1,0:T(8,128)(2,1)S(1)}, bf16[912,1024]{1,0:T(8,128)(2,1)S(1)}, u32[]{:S(2)}, u32[]{:S(2)}) collective-permute-start(bf16[912,1024]{1,0:T(8,128)(2,1)S(1)} %pad_maximum_fusion.refs_4_.refs_0_), channel_id=1, source_target_pairs={{0,1},{1,0},{2,3},{3,2},{4,5},{5,4},{6,7},{7,6},{8,9},{9,8},{10,11... | collective-permute-start | bytes 5603336 | tf_op jit(solution)/shard_map/ppermute | solution.py:355
  55.0 14.5 %collective-permute-start.13 = (bf16[912,1024]{1,0:T(8,128)(2,1)}, bf16[912,1024]{1,0:T(8,128)(2,1)S(1)}, u32[]{:S(2)}, u32[]{:S(2)}) collective-permute-start(bf16[912,1024]{1,0:T(8,128)(2,1)} %collective-permute-done.2.refs_6_.refs_2_), channel_id=1, source_target_pairs={{0,1},{1,0},{2,3},{3,2},{4,5},{5,4},{6,7},{7,6},{8,9},{9,8},{10,11... | collective-permute-start | bytes 5603336 | tf_op jit(solution)/shard_map/ppermute | solution.py:355
  55.1 14.3 %collective-permute-start.16 = (bf16[128,2048]{1,0:T(8,128)(2,1)S(1)}, bf16[128,2048]{1,0:T(8,128)(2,1)S(1)}, u32[]{:S(2)}, u32[]{:S(2)}) collective-permute-start(bf16[128,2048]{1,0:T(8,128)(2,1)S(1)} %slice_select_fusion.1.refs_8_), channel_id=1, source_target_pairs={{0,2},{2,0},{1,3},{3,1},{4,6},{6,4},{5,7},{7,5},{8,10},{10,8},{9,1... | collective-permute-start | bytes 1572872 | tf_op jit(solution)/shard_map/ppermute | solution.py:352
  55.7 13.8 %collective-permute-start.14 = (bf16[768,256]{1,0:T(8,128)(2,1)S(1)}, bf16[768,256]{1,0:T(8,128)(2,1)S(1)}, u32[]{:S(2)}, u32[]{:S(2)}) collective-permute-start(bf16[768,256]{1,0:T(8,128)(2,1)S(1)} %broadcast_select_fusion.1.refs_3_), channel_id=1, source_target_pairs={{0,16},{16,0},{1,17},{17,1},{2,18},{18,2},{3,19},{19,3},{4,20},{20... | collective-permute-start | bytes 1179656 | tf_op jit(solution)/shard_map/ppermute | solution.py:289
  57.2 23.2 %collective-permute-start.15 = (bf16[128,2048]{1,0:T(8,128)(2,1)S(1)}, bf16[128,2048]{1,0:T(8,128)(2,1)S(1)}, u32[]{:S(2)}, u32[]{:S(2)}) collective-permute-start(bf16[128,2048]{1,0:T(8,128)(2,1)S(1)} %slice_select_fusion.1.refs_8_), channel_id=1, source_target_pairs={{0,1},{1,0},{2,3},{3,2},{4,5},{5,4},{6,7},{7,6},{8,9},{9,8},{10,11... | collective-permute-start | bytes 1572872 | tf_op jit(solution)/shard_map/ppermute | solution.py:355
  69.4 11.0 %collective-permute-start.17 = (bf16[128,2048]{1,0:T(8,128)(2,1)S(1)}, bf16[128,2048]{1,0:T(8,128)(2,1)S(1)}, u32[]{:S(2)}, u32[]{:S(2)}) collective-permute-start(bf16[128,2048]{1,0:T(8,128)(2,1)S(1)} %collective-permute-done.16.refs_10_), channel_id=1, source_target_pairs={{0,1},{1,0},{2,3},{3,2},{4,5},{5,4},{6,7},{7,6},{8,9},{9,8},{10,11... | collective-permute-start | bytes 1572872 | tf_op jit(solution)/shard_map/ppermute | solution.py:355
  74.5 5.9 %collective-permute-start.19 = (f32[8,256]{1,0:T(8,128)S(1)}, f32[8,256]{1,0:T(8,128)S(1)}, u32[]{:S(2)}, u32[]{:S(2)}) collective-permute-start(f32[8,256]{1,0:T(8,128)S(1)} %get-tuple-element.53.refs_13_), channel_id=1, source_target_pairs={{0,1},{1,0},{2,3},{3,2},{4,5},{5,4},{6,7},{7,6},{8,9},{9,8},{10,11... | collective-permute-start | bytes 24584 | tf_op jit(solution)/shard_map/ppermute | solution.py:362
  79.8 1.2 collective-permute-start.18
  79.9 30.0 %collective-permute-start.24 = (bf16[1024,256]{1,0:T(8,128)(2,1)S(1)}, bf16[1024,256]{1,0:T(8,128)(2,1)S(1)}, u32[]{:S(2)}, u32[]{:S(2)}) collective-permute-start(bf16[1024,256]{1,0:T(8,128)(2,1)S(1)} %get-tuple-element.60.refs_4_), channel_id=1, source_target_pairs={{0,1},{1,0},{2,3},{3,2},{4,5},{5,4},{6,7},{7,6},{8,9},{9,8},{10,11... | collective-permute-start | bytes 1572872 | tf_op jit(solution)/shard_map/ppermute | solution.py:363
  80.4 29.5 %collective-permute-start.23 = (bf16[1024,256]{1,0:T(8,128)(2,1)S(1)}, bf16[1024,256]{1,0:T(8,128)(2,1)S(1)}, u32[]{:S(2)}, u32[]{:S(2)}) collective-permute-start(bf16[1024,256]{1,0:T(8,128)(2,1)S(1)} %get-tuple-element.59.refs_3_), channel_id=1, source_target_pairs={{0,1},{1,0},{2,3},{3,2},{4,5},{5,4},{6,7},{7,6},{8,9},{9,8},{10,11... | collective-permute-start | bytes 1572872 | tf_op jit(solution)/shard_map/ppermute | solution.py:363
  85.7 14.7 %collective-permute-start.20 = (bf16[144,1024]{1,0:T(8,128)(2,1)S(1)}, bf16[144,1024]{1,0:T(8,128)(2,1)S(1)}, u32[]{:S(2)}, u32[]{:S(2)}) collective-permute-start(bf16[144,1024]{1,0:T(8,128)(2,1)S(1)} %get-tuple-element.56), channel_id=1, source_target_pairs={{0,4},{4,0},{8,12},{12,8},{1,5},{5,1},{9,13},{13,9},{2,6},{6,2},{1... | collective-permute-start | bytes 884744 | tf_op jit(solution)/shard_map/ppermute | solution.py:39
  86.4 23.4 %collective-permute-start.21 = (bf16[144,1024]{1,0:T(8,128)(2,1)S(1)}, bf16[144,1024]{1,0:T(8,128)(2,1)S(1)}, u32[]{:S(2)}, u32[]{:S(2)}) collective-permute-start(bf16[144,1024]{1,0:T(8,128)(2,1)S(1)} %get-tuple-element.57), channel_id=1, source_target_pairs={{0,8},{4,12},{8,0},{12,4},{1,9},{5,13},{9,1},{13,5},{2,10},{6,14},... | collective-permute-start | bytes 884744 | tf_op jit(solution)/shard_map/ppermute | solution.py:39
  88.4 21.5 %collective-permute-start.22 = (bf16[144,1024]{1,0:T(8,128)(2,1)S(1)}, bf16[144,1024]{1,0:T(8,128)(2,1)S(1)}, u32[]{:S(2)}, u32[]{:S(2)}) collective-permute-start(bf16[144,1024]{1,0:T(8,128)(2,1)S(1)} %get-tuple-element.58), channel_id=1, source_target_pairs={{0,12},{4,8},{8,4},{12,0},{1,13},{5,9},{9,5},{13,1},{2,14},{6,10},... | collective-permute-start | bytes 884744 | tf_op jit(solution)/shard_map/ppermute | solution.py:39
  111.8 8.3 %collective-permute-start.25 = (bf16[128,256]{1,0:T(8,128)(2,1)S(1)}, bf16[128,256]{1,0:T(8,128)(2,1)S(1)}, u32[]{:S(2)}, u32[]{:S(2)}) collective-permute-start(bf16[128,256]{1,0:T(8,128)(2,1)S(1)} %get-tuple-element.62), channel_id=1, source_target_pairs={{0,4},{4,0},{8,12},{12,8},{1,5},{5,1},{9,13},{13,9},{2,6},{6,2},{1... | collective-permute-start | bytes 196616 | tf_op jit(solution)/shard_map/ppermute | solution.py:39
  117.7 7.2 %collective-permute-start.26 = (bf16[128,256]{1,0:T(8,128)(2,1)S(1)}, bf16[128,256]{1,0:T(8,128)(2,1)S(1)}, u32[]{:S(2)}, u32[]{:S(2)}) collective-permute-start(bf16[128,256]{1,0:T(8,128)(2,1)S(1)} %get-tuple-element.63), channel_id=1, source_target_pairs={{0,8},{4,12},{8,0},{12,4},{1,9},{5,13},{9,1},{13,5},{2,10},{6,14},... | collective-permute-start | bytes 196616 | tf_op jit(solution)/shard_map/ppermute | solution.py:39
  118.3 6.5 %collective-permute-start.27 = (bf16[128,256]{1,0:T(8,128)(2,1)S(1)}, bf16[128,256]{1,0:T(8,128)(2,1)S(1)}, u32[]{:S(2)}, u32[]{:S(2)}) collective-permute-start(bf16[128,256]{1,0:T(8,128)(2,1)S(1)} %get-tuple-element.64), channel_id=1, source_target_pairs={{0,12},{4,8},{8,4},{12,0},{1,13},{5,9},{9,5},{13,1},{2,14},{6,10},... | collective-permute-start | bytes 196616 | tf_op jit(solution)/shard_map/ppermute | solution.py:39
  126.8 2.0 %collective-permute-start.28 = (bf16[128,2048]{1,0:T(8,128)(2,1)S(1)}, bf16[128,2048]{1,0:T(8,128)(2,1)S(1)}, u32[]{:S(2)}, u32[]{:S(2)}) collective-permute-start(bf16[128,2048]{1,0:T(8,128)(2,1)S(1)} %convert_element_type.24), channel_id=1, source_target_pairs={{0,1},{1,0},{2,3},{3,2},{4,5},{5,4},{6,7},{7,6},{8,9},{9,8},{10,11... | collective-permute-start | bytes 1572872 | tf_op jit(solution)/shard_map/ppermute | solution.py:371
  128.9 8.4 %collective-permute-start.29 = (bf16[64,2048]{1,0:T(8,128)(2,1)S(1)}, bf16[64,2048]{1,0:T(8,128)(2,1)S(1)}, u32[]{:S(2)}, u32[]{:S(2)}) collective-permute-start(bf16[64,2048]{1,0:T(8,128)(2,1)S(1)} %fusion), channel_id=1, source_target_pairs={{0,2},{2,0},{1,3},{3,1},{4,6},{6,4},{5,7},{7,5},{8,10},{10,8},{9,1... | collective-permute-start | bytes 786440 | tf_op jit(solution)/shard_map/ppermute | solution.py:372

commit v5 on v4

--- a/solution.py
+++ b/solution.py
@@ -163,9 +163,7 @@
     own[...] = whole[pl.ds(pl.multiple_of(level * chunk, chunk), chunk)]
     for step in range(1, levels):
         to = pl.multiple_of((level ^ step) * chunk, chunk)
-        message = messages[step - 1]
-        message[pl.ds(0, chunk)] = whole[pl.ds(to, chunk)].astype(bf16)
-        message[pl.ds(chunk, 16)] = jnp.concatenate([high, low])
+        messages[step - 1][...] = jnp.concatenate([whole[pl.ds(to, chunk)].astype(bf16), high[:4], low[:4]])
 
 
 def cross(where, acts, early, bases, pieces, sums, rows, levels):
@@ -176,7 +174,7 @@
     return pl.pallas_call(
         functools.partial(cross_kernel, levels, rows),
         out_shape=[shape((chunk, width), f32), shape((8, width), f32)]
-        + [shape((chunk + 16, width), bf16)] * (levels - 1),
+        + [shape((chunk + 8, width), bf16)] * (levels - 1),
         in_specs=[SMEM] + [ANY] * 12 + [VMEM] * 4,
         out_specs=[VMEM] * (1 + levels),
         scratch_shapes=[
@@ -204,9 +202,10 @@
     total = own[...]
     extra = own_extra[...]
     for message in messages:
-        total = total + message[pl.ds(0, chunk)].astype(f32)
-        more = message[pl.ds(chunk, 16)].astype(f32)
-        extra = extra + (more[0:8] + more[8:16])
+        part_sum = message[...].astype(f32)
+        total = total + part_sum[:chunk]
+        more = part_sum[chunk:]
+        extra = extra + jnp.concatenate([more[0:4] + more[4:8], jnp.zeros_like(more[:4])])
     count = extra[2:3]
     extra = extra / count
     lam_a = extra[1:2]
@@ -324,15 +323,8 @@
     def diagonal(x):
         return lax.ppermute(x, ("chip", "core"), [(i, 3 - i) for i in range(4)])
 
-    beside = lax.ppermute(columns(chip, 1 - core), "core", SWAP)
-    blocks = jnp.stack(
-        [
-            columns(chip, core),
-            beside,
-            lax.ppermute(columns(1 - chip, core), "chip", SWAP),
-            diagonal(columns(1 - chip, 1 - core)),
-        ]
-    )
+    beyond = [lax.ppermute(columns(1 - chip, core), "chip", SWAP), diagonal(columns(1 - chip, 1 - core))]
+    blocks = jnp.stack([columns(chip, core), lax.ppermute(columns(chip, 1 - core), "core", SWAP)] + beyond)
     blocks = [lax.dynamic_index_in_dim(blocks, j ^ (chip * 2 + core), 0, False) for j in range(4)]
     unit = jnp.concatenate([b[:rows_g] for b in blocks] + [b[rows_g:] for b in blocks])
     level_g, level_a = 4 * rows_g, 4 * rows_a
@@ -346,19 +338,18 @@
     early = jnp.where(keep[:half], grads[:half], 0)
     early = jnp.concatenate([jnp.where(keep, acts, 0), marks, early[:, :width_a], early[:, width_a:]])
     late = jnp.where(keep[half:], grads[half:], 0)
-    (early_out, late_out), _ = lax.optimization_barrier(((early, late), beside))
+    (early_out, late_out), _ = lax.optimization_barrier(((early, late), beyond))
 
     def four(mine, out, after):
-        far = lax.ppermute(out, "chip", SWAP)
-        if after is not None:
-            far, after = lax.optimization_barrier((far, after))
+        far, after = lax.optimization_barrier((lax.ppermute(out, "chip", SWAP), after))
         return [mine, lax.ppermute(mine, "core", SWAP), far, lax.ppermute(far, "core", SWAP)], after
 
     early, slots[-1] = four(early, early_out, slots[-1])
-    late, _ = four(late, late_out, None)
-    bases_a, turned_g, bases_g, sums = zip(
-        turn(where, slots, early, rows, level_g, level_a), turn(where, others, early, rows, level_g, level_a)
-    )
+    first = turn(where, slots, early, rows, level_g, level_a)
+    others[-1], first = lax.optimization_barrier((others[-1], first))
+    second = turn(where, others, early, rows, level_g, level_a)
+    late, second = four(late, late_out, second)
+    bases_a, turned_g, bases_g, sums = zip(first, second)
     sums += tuple(lax.ppermute(t, "core", SWAP) for t in sums)
     bases_a += tuple(lax.ppermute(t, "core", SWAP) for t in bases_a)
     own, own_extra, *messages = cross(where, early, turned_g, bases_g, late, sums, rows, levels)

time: 139 us -> 129 us (0.928)
  waiting for transfers between devices: 78.1 us -> 68.9 us
    ppermute x3, waiting for transfers between devices: 12.2 us -> 0.01 us  [the longest x2 0.01 us: four(): lax.ppermute(out, 'chip', SWAP)]
    ppermute x4, waiting for transfers between devices: 15.3 us -> 17.9 us  [over(): return lax.ppermute(slot, 'group', SWAP)]
    ppermute x2, waiting for transfers between devices: 0.01 us -> 1.79 us  [four(): lax.ppermute(far, 'core', SWAP)]
  transfers between devices with their start and end apart: 30 -> 30, of which waited for: 14 -> 16; matrix products, arithmetic and copies ran while one was open for 3% -> 3% of each run, Pallas kernels for 10% -> 11%
where the time goes in v5:
time: 129 us
  waiting for transfers between devices  68.9 us (53%)
  starting transfers between devices  32.9 us (26%)
  Pallas kernels  18.4 us (14%)
  other arithmetic  5.44 us (4%)
  local copies, waits for them, and re-layouts  1.94 us (2%)
    ppermute x7, waiting for transfers between devices, across(): return lax.ppermute(x, 'level', [(i, i ^ step) for i in range(levels)])  30.1 us
    ppermute x4, waiting for transfers between devices, over(): return lax.ppermute(slot, 'group', SWAP)  17.9 us
    ppermute x7, starting transfers between devices, across(): return lax.ppermute(x, 'level', [(i, i ^ step) for i in range(levels)])  14 us
    pallas_call x2, Pallas kernels, turn(): pl.pallas_call(functools.partial(turn_kernel, levels, level_g, level_a, r...  9.94 us
    ppermute x1, waiting for transfers between devices, body(): lax.ppermute((kept[:rows_a] + sent[:rows_a]).astype(bf16), 'chip', SWAP)  6.86 us
    ppermute x1, waiting for transfers between devices, gather_levels(): lax.ppermute(third, 'level', outward)  6.1 us
    ppermute x4, starting transfers between devices, over(): return lax.ppermute(slot, 'group', SWAP)  5.14 us
    pallas_call x1, Pallas kernels, cross(): pl.pallas_call(functools.partial(cross_kernel, levels, rows), out_shape=[...  4.67 us
  transfers between devices with their start and end apart: 30, of which 16 were waited for; matrix products, arithmetic and copies ran while one was open for 3% of the time, Pallas kernels for 11%

profile of v5, /device:TPU:0, one launch (start us, length us, event | category | flops | bytes accessed | tf_op | source)
XLA Modules:
  0.0 128.6 jit_solution(16168800584136102527)
XLA Ops:
  0.0 0.8 constant_dynamic-slice_fusion.2
  0.8 1.0 constant_dynamic-slice_fusion.1
  1.8 0.5 collective-permute-start.4
  2.3 2.6 %collective-permute-start.1 = (bf16[192,256]{1,0:T(8,128)(2,1)S(1)}, bf16[192,256]{1,0:T(8,128)(2,1)S(1)}, u32[]{:S(2)}, u32[]{:S(2)}) collective-permute-start(bf16[192,256]{1,0:T(8,128)(2,1)S(1)} %get-tuple-element.96), channel_id=1, source_target_pairs={{0,2},{2,0},{1,3},{3,1},{4,6},{6,4},{5,7},{7,5},{8,10},{10,8},{9,1... | collective-permute-start | bytes 294920 | tf_op jit(solution)/shard_map/ppermute | solution.py:326
  5.8 1.4 %slice_select_fusion = bf16[256,2048]{1,0:T(8,128)(2,1)S(1)} fusion(bf16[384,2048]{1,0:T(8,128)(2,1)} %param.6, pred[256]{0:T(512)(128)(4,1)S(1)} %slice_reduce_fusion), kind=kLoop, calls=%fused_computation.1 | loop fusion | flops 524288 | bytes 2097408 | tf_op jit(solution)/shard_map/jit(_where)/select_n | solution.py:338
  7.3 1.2 slice_select_fusion.1.refs_8_
  9.2 1.1 collective-permute-done.2
  10.4 1.6 %collective-permute-start.3 = (bf16[912,1024]{1,0:T(8,128)(2,1)S(1)}, bf16[912,1024]{1,0:T(8,128)(2,1)}, u32[]{:S(2)}, u32[]{:S(2)}) collective-permute-start(bf16[912,1024]{1,0:T(8,128)(2,1)S(1)} %pad_maximum_fusion.refs_4_.refs_0_), channel_id=1, source_target_pairs={{0,2},{2,0},{1,3},{3,1},{4,6},{6,4},{5,7},{7,5},{8,10},{10,8},{9,1... | collective-permute-start | bytes 5603336 | tf_op jit(solution)/shard_map/ppermute | solution.py:344
  12.1 1.5 %collective-permute-start.5 = (bf16[768,256]{1,0:T(8,128)(2,1)S(1)}, bf16[768,256]{1,0:T(8,128)(2,1)}, u32[]{:S(2)}, u32[]{:S(2)}) collective-permute-start(bf16[768,256]{1,0:T(8,128)(2,1)S(1)} %fusion.8.refs_0_), channel_id=1, source_target_pairs={{0,4},{4,0},{8,12},{12,8},{1,5},{5,1},{9,13},{13,9},{2,6},{6,2},{1... | collective-permute-start | bytes 1179656 | tf_op jit(solution)/shard_map/ppermute | solution.py:39
  13.6 1.4 %collective-permute-start.6 = (bf16[768,256]{1,0:T(8,128)(2,1)S(1)}, bf16[768,256]{1,0:T(8,128)(2,1)}, u32[]{:S(2)}, u32[]{:S(2)}) collective-permute-start(bf16[768,256]{1,0:T(8,128)(2,1)S(1)} %fusion.8.refs_0_), channel_id=1, source_target_pairs={{4,8},{8,4},{5,9},{9,5},{6,10},{10,6},{7,11},{11,7},{20,24},{24,20... | collective-permute-start | bytes 1179656 | tf_op jit(solution)/shard_map/ppermute | solution.py:296
  15.0 1.5 %collective-permute-start.7 = (bf16[768,256]{1,0:T(8,128)(2,1)S(1)}, bf16[768,256]{1,0:T(8,128)(2,1)S(1)}, u32[]{:S(2)}, u32[]{:S(2)}) collective-permute-start(bf16[768,256]{1,0:T(8,128)(2,1)S(1)} %fusion.8.refs_0_), channel_id=1, source_target_pairs={{0,16},{16,0},{1,17},{17,1},{2,18},{18,2},{3,19},{19,3},{4,20},{20... | collective-permute-start | bytes 1179656 | tf_op jit(solution)/shard_map/ppermute | solution.py:288
  16.5 6.6 %collective-permute-done.5.refs_1_ = bf16[768,256]{1,0:T(8,128)(2,1)} collective-permute-done((bf16[768,256]{1,0:T(8,128)(2,1)S(1)}, bf16[768,256]{1,0:T(8,128)(2,1)}, u32[]{:S(2)}, u32[]{:S(2)}) %collective-permute-start.5) | collective-permute-done | bytes 393248 | tf_op jit(solution)/shard_map/ppermute | solution.py:39
  23.1 2.6 %collective-permute-done.7.refs_0_ = bf16[768,256]{1,0:T(8,128)(2,1)S(1)} collective-permute-done((bf16[768,256]{1,0:T(8,128)(2,1)S(1)}, bf16[768,256]{1,0:T(8,128)(2,1)S(1)}, u32[]{:S(2)}, u32[]{:S(2)}) %collective-permute-start.7) | collective-permute-done | bytes 393248 | tf_op jit(solution)/shard_map/ppermute | solution.py:288
  25.7 1.5 %collective-permute-start.10 = (bf16[768,256]{1,0:T(8,128)(2,1)}, bf16[768,256]{1,0:T(8,128)(2,1)}, u32[]{:S(2)}, u32[]{:S(2)}) collective-permute-start(bf16[768,256]{1,0:T(8,128)(2,1)} %collective-permute-done.5.refs_1_), channel_id=1, source_target_pairs={{0,16},{16,0},{1,17},{17,1},{2,18},{18,2},{3,19},{19,3},{4,20},{20... | collective-permute-start | bytes 1179656 | tf_op jit(solution)/shard_map/ppermute | solution.py:288
  27.2 1.4 %collective-permute-start.8 = (bf16[768,256]{1,0:T(8,128)(2,1)}, bf16[768,256]{1,0:T(8,128)(2,1)}, u32[]{:S(2)}, u32[]{:S(2)}) collective-permute-start(bf16[768,256]{1,0:T(8,128)(2,1)} %collective-permute-done.5.refs_1_), channel_id=1, source_target_pairs={{4,8},{8,4},{5,9},{9,5},{6,10},{10,6},{7,11},{11,7},{20,24},{24,20... | collective-permute-start | bytes 1179656 | tf_op jit(solution)/shard_map/ppermute | solution.py:298
  28.6 1.3 collective-permute-start.9
  29.9 6.0 %collective-permute-done.10.refs_1_ = bf16[768,256]{1,0:T(8,128)(2,1)} collective-permute-done((bf16[768,256]{1,0:T(8,128)(2,1)}, bf16[768,256]{1,0:T(8,128)(2,1)}, u32[]{:S(2)}, u32[]{:S(2)}) %collective-permute-start.10) | collective-permute-done | bytes 393248 | tf_op jit(solution)/shard_map/ppermute | solution.py:288
  35.9 6.1 %collective-permute-done.9 = bf16[768,256]{1,0:T(8,128)(2,1)} collective-permute-done((bf16[768,256]{1,0:T(8,128)(2,1)}, bf16[768,256]{1,0:T(8,128)(2,1)}, u32[]{:S(2)}, u32[]{:S(2)}) %collective-permute-start.9) | collective-permute-done | bytes 393248 | tf_op jit(solution)/shard_map/ppermute | solution.py:298
  42.0 1.0 broadcast_select_fusion.2.refs_2_
  43.1 0.6 collective-permute-start.12
  43.7 1.3 collective-permute-start.11
  45.0 6.8 %collective-permute-done.12.refs_2_ = bf16[768,256]{1,0:T(8,128)(2,1)S(1)} collective-permute-done((bf16[768,256]{1,0:T(8,128)(2,1)S(1)}, bf16[768,256]{1,0:T(8,128)(2,1)S(1)}, u32[]{:S(2)}, u32[]{:S(2)}) %collective-permute-start.12) | collective-permute-done | bytes 393248 | tf_op jit(solution)/shard_map/ppermute | solution.py:288
  51.8 2.3 %collective-permute-done.11 = bf16[768,256]{1,0:T(8,128)(2,1)S(1)} collective-permute-done((bf16[768,256]{1,0:T(8,128)(2,1)}, bf16[768,256]{1,0:T(8,128)(2,1)S(1)}, u32[]{:S(2)}, u32[]{:S(2)}) %collective-permute-start.11) | collective-permute-done | bytes 393248 | tf_op jit(solution)/shard_map/ppermute | solution.py:301
  54.3 1.6 %collective-permute-start.14 = (bf16[768,256]{1,0:T(8,128)(2,1)S(1)}, bf16[768,256]{1,0:T(8,128)(2,1)S(1)}, u32[]{:S(2)}, u32[]{:S(2)}) collective-permute-start(bf16[768,256]{1,0:T(8,128)(2,1)S(1)} %broadcast_select_fusion.1.refs_3_), channel_id=1, source_target_pairs={{0,16},{16,0},{1,17},{17,1},{2,18},{18,2},{3,19},{19,3},{4,20},{20... | collective-permute-start | bytes 1179656 | tf_op jit(solution)/shard_map/ppermute | solution.py:288
  55.9 0.6 collective-permute-start.15
  56.6 1.8 %collective-permute-done.13.refs_7_.refs_3_ = bf16[912,1024]{1,0:T(8,128)(2,1)S(1)} collective-permute-done((bf16[912,1024]{1,0:T(8,128)(2,1)}, bf16[912,1024]{1,0:T(8,128)(2,1)S(1)}, u32[]{:S(2)}, u32[]{:S(2)}) %collective-permute-start.13) | collective-permute-done | bytes 1867808 | tf_op jit(solution)/shard_map/ppermute | solution.py:345
  58.4 5.0 %shard_map.55 = (bf16[1024,256]{1,0:T(8,128)(2,1)S(1)}, bf16[1024,256]{1,0:T(8,128)(2,1)S(1)}, bf16[2048,256]{1,0:T(8,128)(2,1)S(1)}, f32[8,256]{1,0:T(8,128)S(1)}) custom-call(s32[2]{0:T(128)S(1)} %pad_add_fusion.where, bf16[768,256]{1,0:T(8,128)(2,1)S(1)} %fusion.8.refs_0_, bf16[768,256]{1,0:T(8,128)(2,1)} %collective-permute-done.5.refs_1_, ...), custom_call_target="tpu_custom_call" | custom-call | flops 1610612736 | bytes 6291456 | tf_op jit(solution)/shard_map/pallas_call | solution.py:92
  63.3 2.5 %collective-permute-done.14.refs_3_ = bf16[768,256]{1,0:T(8,128)(2,1)S(1)} collective-permute-done((bf16[768,256]{1,0:T(8,128)(2,1)S(1)}, bf16[768,256]{1,0:T(8,128)(2,1)S(1)}, u32[]{:S(2)}, u32[]{:S(2)}) %collective-permute-start.14) | collective-permute-done | bytes 393248 | tf_op jit(solution)/shard_map/ppermute | solution.py:288
  65.9 5.0 %shard_map.56 = (bf16[1024,256]{1,0:T(8,128)(2,1)S(1)}, bf16[1024,256]{1,0:T(8,128)(2,1)S(1)}, bf16[2048,256]{1,0:T(8,128)(2,1)S(1)}, f32[8,256]{1,0:T(8,128)S(1)}) custom-call(s32[2]{0:T(128)S(1)} %pad_add_fusion.where, bf16[768,256]{1,0:T(8,128)(2,1)S(1)} %collective-permute-done.7.refs_0_, bf16[768,256]{1,0:T(8,128)(2,1)} %collective-permute-done.10.refs_1_, ...), custom_call_target="tpu_custom_call" | custom-call | flops 1610612736 | bytes 6291456 | tf_op jit(solution)/shard_map/pallas_call | solution.py:92
  70.9 0.5 collective-permute-start.19
  72.0 0.8 collective-permute-done.19.refs_15_
  72.8 4.7 %shard_map.57 = (f32[128,1024]{1,0:T(8,128)S(1)}, f32[8,1024]{1,0:T(8,128)S(1)}, bf16[136,1024]{1,0:T(8,128)(2,1)S(1)}, bf16[136,1024]{1,0:T(8,128)(2,1)S(1)}, bf16[136,1024]{1,0:T(8,128)(2,1)S(1)}) custom-call(s32[2]{0:T(128)S(1)} %pad_add_fusion.where, bf16[912,1024]{1,0:T(8,128)(2,1)S(1)} %pad_maximum_fusion.refs_4_.refs_0_, ...), custom_call_target="tpu_custom_call" | custom-call | flops 3221225472 | bytes 6291456 | tf_op jit(solution)/shard_map/pallas_call | solution.py:174
  77.5 0.8 collective-permute-start.20
  78.3 2.6 %collective-permute-start.21 = (bf16[136,1024]{1,0:T(8,128)(2,1)S(1)}, bf16[136,1024]{1,0:T(8,128)(2,1)S(1)}, u32[]{:S(2)}, u32[]{:S(2)}) collective-permute-start(bf16[136,1024]{1,0:T(8,128)(2,1)S(1)} %get-tuple-element.77), channel_id=1, source_target_pairs={{0,8},{4,12},{8,0},{12,4},{1,9},{5,13},{9,1},{13,5},{2,10},{6,14},... | collective-permute-start | bytes 835592 | tf_op jit(solution)/shard_map/ppermute | solution.py:39
  80.9 1.1 collective-permute-start.22
  82.0 9.7 %collective-permute-done.20.refs_0_ = bf16[136,1024]{1,0:T(8,128)(2,1)S(1)} collective-permute-done((bf16[136,1024]{1,0:T(8,128)(2,1)S(1)}, bf16[136,1024]{1,0:T(8,128)(2,1)S(1)}, u32[]{:S(2)}, u32[]{:S(2)}) %collective-permute-start.20) | collective-permute-done | bytes 278560 | tf_op jit(solution)/shard_map/ppermute | solution.py:39
  91.7 9.0 %collective-permute-done.21.refs_1_ = bf16[136,1024]{1,0:T(8,128)(2,1)S(1)} collective-permute-done((bf16[136,1024]{1,0:T(8,128)(2,1)S(1)}, bf16[136,1024]{1,0:T(8,128)(2,1)S(1)}, u32[]{:S(2)}, u32[]{:S(2)}) %collective-permute-start.21) | collective-permute-done | bytes 278560 | tf_op jit(solution)/shard_map/ppermute | solution.py:39
  100.7 1.9 %shard_map.58 = (bf16[128,256]{1,0:T(8,128)(2,1)S(1)}, bf16[128,256]{1,0:T(8,128)(2,1)S(1)}, bf16[128,256]{1,0:T(8,128)(2,1)S(1)}, bf16[128,256]{1,0:T(8,128)(2,1)S(1)}) custom-call(s32[2]{0:T(128)S(1)} %pad_add_fusion.where, f32[128,1024]{1,0:T(8,128)S(1)} %get-tuple-element.74.own, f32[8,1024]{1,0:T(8,128)S(1)} %get-tuple-element.75.own_extra, ...), custom_call_target="tpu_custom_call" | custom-call | flops 805306368 | bytes 2097152 | tf_op jit(solution)/shard_map/pallas_call | solution.py:228
  102.6 5.5 %collective-permute-start.25 = (bf16[128,256]{1,0:T(8,128)(2,1)S(1)}, bf16[128,256]{1,0:T(8,128)(2,1)S(1)}, u32[]{:S(2)}, u32[]{:S(2)}) collective-permute-start(bf16[128,256]{1,0:T(8,128)(2,1)S(1)} %get-tuple-element.82), channel_id=1, source_target_pairs={{0,4},{4,0},{8,12},{12,8},{1,5},{5,1},{9,13},{13,9},{2,6},{6,2},{1... | collective-permute-start | bytes 196616 | tf_op jit(solution)/shard_map/ppermute | solution.py:39
  108.2 1.1 collective-permute-start.26
  109.2 1.4 %collective-permute-start.27 = (bf16[128,256]{1,0:T(8,128)(2,1)S(1)}, bf16[128,256]{1,0:T(8,128)(2,1)S(1)}, u32[]{:S(2)}, u32[]{:S(2)}) collective-permute-start(bf16[128,256]{1,0:T(8,128)(2,1)S(1)} %get-tuple-element.84), channel_id=1, source_target_pairs={{0,12},{4,8},{8,4},{12,0},{1,13},{5,9},{9,5},{13,1},{2,14},{6,10},... | collective-permute-start | bytes 196616 | tf_op jit(solution)/shard_map/ppermute | solution.py:39
  110.6 4.0 %collective-permute-done.26.refs_2_ = bf16[128,256]{1,0:T(8,128)(2,1)S(1)} collective-permute-done((bf16[128,256]{1,0:T(8,128)(2,1)S(1)}, bf16[128,256]{1,0:T(8,128)(2,1)S(1)}, u32[]{:S(2)}, u32[]{:S(2)}) %collective-permute-start.26) | collective-permute-done | bytes 65568 | tf_op jit(solution)/shard_map/ppermute | solution.py:39
  114.6 0.8 collective-permute-done.27.refs_3_
  115.4 1.8 %shard_map.59 = (f32[128,2048]{1,0:T(8,128)S(1)}, f32[128,2048]{1,0:T(8,128)S(1)}) custom-call(s32[2]{0:T(128)S(1)} %pad_add_fusion.where, bf16[128,256]{1,0:T(8,128)(2,1)S(1)} %get-tuple-element.81.refs_0_, bf16[128,256]{1,0:T(8,128)(2,1)S(1)} %collective-permute-done.25.refs_1_, bf16[128,256]{1,0:T(8,128)(2,1)S(1)} %collective-permute-done.26.refs_2_, ...), custom_call_target="tpu_custom_call" | custom-call | flops 536870912 | bytes 2097152 | tf_op jit(solution)/shard_map/pallas_call | solution.py:271
  117.4 1.9 %collective-permute-done.28 = bf16[128,2048]{1,0:T(8,128)(2,1)S(1)} collective-permute-done((bf16[128,2048]{1,0:T(8,128)(2,1)S(1)}, bf16[128,2048]{1,0:T(8,128)(2,1)S(1)}, u32[]{:S(2)}, u32[]{:S(2)}) %collective-permute-start.28) | collective-permute-done | bytes 524320 | tf_op jit(solution)/shard_map/ppermute | solution.py:362
  119.4 1.5 %collective-permute-start.29 = (bf16[64,2048]{1,0:T(8,128)(2,1)S(1)}, bf16[64,2048]{1,0:T(8,128)(2,1)S(1)}, u32[]{:S(2)}, u32[]{:S(2)}) collective-permute-start(bf16[64,2048]{1,0:T(8,128)(2,1)S(1)} %fusion), channel_id=1, source_target_pairs={{0,2},{2,0},{1,3},{3,1},{4,6},{6,4},{5,7},{7,5},{8,10},{10,8},{9,1... | collective-permute-start | bytes 786440 | tf_op jit(solution)/shard_map/ppermute | solution.py:363
  121.0 6.9 %collective-permute-done.29 = bf16[64,2048]{1,0:T(8,128)(2,1)S(1)} collective-permute-done((bf16[64,2048]{1,0:T(8,128)(2,1)S(1)}, bf16[64,2048]{1,0:T(8,128)(2,1)S(1)}, u32[]{:S(2)}, u32[]{:S(2)}) %collective-permute-start.29) | collective-permute-done | bytes 262176 | tf_op jit(solution)/shard_map/ppermute | solution.py:363
  127.8 0.8 fusion.2
  (50 shorter events, 2.3 us)
Async XLA Ops:
  1.8 7.4 %collective-permute-start.4 = (bf16[192,256]{1,0:T(8,128)(2,1)S(1)}, bf16[192,256]{1,0:T(8,128)(2,1)S(1)}, u32[]{:S(2)}, u32[]{:S(2)}) collective-permute-start(bf16[192,256]{1,0:T(8,128)(2,1)S(1)} %get-tuple-element.97), channel_id=1, source_target_pairs={{0,1},{1,0},{2,3},{3,2},{4,5},{5,4},{6,7},{7,6},{8,9},{9,8},{10,11... | collective-permute-start | bytes 294920 | tf_op jit(solution)/shard_map/ppermute | solution.py:327
  2.3 6.9 %collective-permute-start.1 = (bf16[192,256]{1,0:T(8,128)(2,1)S(1)}, bf16[192,256]{1,0:T(8,128)(2,1)S(1)}, u32[]{:S(2)}, u32[]{:S(2)}) collective-permute-start(bf16[192,256]{1,0:T(8,128)(2,1)S(1)} %get-tuple-element.96), channel_id=1, source_target_pairs={{0,2},{2,0},{1,3},{3,1},{4,6},{6,4},{5,7},{7,5},{8,10},{10,8},{9,1... | collective-permute-start | bytes 294920 | tf_op jit(solution)/shard_map/ppermute | solution.py:326
  4.9 5.4 %collective-permute-start.2 = (bf16[192,256]{1,0:T(8,128)(2,1)S(1)}, bf16[192,256]{1,0:T(8,128)(2,1)S(1)}, u32[]{:S(2)}, u32[]{:S(2)}) collective-permute-start(bf16[192,256]{1,0:T(8,128)(2,1)S(1)} %get-tuple-element.98), channel_id=1, source_target_pairs={{0,3},{1,2},{2,1},{3,0},{4,7},{5,6},{6,5},{7,4},{8,11},{9,10},{10,... | collective-permute-start | bytes 294920 | tf_op jit(solution)/shard_map/ppermute | solution.py:324
  7.2 1.4 %copy-start = (bf16[384,1024]{1,0:T(8,128)(2,1)S(1)}, bf16[384,1024]{1,0:T(8,128)(2,1)}, u32[]{:S(2)}) copy-start(bf16[384,1024]{1,0:T(8,128)(2,1)} %param.5) | copy-start | bytes 2359300
  10.4 43.8 %collective-permute-start.3 = (bf16[912,1024]{1,0:T(8,128)(2,1)S(1)}, bf16[912,1024]{1,0:T(8,128)(2,1)}, u32[]{:S(2)}, u32[]{:S(2)}) collective-permute-start(bf16[912,1024]{1,0:T(8,128)(2,1)S(1)} %pad_maximum_fusion.refs_4_.refs_0_), channel_id=1, source_target_pairs={{0,2},{2,0},{1,3},{3,1},{4,6},{6,4},{5,7},{7,5},{8,10},{10,8},{9,1... | collective-permute-start | bytes 5603336 | tf_op jit(solution)/shard_map/ppermute | solution.py:344
  12.1 11.1 %collective-permute-start.5 = (bf16[768,256]{1,0:T(8,128)(2,1)S(1)}, bf16[768,256]{1,0:T(8,128)(2,1)}, u32[]{:S(2)}, u32[]{:S(2)}) collective-permute-start(bf16[768,256]{1,0:T(8,128)(2,1)S(1)} %fusion.8.refs_0_), channel_id=1, source_target_pairs={{0,4},{4,0},{8,12},{12,8},{1,5},{5,1},{9,13},{13,9},{2,6},{6,2},{1... | collective-permute-start | bytes 1179656 | tf_op jit(solution)/shard_map/ppermute | solution.py:39
  13.6 9.5 %collective-permute-start.6 = (bf16[768,256]{1,0:T(8,128)(2,1)S(1)}, bf16[768,256]{1,0:T(8,128)(2,1)}, u32[]{:S(2)}, u32[]{:S(2)}) collective-permute-start(bf16[768,256]{1,0:T(8,128)(2,1)S(1)} %fusion.8.refs_0_), channel_id=1, source_target_pairs={{4,8},{8,4},{5,9},{9,5},{6,10},{10,6},{7,11},{11,7},{20,24},{24,20... | collective-permute-start | bytes 1179656 | tf_op jit(solution)/shard_map/ppermute | solution.py:296
  15.0 10.7 %collective-permute-start.7 = (bf16[768,256]{1,0:T(8,128)(2,1)S(1)}, bf16[768,256]{1,0:T(8,128)(2,1)S(1)}, u32[]{:S(2)}, u32[]{:S(2)}) collective-permute-start(bf16[768,256]{1,0:T(8,128)(2,1)S(1)} %fusion.8.refs_0_), channel_id=1, source_target_pairs={{0,16},{16,0},{1,17},{17,1},{2,18},{18,2},{3,19},{19,3},{4,20},{20... | collective-permute-start | bytes 1179656 | tf_op jit(solution)/shard_map/ppermute | solution.py:288
  25.7 10.2 %collective-permute-start.10 = (bf16[768,256]{1,0:T(8,128)(2,1)}, bf16[768,256]{1,0:T(8,128)(2,1)}, u32[]{:S(2)}, u32[]{:S(2)}) collective-permute-start(bf16[768,256]{1,0:T(8,128)(2,1)} %collective-permute-done.5.refs_1_), channel_id=1, source_target_pairs={{0,16},{16,0},{1,17},{17,1},{2,18},{18,2},{3,19},{19,3},{4,20},{20... | collective-permute-start | bytes 1179656 | tf_op jit(solution)/shard_map/ppermute | solution.py:288
  27.2 8.7 %collective-permute-start.8 = (bf16[768,256]{1,0:T(8,128)(2,1)}, bf16[768,256]{1,0:T(8,128)(2,1)}, u32[]{:S(2)}, u32[]{:S(2)}) collective-permute-start(bf16[768,256]{1,0:T(8,128)(2,1)} %collective-permute-done.5.refs_1_), channel_id=1, source_target_pairs={{4,8},{8,4},{5,9},{9,5},{6,10},{10,6},{7,11},{11,7},{20,24},{24,20... | collective-permute-start | bytes 1179656 | tf_op jit(solution)/shard_map/ppermute | solution.py:298
  28.6 13.4 %collective-permute-start.9 = (bf16[768,256]{1,0:T(8,128)(2,1)}, bf16[768,256]{1,0:T(8,128)(2,1)}, u32[]{:S(2)}, u32[]{:S(2)}) collective-permute-start(bf16[768,256]{1,0:T(8,128)(2,1)} %collective-permute-done.6), channel_id=1, source_target_pairs={{4,0},{8,12},{5,1},{9,13},{6,2},{10,14},{7,3},{11,15},{20,16},{24,... | collective-permute-start | bytes 1179656 | tf_op jit(solution)/shard_map/ppermute | solution.py:298
  43.1 8.7 %collective-permute-start.12 = (bf16[768,256]{1,0:T(8,128)(2,1)S(1)}, bf16[768,256]{1,0:T(8,128)(2,1)S(1)}, u32[]{:S(2)}, u32[]{:S(2)}) collective-permute-start(bf16[768,256]{1,0:T(8,128)(2,1)S(1)} %broadcast_select_fusion.2.refs_2_), channel_id=1, source_target_pairs={{0,16},{16,0},{1,17},{17,1},{2,18},{18,2},{3,19},{19,3},{4,20},{20... | collective-permute-start | bytes 1179656 | tf_op jit(solution)/shard_map/ppermute | solution.py:288
  43.7 10.5 %collective-permute-start.11 = (bf16[768,256]{1,0:T(8,128)(2,1)}, bf16[768,256]{1,0:T(8,128)(2,1)S(1)}, u32[]{:S(2)}, u32[]{:S(2)}) collective-permute-start(bf16[768,256]{1,0:T(8,128)(2,1)} %collective-permute-done.8), channel_id=1, source_target_pairs={{4,0},{8,12},{5,1},{9,13},{6,2},{10,14},{7,3},{11,15},{20,16},{24,... | collective-permute-start | bytes 1179656 | tf_op jit(solution)/shard_map/ppermute | solution.py:301
  45.0 11.6 %collective-permute-start = (bf16[912,1024]{1,0:T(8,128)(2,1)S(1)}, bf16[912,1024]{1,0:T(8,128)(2,1)S(1)}, u32[]{:S(2)}, u32[]{:S(2)}) collective-permute-start(bf16[912,1024]{1,0:T(8,128)(2,1)S(1)} %pad_maximum_fusion.refs_4_.refs_0_), channel_id=1, source_target_pairs={{0,1},{1,0},{2,3},{3,2},{4,5},{5,4},{6,7},{7,6},{8,9},{9,8},{10,11... | collective-permute-start | bytes 5603336 | tf_op jit(solution)/shard_map/ppermute | solution.py:345
  54.2 4.1 %collective-permute-start.13 = (bf16[912,1024]{1,0:T(8,128)(2,1)}, bf16[912,1024]{1,0:T(8,128)(2,1)S(1)}, u32[]{:S(2)}, u32[]{:S(2)}) collective-permute-start(bf16[912,1024]{1,0:T(8,128)(2,1)} %collective-permute-done.3.refs_6_.refs_2_), channel_id=1, source_target_pairs={{0,1},{1,0},{2,3},{3,2},{4,5},{5,4},{6,7},{7,6},{8,9},{9,8},{10,11... | collective-permute-start | bytes 5603336 | tf_op jit(solution)/shard_map/ppermute | solution.py:345
  54.3 11.5 %collective-permute-start.14 = (bf16[768,256]{1,0:T(8,128)(2,1)S(1)}, bf16[768,256]{1,0:T(8,128)(2,1)S(1)}, u32[]{:S(2)}, u32[]{:S(2)}) collective-permute-start(bf16[768,256]{1,0:T(8,128)(2,1)S(1)} %broadcast_select_fusion.1.refs_3_), channel_id=1, source_target_pairs={{0,16},{16,0},{1,17},{17,1},{2,18},{18,2},{3,19},{19,3},{4,20},{20... | collective-permute-start | bytes 1179656 | tf_op jit(solution)/shard_map/ppermute | solution.py:288
  55.9 15.0 %collective-permute-start.15 = (bf16[128,2048]{1,0:T(8,128)(2,1)S(1)}, bf16[128,2048]{1,0:T(8,128)(2,1)S(1)}, u32[]{:S(2)}, u32[]{:S(2)}) collective-permute-start(bf16[128,2048]{1,0:T(8,128)(2,1)S(1)} %slice_select_fusion.1.refs_8_), channel_id=1, source_target_pairs={{0,2},{2,0},{1,3},{3,1},{4,6},{6,4},{5,7},{7,5},{8,10},{10,8},{9,1... | collective-permute-start | bytes 1572872 | tf_op jit(solution)/shard_map/ppermute | solution.py:344
  56.5 15.4 %collective-permute-start.16 = (bf16[128,2048]{1,0:T(8,128)(2,1)S(1)}, bf16[128,2048]{1,0:T(8,128)(2,1)S(1)}, u32[]{:S(2)}, u32[]{:S(2)}) collective-permute-start(bf16[128,2048]{1,0:T(8,128)(2,1)S(1)} %slice_select_fusion.1.refs_8_), channel_id=1, source_target_pairs={{0,1},{1,0},{2,3},{3,2},{4,5},{5,4},{6,7},{7,6},{8,9},{9,8},{10,11... | collective-permute-start | bytes 1572872 | tf_op jit(solution)/shard_map/ppermute | solution.py:345
  70.8 2.0 %collective-permute-start.17 = (bf16[128,2048]{1,0:T(8,128)(2,1)S(1)}, bf16[128,2048]{1,0:T(8,128)(2,1)S(1)}, u32[]{:S(2)}, u32[]{:S(2)}) collective-permute-start(bf16[128,2048]{1,0:T(8,128)(2,1)S(1)} %collective-permute-done.15.refs_10_), channel_id=1, source_target_pairs={{0,1},{1,0},{2,3},{3,2},{4,5},{5,4},{6,7},{7,6},{8,9},{9,8},{10,11... | collective-permute-start | bytes 1572872 | tf_op jit(solution)/shard_map/ppermute | solution.py:345
  70.9 1.9 %collective-permute-start.19 = (f32[8,256]{1,0:T(8,128)S(1)}, f32[8,256]{1,0:T(8,128)S(1)}, u32[]{:S(2)}, u32[]{:S(2)}) collective-permute-start(f32[8,256]{1,0:T(8,128)S(1)} %get-tuple-element.73.refs_13_), channel_id=1, source_target_pairs={{0,1},{1,0},{2,3},{3,2},{4,5},{5,4},{6,7},{7,6},{8,9},{9,8},{10,11... | collective-permute-start | bytes 24584 | tf_op jit(solution)/shard_map/ppermute | solution.py:353
  71.4 1.4 %collective-permute-start.18 = (f32[8,256]{1,0:T(8,128)S(1)}, f32[8,256]{1,0:T(8,128)S(1)}, u32[]{:S(2)}, u32[]{:S(2)}) collective-permute-start(f32[8,256]{1,0:T(8,128)S(1)} %get-tuple-element.72.refs_12_), channel_id=1, source_target_pairs={{0,1},{1,0},{2,3},{3,2},{4,5},{5,4},{6,7},{7,6},{8,9},{9,8},{10,11... | collective-permute-start | bytes 24584 | tf_op jit(solution)/shard_map/ppermute | solution.py:353
  71.5 10.5 %collective-permute-start.24 = (bf16[1024,256]{1,0:T(8,128)(2,1)S(1)}, bf16[1024,256]{1,0:T(8,128)(2,1)S(1)}, u32[]{:S(2)}, u32[]{:S(2)}) collective-permute-start(bf16[1024,256]{1,0:T(8,128)(2,1)S(1)} %get-tuple-element.80.refs_4_), channel_id=1, source_target_pairs={{0,1},{1,0},{2,3},{3,2},{4,5},{5,4},{6,7},{7,6},{8,9},{9,8},{10,11... | collective-permute-start | bytes 1572872 | tf_op jit(solution)/shard_map/ppermute | solution.py:354
  71.9 10.0 %collective-permute-start.23 = (bf16[1024,256]{1,0:T(8,128)(2,1)S(1)}, bf16[1024,256]{1,0:T(8,128)(2,1)S(1)}, u32[]{:S(2)}, u32[]{:S(2)}) collective-permute-start(bf16[1024,256]{1,0:T(8,128)(2,1)S(1)} %get-tuple-element.79.refs_3_), channel_id=1, source_target_pairs={{0,1},{1,0},{2,3},{3,2},{4,5},{5,4},{6,7},{7,6},{8,9},{9,8},{10,11... | collective-permute-start | bytes 1572872 | tf_op jit(solution)/shard_map/ppermute | solution.py:354
  77.5 14.1 %collective-permute-start.20 = (bf16[136,1024]{1,0:T(8,128)(2,1)S(1)}, bf16[136,1024]{1,0:T(8,128)(2,1)S(1)}, u32[]{:S(2)}, u32[]{:S(2)}) collective-permute-start(bf16[136,1024]{1,0:T(8,128)(2,1)S(1)} %get-tuple-element.76), channel_id=1, source_target_pairs={{0,4},{4,0},{8,12},{12,8},{1,5},{5,1},{9,13},{13,9},{2,6},{6,2},{1... | collective-permute-start | bytes 835592 | tf_op jit(solution)/shard_map/ppermute | solution.py:39
  78.3 22.4 %collective-permute-start.21 = (bf16[136,1024]{1,0:T(8,128)(2,1)S(1)}, bf16[136,1024]{1,0:T(8,128)(2,1)S(1)}, u32[]{:S(2)}, u32[]{:S(2)}) collective-permute-start(bf16[136,1024]{1,0:T(8,128)(2,1)S(1)} %get-tuple-element.77), channel_id=1, source_target_pairs={{0,8},{4,12},{8,0},{12,4},{1,9},{5,13},{9,1},{13,5},{2,10},{6,14},... | collective-permute-start | bytes 835592 | tf_op jit(solution)/shard_map/ppermute | solution.py:39
  80.9 19.8 %collective-permute-start.22 = (bf16[136,1024]{1,0:T(8,128)(2,1)S(1)}, bf16[136,1024]{1,0:T(8,128)(2,1)S(1)}, u32[]{:S(2)}, u32[]{:S(2)}) collective-permute-start(bf16[136,1024]{1,0:T(8,128)(2,1)S(1)} %get-tuple-element.78), channel_id=1, source_target_pairs={{0,12},{4,8},{8,4},{12,0},{1,13},{5,9},{9,5},{13,1},{2,14},{6,10},... | collective-permute-start | bytes 835592 | tf_op jit(solution)/shard_map/ppermute | solution.py:39
  102.6 8.0 %collective-permute-start.25 = (bf16[128,256]{1,0:T(8,128)(2,1)S(1)}, bf16[128,256]{1,0:T(8,128)(2,1)S(1)}, u32[]{:S(2)}, u32[]{:S(2)}) collective-permute-start(bf16[128,256]{1,0:T(8,128)(2,1)S(1)} %get-tuple-element.82), channel_id=1, source_target_pairs={{0,4},{4,0},{8,12},{12,8},{1,5},{5,1},{9,13},{13,9},{2,6},{6,2},{1... | collective-permute-start | bytes 196616 | tf_op jit(solution)/shard_map/ppermute | solution.py:39
  108.2 6.5 %collective-permute-start.26 = (bf16[128,256]{1,0:T(8,128)(2,1)S(1)}, bf16[128,256]{1,0:T(8,128)(2,1)S(1)}, u32[]{:S(2)}, u32[]{:S(2)}) collective-permute-start(bf16[128,256]{1,0:T(8,128)(2,1)S(1)} %get-tuple-element.83), channel_id=1, source_target_pairs={{0,8},{4,12},{8,0},{12,4},{1,9},{5,13},{9,1},{13,5},{2,10},{6,14},... | collective-permute-start | bytes 196616 | tf_op jit(solution)/shard_map/ppermute | solution.py:39
  109.2 6.1 %collective-permute-start.27 = (bf16[128,256]{1,0:T(8,128)(2,1)S(1)}, bf16[128,256]{1,0:T(8,128)(2,1)S(1)}, u32[]{:S(2)}, u32[]{:S(2)}) collective-permute-start(bf16[128,256]{1,0:T(8,128)(2,1)S(1)} %get-tuple-element.84), channel_id=1, source_target_pairs={{0,12},{4,8},{8,4},{12,0},{1,13},{5,9},{9,5},{13,1},{2,14},{6,10},... | collective-permute-start | bytes 196616 | tf_op jit(solution)/shard_map/ppermute | solution.py:39
  117.3 2.0 %collective-permute-start.28 = (bf16[128,2048]{1,0:T(8,128)(2,1)S(1)}, bf16[128,2048]{1,0:T(8,128)(2,1)S(1)}, u32[]{:S(2)}, u32[]{:S(2)}) collective-permute-start(bf16[128,2048]{1,0:T(8,128)(2,1)S(1)} %convert_element_type.24), channel_id=1, source_target_pairs={{0,1},{1,0},{2,3},{3,2},{4,5},{5,4},{6,7},{7,6},{8,9},{9,8},{10,11... | collective-permute-start | bytes 1572872 | tf_op jit(solution)/shard_map/ppermute | solution.py:362
  119.4 8.4 %collective-permute-start.29 = (bf16[64,2048]{1,0:T(8,128)(2,1)S(1)}, bf16[64,2048]{1,0:T(8,128)(2,1)S(1)}, u32[]{:S(2)}, u32[]{:S(2)}) collective-permute-start(bf16[64,2048]{1,0:T(8,128)(2,1)S(1)} %fusion), channel_id=1, source_target_pairs={{0,2},{2,0},{1,3},{3,1},{4,6},{6,4},{5,7},{7,5},{8,10},{10,8},{9,1... | collective-permute-start | bytes 786440 | tf_op jit(solution)/shard_map/ppermute | solution.py:363

commit v6 on v5

--- a/solution.py
+++ b/solution.py
@@ -191,9 +191,140 @@
     )(where, *acts, *early, *bases, *pieces, *sums)
 
 
+def far_kernel(levels, rows, where, *refs):
+    acts, early, bases, pieces, sums = refs[:4], refs[4:6], refs[6:8], refs[8:12], refs[12:16]
+    message, kept, extra, right, left, basis, held, sems = refs[16:]
+    half, late = split(rows)
+    part = bases[0].shape[1]
+    cols = 2 * part
+    chunk = cols // levels
+    level = where[0]
+    count = 0
+
+    def copy(source, target):
+        nonlocal count
+        made = pltpu.make_async_copy(source, target, sems.at[count])
+        made.start()
+        count += 1
+        return made
+
+    first = [copy(b, basis.at[:, pl.ds(i * part, part)]) for i, b in enumerate(bases)]
+    moves = [copy(p, held.at[pl.ds(i * late, late)]) for i, p in enumerate(pieces)]
+    rest = [copy(a.at[pl.ds(0, rows)], left.at[pl.ds(i * rows, rows)]) for i, a in enumerate(acts)]
+    for i in range(2):
+        for j in range(4):
+            rest.append(
+                copy(early[i].at[pl.ds(j * half, half)], right.at[pl.ds(j * rows, half), pl.ds(i * part, part)])
+            )
+    for made in first:
+        made.wait()
+    total = jnp.concatenate([sums[0][0:1], sums[1][0:1]], axis=1)
+    for i in range(0, 4, 2):
+        moves[i].wait()
+        moves[i + 1].wait()
+        block = jnp.dot(held[pl.ds(i * late, 2 * late)], basis[...], preferred_element_type=f32).astype(bf16)
+        right[pl.ds(i * rows + half, late)] = block[:late]
+        right[pl.ds(i * rows + rows + half, late)] = block[late:]
+        total = total + jnp.sum(jnp.square(block.astype(f32)), axis=0, keepdims=True)
+    for made in rest:
+        made.wait()
+    extra[...] = jnp.zeros_like(extra)
+    extra[0:1, :cols] = total
+    for i in range(4):
+        extra[1:2, pl.ds(i * part, part)] = sums[i][2:3]
+        extra[2:3, pl.ds(i * part, part)] = sums[i][1:2]
+    high, low = high_low(extra[...])
+    side, place = level // 2, level % 2
+    for other, target in ((place, None), (1 - place, kept)):
+        columns = pl.ds(pl.multiple_of(((1 - side) * 2 + other) * chunk, chunk), chunk)
+        block = lax.dot_general(
+            right[:, columns], left[...], (((0,), (0,)), ((), ())), preferred_element_type=f32
+        )
+        if target is None:
+            message[...] = jnp.concatenate([block.astype(bf16), high[:4], low[:4]])
+        else:
+            target[...] = block
+
+
+def far(where, acts, early, bases, pieces, sums, rows, levels):
+    width_g, part = bases[0].shape
+    width = acts[0].shape[1]
+    cols = 2 * part
+    chunk = cols // levels
+    return pl.pallas_call(
+        functools.partial(far_kernel, levels, rows),
+        out_shape=(
+            shape((chunk + 8, width), bf16),
+            shape((chunk, width), f32),
+            shape((8, width), f32),
+            shape((4 * rows, cols), bf16),
+        ),
+        in_specs=[SMEM] + [ANY] * 12 + [VMEM] * 4,
+        out_specs=(VMEM,) * 4,
+        scratch_shapes=[
+            pltpu.VMEM((4 * rows, width), bf16),
+            pltpu.VMEM((width_g, cols), bf16),
+            pltpu.VMEM((4 * split(rows)[1], width_g), bf16),
+            pltpu.SemaphoreType.DMA((18,)),
+        ],
+        compiler_params=params(LARGE),
+        cost_estimate=cost(4 * rows * cols * (width_g + width), 16 * rows * width),
+    )(where, *acts, *early, *bases, *pieces, *sums)
+
+
+def near_kernel(levels, rows, where, right, extra, *refs):
+    acts, own, message = refs[:4], refs[4], refs[5]
+    chunk = right.shape[1] // levels
+    high, low = high_low(extra[...])
+    for step, target in enumerate((own, message)):
+        columns = pl.ds(pl.multiple_of((where[0] ^ step) * chunk, chunk), chunk)
+        block = sum(
+            lax.dot_general(
+                right[pl.ds(i * rows, rows), columns], a[:rows], (((0,), (0,)), ((), ())), preferred_element_type=f32
+            )
+            for i, a in enumerate(acts)
+        )
+        if step == 0:
+            target[...] = block
+        else:
+            target[...] = jnp.concatenate([block.astype(bf16), high[:4], low[:4]])
+
+
+def near(where, right, extra, acts, rows, levels):
+    width = acts[0].shape[1]
+    chunk = right.shape[1] // levels
+    return pl.pallas_call(
+        functools.partial(near_kernel, levels, rows),
+        out_shape=(shape((chunk, width), f32), shape((chunk + 8, width), bf16)),
+        in_specs=[SMEM] + [VMEM] * 6,
+        out_specs=(VMEM, VMEM),
+        compiler_params=params(LARGE),
+        cost_estimate=cost(16 * rows * chunk * width, 16 * rows * width),
+    )(where, right, extra, *acts)
+
+
+def add_kernel(kept, extra, got, out):
+    chunk = kept.shape[0]
+    more = got[...].astype(f32)
+    high, low = high_low(extra[0:4] + (more[chunk : chunk + 4] + more[chunk + 4 :]))
+    out[...] = jnp.concatenate([(kept[...] + more[:chunk]).astype(bf16), high, low])
+
+
+def add(kept, extra, got):
+    return pl.pallas_call(
+        add_kernel,
+        out_shape=shape(got.shape, bf16),
+        in_specs=[VMEM] * 3,
+        out_specs=VMEM,
+        compiler_params=params(SMALL),
+        cost_estimate=cost(kept.size, 8 * kept.size),
+    )(kept, extra, got)
+
+
 def middle_kernel(levels, where, own, own_extra, *refs):
-    messages, bases, outs = refs[: levels - 1], refs[levels - 1 : levels + 3], refs[levels + 3 : 2 * levels + 3]
-    basis, turned = refs[2 * levels + 3 :]
+    count = len(refs) - levels - 6
+    messages, bases, outs = refs[:count], refs[count : count + 4], refs[count + 4 : -2]
+    basis, turned = refs[-2:]
     chunk, width = own.shape
     cols = chunk * levels
     part = bases[0].shape[1]
@@ -222,13 +353,12 @@
         ).astype(bf16)
 
 
-def middle(where, own, own_extra, messages, bases):
-    levels = len(messages) + 1
+def middle(where, own, own_extra, messages, bases, levels):
     chunk, width = own.shape
     return pl.pallas_call(
         functools.partial(middle_kernel, levels),
         out_shape=[shape((chunk, width // levels), bf16)] * levels,
-        in_specs=[SMEM] + [VMEM] * (levels + 5),
+        in_specs=[SMEM] + [VMEM] * (len(messages) + 6),
         out_specs=[VMEM] * levels,
         scratch_shapes=[pltpu.VMEM((width, width), bf16), pltpu.VMEM((chunk * levels, 8), f32)],
         compiler_params=params(SMALL),
@@ -352,10 +482,15 @@
     bases_a, turned_g, bases_g, sums = zip(first, second)
     sums += tuple(lax.ppermute(t, "core", SWAP) for t in sums)
     bases_a += tuple(lax.ppermute(t, "core", SWAP) for t in bases_a)
-    own, own_extra, *messages = cross(where, early, turned_g, bases_g, late, sums, rows, levels)
-
-    got = [across(m, step + 1, levels) for step, m in enumerate(messages)]
-    mids = middle(where, own, own_extra, got, bases_a)
+    if levels == 4:
+        message, kept, own_extra, right = far(where, early, turned_g, bases_g, late, sums, rows, levels)
+        message = across(message, 1, levels)
+        own, beside = near(where, right, own_extra, early, rows, levels)
+        got = [across(add(kept, own_extra, message), 3, levels), across(beside, 1, levels)]
+    else:
+        own, own_extra, *messages = cross(where, early, turned_g, bases_g, late, sums, rows, levels)
+        got = [across(m, step + 1, levels) for step, m in enumerate(messages)]
+    mids = middle(where, own, own_extra, got, bases_a, levels)
     mids = [m if step == 0 else across(m, step, levels) for step, m in enumerate(mids)]
 
     sent, kept = result(where, mids, bases_g)

time: 129 us -> 123 us (0.953)
  waiting for transfers between devices: 68.9 us -> 63.9 us
  starting transfers between devices: 32.9 us -> 30 us
  Pallas kernels: 18.4 us -> 20.3 us
    ppermute x7, waiting for transfers between devices: 30.1 us -> 24.6 us  [across(): return lax.ppermute(x, 'level', [(i, i ^ step) for i in range(levels)])]
    ppermute x7, starting transfers between devices: 14 us -> 11 us  [across(): return lax.ppermute(x, 'level', [(i, i ^ step) for i in range(levels)])]
    pallas_call x1 -> x3, Pallas kernels: 4.67 us -> 6.62 us  [the longest x1 3.76 us: far(): pl.pallas_call(functools.partial(far_kernel, levels, rows), out_shape=(sh...]
  transfers between devices with their start and end apart: 30 -> 30, of which waited for: 16 -> 17; matrix products, arithmetic and copies ran while one was open for 3% -> 4% of each run, Pallas kernels for 11% -> 10%
where the time goes in v6:
time: 123 us
  waiting for transfers between devices  63.9 us (52%)
  starting transfers between devices  30 us (24%)
  Pallas kernels  20.3 us (17%)
  other arithmetic  5.44 us (4%)
  local copies, waits for them, and re-layouts  1.94 us (2%)
    ppermute x7, waiting for transfers between devices, across(): return lax.ppermute(x, 'level', [(i, i ^ step) for i in range(levels)])  24.6 us
    ppermute x4, waiting for transfers between devices, over(): return lax.ppermute(slot, 'group', SWAP)  17.9 us
    ppermute x7, starting transfers between devices, across(): return lax.ppermute(x, 'level', [(i, i ^ step) for i in range(levels)])  11 us
    pallas_call x2, Pallas kernels, turn(): pl.pallas_call(functools.partial(turn_kernel, levels, level_g, level_a, r...  9.94 us
    ppermute x1, waiting for transfers between devices, body(): lax.ppermute((kept[:rows_a] + sent[:rows_a]).astype(bf16), 'chip', SWAP)  6.83 us
    ppermute x1, waiting for transfers between devices, gather_levels(): lax.ppermute(third, 'level', outward)  6.11 us
    ppermute x4, starting transfers between devices, over(): return lax.ppermute(slot, 'group', SWAP)  5.14 us
    pallas_call x1, Pallas kernels, far(): pl.pallas_call(functools.partial(far_kernel, levels, rows), out_shape=(sh...  3.76 us
  transfers between devices with their start and end apart: 30, of which 17 were waited for; matrix products, arithmetic and copies ran while one was open for 4% of the time, Pallas kernels for 10%

profile of v6, /device:TPU:0, one launch (start us, length us, event | category | flops | bytes accessed | tf_op | source)
XLA Modules:
  0.0 122.6 jit_solution(5118244352809003043)
XLA Ops:
  0.0 0.8 constant_dynamic-slice_fusion.2
  0.8 1.0 constant_dynamic-slice_fusion.1
  2.3 2.6 %collective-permute-start.1 = (bf16[192,256]{1,0:T(8,128)(2,1)S(1)}, bf16[192,256]{1,0:T(8,128)(2,1)S(1)}, u32[]{:S(2)}, u32[]{:S(2)}) collective-permute-start(bf16[192,256]{1,0:T(8,128)(2,1)S(1)} %get-tuple-element.98), channel_id=1, source_target_pairs={{0,2},{2,0},{1,3},{3,1},{4,6},{6,4},{5,7},{7,5},{8,10},{10,8},{9,1... | collective-permute-start | bytes 294920 | tf_op jit(solution)/shard_map/ppermute | solution.py:456
  5.8 1.4 %slice_select_fusion = bf16[256,2048]{1,0:T(8,128)(2,1)S(1)} fusion(bf16[384,2048]{1,0:T(8,128)(2,1)} %param.6, pred[256]{0:T(512)(128)(4,1)S(1)} %slice_reduce_fusion), kind=kLoop, calls=%fused_computation.1 | loop fusion | flops 524288 | bytes 2097408 | tf_op jit(solution)/shard_map/jit(_where)/select_n | solution.py:468
  7.3 1.2 slice_select_fusion.1.refs_8_
  9.2 1.1 collective-permute-done.2
  10.4 1.6 %collective-permute-start.3 = (bf16[912,1024]{1,0:T(8,128)(2,1)S(1)}, bf16[912,1024]{1,0:T(8,128)(2,1)}, u32[]{:S(2)}, u32[]{:S(2)}) collective-permute-start(bf16[912,1024]{1,0:T(8,128)(2,1)S(1)} %pad_maximum_fusion.refs_4_.refs_0_), channel_id=1, source_target_pairs={{0,2},{2,0},{1,3},{3,1},{4,6},{6,4},{5,7},{7,5},{8,10},{10,8},{9,1... | collective-permute-start | bytes 5603336 | tf_op jit(solution)/shard_map/ppermute | solution.py:474
  12.1 1.5 %collective-permute-start.5 = (bf16[768,256]{1,0:T(8,128)(2,1)S(1)}, bf16[768,256]{1,0:T(8,128)(2,1)}, u32[]{:S(2)}, u32[]{:S(2)}) collective-permute-start(bf16[768,256]{1,0:T(8,128)(2,1)S(1)} %fusion.8.refs_0_), channel_id=1, source_target_pairs={{0,4},{4,0},{8,12},{12,8},{1,5},{5,1},{9,13},{13,9},{2,6},{6,2},{1... | collective-permute-start | bytes 1179656 | tf_op jit(solution)/shard_map/ppermute | solution.py:39
  13.6 1.4 %collective-permute-start.6 = (bf16[768,256]{1,0:T(8,128)(2,1)S(1)}, bf16[768,256]{1,0:T(8,128)(2,1)}, u32[]{:S(2)}, u32[]{:S(2)}) collective-permute-start(bf16[768,256]{1,0:T(8,128)(2,1)S(1)} %fusion.8.refs_0_), channel_id=1, source_target_pairs={{4,8},{8,4},{5,9},{9,5},{6,10},{10,6},{7,11},{11,7},{20,24},{24,20... | collective-permute-start | bytes 1179656 | tf_op jit(solution)/shard_map/ppermute | solution.py:426
  15.0 1.5 %collective-permute-start.7 = (bf16[768,256]{1,0:T(8,128)(2,1)S(1)}, bf16[768,256]{1,0:T(8,128)(2,1)S(1)}, u32[]{:S(2)}, u32[]{:S(2)}) collective-permute-start(bf16[768,256]{1,0:T(8,128)(2,1)S(1)} %fusion.8.refs_0_), channel_id=1, source_target_pairs={{0,16},{16,0},{1,17},{17,1},{2,18},{18,2},{3,19},{19,3},{4,20},{20... | collective-permute-start | bytes 1179656 | tf_op jit(solution)/shard_map/ppermute | solution.py:418
  16.5 6.6 %collective-permute-done.5.refs_1_ = bf16[768,256]{1,0:T(8,128)(2,1)} collective-permute-done((bf16[768,256]{1,0:T(8,128)(2,1)S(1)}, bf16[768,256]{1,0:T(8,128)(2,1)}, u32[]{:S(2)}, u32[]{:S(2)}) %collective-permute-start.5) | collective-permute-done | bytes 393248 | tf_op jit(solution)/shard_map/ppermute | solution.py:39
  23.1 2.6 %collective-permute-done.7.refs_0_ = bf16[768,256]{1,0:T(8,128)(2,1)S(1)} collective-permute-done((bf16[768,256]{1,0:T(8,128)(2,1)S(1)}, bf16[768,256]{1,0:T(8,128)(2,1)S(1)}, u32[]{:S(2)}, u32[]{:S(2)}) %collective-permute-start.7) | collective-permute-done | bytes 393248 | tf_op jit(solution)/shard_map/ppermute | solution.py:418
  25.7 1.5 %collective-permute-start.10 = (bf16[768,256]{1,0:T(8,128)(2,1)}, bf16[768,256]{1,0:T(8,128)(2,1)}, u32[]{:S(2)}, u32[]{:S(2)}) collective-permute-start(bf16[768,256]{1,0:T(8,128)(2,1)} %collective-permute-done.5.refs_1_), channel_id=1, source_target_pairs={{0,16},{16,0},{1,17},{17,1},{2,18},{18,2},{3,19},{19,3},{4,20},{20... | collective-permute-start | bytes 1179656 | tf_op jit(solution)/shard_map/ppermute | solution.py:418
  27.2 1.4 %collective-permute-start.8 = (bf16[768,256]{1,0:T(8,128)(2,1)}, bf16[768,256]{1,0:T(8,128)(2,1)}, u32[]{:S(2)}, u32[]{:S(2)}) collective-permute-start(bf16[768,256]{1,0:T(8,128)(2,1)} %collective-permute-done.5.refs_1_), channel_id=1, source_target_pairs={{4,8},{8,4},{5,9},{9,5},{6,10},{10,6},{7,11},{11,7},{20,24},{24,20... | collective-permute-start | bytes 1179656 | tf_op jit(solution)/shard_map/ppermute | solution.py:428
  28.6 1.3 %collective-permute-start.9 = (bf16[768,256]{1,0:T(8,128)(2,1)}, bf16[768,256]{1,0:T(8,128)(2,1)}, u32[]{:S(2)}, u32[]{:S(2)}) collective-permute-start(bf16[768,256]{1,0:T(8,128)(2,1)} %collective-permute-done.6), channel_id=1, source_target_pairs={{4,0},{8,12},{5,1},{9,13},{6,2},{10,14},{7,3},{11,15},{20,16},{24,... | collective-permute-start | bytes 1179656 | tf_op jit(solution)/shard_map/ppermute | solution.py:428
  29.9 6.0 %collective-permute-done.10.refs_1_ = bf16[768,256]{1,0:T(8,128)(2,1)} collective-permute-done((bf16[768,256]{1,0:T(8,128)(2,1)}, bf16[768,256]{1,0:T(8,128)(2,1)}, u32[]{:S(2)}, u32[]{:S(2)}) %collective-permute-start.10) | collective-permute-done | bytes 393248 | tf_op jit(solution)/shard_map/ppermute | solution.py:418
  35.9 6.1 %collective-permute-done.9 = bf16[768,256]{1,0:T(8,128)(2,1)} collective-permute-done((bf16[768,256]{1,0:T(8,128)(2,1)}, bf16[768,256]{1,0:T(8,128)(2,1)}, u32[]{:S(2)}, u32[]{:S(2)}) %collective-permute-start.9) | collective-permute-done | bytes 393248 | tf_op jit(solution)/shard_map/ppermute | solution.py:428
  42.0 1.0 broadcast_select_fusion.2.refs_2_
  43.1 0.6 collective-permute-start.12
  43.7 1.3 %collective-permute-start.11 = (bf16[768,256]{1,0:T(8,128)(2,1)}, bf16[768,256]{1,0:T(8,128)(2,1)S(1)}, u32[]{:S(2)}, u32[]{:S(2)}) collective-permute-start(bf16[768,256]{1,0:T(8,128)(2,1)} %collective-permute-done.8), channel_id=1, source_target_pairs={{4,0},{8,12},{5,1},{9,13},{6,2},{10,14},{7,3},{11,15},{20,16},{24,... | collective-permute-start | bytes 1179656 | tf_op jit(solution)/shard_map/ppermute | solution.py:431
  45.0 6.8 %collective-permute-done.12.refs_2_ = bf16[768,256]{1,0:T(8,128)(2,1)S(1)} collective-permute-done((bf16[768,256]{1,0:T(8,128)(2,1)S(1)}, bf16[768,256]{1,0:T(8,128)(2,1)S(1)}, u32[]{:S(2)}, u32[]{:S(2)}) %collective-permute-start.12) | collective-permute-done | bytes 393248 | tf_op jit(solution)/shard_map/ppermute | solution.py:418
  51.8 2.3 %collective-permute-done.11 = bf16[768,256]{1,0:T(8,128)(2,1)S(1)} collective-permute-done((bf16[768,256]{1,0:T(8,128)(2,1)}, bf16[768,256]{1,0:T(8,128)(2,1)S(1)}, u32[]{:S(2)}, u32[]{:S(2)}) %collective-permute-start.11) | collective-permute-done | bytes 393248 | tf_op jit(solution)/shard_map/ppermute | solution.py:431
  54.3 1.6 %collective-permute-start.14 = (bf16[768,256]{1,0:T(8,128)(2,1)S(1)}, bf16[768,256]{1,0:T(8,128)(2,1)S(1)}, u32[]{:S(2)}, u32[]{:S(2)}) collective-permute-start(bf16[768,256]{1,0:T(8,128)(2,1)S(1)} %broadcast_select_fusion.1.refs_3_), channel_id=1, source_target_pairs={{0,16},{16,0},{1,17},{17,1},{2,18},{18,2},{3,19},{19,3},{4,20},{20... | collective-permute-start | bytes 1179656 | tf_op jit(solution)/shard_map/ppermute | solution.py:418
  55.9 0.6 collective-permute-start.15
  56.6 1.8 %collective-permute-done.13.refs_7_.refs_3_ = bf16[912,1024]{1,0:T(8,128)(2,1)S(1)} collective-permute-done((bf16[912,1024]{1,0:T(8,128)(2,1)}, bf16[912,1024]{1,0:T(8,128)(2,1)S(1)}, u32[]{:S(2)}, u32[]{:S(2)}) %collective-permute-start.13) | collective-permute-done | bytes 1867808 | tf_op jit(solution)/shard_map/ppermute | solution.py:475
  58.4 5.0 %shard_map.55 = (bf16[1024,256]{1,0:T(8,128)(2,1)S(1)}, bf16[1024,256]{1,0:T(8,128)(2,1)S(1)}, bf16[2048,256]{1,0:T(8,128)(2,1)S(1)}, f32[8,256]{1,0:T(8,128)S(1)}) custom-call(s32[2]{0:T(128)S(1)} %pad_add_fusion.where, bf16[768,256]{1,0:T(8,128)(2,1)S(1)} %fusion.8.refs_0_, bf16[768,256]{1,0:T(8,128)(2,1)} %collective-permute-done.5.refs_1_, ...), custom_call_target="tpu_custom_call" | custom-call | flops 1610612736 | bytes 6291456 | tf_op jit(solution)/shard_map/pallas_call | solution.py:92
  63.3 2.5 %collective-permute-done.14.refs_3_ = bf16[768,256]{1,0:T(8,128)(2,1)S(1)} collective-permute-done((bf16[768,256]{1,0:T(8,128)(2,1)S(1)}, bf16[768,256]{1,0:T(8,128)(2,1)S(1)}, u32[]{:S(2)}, u32[]{:S(2)}) %collective-permute-start.14) | collective-permute-done | bytes 393248 | tf_op jit(solution)/shard_map/ppermute | solution.py:418
  65.9 5.0 %shard_map.56 = (bf16[1024,256]{1,0:T(8,128)(2,1)S(1)}, bf16[1024,256]{1,0:T(8,128)(2,1)S(1)}, bf16[2048,256]{1,0:T(8,128)(2,1)S(1)}, f32[8,256]{1,0:T(8,128)S(1)}) custom-call(s32[2]{0:T(128)S(1)} %pad_add_fusion.where, bf16[768,256]{1,0:T(8,128)(2,1)S(1)} %collective-permute-done.7.refs_0_, bf16[768,256]{1,0:T(8,128)(2,1)} %collective-permute-done.10.refs_1_, ...), custom_call_target="tpu_custom_call" | custom-call | flops 1610612736 | bytes 6291456 | tf_op jit(solution)/shard_map/pallas_call | solution.py:92
  71.5 1.3 %collective-permute-done.19.refs_15_ = f32[8,256]{1,0:T(8,128)S(1)} collective-permute-done((f32[8,256]{1,0:T(8,128)S(1)}, f32[8,256]{1,0:T(8,128)S(1)}, u32[]{:S(2)}, u32[]{:S(2)}) %collective-permute-start.19) | collective-permute-done | bytes 8224 | tf_op jit(solution)/shard_map/ppermute | solution.py:483
  72.8 3.8 %shard_map.57 = (bf16[136,1024]{1,0:T(8,128)(2,1)S(1)}, f32[128,1024]{1,0:T(8,128)S(1)}, f32[8,1024]{1,0:T(8,128)S(1)}, bf16[1536,512]{1,0:T(8,128)(2,1)S(1)}) custom-call(s32[2]{0:T(128)S(1)} %pad_add_fusion.where, bf16[912,1024]{1,0:T(8,128)(2,1)S(1)} %pad_maximum_fusion.refs_4_.refs_0_, bf16[912,1024]{1,0:T(8,128)(2,1)S(1)} %collective-permute-done.refs_5_.refs_1_, ...), custom_call_target="tpu_custom_call" | custom-call | flops 2415919104 | bytes 6291456 | tf_op jit(solution)/shard_map/pallas_call | solution.py:254
  76.6 0.8 collective-permute-start.20
  77.9 2.8 %shard_map.58 = (f32[128,1024]{1,0:T(8,128)S(1)}, bf16[136,1024]{1,0:T(8,128)(2,1)S(1)}) custom-call(s32[2]{0:T(128)S(1)} %pad_add_fusion.where, bf16[1536,512]{1,0:T(8,128)(2,1)S(1)} %get-tuple-element.75.right, f32[8,1024]{1,0:T(8,128)S(1)} %get-tuple-element.76.extra.own_extra, bf16[912,1024]{1,0:T(8,128)(2,1)S(1)} %pad_maximum_fusion.refs_4_.refs_0_, ...), custom_call_target="tpu_custom_call" | custom-call | flops 805306368 | bytes 6291456 | tf_op jit(solution)/shard_map/pallas_call | solution.py:296
  80.7 1.4 %collective-permute-start.22 = (bf16[136,1024]{1,0:T(8,128)(2,1)S(1)}, bf16[136,1024]{1,0:T(8,128)(2,1)S(1)}, u32[]{:S(2)}, u32[]{:S(2)}) collective-permute-start(bf16[136,1024]{1,0:T(8,128)(2,1)S(1)} %get-tuple-element.80), channel_id=1, source_target_pairs={{0,4},{4,0},{8,12},{12,8},{1,5},{5,1},{9,13},{13,9},{2,6},{6,2},{1... | collective-permute-start | bytes 835592 | tf_op jit(solution)/shard_map/ppermute | solution.py:39
  82.1 4.1 %collective-permute-done.20.got = bf16[136,1024]{1,0:T(8,128)(2,1)S(1)} collective-permute-done((bf16[136,1024]{1,0:T(8,128)(2,1)S(1)}, bf16[136,1024]{1,0:T(8,128)(2,1)S(1)}, u32[]{:S(2)}, u32[]{:S(2)}) %collective-permute-start.20) | collective-permute-done | bytes 278560 | tf_op jit(solution)/shard_map/ppermute | solution.py:39
  86.2 2.8 %collective-permute-start.21 = (bf16[136,1024]{1,0:T(8,128)(2,1)S(1)}, bf16[136,1024]{1,0:T(8,128)(2,1)S(1)}, u32[]{:S(2)}, u32[]{:S(2)}) collective-permute-start(bf16[136,1024]{1,0:T(8,128)(2,1)S(1)} %shard_map.59), channel_id=1, source_target_pairs={{0,12},{4,8},{8,4},{12,0},{1,13},{5,9},{9,5},{13,1},{2,14},{6,10},... | collective-permute-start | bytes 835592 | tf_op jit(solution)/shard_map/ppermute | solution.py:39
  89.1 2.2 %collective-permute-done.22.refs_1_ = bf16[136,1024]{1,0:T(8,128)(2,1)S(1)} collective-permute-done((bf16[136,1024]{1,0:T(8,128)(2,1)S(1)}, bf16[136,1024]{1,0:T(8,128)(2,1)S(1)}, u32[]{:S(2)}, u32[]{:S(2)}) %collective-permute-start.22) | collective-permute-done | bytes 278560 | tf_op jit(solution)/shard_map/ppermute | solution.py:39
  91.3 7.3 %collective-permute-done.21.refs_0_ = bf16[136,1024]{1,0:T(8,128)(2,1)S(1)} collective-permute-done((bf16[136,1024]{1,0:T(8,128)(2,1)S(1)}, bf16[136,1024]{1,0:T(8,128)(2,1)S(1)}, u32[]{:S(2)}, u32[]{:S(2)}) %collective-permute-start.21) | collective-permute-done | bytes 278560 | tf_op jit(solution)/shard_map/ppermute | solution.py:39
  98.6 1.9 %shard_map.60 = (bf16[128,256]{1,0:T(8,128)(2,1)S(1)}, bf16[128,256]{1,0:T(8,128)(2,1)S(1)}, bf16[128,256]{1,0:T(8,128)(2,1)S(1)}, bf16[128,256]{1,0:T(8,128)(2,1)S(1)}) custom-call(s32[2]{0:T(128)S(1)} %pad_add_fusion.where, f32[128,1024]{1,0:T(8,128)S(1)} %get-tuple-element.77.own, f32[8,1024]{1,0:T(8,128)S(1)} %get-tuple-element.76.extra.own_extra, ...), custom_call_target="tpu_custom_call" | custom-call | flops 805306368 | bytes 2097152 | tf_op jit(solution)/shard_map/pallas_call | solution.py:358
  100.6 1.5 %collective-permute-start.25 = (bf16[128,256]{1,0:T(8,128)(2,1)S(1)}, bf16[128,256]{1,0:T(8,128)(2,1)S(1)}, u32[]{:S(2)}, u32[]{:S(2)}) collective-permute-start(bf16[128,256]{1,0:T(8,128)(2,1)S(1)} %get-tuple-element.84), channel_id=1, source_target_pairs={{0,4},{4,0},{8,12},{12,8},{1,5},{5,1},{9,13},{13,9},{2,6},{6,2},{1... | collective-permute-start | bytes 196616 | tf_op jit(solution)/shard_map/ppermute | solution.py:39
  102.1 1.1 collective-permute-start.26
  103.2 1.8 %collective-permute-start.27 = (bf16[128,256]{1,0:T(8,128)(2,1)S(1)}, bf16[128,256]{1,0:T(8,128)(2,1)S(1)}, u32[]{:S(2)}, u32[]{:S(2)}) collective-permute-start(bf16[128,256]{1,0:T(8,128)(2,1)S(1)} %get-tuple-element.86), channel_id=1, source_target_pairs={{0,12},{4,8},{8,4},{12,0},{1,13},{5,9},{9,5},{13,1},{2,14},{6,10},... | collective-permute-start | bytes 196616 | tf_op jit(solution)/shard_map/ppermute | solution.py:39
  105.0 2.9 %collective-permute-done.26.refs_2_ = bf16[128,256]{1,0:T(8,128)(2,1)S(1)} collective-permute-done((bf16[128,256]{1,0:T(8,128)(2,1)S(1)}, bf16[128,256]{1,0:T(8,128)(2,1)S(1)}, u32[]{:S(2)}, u32[]{:S(2)}) %collective-permute-start.26) | collective-permute-done | bytes 65568 | tf_op jit(solution)/shard_map/ppermute | solution.py:39
  107.9 1.4 %collective-permute-done.27.refs_3_ = bf16[128,256]{1,0:T(8,128)(2,1)S(1)} collective-permute-done((bf16[128,256]{1,0:T(8,128)(2,1)S(1)}, bf16[128,256]{1,0:T(8,128)(2,1)S(1)}, u32[]{:S(2)}, u32[]{:S(2)}) %collective-permute-start.27) | collective-permute-done | bytes 65568 | tf_op jit(solution)/shard_map/ppermute | solution.py:39
  109.4 1.8 %shard_map.61 = (f32[128,2048]{1,0:T(8,128)S(1)}, f32[128,2048]{1,0:T(8,128)S(1)}) custom-call(s32[2]{0:T(128)S(1)} %pad_add_fusion.where, bf16[128,256]{1,0:T(8,128)(2,1)S(1)} %get-tuple-element.83.refs_0_, bf16[128,256]{1,0:T(8,128)(2,1)S(1)} %collective-permute-done.25.refs_1_, bf16[128,256]{1,0:T(8,128)(2,1)S(1)} %collective-permute-done.26.refs_2_, ...), custom_call_target="tpu_custom_call" | custom-call | flops 536870912 | bytes 2097152 | tf_op jit(solution)/shard_map/pallas_call | solution.py:401
  111.3 1.9 %collective-permute-done.28 = bf16[128,2048]{1,0:T(8,128)(2,1)S(1)} collective-permute-done((bf16[128,2048]{1,0:T(8,128)(2,1)S(1)}, bf16[128,2048]{1,0:T(8,128)(2,1)S(1)}, u32[]{:S(2)}, u32[]{:S(2)}) %collective-permute-start.28) | collective-permute-done | bytes 524320 | tf_op jit(solution)/shard_map/ppermute | solution.py:497
  113.4 1.6 %collective-permute-start.29 = (bf16[64,2048]{1,0:T(8,128)(2,1)S(1)}, bf16[64,2048]{1,0:T(8,128)(2,1)S(1)}, u32[]{:S(2)}, u32[]{:S(2)}) collective-permute-start(bf16[64,2048]{1,0:T(8,128)(2,1)S(1)} %fusion), channel_id=1, source_target_pairs={{0,2},{2,0},{1,3},{3,1},{4,6},{6,4},{5,7},{7,5},{8,10},{10,8},{9,1... | collective-permute-start | bytes 786440 | tf_op jit(solution)/shard_map/ppermute | solution.py:498
  115.0 6.8 %collective-permute-done.29 = bf16[64,2048]{1,0:T(8,128)(2,1)S(1)} collective-permute-done((bf16[64,2048]{1,0:T(8,128)(2,1)S(1)}, bf16[64,2048]{1,0:T(8,128)(2,1)S(1)}, u32[]{:S(2)}, u32[]{:S(2)}) %collective-permute-start.29) | collective-permute-done | bytes 262176 | tf_op jit(solution)/shard_map/ppermute | solution.py:498
  121.8 0.8 fusion.2
  (52 shorter events, 3.4 us)
Async XLA Ops:
  1.8 7.4 %collective-permute-start.4 = (bf16[192,256]{1,0:T(8,128)(2,1)S(1)}, bf16[192,256]{1,0:T(8,128)(2,1)S(1)}, u32[]{:S(2)}, u32[]{:S(2)}) collective-permute-start(bf16[192,256]{1,0:T(8,128)(2,1)S(1)} %get-tuple-element.99), channel_id=1, source_target_pairs={{0,1},{1,0},{2,3},{3,2},{4,5},{5,4},{6,7},{7,6},{8,9},{9,8},{10,11... | collective-permute-start | bytes 294920 | tf_op jit(solution)/shard_map/ppermute | solution.py:457
  2.3 6.9 %collective-permute-start.1 = (bf16[192,256]{1,0:T(8,128)(2,1)S(1)}, bf16[192,256]{1,0:T(8,128)(2,1)S(1)}, u32[]{:S(2)}, u32[]{:S(2)}) collective-permute-start(bf16[192,256]{1,0:T(8,128)(2,1)S(1)} %get-tuple-element.98), channel_id=1, source_target_pairs={{0,2},{2,0},{1,3},{3,1},{4,6},{6,4},{5,7},{7,5},{8,10},{10,8},{9,1... | collective-permute-start | bytes 294920 | tf_op jit(solution)/shard_map/ppermute | solution.py:456
  4.9 5.4 %collective-permute-start.2 = (bf16[192,256]{1,0:T(8,128)(2,1)S(1)}, bf16[192,256]{1,0:T(8,128)(2,1)S(1)}, u32[]{:S(2)}, u32[]{:S(2)}) collective-permute-start(bf16[192,256]{1,0:T(8,128)(2,1)S(1)} %get-tuple-element.100), channel_id=1, source_target_pairs={{0,3},{1,2},{2,1},{3,0},{4,7},{5,6},{6,5},{7,4},{8,11},{9,10},{10,... | collective-permute-start | bytes 294920 | tf_op jit(solution)/shard_map/ppermute | solution.py:454
  7.2 1.4 %copy-start = (bf16[384,1024]{1,0:T(8,128)(2,1)S(1)}, bf16[384,1024]{1,0:T(8,128)(2,1)}, u32[]{:S(2)}) copy-start(bf16[384,1024]{1,0:T(8,128)(2,1)} %param.5) | copy-start | bytes 2359300
  10.4 43.8 %collective-permute-start.3 = (bf16[912,1024]{1,0:T(8,128)(2,1)S(1)}, bf16[912,1024]{1,0:T(8,128)(2,1)}, u32[]{:S(2)}, u32[]{:S(2)}) collective-permute-start(bf16[912,1024]{1,0:T(8,128)(2,1)S(1)} %pad_maximum_fusion.refs_4_.refs_0_), channel_id=1, source_target_pairs={{0,2},{2,0},{1,3},{3,1},{4,6},{6,4},{5,7},{7,5},{8,10},{10,8},{9,1... | collective-permute-start | bytes 5603336 | tf_op jit(solution)/shard_map/ppermute | solution.py:474
  12.1 11.1 %collective-permute-start.5 = (bf16[768,256]{1,0:T(8,128)(2,1)S(1)}, bf16[768,256]{1,0:T(8,128)(2,1)}, u32[]{:S(2)}, u32[]{:S(2)}) collective-permute-start(bf16[768,256]{1,0:T(8,128)(2,1)S(1)} %fusion.8.refs_0_), channel_id=1, source_target_pairs={{0,4},{4,0},{8,12},{12,8},{1,5},{5,1},{9,13},{13,9},{2,6},{6,2},{1... | collective-permute-start | bytes 1179656 | tf_op jit(solution)/shard_map/ppermute | solution.py:39
  13.6 9.5 %collective-permute-start.6 = (bf16[768,256]{1,0:T(8,128)(2,1)S(1)}, bf16[768,256]{1,0:T(8,128)(2,1)}, u32[]{:S(2)}, u32[]{:S(2)}) collective-permute-start(bf16[768,256]{1,0:T(8,128)(2,1)S(1)} %fusion.8.refs_0_), channel_id=1, source_target_pairs={{4,8},{8,4},{5,9},{9,5},{6,10},{10,6},{7,11},{11,7},{20,24},{24,20... | collective-permute-start | bytes 1179656 | tf_op jit(solution)/shard_map/ppermute | solution.py:426
  15.0 10.7 %collective-permute-start.7 = (bf16[768,256]{1,0:T(8,128)(2,1)S(1)}, bf16[768,256]{1,0:T(8,128)(2,1)S(1)}, u32[]{:S(2)}, u32[]{:S(2)}) collective-permute-start(bf16[768,256]{1,0:T(8,128)(2,1)S(1)} %fusion.8.refs_0_), channel_id=1, source_target_pairs={{0,16},{16,0},{1,17},{17,1},{2,18},{18,2},{3,19},{19,3},{4,20},{20... | collective-permute-start | bytes 1179656 | tf_op jit(solution)/shard_map/ppermute | solution.py:418
  25.7 10.2 %collective-permute-start.10 = (bf16[768,256]{1,0:T(8,128)(2,1)}, bf16[768,256]{1,0:T(8,128)(2,1)}, u32[]{:S(2)}, u32[]{:S(2)}) collective-permute-start(bf16[768,256]{1,0:T(8,128)(2,1)} %collective-permute-done.5.refs_1_), channel_id=1, source_target_pairs={{0,16},{16,0},{1,17},{17,1},{2,18},{18,2},{3,19},{19,3},{4,20},{20... | collective-permute-start | bytes 1179656 | tf_op jit(solution)/shard_map/ppermute | solution.py:418
  27.2 8.7 %collective-permute-start.8 = (bf16[768,256]{1,0:T(8,128)(2,1)}, bf16[768,256]{1,0:T(8,128)(2,1)}, u32[]{:S(2)}, u32[]{:S(2)}) collective-permute-start(bf16[768,256]{1,0:T(8,128)(2,1)} %collective-permute-done.5.refs_1_), channel_id=1, source_target_pairs={{4,8},{8,4},{5,9},{9,5},{6,10},{10,6},{7,11},{11,7},{20,24},{24,20... | collective-permute-start | bytes 1179656 | tf_op jit(solution)/shard_map/ppermute | solution.py:428
  28.6 13.4 %collective-permute-start.9 = (bf16[768,256]{1,0:T(8,128)(2,1)}, bf16[768,256]{1,0:T(8,128)(2,1)}, u32[]{:S(2)}, u32[]{:S(2)}) collective-permute-start(bf16[768,256]{1,0:T(8,128)(2,1)} %collective-permute-done.6), channel_id=1, source_target_pairs={{4,0},{8,12},{5,1},{9,13},{6,2},{10,14},{7,3},{11,15},{20,16},{24,... | collective-permute-start | bytes 1179656 | tf_op jit(solution)/shard_map/ppermute | solution.py:428
  43.1 8.7 %collective-permute-start.12 = (bf16[768,256]{1,0:T(8,128)(2,1)S(1)}, bf16[768,256]{1,0:T(8,128)(2,1)S(1)}, u32[]{:S(2)}, u32[]{:S(2)}) collective-permute-start(bf16[768,256]{1,0:T(8,128)(2,1)S(1)} %broadcast_select_fusion.2.refs_2_), channel_id=1, source_target_pairs={{0,16},{16,0},{1,17},{17,1},{2,18},{18,2},{3,19},{19,3},{4,20},{20... | collective-permute-start | bytes 1179656 | tf_op jit(solution)/shard_map/ppermute | solution.py:418
  43.7 10.5 %collective-permute-start.11 = (bf16[768,256]{1,0:T(8,128)(2,1)}, bf16[768,256]{1,0:T(8,128)(2,1)S(1)}, u32[]{:S(2)}, u32[]{:S(2)}) collective-permute-start(bf16[768,256]{1,0:T(8,128)(2,1)} %collective-permute-done.8), channel_id=1, source_target_pairs={{4,0},{8,12},{5,1},{9,13},{6,2},{10,14},{7,3},{11,15},{20,16},{24,... | collective-permute-start | bytes 1179656 | tf_op jit(solution)/shard_map/ppermute | solution.py:431
  45.0 11.6 %collective-permute-start = (bf16[912,1024]{1,0:T(8,128)(2,1)S(1)}, bf16[912,1024]{1,0:T(8,128)(2,1)S(1)}, u32[]{:S(2)}, u32[]{:S(2)}) collective-permute-start(bf16[912,1024]{1,0:T(8,128)(2,1)S(1)} %pad_maximum_fusion.refs_4_.refs_0_), channel_id=1, source_target_pairs={{0,1},{1,0},{2,3},{3,2},{4,5},{5,4},{6,7},{7,6},{8,9},{9,8},{10,11... | collective-permute-start | bytes 5603336 | tf_op jit(solution)/shard_map/ppermute | solution.py:475
  54.2 4.1 %collective-permute-start.13 = (bf16[912,1024]{1,0:T(8,128)(2,1)}, bf16[912,1024]{1,0:T(8,128)(2,1)S(1)}, u32[]{:S(2)}, u32[]{:S(2)}) collective-permute-start(bf16[912,1024]{1,0:T(8,128)(2,1)} %collective-permute-done.3.refs_6_.refs_2_), channel_id=1, source_target_pairs={{0,1},{1,0},{2,3},{3,2},{4,5},{5,4},{6,7},{7,6},{8,9},{9,8},{10,11... | collective-permute-start | bytes 5603336 | tf_op jit(solution)/shard_map/ppermute | solution.py:475
  54.3 11.5 %collective-permute-start.14 = (bf16[768,256]{1,0:T(8,128)(2,1)S(1)}, bf16[768,256]{1,0:T(8,128)(2,1)S(1)}, u32[]{:S(2)}, u32[]{:S(2)}) collective-permute-start(bf16[768,256]{1,0:T(8,128)(2,1)S(1)} %broadcast_select_fusion.1.refs_3_), channel_id=1, source_target_pairs={{0,16},{16,0},{1,17},{17,1},{2,18},{18,2},{3,19},{19,3},{4,20},{20... | collective-permute-start | bytes 1179656 | tf_op jit(solution)/shard_map/ppermute | solution.py:418
  55.9 15.0 %collective-permute-start.15 = (bf16[128,2048]{1,0:T(8,128)(2,1)S(1)}, bf16[128,2048]{1,0:T(8,128)(2,1)S(1)}, u32[]{:S(2)}, u32[]{:S(2)}) collective-permute-start(bf16[128,2048]{1,0:T(8,128)(2,1)S(1)} %slice_select_fusion.1.refs_8_), channel_id=1, source_target_pairs={{0,2},{2,0},{1,3},{3,1},{4,6},{6,4},{5,7},{7,5},{8,10},{10,8},{9,1... | collective-permute-start | bytes 1572872 | tf_op jit(solution)/shard_map/ppermute | solution.py:474
  56.5 15.0 %collective-permute-start.16 = (bf16[128,2048]{1,0:T(8,128)(2,1)S(1)}, bf16[128,2048]{1,0:T(8,128)(2,1)S(1)}, u32[]{:S(2)}, u32[]{:S(2)}) collective-permute-start(bf16[128,2048]{1,0:T(8,128)(2,1)S(1)} %slice_select_fusion.1.refs_8_), channel_id=1, source_target_pairs={{0,1},{1,0},{2,3},{3,2},{4,5},{5,4},{6,7},{7,6},{8,9},{9,8},{10,11... | collective-permute-start | bytes 1572872 | tf_op jit(solution)/shard_map/ppermute | solution.py:475
  70.8 2.0 %collective-permute-start.17 = (bf16[128,2048]{1,0:T(8,128)(2,1)S(1)}, bf16[128,2048]{1,0:T(8,128)(2,1)S(1)}, u32[]{:S(2)}, u32[]{:S(2)}) collective-permute-start(bf16[128,2048]{1,0:T(8,128)(2,1)S(1)} %collective-permute-done.15.refs_10_), channel_id=1, source_target_pairs={{0,1},{1,0},{2,3},{3,2},{4,5},{5,4},{6,7},{7,6},{8,9},{9,8},{10,11... | collective-permute-start | bytes 1572872 | tf_op jit(solution)/shard_map/ppermute | solution.py:475
  70.9 1.9 %collective-permute-start.19 = (f32[8,256]{1,0:T(8,128)S(1)}, f32[8,256]{1,0:T(8,128)S(1)}, u32[]{:S(2)}, u32[]{:S(2)}) collective-permute-start(f32[8,256]{1,0:T(8,128)S(1)} %get-tuple-element.74.refs_13_), channel_id=1, source_target_pairs={{0,1},{1,0},{2,3},{3,2},{4,5},{5,4},{6,7},{7,6},{8,9},{9,8},{10,11... | collective-permute-start | bytes 24584 | tf_op jit(solution)/shard_map/ppermute | solution.py:483
  71.4 1.4 %collective-permute-start.18 = (f32[8,256]{1,0:T(8,128)S(1)}, f32[8,256]{1,0:T(8,128)S(1)}, u32[]{:S(2)}, u32[]{:S(2)}) collective-permute-start(f32[8,256]{1,0:T(8,128)S(1)} %get-tuple-element.73.refs_12_), channel_id=1, source_target_pairs={{0,1},{1,0},{2,3},{3,2},{4,5},{5,4},{6,7},{7,6},{8,9},{9,8},{10,11... | collective-permute-start | bytes 24584 | tf_op jit(solution)/shard_map/ppermute | solution.py:483
  76.6 9.6 %collective-permute-start.20 = (bf16[136,1024]{1,0:T(8,128)(2,1)S(1)}, bf16[136,1024]{1,0:T(8,128)(2,1)S(1)}, u32[]{:S(2)}, u32[]{:S(2)}) collective-permute-start(bf16[136,1024]{1,0:T(8,128)(2,1)S(1)} %get-tuple-element.79), channel_id=1, source_target_pairs={{0,4},{4,0},{8,12},{12,8},{1,5},{5,1},{9,13},{13,9},{2,6},{6,2},{1... | collective-permute-start | bytes 835592 | tf_op jit(solution)/shard_map/ppermute | solution.py:39
  77.4 11.7 %collective-permute-start.24 = (bf16[1024,256]{1,0:T(8,128)(2,1)S(1)}, bf16[1024,256]{1,0:T(8,128)(2,1)S(1)}, u32[]{:S(2)}, u32[]{:S(2)}) collective-permute-start(bf16[1024,256]{1,0:T(8,128)(2,1)S(1)} %get-tuple-element.82.refs_3_), channel_id=1, source_target_pairs={{0,1},{1,0},{2,3},{3,2},{4,5},{5,4},{6,7},{7,6},{8,9},{9,8},{10,11... | collective-permute-start | bytes 1572872 | tf_op jit(solution)/shard_map/ppermute | solution.py:484
  77.4 11.7 %collective-permute-start.23 = (bf16[1024,256]{1,0:T(8,128)(2,1)S(1)}, bf16[1024,256]{1,0:T(8,128)(2,1)S(1)}, u32[]{:S(2)}, u32[]{:S(2)}) collective-permute-start(bf16[1024,256]{1,0:T(8,128)(2,1)S(1)} %get-tuple-element.81.refs_2_), channel_id=1, source_target_pairs={{0,1},{1,0},{2,3},{3,2},{4,5},{5,4},{6,7},{7,6},{8,9},{9,8},{10,11... | collective-permute-start | bytes 1572872 | tf_op jit(solution)/shard_map/ppermute | solution.py:484
  80.7 10.6 %collective-permute-start.22 = (bf16[136,1024]{1,0:T(8,128)(2,1)S(1)}, bf16[136,1024]{1,0:T(8,128)(2,1)S(1)}, u32[]{:S(2)}, u32[]{:S(2)}) collective-permute-start(bf16[136,1024]{1,0:T(8,128)(2,1)S(1)} %get-tuple-element.80), channel_id=1, source_target_pairs={{0,4},{4,0},{8,12},{12,8},{1,5},{5,1},{9,13},{13,9},{2,6},{6,2},{1... | collective-permute-start | bytes 835592 | tf_op jit(solution)/shard_map/ppermute | solution.py:39
  86.2 12.4 %collective-permute-start.21 = (bf16[136,1024]{1,0:T(8,128)(2,1)S(1)}, bf16[136,1024]{1,0:T(8,128)(2,1)S(1)}, u32[]{:S(2)}, u32[]{:S(2)}) collective-permute-start(bf16[136,1024]{1,0:T(8,128)(2,1)S(1)} %shard_map.59), channel_id=1, source_target_pairs={{0,12},{4,8},{8,4},{12,0},{1,13},{5,9},{9,5},{13,1},{2,14},{6,10},... | collective-permute-start | bytes 835592 | tf_op jit(solution)/shard_map/ppermute | solution.py:39
  100.6 4.5 %collective-permute-start.25 = (bf16[128,256]{1,0:T(8,128)(2,1)S(1)}, bf16[128,256]{1,0:T(8,128)(2,1)S(1)}, u32[]{:S(2)}, u32[]{:S(2)}) collective-permute-start(bf16[128,256]{1,0:T(8,128)(2,1)S(1)} %get-tuple-element.84), channel_id=1, source_target_pairs={{0,4},{4,0},{8,12},{12,8},{1,5},{5,1},{9,13},{13,9},{2,6},{6,2},{1... | collective-permute-start | bytes 196616 | tf_op jit(solution)/shard_map/ppermute | solution.py:39
  102.1 5.9 %collective-permute-start.26 = (bf16[128,256]{1,0:T(8,128)(2,1)S(1)}, bf16[128,256]{1,0:T(8,128)(2,1)S(1)}, u32[]{:S(2)}, u32[]{:S(2)}) collective-permute-start(bf16[128,256]{1,0:T(8,128)(2,1)S(1)} %get-tuple-element.85), channel_id=1, source_target_pairs={{0,8},{4,12},{8,0},{12,4},{1,9},{5,13},{9,1},{13,5},{2,10},{6,14},... | collective-permute-start | bytes 196616 | tf_op jit(solution)/shard_map/ppermute | solution.py:39
  103.2 6.2 %collective-permute-start.27 = (bf16[128,256]{1,0:T(8,128)(2,1)S(1)}, bf16[128,256]{1,0:T(8,128)(2,1)S(1)}, u32[]{:S(2)}, u32[]{:S(2)}) collective-permute-start(bf16[128,256]{1,0:T(8,128)(2,1)S(1)} %get-tuple-element.86), channel_id=1, source_target_pairs={{0,12},{4,8},{8,4},{12,0},{1,13},{5,9},{9,5},{13,1},{2,14},{6,10},... | collective-permute-start | bytes 196616 | tf_op jit(solution)/shard_map/ppermute | solution.py:39
  111.3 2.0 %collective-permute-start.28 = (bf16[128,2048]{1,0:T(8,128)(2,1)S(1)}, bf16[128,2048]{1,0:T(8,128)(2,1)S(1)}, u32[]{:S(2)}, u32[]{:S(2)}) collective-permute-start(bf16[128,2048]{1,0:T(8,128)(2,1)S(1)} %convert_element_type.24), channel_id=1, source_target_pairs={{0,1},{1,0},{2,3},{3,2},{4,5},{5,4},{6,7},{7,6},{8,9},{9,8},{10,11... | collective-permute-start | bytes 1572872 | tf_op jit(solution)/shard_map/ppermute | solution.py:497
  113.4 8.4 %collective-permute-start.29 = (bf16[64,2048]{1,0:T(8,128)(2,1)S(1)}, bf16[64,2048]{1,0:T(8,128)(2,1)S(1)}, u32[]{:S(2)}, u32[]{:S(2)}) collective-permute-start(bf16[64,2048]{1,0:T(8,128)(2,1)S(1)} %fusion), channel_id=1, source_target_pairs={{0,2},{2,0},{1,3},{3,1},{4,6},{6,4},{5,7},{7,5},{8,10},{10,8},{9,1... | collective-permute-start | bytes 786440 | tf_op jit(solution)/shard_map/ppermute | solution.py:498

commit v7 on v6

--- a/solution.py
+++ b/solution.py
@@ -413,24 +413,22 @@
     )(where, *slots, *bases)
 
 
-def gather_levels(unit, level, levels):
+def gather_levels(unit, level, levels, ready):
     def over(slot):
         return lax.ppermute(slot, "group", SWAP)
 
     if levels != 4:
         slots = [unit] + [across(unit, step, levels) for step in range(1, levels)]
-        return slots, [over(slot) for slot in slots]
+        return slots, [over(slot) for slot in slots], ready
     middle = (level == 1) | (level == 2)
-    inner, outward = [(1, 2), (2, 1)], [(1, 0), (2, 3)]
     together = lax.optimization_barrier
-    first, third, other0 = together((across(unit, 1, levels), lax.ppermute(unit, "level", inner), over(unit)))
-    inside, outside, other1 = together(
-        (lax.ppermute(first, "level", inner), lax.ppermute(third, "level", outward), over(first))
-    )
-    second = jnp.where(middle, inside, outside)
-    outside, other2 = together((lax.ppermute(inside, "level", outward), over(second)))
-    third = jnp.where(middle, third, outside)
-    return [unit, first, second, third], [other0, other1, other2, over(third)]
+    inner = lax.ppermute(unit, "level", [(1, 2), (2, 1)])
+    first, inner, other0, ready = together((across(unit, 1, levels), inner, over(unit), ready))
+    held, inner = together((unit, inner))
+    outer, other1 = together((lax.ppermute(held, "level", [(0, 3), (3, 0)]), over(first)))
+    third = jnp.where(middle, inner, outer)
+    second, other3 = together((across(third, 1, levels), over(third)))
+    return [unit, first, second, third], [other0, other1, over(second), other3], ready
 
 
 def body(acts, grads, counts, basis_a, basis_g):
@@ -454,31 +452,32 @@
         return lax.ppermute(x, ("chip", "core"), [(i, 3 - i) for i in range(4)])
 
     beyond = [lax.ppermute(columns(1 - chip, core), "chip", SWAP), diagonal(columns(1 - chip, 1 - core))]
-    blocks = jnp.stack([columns(chip, core), lax.ppermute(columns(chip, 1 - core), "core", SWAP)] + beyond)
+    beside = lax.ppermute(columns(chip, 1 - core), "core", SWAP)
+    blocks = jnp.stack([columns(chip, core), beside] + beyond)
     blocks = [lax.dynamic_index_in_dim(blocks, j ^ (chip * 2 + core), 0, False) for j in range(4)]
     unit = jnp.concatenate([b[:rows_g] for b in blocks] + [b[rows_g:] for b in blocks])
     level_g, level_a = 4 * rows_g, 4 * rows_a
 
-    slots, others = gather_levels(unit, level, levels)
     valid = counts[0]
     keep = jnp.arange(rows, dtype=jnp.int32)[:, None] < valid
+    half = split(rows)[0]
+    later, _ = lax.optimization_barrier((grads, unit))
+    slots, others, late = gather_levels(unit, level, levels, jnp.where(keep[half:], later[half:], 0))
     marks = jnp.stack([valid // 16 * 16, valid % 16]).astype(bf16)
     marks = jnp.broadcast_to(jnp.pad(marks, (0, 14))[:, None], (16, width_a))
-    half = split(rows)[0]
     early = jnp.where(keep[:half], grads[:half], 0)
     early = jnp.concatenate([jnp.where(keep, acts, 0), marks, early[:, :width_a], early[:, width_a:]])
-    late = jnp.where(keep[half:], grads[half:], 0)
-    (early_out, late_out), _ = lax.optimization_barrier(((early, late), beyond))
+    early_out, _ = lax.optimization_barrier((early, beyond[0]))
 
     def four(mine, out, after):
         far, after = lax.optimization_barrier((lax.ppermute(out, "chip", SWAP), after))
         return [mine, lax.ppermute(mine, "core", SWAP), far, lax.ppermute(far, "core", SWAP)], after
 
-    early, slots[-1] = four(early, early_out, slots[-1])
+    early, slots[2] = four(early, early_out, slots[2])
     first = turn(where, slots, early, rows, level_g, level_a)
-    others[-1], first = lax.optimization_barrier((others[-1], first))
+    others[2], first = lax.optimization_barrier((others[2], first))
     second = turn(where, others, early, rows, level_g, level_a)
-    late, second = four(late, late_out, second)
+    late, second = four(late, late, second)
     bases_a, turned_g, bases_g, sums = zip(first, second)
     sums += tuple(lax.ppermute(t, "core", SWAP) for t in sums)
     bases_a += tuple(lax.ppermute(t, "core", SWAP) for t in bases_a)

time: 123 us -> 121 us (0.984)
  waiting for transfers between devices: 63.9 us -> 57.7 us
  starting transfers between devices: 30 us -> 34 us
    ppermute x4, waiting for transfers between devices: 17.9 us -> 5.83 us  [over(): return lax.ppermute(slot, 'group', SWAP)]
    ppermute x7 -> x8, waiting for transfers between devices: 24.6 us -> 30.5 us  [across(): return lax.ppermute(x, 'level', [(i, i ^ step) for i in range(levels)])]
    ppermute x2, waiting for transfers between devices: 0.01 us -> 2.16 us  [four(): lax.ppermute(out, 'chip', SWAP)]
    ppermute x7 -> x8, starting transfers between devices: 11 us -> 13.1 us  [across(): return lax.ppermute(x, 'level', [(i, i ^ step) for i in range(levels)])]
    ppermute x5 -> x3, waiting for transfers between devices: 8.46 us -> 7.81 us  [the longest x1 7.8 us: gather_levels(): lax.ppermute(held, 'level', [(0, 3), (3, 0)])]
    ppermute x5 -> x3, starting transfers between devices: 5.88 us -> 5.56 us  [the longest x1 4.37 us: gather_levels(): lax.ppermute(held, 'level', [(0, 3), (3, 0)])]
  transfers between devices with their start and end apart: 30 -> 29, of which waited for: 17 -> 18; matrix products, arithmetic and copies ran while one was open for 4% -> 4% of each run, Pallas kernels for 10% -> 11%
where the time goes in v7:
time: 121 us; the launch traced here: 120 us
  waiting for transfers between devices  57.7 us (48%)
  starting transfers between devices  34 us (28%)
  Pallas kernels  20.3 us (17%)
  other arithmetic  5.33 us (4%)
  local copies, waits for them, and re-layouts  1.96 us (2%)
    ppermute x8, waiting for transfers between devices, across(): return lax.ppermute(x, 'level', [(i, i ^ step) for i in range(levels)])  30.5 us
    ppermute x8, starting transfers between devices, across(): return lax.ppermute(x, 'level', [(i, i ^ step) for i in range(levels)])  13.1 us
    pallas_call x2, Pallas kernels, turn(): pl.pallas_call(functools.partial(turn_kernel, levels, level_g, level_a, r...  9.94 us
    ppermute x1, waiting for transfers between devices, gather_levels(): lax.ppermute(held, 'level', [(0, 3), (3, 0)])  7.8 us
    ppermute x1, waiting for transfers between devices, body(): lax.ppermute((kept[:rows_a] + sent[:rows_a]).astype(bf16), 'chip', SWAP)  6.83 us
    ppermute x4, starting transfers between devices, over(): return lax.ppermute(slot, 'group', SWAP)  6.31 us
    ppermute x4, waiting for transfers between devices, over(): return lax.ppermute(slot, 'group', SWAP)  5.83 us
    ppermute x1, starting transfers between devices, gather_levels(): lax.ppermute(held, 'level', [(0, 3), (3, 0)])  4.37 us
  transfers between devices with their start and end apart: 29, of which 18 were waited for; matrix products, arithmetic and copies ran while one was open for 4% of the time, Pallas kernels for 11%

profile of v7, /device:TPU:0, one launch (start us, length us, event | category | flops | bytes accessed | tf_op | source)
XLA Modules:
  0.0 120.4 jit_solution(803685666793864464)
XLA Ops:
  0.0 0.8 constant_dynamic-slice_fusion.1
  0.8 1.0 constant_dynamic-slice_fusion.3
  1.8 0.5 collective-permute-start.3
  2.3 2.6 %collective-permute-start.1 = (bf16[192,256]{1,0:T(8,128)(2,1)S(1)}, bf16[192,256]{1,0:T(8,128)(2,1)S(1)}, u32[]{:S(2)}, u32[]{:S(2)}) collective-permute-start(bf16[192,256]{1,0:T(8,128)(2,1)S(1)} %get-tuple-element.102), channel_id=1, source_target_pairs={{0,2},{2,0},{1,3},{3,1},{4,6},{6,4},{5,7},{7,5},{8,10},{10,8},{9,1... | collective-permute-start | bytes 294920 | tf_op jit(solution)/shard_map/ppermute | solution.py:454
  5.8 1.4 %slice_select_fusion = bf16[256,2048]{1,0:T(8,128)(2,1)S(1)} fusion(bf16[384,2048]{1,0:T(8,128)(2,1)} %param.6, pred[256]{0:T(512)(128)(4,1)S(1)} %slice_reduce_fusion), kind=kLoop, calls=%fused_computation.1 | loop fusion | flops 524288 | bytes 2097408 | tf_op jit(solution)/shard_map/jit(_where)/select_n | solution.py:468
  8.0 0.6 collective-permute-done.1
  8.5 1.9 %collective-permute-start.2 = (bf16[912,1024]{1,0:T(8,128)(2,1)S(1)}, bf16[912,1024]{1,0:T(8,128)(2,1)}, u32[]{:S(2)}, u32[]{:S(2)}) collective-permute-start(bf16[912,1024]{1,0:T(8,128)(2,1)S(1)} %pad_maximum_fusion.refs_4_.refs_0_), channel_id=1, source_target_pairs={{0,2},{2,0},{1,3},{3,1},{4,6},{6,4},{5,7},{7,5},{8,10},{10,8},{9,1... | collective-permute-start | bytes 5603336 | tf_op jit(solution)/shard_map/ppermute | solution.py:473
  10.7 1.6 %collective-permute-start.5 = (bf16[768,256]{1,0:T(8,128)(2,1)S(1)}, bf16[768,256]{1,0:T(8,128)(2,1)}, u32[]{:S(2)}, u32[]{:S(2)}) collective-permute-start(bf16[768,256]{1,0:T(8,128)(2,1)S(1)} %fusion.8.refs_0_), channel_id=1, source_target_pairs={{0,4},{4,0},{8,12},{12,8},{1,5},{5,1},{9,13},{13,9},{2,6},{6,2},{1... | collective-permute-start | bytes 1179656 | tf_op jit(solution)/shard_map/ppermute | solution.py:39
  12.4 0.7 collective-permute-start.6
  13.0 1.6 %collective-permute-start.7 = (bf16[768,256]{1,0:T(8,128)(2,1)S(1)}, bf16[768,256]{1,0:T(8,128)(2,1)S(1)}, u32[]{:S(2)}, u32[]{:S(2)}) collective-permute-start(bf16[768,256]{1,0:T(8,128)(2,1)S(1)} %fusion.8.refs_0_), channel_id=1, source_target_pairs={{0,16},{16,0},{1,17},{17,1},{2,18},{18,2},{3,19},{19,3},{4,20},{20... | collective-permute-start | bytes 1179656 | tf_op jit(solution)/shard_map/ppermute | solution.py:418
  14.6 1.1 slice_select_fusion.1.refs_8_
  15.8 6.0 %collective-permute-done.5.refs_1_ = bf16[768,256]{1,0:T(8,128)(2,1)} collective-permute-done((bf16[768,256]{1,0:T(8,128)(2,1)S(1)}, bf16[768,256]{1,0:T(8,128)(2,1)}, u32[]{:S(2)}, u32[]{:S(2)}) %collective-permute-start.5) | collective-permute-done | bytes 393248 | tf_op jit(solution)/shard_map/ppermute | solution.py:39
  21.8 2.1 %collective-permute-done.7.refs_0_ = bf16[768,256]{1,0:T(8,128)(2,1)S(1)} collective-permute-done((bf16[768,256]{1,0:T(8,128)(2,1)S(1)}, bf16[768,256]{1,0:T(8,128)(2,1)S(1)}, u32[]{:S(2)}, u32[]{:S(2)}) %collective-permute-start.7) | collective-permute-done | bytes 393248 | tf_op jit(solution)/shard_map/ppermute | solution.py:418
  23.9 4.4 %collective-permute-start.8 = (bf16[768,256]{1,0:T(8,128)(2,1)S(1)}, bf16[768,256]{1,0:T(8,128)(2,1)}, u32[]{:S(2)}, u32[]{:S(2)}) collective-permute-start(bf16[768,256]{1,0:T(8,128)(2,1)S(1)} %fusion.8.refs_0_), channel_id=1, source_target_pairs={{0,12},{12,0},{1,13},{13,1},{2,14},{14,2},{3,15},{15,3},{16,28},{2... | collective-permute-start | bytes 1179656 | tf_op jit(solution)/shard_map/ppermute | solution.py:428
  28.2 1.6 %collective-permute-start.9 = (bf16[768,256]{1,0:T(8,128)(2,1)}, bf16[768,256]{1,0:T(8,128)(2,1)}, u32[]{:S(2)}, u32[]{:S(2)}) collective-permute-start(bf16[768,256]{1,0:T(8,128)(2,1)} %collective-permute-done.5.refs_1_), channel_id=1, source_target_pairs={{0,16},{16,0},{1,17},{17,1},{2,18},{18,2},{3,19},{19,3},{4,20},{20... | collective-permute-start | bytes 1179656 | tf_op jit(solution)/shard_map/ppermute | solution.py:418
  29.8 7.8 %collective-permute-done.8 = bf16[768,256]{1,0:T(8,128)(2,1)} collective-permute-done((bf16[768,256]{1,0:T(8,128)(2,1)S(1)}, bf16[768,256]{1,0:T(8,128)(2,1)}, u32[]{:S(2)}, u32[]{:S(2)}) %collective-permute-start.8) | collective-permute-done | bytes 393248 | tf_op jit(solution)/shard_map/ppermute | solution.py:428
  37.6 0.8 collective-permute-done.9.refs_1_
  38.4 1.0 broadcast_select_fusion.1.refs_3_
  39.5 0.9 collective-permute-start.10
  40.4 1.5 %collective-permute-start.11 = (bf16[768,256]{1,0:T(8,128)(2,1)S(1)}, bf16[768,256]{1,0:T(8,128)(2,1)S(1)}, u32[]{:S(2)}, u32[]{:S(2)}) collective-permute-start(bf16[768,256]{1,0:T(8,128)(2,1)S(1)} %broadcast_select_fusion.1.refs_3_), channel_id=1, source_target_pairs={{0,16},{16,0},{1,17},{17,1},{2,18},{18,2},{3,19},{19,3},{4,20},{20... | collective-permute-start | bytes 1179656 | tf_op jit(solution)/shard_map/ppermute | solution.py:418
  41.9 6.5 %collective-permute-done.10.refs_2_ = bf16[768,256]{1,0:T(8,128)(2,1)S(1)} collective-permute-done((bf16[768,256]{1,0:T(8,128)(2,1)S(1)}, bf16[768,256]{1,0:T(8,128)(2,1)S(1)}, u32[]{:S(2)}, u32[]{:S(2)}) %collective-permute-start.10) | collective-permute-done | bytes 393248 | tf_op jit(solution)/shard_map/ppermute | solution.py:39
  48.9 2.2 %collective-permute-done.2.refs_6_.refs_2_ = bf16[912,1024]{1,0:T(8,128)(2,1)} collective-permute-done((bf16[912,1024]{1,0:T(8,128)(2,1)S(1)}, bf16[912,1024]{1,0:T(8,128)(2,1)}, u32[]{:S(2)}, u32[]{:S(2)}) %collective-permute-start.2) | collective-permute-done | bytes 1867808 | tf_op jit(solution)/shard_map/ppermute | solution.py:473
  51.0 1.7 %collective-permute-start.13 = (bf16[768,256]{1,0:T(8,128)(2,1)S(1)}, bf16[768,256]{1,0:T(8,128)(2,1)S(1)}, u32[]{:S(2)}, u32[]{:S(2)}) collective-permute-start(bf16[768,256]{1,0:T(8,128)(2,1)S(1)} %collective-permute-done.10.refs_2_), channel_id=1, source_target_pairs={{0,16},{16,0},{1,17},{17,1},{2,18},{18,2},{3,19},{19,3},{4,20},{20... | collective-permute-start | bytes 1179656 | tf_op jit(solution)/shard_map/ppermute | solution.py:418
  52.7 1.5 %collective-permute-start.14 = (bf16[128,2048]{1,0:T(8,128)(2,1)S(1)}, bf16[128,2048]{1,0:T(8,128)(2,1)S(1)}, u32[]{:S(2)}, u32[]{:S(2)}) collective-permute-start(bf16[128,2048]{1,0:T(8,128)(2,1)S(1)} %slice_select_fusion.1.refs_8_), channel_id=1, source_target_pairs={{0,2},{2,0},{1,3},{3,1},{4,6},{6,4},{5,7},{7,5},{8,10},{10,8},{9,1... | collective-permute-start | bytes 1572872 | tf_op jit(solution)/shard_map/ppermute | solution.py:473
  54.3 0.7 collective-permute-done.12.refs_7_.refs_3_
  55.1 5.0 %shard_map.55 = (bf16[1024,256]{1,0:T(8,128)(2,1)S(1)}, bf16[1024,256]{1,0:T(8,128)(2,1)S(1)}, bf16[2048,256]{1,0:T(8,128)(2,1)S(1)}, f32[8,256]{1,0:T(8,128)S(1)}) custom-call(s32[2]{0:T(128)S(1)} %pad_add_fusion.where, bf16[768,256]{1,0:T(8,128)(2,1)S(1)} %fusion.8.refs_0_, bf16[768,256]{1,0:T(8,128)(2,1)} %collective-permute-done.5.refs_1_, ...), custom_call_target="tpu_custom_call" | custom-call | flops 1610612736 | bytes 6291456 | tf_op jit(solution)/shard_map/pallas_call | solution.py:92
  60.0 2.5 %collective-permute-done.13.refs_2_ = bf16[768,256]{1,0:T(8,128)(2,1)S(1)} collective-permute-done((bf16[768,256]{1,0:T(8,128)(2,1)S(1)}, bf16[768,256]{1,0:T(8,128)(2,1)S(1)}, u32[]{:S(2)}, u32[]{:S(2)}) %collective-permute-start.13) | collective-permute-done | bytes 393248 | tf_op jit(solution)/shard_map/ppermute | solution.py:418
  62.6 5.0 %shard_map.56 = (bf16[1024,256]{1,0:T(8,128)(2,1)S(1)}, bf16[1024,256]{1,0:T(8,128)(2,1)S(1)}, bf16[2048,256]{1,0:T(8,128)(2,1)S(1)}, f32[8,256]{1,0:T(8,128)S(1)}) custom-call(s32[2]{0:T(128)S(1)} %pad_add_fusion.where, bf16[768,256]{1,0:T(8,128)(2,1)S(1)} %collective-permute-done.7.refs_0_, bf16[768,256]{1,0:T(8,128)(2,1)} %collective-permute-done.9.refs_1_, ...), custom_call_target="tpu_custom_call" | custom-call | flops 1610612736 | bytes 6291456 | tf_op jit(solution)/shard_map/pallas_call | solution.py:92
  68.2 1.3 %collective-permute-done.18.refs_15_ = f32[8,256]{1,0:T(8,128)S(1)} collective-permute-done((f32[8,256]{1,0:T(8,128)S(1)}, f32[8,256]{1,0:T(8,128)S(1)}, u32[]{:S(2)}, u32[]{:S(2)}) %collective-permute-start.18) | collective-permute-done | bytes 8224 | tf_op jit(solution)/shard_map/ppermute | solution.py:482
  69.5 3.8 %shard_map.57 = (bf16[136,1024]{1,0:T(8,128)(2,1)S(1)}, f32[128,1024]{1,0:T(8,128)S(1)}, f32[8,1024]{1,0:T(8,128)S(1)}, bf16[1536,512]{1,0:T(8,128)(2,1)S(1)}) custom-call(s32[2]{0:T(128)S(1)} %pad_add_fusion.where, bf16[912,1024]{1,0:T(8,128)(2,1)S(1)} %pad_maximum_fusion.refs_4_.refs_0_, bf16[912,1024]{1,0:T(8,128)(2,1)S(1)} %collective-permute-done.refs_5_.refs_1_, ...), custom_call_target="tpu_custom_call" | custom-call | flops 2415919104 | bytes 6291456 | tf_op jit(solution)/shard_map/pallas_call | solution.py:254
  73.3 1.9 %collective-permute-start.19 = (bf16[136,1024]{1,0:T(8,128)(2,1)S(1)}, bf16[136,1024]{1,0:T(8,128)(2,1)S(1)}, u32[]{:S(2)}, u32[]{:S(2)}) collective-permute-start(bf16[136,1024]{1,0:T(8,128)(2,1)S(1)} %get-tuple-element.83), channel_id=1, source_target_pairs={{0,4},{4,0},{8,12},{12,8},{1,5},{5,1},{9,13},{13,9},{2,6},{6,2},{1... | collective-permute-start | bytes 835592 | tf_op jit(solution)/shard_map/ppermute | solution.py:39
  75.2 0.5 collective-permute-start.22
  75.7 2.8 %shard_map.58 = (f32[128,1024]{1,0:T(8,128)S(1)}, bf16[136,1024]{1,0:T(8,128)(2,1)S(1)}) custom-call(s32[2]{0:T(128)S(1)} %pad_add_fusion.where, bf16[1536,512]{1,0:T(8,128)(2,1)S(1)} %get-tuple-element.79.right, f32[8,1024]{1,0:T(8,128)S(1)} %get-tuple-element.80.extra.own_extra, bf16[912,1024]{1,0:T(8,128)(2,1)S(1)} %pad_maximum_fusion.refs_4_.refs_0_, ...), custom_call_target="tpu_custom_call" | custom-call | flops 805306368 | bytes 6291456 | tf_op jit(solution)/shard_map/pallas_call | solution.py:296
  78.8 4.1 %collective-permute-done.19.got = bf16[136,1024]{1,0:T(8,128)(2,1)S(1)} collective-permute-done((bf16[136,1024]{1,0:T(8,128)(2,1)S(1)}, bf16[136,1024]{1,0:T(8,128)(2,1)S(1)}, u32[]{:S(2)}, u32[]{:S(2)}) %collective-permute-start.19) | collective-permute-done | bytes 278560 | tf_op jit(solution)/shard_map/ppermute | solution.py:39
  82.9 3.9 %collective-permute-start.20 = (bf16[136,1024]{1,0:T(8,128)(2,1)S(1)}, bf16[136,1024]{1,0:T(8,128)(2,1)S(1)}, u32[]{:S(2)}, u32[]{:S(2)}) collective-permute-start(bf16[136,1024]{1,0:T(8,128)(2,1)S(1)} %shard_map.59), channel_id=1, source_target_pairs={{0,12},{4,8},{8,4},{12,0},{1,13},{5,9},{9,5},{13,1},{2,14},{6,10},... | collective-permute-start | bytes 835592 | tf_op jit(solution)/shard_map/ppermute | solution.py:39
  86.9 1.3 %collective-permute-done.21.refs_1_ = bf16[136,1024]{1,0:T(8,128)(2,1)S(1)} collective-permute-done((bf16[136,1024]{1,0:T(8,128)(2,1)S(1)}, bf16[136,1024]{1,0:T(8,128)(2,1)S(1)}, u32[]{:S(2)}, u32[]{:S(2)}) %collective-permute-start.21) | collective-permute-done | bytes 278560 | tf_op jit(solution)/shard_map/ppermute | solution.py:39
  88.2 8.2 %collective-permute-done.20.refs_0_ = bf16[136,1024]{1,0:T(8,128)(2,1)S(1)} collective-permute-done((bf16[136,1024]{1,0:T(8,128)(2,1)S(1)}, bf16[136,1024]{1,0:T(8,128)(2,1)S(1)}, u32[]{:S(2)}, u32[]{:S(2)}) %collective-permute-start.20) | collective-permute-done | bytes 278560 | tf_op jit(solution)/shard_map/ppermute | solution.py:39
  96.4 1.9 %shard_map.60 = (bf16[128,256]{1,0:T(8,128)(2,1)S(1)}, bf16[128,256]{1,0:T(8,128)(2,1)S(1)}, bf16[128,256]{1,0:T(8,128)(2,1)S(1)}, bf16[128,256]{1,0:T(8,128)(2,1)S(1)}) custom-call(s32[2]{0:T(128)S(1)} %pad_add_fusion.where, f32[128,1024]{1,0:T(8,128)S(1)} %get-tuple-element.81.own, f32[8,1024]{1,0:T(8,128)S(1)} %get-tuple-element.80.extra.own_extra, ...), custom_call_target="tpu_custom_call" | custom-call | flops 805306368 | bytes 2097152 | tf_op jit(solution)/shard_map/pallas_call | solution.py:358
  98.3 1.5 %collective-permute-start.24 = (bf16[128,256]{1,0:T(8,128)(2,1)S(1)}, bf16[128,256]{1,0:T(8,128)(2,1)S(1)}, u32[]{:S(2)}, u32[]{:S(2)}) collective-permute-start(bf16[128,256]{1,0:T(8,128)(2,1)S(1)} %get-tuple-element.88), channel_id=1, source_target_pairs={{0,4},{4,0},{8,12},{12,8},{1,5},{5,1},{9,13},{13,9},{2,6},{6,2},{1... | collective-permute-start | bytes 196616 | tf_op jit(solution)/shard_map/ppermute | solution.py:39
  99.8 1.1 collective-permute-start.25
  101.0 1.8 %collective-permute-start.26 = (bf16[128,256]{1,0:T(8,128)(2,1)S(1)}, bf16[128,256]{1,0:T(8,128)(2,1)S(1)}, u32[]{:S(2)}, u32[]{:S(2)}) collective-permute-start(bf16[128,256]{1,0:T(8,128)(2,1)S(1)} %get-tuple-element.90), channel_id=1, source_target_pairs={{0,12},{4,8},{8,4},{12,0},{1,13},{5,9},{9,5},{13,1},{2,14},{6,10},... | collective-permute-start | bytes 196616 | tf_op jit(solution)/shard_map/ppermute | solution.py:39
  102.8 2.9 %collective-permute-done.25.refs_2_ = bf16[128,256]{1,0:T(8,128)(2,1)S(1)} collective-permute-done((bf16[128,256]{1,0:T(8,128)(2,1)S(1)}, bf16[128,256]{1,0:T(8,128)(2,1)S(1)}, u32[]{:S(2)}, u32[]{:S(2)}) %collective-permute-start.25) | collective-permute-done | bytes 65568 | tf_op jit(solution)/shard_map/ppermute | solution.py:39
  105.7 1.4 %collective-permute-done.26.refs_3_ = bf16[128,256]{1,0:T(8,128)(2,1)S(1)} collective-permute-done((bf16[128,256]{1,0:T(8,128)(2,1)S(1)}, bf16[128,256]{1,0:T(8,128)(2,1)S(1)}, u32[]{:S(2)}, u32[]{:S(2)}) %collective-permute-start.26) | collective-permute-done | bytes 65568 | tf_op jit(solution)/shard_map/ppermute | solution.py:39
  107.1 1.8 %shard_map.61 = (f32[128,2048]{1,0:T(8,128)S(1)}, f32[128,2048]{1,0:T(8,128)S(1)}) custom-call(s32[2]{0:T(128)S(1)} %pad_add_fusion.where, bf16[128,256]{1,0:T(8,128)(2,1)S(1)} %get-tuple-element.87.refs_0_, bf16[128,256]{1,0:T(8,128)(2,1)S(1)} %collective-permute-done.24.refs_1_, bf16[128,256]{1,0:T(8,128)(2,1)S(1)} %collective-permute-done.25.refs_2_, ...), custom_call_target="tpu_custom_call" | custom-call | flops 536870912 | bytes 2097152 | tf_op jit(solution)/shard_map/pallas_call | solution.py:401
  109.1 1.9 %collective-permute-done.27 = bf16[128,2048]{1,0:T(8,128)(2,1)S(1)} collective-permute-done((bf16[128,2048]{1,0:T(8,128)(2,1)S(1)}, bf16[128,2048]{1,0:T(8,128)(2,1)S(1)}, u32[]{:S(2)}, u32[]{:S(2)}) %collective-permute-start.27) | collective-permute-done | bytes 524320 | tf_op jit(solution)/shard_map/ppermute | solution.py:496
  111.2 1.6 %collective-permute-start.28 = (bf16[64,2048]{1,0:T(8,128)(2,1)S(1)}, bf16[64,2048]{1,0:T(8,128)(2,1)S(1)}, u32[]{:S(2)}, u32[]{:S(2)}) collective-permute-start(bf16[64,2048]{1,0:T(8,128)(2,1)S(1)} %fusion), channel_id=1, source_target_pairs={{0,2},{2,0},{1,3},{3,1},{4,6},{6,4},{5,7},{7,5},{8,10},{10,8},{9,1... | collective-permute-start | bytes 786440 | tf_op jit(solution)/shard_map/ppermute | solution.py:497
  112.8 6.8 %collective-permute-done.28 = bf16[64,2048]{1,0:T(8,128)(2,1)S(1)} collective-permute-done((bf16[64,2048]{1,0:T(8,128)(2,1)S(1)}, bf16[64,2048]{1,0:T(8,128)(2,1)S(1)}, u32[]{:S(2)}, u32[]{:S(2)}) %collective-permute-start.28) | collective-permute-done | bytes 262176 | tf_op jit(solution)/shard_map/ppermute | solution.py:497
  119.6 0.8 fusion.2
  (51 shorter events, 2.9 us)
Async XLA Ops:
  1.8 8.7 %collective-permute-start.3 = (bf16[192,256]{1,0:T(8,128)(2,1)S(1)}, bf16[192,256]{1,0:T(8,128)(2,1)S(1)}, u32[]{:S(2)}, u32[]{:S(2)}) collective-permute-start(bf16[192,256]{1,0:T(8,128)(2,1)S(1)} %get-tuple-element.103), channel_id=1, source_target_pairs={{0,1},{1,0},{2,3},{3,2},{4,5},{5,4},{6,7},{7,6},{8,9},{9,8},{10,11... | collective-permute-start | bytes 294920 | tf_op jit(solution)/shard_map/ppermute | solution.py:455
  2.3 6.2 %collective-permute-start.1 = (bf16[192,256]{1,0:T(8,128)(2,1)S(1)}, bf16[192,256]{1,0:T(8,128)(2,1)S(1)}, u32[]{:S(2)}, u32[]{:S(2)}) collective-permute-start(bf16[192,256]{1,0:T(8,128)(2,1)S(1)} %get-tuple-element.102), channel_id=1, source_target_pairs={{0,2},{2,0},{1,3},{3,1},{4,6},{6,4},{5,7},{7,5},{8,10},{10,8},{9,1... | collective-permute-start | bytes 294920 | tf_op jit(solution)/shard_map/ppermute | solution.py:454
  4.9 5.6 %collective-permute-start.4 = (bf16[192,256]{1,0:T(8,128)(2,1)S(1)}, bf16[192,256]{1,0:T(8,128)(2,1)S(1)}, u32[]{:S(2)}, u32[]{:S(2)}) collective-permute-start(bf16[192,256]{1,0:T(8,128)(2,1)S(1)} %get-tuple-element.104), channel_id=1, source_target_pairs={{0,3},{1,2},{2,1},{3,0},{4,7},{5,6},{6,5},{7,4},{8,11},{9,10},{10,... | collective-permute-start | bytes 294920 | tf_op jit(solution)/shard_map/ppermute | solution.py:452
  5.8 1.6 %copy-start = (bf16[384,1024]{1,0:T(8,128)(2,1)S(1)}, bf16[384,1024]{1,0:T(8,128)(2,1)}, u32[]{:S(2)}) copy-start(bf16[384,1024]{1,0:T(8,128)(2,1)} %param.5) | copy-start | bytes 2359300
  8.5 42.5 %collective-permute-start.2 = (bf16[912,1024]{1,0:T(8,128)(2,1)S(1)}, bf16[912,1024]{1,0:T(8,128)(2,1)}, u32[]{:S(2)}, u32[]{:S(2)}) collective-permute-start(bf16[912,1024]{1,0:T(8,128)(2,1)S(1)} %pad_maximum_fusion.refs_4_.refs_0_), channel_id=1, source_target_pairs={{0,2},{2,0},{1,3},{3,1},{4,6},{6,4},{5,7},{7,5},{8,10},{10,8},{9,1... | collective-permute-start | bytes 5603336 | tf_op jit(solution)/shard_map/ppermute | solution.py:473
  10.7 11.1 %collective-permute-start.5 = (bf16[768,256]{1,0:T(8,128)(2,1)S(1)}, bf16[768,256]{1,0:T(8,128)(2,1)}, u32[]{:S(2)}, u32[]{:S(2)}) collective-permute-start(bf16[768,256]{1,0:T(8,128)(2,1)S(1)} %fusion.8.refs_0_), channel_id=1, source_target_pairs={{0,4},{4,0},{8,12},{12,8},{1,5},{5,1},{9,13},{13,9},{2,6},{6,2},{1... | collective-permute-start | bytes 1179656 | tf_op jit(solution)/shard_map/ppermute | solution.py:39
  12.4 9.4 %collective-permute-start.6 = (bf16[768,256]{1,0:T(8,128)(2,1)S(1)}, bf16[768,256]{1,0:T(8,128)(2,1)S(1)}, u32[]{:S(2)}, u32[]{:S(2)}) collective-permute-start(bf16[768,256]{1,0:T(8,128)(2,1)S(1)} %fusion.8.refs_0_), channel_id=1, source_target_pairs={{4,8},{8,4},{5,9},{9,5},{6,10},{10,6},{7,11},{11,7},{20,24},{24,20... | collective-permute-start | bytes 1179656 | tf_op jit(solution)/shard_map/ppermute | solution.py:425
  13.0 10.8 %collective-permute-start.7 = (bf16[768,256]{1,0:T(8,128)(2,1)S(1)}, bf16[768,256]{1,0:T(8,128)(2,1)S(1)}, u32[]{:S(2)}, u32[]{:S(2)}) collective-permute-start(bf16[768,256]{1,0:T(8,128)(2,1)S(1)} %fusion.8.refs_0_), channel_id=1, source_target_pairs={{0,16},{16,0},{1,17},{17,1},{2,18},{18,2},{3,19},{19,3},{4,20},{20... | collective-permute-start | bytes 1179656 | tf_op jit(solution)/shard_map/ppermute | solution.py:418
  21.8 2.1 %copy-start.1 = (bf16[768,256]{1,0:T(8,128)(2,1)}, bf16[768,256]{1,0:T(8,128)(2,1)S(1)}, u32[]{:S(2)}) copy-start(bf16[768,256]{1,0:T(8,128)(2,1)S(1)} %collective-permute-done.6) | copy-start | bytes 1179652
  23.9 13.7 %collective-permute-start.8 = (bf16[768,256]{1,0:T(8,128)(2,1)S(1)}, bf16[768,256]{1,0:T(8,128)(2,1)}, u32[]{:S(2)}, u32[]{:S(2)}) collective-permute-start(bf16[768,256]{1,0:T(8,128)(2,1)S(1)} %fusion.8.refs_0_), channel_id=1, source_target_pairs={{0,12},{12,0},{1,13},{13,1},{2,14},{14,2},{3,15},{15,3},{16,28},{2... | collective-permute-start | bytes 1179656 | tf_op jit(solution)/shard_map/ppermute | solution.py:428
  28.2 10.2 %collective-permute-start.9 = (bf16[768,256]{1,0:T(8,128)(2,1)}, bf16[768,256]{1,0:T(8,128)(2,1)}, u32[]{:S(2)}, u32[]{:S(2)}) collective-permute-start(bf16[768,256]{1,0:T(8,128)(2,1)} %collective-permute-done.5.refs_1_), channel_id=1, source_target_pairs={{0,16},{16,0},{1,17},{17,1},{2,18},{18,2},{3,19},{19,3},{4,20},{20... | collective-permute-start | bytes 1179656 | tf_op jit(solution)/shard_map/ppermute | solution.py:418
  39.5 9.0 %collective-permute-start.10 = (bf16[768,256]{1,0:T(8,128)(2,1)S(1)}, bf16[768,256]{1,0:T(8,128)(2,1)S(1)}, u32[]{:S(2)}, u32[]{:S(2)}) collective-permute-start(bf16[768,256]{1,0:T(8,128)(2,1)S(1)} %broadcast_select_fusion.1.refs_3_), channel_id=1, source_target_pairs={{0,4},{4,0},{8,12},{12,8},{1,5},{5,1},{9,13},{13,9},{2,6},{6,2},{1... | collective-permute-start | bytes 1179656 | tf_op jit(solution)/shard_map/ppermute | solution.py:39
  40.4 8.4 %collective-permute-start.11 = (bf16[768,256]{1,0:T(8,128)(2,1)S(1)}, bf16[768,256]{1,0:T(8,128)(2,1)S(1)}, u32[]{:S(2)}, u32[]{:S(2)}) collective-permute-start(bf16[768,256]{1,0:T(8,128)(2,1)S(1)} %broadcast_select_fusion.1.refs_3_), channel_id=1, source_target_pairs={{0,16},{16,0},{1,17},{17,1},{2,18},{18,2},{3,19},{19,3},{4,20},{20... | collective-permute-start | bytes 1179656 | tf_op jit(solution)/shard_map/ppermute | solution.py:418
  41.9 12.4 %collective-permute-start = (bf16[912,1024]{1,0:T(8,128)(2,1)S(1)}, bf16[912,1024]{1,0:T(8,128)(2,1)S(1)}, u32[]{:S(2)}, u32[]{:S(2)}) collective-permute-start(bf16[912,1024]{1,0:T(8,128)(2,1)S(1)} %pad_maximum_fusion.refs_4_.refs_0_), channel_id=1, source_target_pairs={{0,1},{1,0},{2,3},{3,2},{4,5},{5,4},{6,7},{7,6},{8,9},{9,8},{10,11... | collective-permute-start | bytes 5603336 | tf_op jit(solution)/shard_map/ppermute | solution.py:474
  51.0 4.0 %collective-permute-start.12 = (bf16[912,1024]{1,0:T(8,128)(2,1)}, bf16[912,1024]{1,0:T(8,128)(2,1)S(1)}, u32[]{:S(2)}, u32[]{:S(2)}) collective-permute-start(bf16[912,1024]{1,0:T(8,128)(2,1)} %collective-permute-done.2.refs_6_.refs_2_), channel_id=1, source_target_pairs={{0,1},{1,0},{2,3},{3,2},{4,5},{5,4},{6,7},{7,6},{8,9},{9,8},{10,11... | collective-permute-start | bytes 5603336 | tf_op jit(solution)/shard_map/ppermute | solution.py:474
  51.0 11.5 %collective-permute-start.13 = (bf16[768,256]{1,0:T(8,128)(2,1)S(1)}, bf16[768,256]{1,0:T(8,128)(2,1)S(1)}, u32[]{:S(2)}, u32[]{:S(2)}) collective-permute-start(bf16[768,256]{1,0:T(8,128)(2,1)S(1)} %collective-permute-done.10.refs_2_), channel_id=1, source_target_pairs={{0,16},{16,0},{1,17},{17,1},{2,18},{18,2},{3,19},{19,3},{4,20},{20... | collective-permute-start | bytes 1179656 | tf_op jit(solution)/shard_map/ppermute | solution.py:418
  52.7 14.8 %collective-permute-start.14 = (bf16[128,2048]{1,0:T(8,128)(2,1)S(1)}, bf16[128,2048]{1,0:T(8,128)(2,1)S(1)}, u32[]{:S(2)}, u32[]{:S(2)}) collective-permute-start(bf16[128,2048]{1,0:T(8,128)(2,1)S(1)} %slice_select_fusion.1.refs_8_), channel_id=1, source_target_pairs={{0,2},{2,0},{1,3},{3,1},{4,6},{6,4},{5,7},{7,5},{8,10},{10,8},{9,1... | collective-permute-start | bytes 1572872 | tf_op jit(solution)/shard_map/ppermute | solution.py:473
  54.3 13.9 %collective-permute-start.15 = (bf16[128,2048]{1,0:T(8,128)(2,1)S(1)}, bf16[128,2048]{1,0:T(8,128)(2,1)S(1)}, u32[]{:S(2)}, u32[]{:S(2)}) collective-permute-start(bf16[128,2048]{1,0:T(8,128)(2,1)S(1)} %slice_select_fusion.1.refs_8_), channel_id=1, source_target_pairs={{0,1},{1,0},{2,3},{3,2},{4,5},{5,4},{6,7},{7,6},{8,9},{9,8},{10,11... | collective-permute-start | bytes 1572872 | tf_op jit(solution)/shard_map/ppermute | solution.py:474
  67.5 2.0 %collective-permute-start.16 = (bf16[128,2048]{1,0:T(8,128)(2,1)S(1)}, bf16[128,2048]{1,0:T(8,128)(2,1)S(1)}, u32[]{:S(2)}, u32[]{:S(2)}) collective-permute-start(bf16[128,2048]{1,0:T(8,128)(2,1)S(1)} %collective-permute-done.14.refs_10_), channel_id=1, source_target_pairs={{0,1},{1,0},{2,3},{3,2},{4,5},{5,4},{6,7},{7,6},{8,9},{9,8},{10,11... | collective-permute-start | bytes 1572872 | tf_op jit(solution)/shard_map/ppermute | solution.py:474
  67.6 1.9 %collective-permute-start.18 = (f32[8,256]{1,0:T(8,128)S(1)}, f32[8,256]{1,0:T(8,128)S(1)}, u32[]{:S(2)}, u32[]{:S(2)}) collective-permute-start(f32[8,256]{1,0:T(8,128)S(1)} %get-tuple-element.78.refs_13_), channel_id=1, source_target_pairs={{0,1},{1,0},{2,3},{3,2},{4,5},{5,4},{6,7},{7,6},{8,9},{9,8},{10,11... | collective-permute-start | bytes 24584 | tf_op jit(solution)/shard_map/ppermute | solution.py:482
  68.1 1.4 %collective-permute-start.17 = (f32[8,256]{1,0:T(8,128)S(1)}, f32[8,256]{1,0:T(8,128)S(1)}, u32[]{:S(2)}, u32[]{:S(2)}) collective-permute-start(f32[8,256]{1,0:T(8,128)S(1)} %get-tuple-element.77.refs_12_), channel_id=1, source_target_pairs={{0,1},{1,0},{2,3},{3,2},{4,5},{5,4},{6,7},{7,6},{8,9},{9,8},{10,11... | collective-permute-start | bytes 24584 | tf_op jit(solution)/shard_map/ppermute | solution.py:482
  73.3 9.6 %collective-permute-start.19 = (bf16[136,1024]{1,0:T(8,128)(2,1)S(1)}, bf16[136,1024]{1,0:T(8,128)(2,1)S(1)}, u32[]{:S(2)}, u32[]{:S(2)}) collective-permute-start(bf16[136,1024]{1,0:T(8,128)(2,1)S(1)} %get-tuple-element.83), channel_id=1, source_target_pairs={{0,4},{4,0},{8,12},{12,8},{1,5},{5,1},{9,13},{13,9},{2,6},{6,2},{1... | collective-permute-start | bytes 835592 | tf_op jit(solution)/shard_map/ppermute | solution.py:39
  75.2 11.7 %collective-permute-start.23 = (bf16[1024,256]{1,0:T(8,128)(2,1)S(1)}, bf16[1024,256]{1,0:T(8,128)(2,1)S(1)}, u32[]{:S(2)}, u32[]{:S(2)}) collective-permute-start(bf16[1024,256]{1,0:T(8,128)(2,1)S(1)} %get-tuple-element.86.refs_3_), channel_id=1, source_target_pairs={{0,1},{1,0},{2,3},{3,2},{4,5},{5,4},{6,7},{7,6},{8,9},{9,8},{10,11... | collective-permute-start | bytes 1572872 | tf_op jit(solution)/shard_map/ppermute | solution.py:483
  75.2 11.7 %collective-permute-start.22 = (bf16[1024,256]{1,0:T(8,128)(2,1)S(1)}, bf16[1024,256]{1,0:T(8,128)(2,1)S(1)}, u32[]{:S(2)}, u32[]{:S(2)}) collective-permute-start(bf16[1024,256]{1,0:T(8,128)(2,1)S(1)} %get-tuple-element.85.refs_2_), channel_id=1, source_target_pairs={{0,1},{1,0},{2,3},{3,2},{4,5},{5,4},{6,7},{7,6},{8,9},{9,8},{10,11... | collective-permute-start | bytes 1572872 | tf_op jit(solution)/shard_map/ppermute | solution.py:483
  78.5 9.7 %collective-permute-start.21 = (bf16[136,1024]{1,0:T(8,128)(2,1)S(1)}, bf16[136,1024]{1,0:T(8,128)(2,1)S(1)}, u32[]{:S(2)}, u32[]{:S(2)}) collective-permute-start(bf16[136,1024]{1,0:T(8,128)(2,1)S(1)} %get-tuple-element.84), channel_id=1, source_target_pairs={{0,4},{4,0},{8,12},{12,8},{1,5},{5,1},{9,13},{13,9},{2,6},{6,2},{1... | collective-permute-start | bytes 835592 | tf_op jit(solution)/shard_map/ppermute | solution.py:39
  82.9 13.4 %collective-permute-start.20 = (bf16[136,1024]{1,0:T(8,128)(2,1)S(1)}, bf16[136,1024]{1,0:T(8,128)(2,1)S(1)}, u32[]{:S(2)}, u32[]{:S(2)}) collective-permute-start(bf16[136,1024]{1,0:T(8,128)(2,1)S(1)} %shard_map.59), channel_id=1, source_target_pairs={{0,12},{4,8},{8,4},{12,0},{1,13},{5,9},{9,5},{13,1},{2,14},{6,10},... | collective-permute-start | bytes 835592 | tf_op jit(solution)/shard_map/ppermute | solution.py:39
  98.3 4.5 %collective-permute-start.24 = (bf16[128,256]{1,0:T(8,128)(2,1)S(1)}, bf16[128,256]{1,0:T(8,128)(2,1)S(1)}, u32[]{:S(2)}, u32[]{:S(2)}) collective-permute-start(bf16[128,256]{1,0:T(8,128)(2,1)S(1)} %get-tuple-element.88), channel_id=1, source_target_pairs={{0,4},{4,0},{8,12},{12,8},{1,5},{5,1},{9,13},{13,9},{2,6},{6,2},{1... | collective-permute-start | bytes 196616 | tf_op jit(solution)/shard_map/ppermute | solution.py:39
  99.8 5.9 %collective-permute-start.25 = (bf16[128,256]{1,0:T(8,128)(2,1)S(1)}, bf16[128,256]{1,0:T(8,128)(2,1)S(1)}, u32[]{:S(2)}, u32[]{:S(2)}) collective-permute-start(bf16[128,256]{1,0:T(8,128)(2,1)S(1)} %get-tuple-element.89), channel_id=1, source_target_pairs={{0,8},{4,12},{8,0},{12,4},{1,9},{5,13},{9,1},{13,5},{2,10},{6,14},... | collective-permute-start | bytes 196616 | tf_op jit(solution)/shard_map/ppermute | solution.py:39
  101.0 6.2 %collective-permute-start.26 = (bf16[128,256]{1,0:T(8,128)(2,1)S(1)}, bf16[128,256]{1,0:T(8,128)(2,1)S(1)}, u32[]{:S(2)}, u32[]{:S(2)}) collective-permute-start(bf16[128,256]{1,0:T(8,128)(2,1)S(1)} %get-tuple-element.90), channel_id=1, source_target_pairs={{0,12},{4,8},{8,4},{12,0},{1,13},{5,9},{9,5},{13,1},{2,14},{6,10},... | collective-permute-start | bytes 196616 | tf_op jit(solution)/shard_map/ppermute | solution.py:39
  109.0 2.0 %collective-permute-start.27 = (bf16[128,2048]{1,0:T(8,128)(2,1)S(1)}, bf16[128,2048]{1,0:T(8,128)(2,1)S(1)}, u32[]{:S(2)}, u32[]{:S(2)}) collective-permute-start(bf16[128,2048]{1,0:T(8,128)(2,1)S(1)} %convert_element_type.24), channel_id=1, source_target_pairs={{0,1},{1,0},{2,3},{3,2},{4,5},{5,4},{6,7},{7,6},{8,9},{9,8},{10,11... | collective-permute-start | bytes 1572872 | tf_op jit(solution)/shard_map/ppermute | solution.py:496
  111.2 8.4 %collective-permute-start.28 = (bf16[64,2048]{1,0:T(8,128)(2,1)S(1)}, bf16[64,2048]{1,0:T(8,128)(2,1)S(1)}, u32[]{:S(2)}, u32[]{:S(2)}) collective-permute-start(bf16[64,2048]{1,0:T(8,128)(2,1)S(1)} %fusion), channel_id=1, source_target_pairs={{0,2},{2,0},{1,3},{3,1},{4,6},{6,4},{5,7},{7,5},{8,10},{10,8},{9,1... | collective-permute-start | bytes 786440 | tf_op jit(solution)/shard_map/ppermute | solution.py:497

commit v8 on v7

--- a/solution.py
+++ b/solution.py
@@ -40,13 +40,13 @@
 
 
 def split(rows):
-    return rows * 2 // 3, rows - rows * 2 // 3
+    return rows * 5 // 8, rows - rows * 5 // 8
 
 
 def turn_kernel(levels, level_g, level_a, rows, where, *refs):
-    slots, pieces = refs[:levels], refs[levels : levels + 4]
-    basis_a, out_g, basis_g, sums, sems = refs[levels + 4 :]
-    half, width = split(rows)[0], basis_a.shape[0]
+    slots, pieces, later = refs[:levels], refs[levels : levels + 4], refs[levels + 4 : levels + 6]
+    basis_a, out_g, basis_g, sums, sems = refs[levels + 6 :]
+    (half, late), width = split(rows), basis_a.shape[0]
     part = basis_a.shape[1]
     copies = []
     for i, (first, height, target) in enumerate(((level_g, level_a, basis_a), (0, level_g, basis_g))):
@@ -77,6 +77,10 @@
         ).astype(bf16)
         out_g[pl.ds(i * half, half)] = turned
         total_g = total_g + jnp.sum(jnp.square(turned.astype(f32)), axis=0, keepdims=True)
+    for i, piece in enumerate(later):
+        turned = jnp.dot(piece[...], basis_g[...], preferred_element_type=f32).astype(bf16)
+        out_g[pl.ds(4 * half + i * late, late)] = turned
+        total_g = total_g + jnp.sum(jnp.square(turned.astype(f32)), axis=0, keepdims=True)
     marks = sum(piece[rows : rows + 16, :part].astype(f32) for piece in pieces)
     sums[0:1] = total_g
     sums[1:2] = marks[0:1] + marks[1:2]
@@ -84,25 +88,25 @@
     sums[3:8] = jnp.zeros((5, part), f32)
 
 
-def turn(where, slots, pieces, rows, level_g, level_a):
+def turn(where, slots, pieces, later, rows, level_g, level_a):
     levels = len(slots)
     width_a, width_g = levels * level_a, levels * level_g
     part = slots[0].shape[1]
-    half = split(rows)[0]
+    half, late = split(rows)
     return pl.pallas_call(
         functools.partial(turn_kernel, levels, level_g, level_a, rows),
         out_shape=(
             shape((width_a, part), bf16),
-            shape((4 * half, part), bf16),
+            shape((4 * half + 2 * late, part), bf16),
             shape((width_g, part), bf16),
             shape((8, part), f32),
         ),
-        in_specs=[SMEM] + [ANY] * levels + [VMEM] * 4,
+        in_specs=[SMEM] + [ANY] * levels + [VMEM] * 6,
         out_specs=(VMEM,) * 4,
         scratch_shapes=[pltpu.SemaphoreType.DMA((2 * levels,))],
         compiler_params=params(MIDDLE),
         cost_estimate=cost(8 * rows * part * (width_a + width_g // 2), 8 * rows * (width_a + width_g // 2)),
-    )(where, *slots, *pieces)
+    )(where, *slots, *pieces, *later)
 
 
 def high_low(v):
@@ -110,15 +114,10 @@
     return high, (v - high.astype(f32)).astype(bf16)
 
 
-def cross_kernel(levels, rows, where, *refs):
-    acts, early, bases, pieces, sums = refs[:4], refs[4:6], refs[6:8], refs[8:12], refs[12:16]
-    own, own_extra, messages = refs[16], refs[17], refs[18 : 17 + levels]
-    left, right, basis, held, whole, extra, sems = refs[17 + levels :]
+def turn_late(rows, acts, early, bases, pieces, sums, right, left, basis, held, sems, extra):
     half, late = split(rows)
     part = bases[0].shape[1]
     cols = 2 * part
-    chunk = cols // levels
-    level = where[0]
     count = 0
 
     def copy(source, target):
@@ -129,41 +128,54 @@
         return made
 
     first = [copy(b, basis.at[:, pl.ds(i * part, part)]) for i, b in enumerate(bases)]
-    moves = [copy(p, held.at[pl.ds(i * late, late)]) for i, p in enumerate(pieces)]
+    first += [copy(p, held.at[pl.ds(i * late, late)]) for i, p in enumerate(pieces)]
     rest = [copy(a.at[pl.ds(0, rows)], left.at[pl.ds(i * rows, rows)]) for i, a in enumerate(acts)]
     for i in range(2):
+        columns = pl.ds(i * part, part)
         for j in range(4):
-            rest.append(
-                copy(early[i].at[pl.ds(j * half, half)], right.at[pl.ds(j * rows, half), pl.ds(i * part, part)])
-            )
+            rest.append(copy(early[i].at[pl.ds(j * half, half)], right.at[pl.ds(j * rows, half), columns]))
+        for j in range(2):
+            source = early[i].at[pl.ds(4 * half + j * late, late)]
+            rest.append(copy(source, right.at[pl.ds(j * rows + half, late), columns]))
     for made in first:
         made.wait()
+    block = jnp.dot(held[...], basis[...], preferred_element_type=f32).astype(bf16)
+    right[pl.ds(2 * rows + half, late)] = block[:late]
+    right[pl.ds(3 * rows + half, late)] = block[late:]
     total = jnp.concatenate([sums[0][0:1], sums[1][0:1]], axis=1)
-    for i in range(0, 4, 2):
-        moves[i].wait()
-        moves[i + 1].wait()
-        block = jnp.dot(held[pl.ds(i * late, 2 * late)], basis[...], preferred_element_type=f32).astype(bf16)
-        right[pl.ds(i * rows + half, late)] = block[:late]
-        right[pl.ds(i * rows + rows + half, late)] = block[late:]
-        total = total + jnp.sum(jnp.square(block.astype(f32)), axis=0, keepdims=True)
-    for made in rest:
-        made.wait()
     extra[...] = jnp.zeros_like(extra)
-    extra[0:1, :cols] = total
+    extra[0:1, :cols] = total + jnp.sum(jnp.square(block.astype(f32)), axis=0, keepdims=True)
     for i in range(4):
         extra[1:2, pl.ds(i * part, part)] = sums[i][2:3]
         extra[2:3, pl.ds(i * part, part)] = sums[i][1:2]
-    for i in range(2):
-        block = pl.ds(i * part, part)
-        whole[block] = lax.dot_general(
-            right[:, block], left[...], (((0,), (0,)), ((), ())), preferred_element_type=f32
-        )
-    high, low = high_low(extra[...])
-    own_extra[...] = extra[...]
-    own[...] = whole[pl.ds(pl.multiple_of(level * chunk, chunk), chunk)]
+    for made in rest:
+        made.wait()
+
+
+def with_sums(block, sums):
+    high, low = high_low(sums[0:4])
+    return jnp.concatenate([block.astype(bf16), high, low])
+
+
+def cross_kernel(levels, rows, where, *refs):
+    acts, early, bases, pieces, sums = refs[:4], refs[4:6], refs[6:8], refs[8:10], refs[10:14]
+    own, extra, messages = refs[14], refs[15], refs[16 : 15 + levels]
+    right, left, basis, held, whole, sems = refs[15 + levels :]
+    chunk = right.shape[1] // levels
+    turn_late(rows, acts, early, bases, pieces, sums, right, left, basis, held, sems, extra)
+    whole[...] = lax.dot_general(right[...], left[...], (((0,), (0,)), ((), ())), preferred_element_type=f32)
+    own[...] = whole[pl.ds(pl.multiple_of(where[0] * chunk, chunk), chunk)]
     for step in range(1, levels):
-        to = pl.multiple_of((level ^ step) * chunk, chunk)
-        messages[step - 1][...] = jnp.concatenate([whole[pl.ds(to, chunk)].astype(bf16), high[:4], low[:4]])
+        block = whole[pl.ds(pl.multiple_of((where[0] ^ step) * chunk, chunk), chunk)]
+        messages[step - 1][...] = with_sums(block, extra)
+
+
+def scratch(rows, width, width_g, cols):
+    return [
+        pltpu.VMEM((4 * rows, width), bf16),
+        pltpu.VMEM((width_g, cols), bf16),
+        pltpu.VMEM((2 * split(rows)[1], width_g), bf16),
+    ]
 
 
 def cross(where, acts, early, bases, pieces, sums, rows, levels):
@@ -175,75 +187,24 @@
         functools.partial(cross_kernel, levels, rows),
         out_shape=[shape((chunk, width), f32), shape((8, width), f32)]
         + [shape((chunk + 8, width), bf16)] * (levels - 1),
-        in_specs=[SMEM] + [ANY] * 12 + [VMEM] * 4,
+        in_specs=[SMEM] + [ANY] * 10 + [VMEM] * 4,
         out_specs=[VMEM] * (1 + levels),
-        scratch_shapes=[
-            pltpu.VMEM((4 * rows, width), bf16),
-            pltpu.VMEM((4 * rows, cols), bf16),
-            pltpu.VMEM((width_g, cols), bf16),
-            pltpu.VMEM((4 * split(rows)[1], width_g), bf16),
-            pltpu.VMEM((cols, width), f32),
-            pltpu.VMEM((8, width), f32),
-            pltpu.SemaphoreType.DMA((18,)),
-        ],
+        scratch_shapes=[pltpu.VMEM((4 * rows, cols), bf16)]
+        + scratch(rows, width, width_g, cols)
+        + [pltpu.VMEM((cols, width), f32), pltpu.SemaphoreType.DMA((20,))],
         compiler_params=params(LARGE),
-        cost_estimate=cost(4 * rows * cols * (width_g + 2 * width), 16 * rows * width),
+        cost_estimate=cost(8 * rows * cols * width, 16 * rows * width),
     )(where, *acts, *early, *bases, *pieces, *sums)
 
 
 def far_kernel(levels, rows, where, *refs):
-    acts, early, bases, pieces, sums = refs[:4], refs[4:6], refs[6:8], refs[8:12], refs[12:16]
-    message, kept, extra, right, left, basis, held, sems = refs[16:]
-    half, late = split(rows)
-    part = bases[0].shape[1]
-    cols = 2 * part
-    chunk = cols // levels
-    level = where[0]
-    count = 0
-
-    def copy(source, target):
-        nonlocal count
-        made = pltpu.make_async_copy(source, target, sems.at[count])
-        made.start()
-        count += 1
-        return made
-
-    first = [copy(b, basis.at[:, pl.ds(i * part, part)]) for i, b in enumerate(bases)]
-    moves = [copy(p, held.at[pl.ds(i * late, late)]) for i, p in enumerate(pieces)]
-    rest = [copy(a.at[pl.ds(0, rows)], left.at[pl.ds(i * rows, rows)]) for i, a in enumerate(acts)]
-    for i in range(2):
-        for j in range(4):
-            rest.append(
-                copy(early[i].at[pl.ds(j * half, half)], right.at[pl.ds(j * rows, half), pl.ds(i * part, part)])
-            )
-    for made in first:
-        made.wait()
-    total = jnp.concatenate([sums[0][0:1], sums[1][0:1]], axis=1)
-    for i in range(0, 4, 2):
-        moves[i].wait()
-        moves[i + 1].wait()
-        block = jnp.dot(held[pl.ds(i * late, 2 * late)], basis[...], preferred_element_type=f32).astype(bf16)
-        right[pl.ds(i * rows + half, late)] = block[:late]
-        right[pl.ds(i * rows + rows + half, late)] = block[late:]
-        total = total + jnp.sum(jnp.square(block.astype(f32)), axis=0, keepdims=True)
-    for made in rest:
-        made.wait()
-    extra[...] = jnp.zeros_like(extra)
-    extra[0:1, :cols] = total
-    for i in range(4):
-        extra[1:2, pl.ds(i * part, part)] = sums[i][2:3]
-        extra[2:3, pl.ds(i * part, part)] = sums[i][1:2]
-    high, low = high_low(extra[...])
-    side, place = level // 2, level % 2
-    for other, target in ((place, None), (1 - place, kept)):
-        columns = pl.ds(pl.multiple_of(((1 - side) * 2 + other) * chunk, chunk), chunk)
-        block = lax.dot_general(
-            right[:, columns], left[...], (((0,), (0,)), ((), ())), preferred_element_type=f32
-        )
-        if target is None:
-            message[...] = jnp.concatenate([block.astype(bf16), high[:4], low[:4]])
-        else:
-            target[...] = block
+    acts, early, bases, pieces, sums = refs[:4], refs[4:6], refs[6:8], refs[8:10], refs[10:14]
+    message, extra, right, left, basis, held, sems = refs[14:]
+    chunk = right.shape[1] // levels
+    turn_late(rows, acts, early, bases, pieces, sums, right, left, basis, held, sems, extra)
+    columns = pl.ds(pl.multiple_of((where[0] ^ 2) * chunk, chunk), chunk)
+    block = lax.dot_general(right[:, columns], left[...], (((0,), (0,)), ((), ())), preferred_element_type=f32)
+    message[...] = with_sums(block, extra)
 
 
 def far(where, acts, early, bases, pieces, sums, rows, levels):
@@ -253,30 +214,19 @@
     chunk = cols // levels
     return pl.pallas_call(
         functools.partial(far_kernel, levels, rows),
-        out_shape=(
-            shape((chunk + 8, width), bf16),
-            shape((chunk, width), f32),
-            shape((8, width), f32),
-            shape((4 * rows, cols), bf16),
-        ),
-        in_specs=[SMEM] + [ANY] * 12 + [VMEM] * 4,
-        out_specs=(VMEM,) * 4,
-        scratch_shapes=[
-            pltpu.VMEM((4 * rows, width), bf16),
-            pltpu.VMEM((width_g, cols), bf16),
-            pltpu.VMEM((4 * split(rows)[1], width_g), bf16),
-            pltpu.SemaphoreType.DMA((18,)),
-        ],
+        out_shape=(shape((chunk + 8, width), bf16), shape((8, width), f32), shape((4 * rows, cols), bf16)),
+        in_specs=[SMEM] + [ANY] * 10 + [VMEM] * 4,
+        out_specs=(VMEM,) * 3,
+        scratch_shapes=scratch(rows, width, width_g, cols) + [pltpu.SemaphoreType.DMA((20,))],
         compiler_params=params(LARGE),
-        cost_estimate=cost(4 * rows * cols * (width_g + width), 16 * rows * width),
+        cost_estimate=cost(2 * rows * cols * width, 16 * rows * width),
     )(where, *acts, *early, *bases, *pieces, *sums)
 
 
 def near_kernel(levels, rows, where, right, extra, *refs):
-    acts, own, message = refs[:4], refs[4], refs[5]
+    acts, own, message, kept = refs[:4], refs[4], refs[5], refs[6]
     chunk = right.shape[1] // levels
-    high, low = high_low(extra[...])
-    for step, target in enumerate((own, message)):
+    for step, target in ((0, own), (1, message), (3, kept)):
         columns = pl.ds(pl.multiple_of((where[0] ^ step) * chunk, chunk), chunk)
         block = sum(
             lax.dot_general(
@@ -284,10 +234,7 @@
             )
             for i, a in enumerate(acts)
         )
-        if step == 0:
-            target[...] = block
-        else:
-            target[...] = jnp.concatenate([block.astype(bf16), high[:4], low[:4]])
+        target[...] = with_sums(block, extra) if step == 1 else block
 
 
 def near(where, right, extra, acts, rows, levels):
@@ -295,11 +242,11 @@
     chunk = right.shape[1] // levels
     return pl.pallas_call(
         functools.partial(near_kernel, levels, rows),
-        out_shape=(shape((chunk, width), f32), shape((chunk + 8, width), bf16)),
+        out_shape=(shape((chunk, width), f32), shape((chunk + 8, width), bf16), shape((chunk, width), f32)),
         in_specs=[SMEM] + [VMEM] * 6,
-        out_specs=(VMEM, VMEM),
+        out_specs=(VMEM,) * 3,
         compiler_params=params(LARGE),
-        cost_estimate=cost(16 * rows * chunk * width, 16 * rows * width),
+        cost_estimate=cost(24 * rows * chunk * width, 16 * rows * width),
     )(where, right, extra, *acts)
 
 
@@ -469,22 +416,23 @@
     early = jnp.concatenate([jnp.where(keep, acts, 0), marks, early[:, :width_a], early[:, width_a:]])
     early_out, _ = lax.optimization_barrier((early, beyond[0]))
 
-    def four(mine, out, after):
-        far, after = lax.optimization_barrier((lax.ppermute(out, "chip", SWAP), after))
-        return [mine, lax.ppermute(mine, "core", SWAP), far, lax.ppermute(far, "core", SWAP)], after
-
-    early, slots[2] = four(early, early_out, slots[2])
-    first = turn(where, slots, early, rows, level_g, level_a)
-    others[2], first = lax.optimization_barrier((others[2], first))
-    second = turn(where, others, early, rows, level_g, level_a)
-    late, second = four(late, late, second)
+    together = lax.optimization_barrier
+    far_rows, slots[2] = together((lax.ppermute(early_out, "chip", SWAP), slots[2]))
+    early = [early, lax.ppermute(early, "core", SWAP), far_rows, lax.ppermute(far_rows, "core", SWAP)]
+    later = [late, lax.ppermute(late, "core", SWAP)]
+    first = turn(where, slots, early, later, rows, level_g, level_a)
+    others[2], first = together((others[2], first))
+    second = turn(where, others, early, later, rows, level_g, level_a)
+    far_rows, second = together((lax.ppermute(late, "chip", SWAP), second))
+    late = [far_rows, lax.ppermute(far_rows, "core", SWAP)]
     bases_a, turned_g, bases_g, sums = zip(first, second)
     sums += tuple(lax.ppermute(t, "core", SWAP) for t in sums)
     bases_a += tuple(lax.ppermute(t, "core", SWAP) for t in bases_a)
+
     if levels == 4:
-        message, kept, own_extra, right = far(where, early, turned_g, bases_g, late, sums, rows, levels)
+        message, own_extra, right = far(where, early, turned_g, bases_g, late, sums, rows, levels)
         message = across(message, 1, levels)
-        own, beside = near(where, right, own_extra, early, rows, levels)
+        own, beside, kept = near(where, right, own_extra, early, rows, levels)
         got = [across(add(kept, own_extra, message), 3, levels), across(beside, 1, levels)]
     else:
         own, own_extra, *messages = cross(where, early, turned_g, bases_g, late, sums, rows, levels)

time: 121 us -> 120 us (level)
  other arithmetic: 5.33 us -> 4.05 us
    select_n x1, other arithmetic: 1.44 us -> 0.13 us  [body(): early = jnp.where(keep[:half], grads[:half], 0)]
  transfers between devices with their start and end apart: 29 -> 29, of which waited for: 18 -> 20; matrix products, arithmetic and copies ran while one was open for 4% -> 3% of each run, Pallas kernels for 11% -> 12%
where the time goes in v8:
time: 120 us
  waiting for transfers between devices  57.6 us (48%)
  starting transfers between devices  33.3 us (28%)
  Pallas kernels  20.5 us (17%)
  other arithmetic  4.05 us (3%)
  local copies, waits for them, and re-layouts  3.1 us (3%)
    ppermute x8, waiting for transfers between devices, across(): return lax.ppermute(x, 'level', [(i, i ^ step) for i in range(levels)])  29.8 us
    ppermute x8, starting transfers between devices, across(): return lax.ppermute(x, 'level', [(i, i ^ step) for i in range(levels)])  13 us
    pallas_call x2, Pallas kernels, turn(): pl.pallas_call(functools.partial(turn_kernel, levels, level_g, level_a, r...  10.4 us
    ppermute x1, waiting for transfers between devices, body(): lax.ppermute((kept[:rows_a] + sent[:rows_a]).astype(bf16), 'chip', SWAP)  7.84 us
    ppermute x1, waiting for transfers between devices, gather_levels(): lax.ppermute(held, 'level', [(0, 3), (3, 0)])  7.8 us
    ppermute x4, waiting for transfers between devices, over(): return lax.ppermute(slot, 'group', SWAP)  6.13 us
    ppermute x4, starting transfers between devices, over(): return lax.ppermute(slot, 'group', SWAP)  6.06 us
    ppermute x1, starting transfers between devices, gather_levels(): lax.ppermute(held, 'level', [(0, 3), (3, 0)])  4.37 us
  transfers between devices with their start and end apart: 29, of which 20 were waited for; matrix products, arithmetic and copies ran while one was open for 3% of the time, Pallas kernels for 12%

profile of v8, /device:TPU:0, one launch (start us, length us, event | category | flops | bytes accessed | tf_op | source)
XLA Modules:
  0.0 119.6 jit_solution(9648879076254075505)
XLA Ops:
  0.0 0.9 constant_dynamic-slice_fusion.1
  0.9 1.0 constant_dynamic-slice_fusion.3
  2.4 2.6 %collective-permute-start.1 = (bf16[192,256]{1,0:T(8,128)(2,1)S(1)}, bf16[192,256]{1,0:T(8,128)(2,1)S(1)}, u32[]{:S(2)}, u32[]{:S(2)}) collective-permute-start(bf16[192,256]{1,0:T(8,128)(2,1)S(1)} %get-tuple-element.102), channel_id=1, source_target_pairs={{0,2},{2,0},{1,3},{3,1},{4,6},{6,4},{5,7},{7,5},{8,10},{10,8},{9,1... | collective-permute-start | bytes 294920 | tf_op jit(solution)/shard_map/ppermute | solution.py:401
  6.3 0.9 copy-done.1
  7.8 0.9 collective-permute-done.1
  8.7 1.9 %collective-permute-start.2 = (bf16[880,1024]{1,0:T(8,128)(2,1)S(1)}, bf16[880,1024]{1,0:T(8,128)(2,1)}, u32[]{:S(2)}, u32[]{:S(2)}) collective-permute-start(bf16[880,1024]{1,0:T(8,128)(2,1)S(1)} %pad_maximum_fusion.refs_4_.refs_0_), channel_id=1, source_target_pairs={{0,2},{2,0},{1,3},{3,1},{4,6},{6,4},{5,7},{7,5},{8,10},{10,8},{9,1... | collective-permute-start | bytes 5406728 | tf_op jit(solution)/shard_map/ppermute | solution.py:420
  10.8 1.6 %collective-permute-start.5 = (bf16[768,256]{1,0:T(8,128)(2,1)S(1)}, bf16[768,256]{1,0:T(8,128)(2,1)}, u32[]{:S(2)}, u32[]{:S(2)}) collective-permute-start(bf16[768,256]{1,0:T(8,128)(2,1)S(1)} %fusion.8.refs_0_), channel_id=1, source_target_pairs={{0,4},{4,0},{8,12},{12,8},{1,5},{5,1},{9,13},{13,9},{2,6},{6,2},{1... | collective-permute-start | bytes 1179656 | tf_op jit(solution)/shard_map/ppermute | solution.py:39
  12.5 0.7 collective-permute-start.6
  13.2 1.6 %collective-permute-start.7 = (bf16[768,256]{1,0:T(8,128)(2,1)S(1)}, bf16[768,256]{1,0:T(8,128)(2,1)S(1)}, u32[]{:S(2)}, u32[]{:S(2)}) collective-permute-start(bf16[768,256]{1,0:T(8,128)(2,1)S(1)} %fusion.8.refs_0_), channel_id=1, source_target_pairs={{0,16},{16,0},{1,17},{17,1},{2,18},{18,2},{3,19},{19,3},{4,20},{20... | collective-permute-start | bytes 1179656 | tf_op jit(solution)/shard_map/ppermute | solution.py:365
  14.7 1.2 slice_select_fusion.1.refs_8_
  15.9 6.0 %collective-permute-done.5.refs_1_ = bf16[768,256]{1,0:T(8,128)(2,1)} collective-permute-done((bf16[768,256]{1,0:T(8,128)(2,1)S(1)}, bf16[768,256]{1,0:T(8,128)(2,1)}, u32[]{:S(2)}, u32[]{:S(2)}) %collective-permute-start.5) | collective-permute-done | bytes 393248 | tf_op jit(solution)/shard_map/ppermute | solution.py:39
  21.9 2.1 %collective-permute-done.7.refs_0_ = bf16[768,256]{1,0:T(8,128)(2,1)S(1)} collective-permute-done((bf16[768,256]{1,0:T(8,128)(2,1)S(1)}, bf16[768,256]{1,0:T(8,128)(2,1)S(1)}, u32[]{:S(2)}, u32[]{:S(2)}) %collective-permute-start.7) | collective-permute-done | bytes 393248 | tf_op jit(solution)/shard_map/ppermute | solution.py:365
  24.0 4.4 %collective-permute-start.8 = (bf16[768,256]{1,0:T(8,128)(2,1)S(1)}, bf16[768,256]{1,0:T(8,128)(2,1)}, u32[]{:S(2)}, u32[]{:S(2)}) collective-permute-start(bf16[768,256]{1,0:T(8,128)(2,1)S(1)} %fusion.8.refs_0_), channel_id=1, source_target_pairs={{0,12},{12,0},{1,13},{13,1},{2,14},{14,2},{3,15},{15,3},{16,28},{2... | collective-permute-start | bytes 1179656 | tf_op jit(solution)/shard_map/ppermute | solution.py:375
  28.4 1.6 %collective-permute-start.9 = (bf16[768,256]{1,0:T(8,128)(2,1)}, bf16[768,256]{1,0:T(8,128)(2,1)}, u32[]{:S(2)}, u32[]{:S(2)}) collective-permute-start(bf16[768,256]{1,0:T(8,128)(2,1)} %collective-permute-done.5.refs_1_), channel_id=1, source_target_pairs={{0,16},{16,0},{1,17},{17,1},{2,18},{18,2},{3,19},{19,3},{4,20},{20... | collective-permute-start | bytes 1179656 | tf_op jit(solution)/shard_map/ppermute | solution.py:365
  29.9 7.8 %collective-permute-done.8 = bf16[768,256]{1,0:T(8,128)(2,1)} collective-permute-done((bf16[768,256]{1,0:T(8,128)(2,1)S(1)}, bf16[768,256]{1,0:T(8,128)(2,1)}, u32[]{:S(2)}, u32[]{:S(2)}) %collective-permute-start.8) | collective-permute-done | bytes 393248 | tf_op jit(solution)/shard_map/ppermute | solution.py:375
  37.7 0.8 collective-permute-done.9.refs_1_
  38.6 1.0 broadcast_select_fusion.1.refs_3_
  39.6 0.9 collective-permute-start.10
  40.5 1.5 %collective-permute-start.11 = (bf16[768,256]{1,0:T(8,128)(2,1)S(1)}, bf16[768,256]{1,0:T(8,128)(2,1)S(1)}, u32[]{:S(2)}, u32[]{:S(2)}) collective-permute-start(bf16[768,256]{1,0:T(8,128)(2,1)S(1)} %broadcast_select_fusion.1.refs_3_), channel_id=1, source_target_pairs={{0,16},{16,0},{1,17},{17,1},{2,18},{18,2},{3,19},{19,3},{4,20},{20... | collective-permute-start | bytes 1179656 | tf_op jit(solution)/shard_map/ppermute | solution.py:365
  42.0 6.5 %collective-permute-done.10.refs_2_ = bf16[768,256]{1,0:T(8,128)(2,1)S(1)} collective-permute-done((bf16[768,256]{1,0:T(8,128)(2,1)S(1)}, bf16[768,256]{1,0:T(8,128)(2,1)S(1)}, u32[]{:S(2)}, u32[]{:S(2)}) %collective-permute-start.10) | collective-permute-done | bytes 393248 | tf_op jit(solution)/shard_map/ppermute | solution.py:39
  49.0 0.7 collective-permute-done.2.refs_6_.refs_2_
  50.2 1.6 %collective-permute-start.15 = (bf16[144,2048]{1,0:T(8,128)(2,1)S(1)}, bf16[144,2048]{1,0:T(8,128)(2,1)S(1)}, u32[]{:S(2)}, u32[]{:S(2)}) collective-permute-start(bf16[144,2048]{1,0:T(8,128)(2,1)S(1)} %slice_select_fusion.1.refs_8_), channel_id=1, source_target_pairs={{0,2},{2,0},{1,3},{3,1},{4,6},{6,4},{5,7},{7,5},{8,10},{10,8},{9,1... | collective-permute-start | bytes 1769480 | tf_op jit(solution)/shard_map/ppermute | solution.py:426
  51.8 1.5 %collective-permute-start.13 = (bf16[768,256]{1,0:T(8,128)(2,1)S(1)}, bf16[768,256]{1,0:T(8,128)(2,1)S(1)}, u32[]{:S(2)}, u32[]{:S(2)}) collective-permute-start(bf16[768,256]{1,0:T(8,128)(2,1)S(1)} %collective-permute-done.10.refs_2_), channel_id=1, source_target_pairs={{0,16},{16,0},{1,17},{17,1},{2,18},{18,2},{3,19},{19,3},{4,20},{20... | collective-permute-start | bytes 1179656 | tf_op jit(solution)/shard_map/ppermute | solution.py:365
  53.3 0.6 collective-permute-done.14.refs_9_
  53.9 0.6 collective-permute-done.12.refs_7_.refs_3_
  54.5 5.2 %shard_map.55 = (bf16[1024,256]{1,0:T(8,128)(2,1)S(1)}, bf16[1248,256]{1,0:T(8,128)(2,1)S(1)}, bf16[2048,256]{1,0:T(8,128)(2,1)S(1)}, f32[8,256]{1,0:T(8,128)S(1)}) custom-call(s32[2]{0:T(128)S(1)} %pad_add_fusion.where, bf16[768,256]{1,0:T(8,128)(2,1)S(1)} %fusion.8.refs_0_, bf16[768,256]{1,0:T(8,128)(2,1)} %collective-permute-done.5.refs_1_, ...), custom_call_target="tpu_custom_call" | custom-call | flops 1610612736 | bytes 6291456 | tf_op jit(solution)/shard_map/pallas_call | solution.py:96
  59.7 2.8 %collective-permute-done.13.refs_2_ = bf16[768,256]{1,0:T(8,128)(2,1)S(1)} collective-permute-done((bf16[768,256]{1,0:T(8,128)(2,1)S(1)}, bf16[768,256]{1,0:T(8,128)(2,1)S(1)}, u32[]{:S(2)}, u32[]{:S(2)}) %collective-permute-start.13) | collective-permute-done | bytes 393248 | tf_op jit(solution)/shard_map/ppermute | solution.py:365
  62.5 5.2 %shard_map.56 = (bf16[1024,256]{1,0:T(8,128)(2,1)S(1)}, bf16[1248,256]{1,0:T(8,128)(2,1)S(1)}, bf16[2048,256]{1,0:T(8,128)(2,1)S(1)}, f32[8,256]{1,0:T(8,128)S(1)}) custom-call(s32[2]{0:T(128)S(1)} %pad_add_fusion.where, bf16[768,256]{1,0:T(8,128)(2,1)S(1)} %collective-permute-done.7.refs_0_, bf16[768,256]{1,0:T(8,128)(2,1)} %collective-permute-done.9.refs_1_, ...), custom_call_target="tpu_custom_call" | custom-call | flops 1610612736 | bytes 6291456 | tf_op jit(solution)/shard_map/pallas_call | solution.py:96
  68.4 1.4 %collective-permute-done.18.refs_13_ = f32[8,256]{1,0:T(8,128)S(1)} collective-permute-done((f32[8,256]{1,0:T(8,128)S(1)}, f32[8,256]{1,0:T(8,128)S(1)}, u32[]{:S(2)}, u32[]{:S(2)}) %collective-permute-start.18) | collective-permute-done | bytes 8224 | tf_op jit(solution)/shard_map/ppermute | solution.py:429
  69.8 3.0 %shard_map.57 = (bf16[136,1024]{1,0:T(8,128)(2,1)S(1)}, f32[8,1024]{1,0:T(8,128)S(1)}, bf16[1536,512]{1,0:T(8,128)(2,1)S(1)}) custom-call(s32[2]{0:T(128)S(1)} %pad_add_fusion.where, bf16[880,1024]{1,0:T(8,128)(2,1)S(1)} %pad_maximum_fusion.refs_4_.refs_0_, bf16[880,1024]{1,0:T(8,128)(2,1)S(1)} %collective-permute-done.refs_5_.refs_1_, ...), custom_call_target="tpu_custom_call" | custom-call | flops 402653184 | bytes 6291456 | tf_op jit(solution)/shard_map/pallas_call | solution.py:215
  72.9 1.6 %collective-permute-start.19 = (bf16[136,1024]{1,0:T(8,128)(2,1)S(1)}, bf16[136,1024]{1,0:T(8,128)(2,1)S(1)}, u32[]{:S(2)}, u32[]{:S(2)}) collective-permute-start(bf16[136,1024]{1,0:T(8,128)(2,1)S(1)} %get-tuple-element.83), channel_id=1, source_target_pairs={{0,4},{4,0},{8,12},{12,8},{1,5},{5,1},{9,13},{13,9},{2,6},{6,2},{1... | collective-permute-start | bytes 835592 | tf_op jit(solution)/shard_map/ppermute | solution.py:39
  75.0 3.3 %shard_map.58 = (f32[128,1024]{1,0:T(8,128)S(1)}, bf16[136,1024]{1,0:T(8,128)(2,1)S(1)}, f32[128,1024]{1,0:T(8,128)S(1)}) custom-call(s32[2]{0:T(128)S(1)} %pad_add_fusion.where, bf16[1536,512]{1,0:T(8,128)(2,1)S(1)} %get-tuple-element.79.right, f32[8,1024]{1,0:T(8,128)S(1)} %get-tuple-element.80.extra.own_extra, ...), custom_call_target="tpu_custom_call" | custom-call | flops 1207959552 | bytes 6291456 | tf_op jit(solution)/shard_map/pallas_call | solution.py:243
  78.3 0.5 collective-permute-start.21
  78.8 3.3 %collective-permute-done.19.got = bf16[136,1024]{1,0:T(8,128)(2,1)S(1)} collective-permute-done((bf16[136,1024]{1,0:T(8,128)(2,1)S(1)}, bf16[136,1024]{1,0:T(8,128)(2,1)S(1)}, u32[]{:S(2)}, u32[]{:S(2)}) %collective-permute-start.19) | collective-permute-done | bytes 278560 | tf_op jit(solution)/shard_map/ppermute | solution.py:39
  82.2 3.9 %collective-permute-start.20 = (bf16[136,1024]{1,0:T(8,128)(2,1)S(1)}, bf16[136,1024]{1,0:T(8,128)(2,1)S(1)}, u32[]{:S(2)}, u32[]{:S(2)}) collective-permute-start(bf16[136,1024]{1,0:T(8,128)(2,1)S(1)} %shard_map.59), channel_id=1, source_target_pairs={{0,12},{4,8},{8,4},{12,0},{1,13},{5,9},{9,5},{13,1},{2,14},{6,10},... | collective-permute-start | bytes 835592 | tf_op jit(solution)/shard_map/ppermute | solution.py:39
  86.1 1.4 %collective-permute-done.21.refs_1_ = bf16[136,1024]{1,0:T(8,128)(2,1)S(1)} collective-permute-done((bf16[136,1024]{1,0:T(8,128)(2,1)S(1)}, bf16[136,1024]{1,0:T(8,128)(2,1)S(1)}, u32[]{:S(2)}, u32[]{:S(2)}) %collective-permute-start.21) | collective-permute-done | bytes 278560 | tf_op jit(solution)/shard_map/ppermute | solution.py:39
  87.6 8.1 %collective-permute-done.20.refs_0_ = bf16[136,1024]{1,0:T(8,128)(2,1)S(1)} collective-permute-done((bf16[136,1024]{1,0:T(8,128)(2,1)S(1)}, bf16[136,1024]{1,0:T(8,128)(2,1)S(1)}, u32[]{:S(2)}, u32[]{:S(2)}) %collective-permute-start.20) | collective-permute-done | bytes 278560 | tf_op jit(solution)/shard_map/ppermute | solution.py:39
  95.7 1.9 %shard_map.60 = (bf16[128,256]{1,0:T(8,128)(2,1)S(1)}, bf16[128,256]{1,0:T(8,128)(2,1)S(1)}, bf16[128,256]{1,0:T(8,128)(2,1)S(1)}, bf16[128,256]{1,0:T(8,128)(2,1)S(1)}) custom-call(s32[2]{0:T(128)S(1)} %pad_add_fusion.where, f32[128,1024]{1,0:T(8,128)S(1)} %get-tuple-element.81.own, f32[8,1024]{1,0:T(8,128)S(1)} %get-tuple-element.80.extra.own_extra, ...), custom_call_target="tpu_custom_call" | custom-call | flops 805306368 | bytes 2097152 | tf_op jit(solution)/shard_map/pallas_call | solution.py:305
  97.6 1.5 %collective-permute-start.24 = (bf16[128,256]{1,0:T(8,128)(2,1)S(1)}, bf16[128,256]{1,0:T(8,128)(2,1)S(1)}, u32[]{:S(2)}, u32[]{:S(2)}) collective-permute-start(bf16[128,256]{1,0:T(8,128)(2,1)S(1)} %get-tuple-element.88), channel_id=1, source_target_pairs={{0,4},{4,0},{8,12},{12,8},{1,5},{5,1},{9,13},{13,9},{2,6},{6,2},{1... | collective-permute-start | bytes 196616 | tf_op jit(solution)/shard_map/ppermute | solution.py:39
  99.1 1.1 collective-permute-start.25
  100.2 1.8 %collective-permute-start.26 = (bf16[128,256]{1,0:T(8,128)(2,1)S(1)}, bf16[128,256]{1,0:T(8,128)(2,1)S(1)}, u32[]{:S(2)}, u32[]{:S(2)}) collective-permute-start(bf16[128,256]{1,0:T(8,128)(2,1)S(1)} %get-tuple-element.90), channel_id=1, source_target_pairs={{0,12},{4,8},{8,4},{12,0},{1,13},{5,9},{9,5},{13,1},{2,14},{6,10},... | collective-permute-start | bytes 196616 | tf_op jit(solution)/shard_map/ppermute | solution.py:39
  102.2 2.9 %collective-permute-done.25.refs_2_ = bf16[128,256]{1,0:T(8,128)(2,1)S(1)} collective-permute-done((bf16[128,256]{1,0:T(8,128)(2,1)S(1)}, bf16[128,256]{1,0:T(8,128)(2,1)S(1)}, u32[]{:S(2)}, u32[]{:S(2)}) %collective-permute-start.25) | collective-permute-done | bytes 65568 | tf_op jit(solution)/shard_map/ppermute | solution.py:39
  105.0 1.4 %collective-permute-done.26.refs_3_ = bf16[128,256]{1,0:T(8,128)(2,1)S(1)} collective-permute-done((bf16[128,256]{1,0:T(8,128)(2,1)S(1)}, bf16[128,256]{1,0:T(8,128)(2,1)S(1)}, u32[]{:S(2)}, u32[]{:S(2)}) %collective-permute-start.26) | collective-permute-done | bytes 65568 | tf_op jit(solution)/shard_map/ppermute | solution.py:39
  106.4 1.8 %shard_map.61 = (f32[128,2048]{1,0:T(8,128)S(1)}, f32[128,2048]{1,0:T(8,128)S(1)}) custom-call(s32[2]{0:T(128)S(1)} %pad_add_fusion.where, bf16[128,256]{1,0:T(8,128)(2,1)S(1)} %get-tuple-element.87.refs_0_, bf16[128,256]{1,0:T(8,128)(2,1)S(1)} %collective-permute-done.24.refs_1_, bf16[128,256]{1,0:T(8,128)(2,1)S(1)} %collective-permute-done.25.refs_2_, ...), custom_call_target="tpu_custom_call" | custom-call | flops 536870912 | bytes 2097152 | tf_op jit(solution)/shard_map/pallas_call | solution.py:348
  108.4 1.9 %collective-permute-done.27 = bf16[128,2048]{1,0:T(8,128)(2,1)S(1)} collective-permute-done((bf16[128,2048]{1,0:T(8,128)(2,1)S(1)}, bf16[128,2048]{1,0:T(8,128)(2,1)S(1)}, u32[]{:S(2)}, u32[]{:S(2)}) %collective-permute-start.27) | collective-permute-done | bytes 524320 | tf_op jit(solution)/shard_map/ppermute | solution.py:444
  110.4 0.6 collective-permute-start.28
  111.0 7.8 %collective-permute-done.28 = bf16[64,2048]{1,0:T(8,128)(2,1)S(1)} collective-permute-done((bf16[64,2048]{1,0:T(8,128)(2,1)S(1)}, bf16[64,2048]{1,0:T(8,128)(2,1)S(1)}, u32[]{:S(2)}, u32[]{:S(2)}) %collective-permute-start.28) | collective-permute-done | bytes 262176 | tf_op jit(solution)/shard_map/ppermute | solution.py:445
  118.8 0.8 fusion.2
  (53 shorter events, 4.4 us)
Async XLA Ops:
  0.0 5.9 %copy-start = (bf16[384,2048]{1,0:T(8,128)(2,1)S(1)}, bf16[384,2048]{1,0:T(8,128)(2,1)}, u32[]{:S(2)}) copy-start(bf16[384,2048]{1,0:T(8,128)(2,1)} %param.6) | copy-start | bytes 4718596
  1.9 8.7 %collective-permute-start.3 = (bf16[192,256]{1,0:T(8,128)(2,1)S(1)}, bf16[192,256]{1,0:T(8,128)(2,1)S(1)}, u32[]{:S(2)}, u32[]{:S(2)}) collective-permute-start(bf16[192,256]{1,0:T(8,128)(2,1)S(1)} %get-tuple-element.103), channel_id=1, source_target_pairs={{0,1},{1,0},{2,3},{3,2},{4,5},{5,4},{6,7},{7,6},{8,9},{9,8},{10,11... | collective-permute-start | bytes 294920 | tf_op jit(solution)/shard_map/ppermute | solution.py:402
  2.4 6.2 %collective-permute-start.1 = (bf16[192,256]{1,0:T(8,128)(2,1)S(1)}, bf16[192,256]{1,0:T(8,128)(2,1)S(1)}, u32[]{:S(2)}, u32[]{:S(2)}) collective-permute-start(bf16[192,256]{1,0:T(8,128)(2,1)S(1)} %get-tuple-element.102), channel_id=1, source_target_pairs={{0,2},{2,0},{1,3},{3,1},{4,6},{6,4},{5,7},{7,5},{8,10},{10,8},{9,1... | collective-permute-start | bytes 294920 | tf_op jit(solution)/shard_map/ppermute | solution.py:401
  5.0 5.6 %collective-permute-start.4 = (bf16[192,256]{1,0:T(8,128)(2,1)S(1)}, bf16[192,256]{1,0:T(8,128)(2,1)S(1)}, u32[]{:S(2)}, u32[]{:S(2)}) collective-permute-start(bf16[192,256]{1,0:T(8,128)(2,1)S(1)} %get-tuple-element.104), channel_id=1, source_target_pairs={{0,3},{1,2},{2,1},{3,0},{4,7},{5,6},{6,5},{7,4},{8,11},{9,10},{10,... | collective-permute-start | bytes 294920 | tf_op jit(solution)/shard_map/ppermute | solution.py:399
  6.1 1.1 copy-start.1
  8.7 41.0 %collective-permute-start.2 = (bf16[880,1024]{1,0:T(8,128)(2,1)S(1)}, bf16[880,1024]{1,0:T(8,128)(2,1)}, u32[]{:S(2)}, u32[]{:S(2)}) collective-permute-start(bf16[880,1024]{1,0:T(8,128)(2,1)S(1)} %pad_maximum_fusion.refs_4_.refs_0_), channel_id=1, source_target_pairs={{0,2},{2,0},{1,3},{3,1},{4,6},{6,4},{5,7},{7,5},{8,10},{10,8},{9,1... | collective-permute-start | bytes 5406728 | tf_op jit(solution)/shard_map/ppermute | solution.py:420
  10.8 11.1 %collective-permute-start.5 = (bf16[768,256]{1,0:T(8,128)(2,1)S(1)}, bf16[768,256]{1,0:T(8,128)(2,1)}, u32[]{:S(2)}, u32[]{:S(2)}) collective-permute-start(bf16[768,256]{1,0:T(8,128)(2,1)S(1)} %fusion.8.refs_0_), channel_id=1, source_target_pairs={{0,4},{4,0},{8,12},{12,8},{1,5},{5,1},{9,13},{13,9},{2,6},{6,2},{1... | collective-permute-start | bytes 1179656 | tf_op jit(solution)/shard_map/ppermute | solution.py:39
  12.5 9.4 %collective-permute-start.6 = (bf16[768,256]{1,0:T(8,128)(2,1)S(1)}, bf16[768,256]{1,0:T(8,128)(2,1)S(1)}, u32[]{:S(2)}, u32[]{:S(2)}) collective-permute-start(bf16[768,256]{1,0:T(8,128)(2,1)S(1)} %fusion.8.refs_0_), channel_id=1, source_target_pairs={{4,8},{8,4},{5,9},{9,5},{6,10},{10,6},{7,11},{11,7},{20,24},{24,20... | collective-permute-start | bytes 1179656 | tf_op jit(solution)/shard_map/ppermute | solution.py:372
  13.2 10.8 %collective-permute-start.7 = (bf16[768,256]{1,0:T(8,128)(2,1)S(1)}, bf16[768,256]{1,0:T(8,128)(2,1)S(1)}, u32[]{:S(2)}, u32[]{:S(2)}) collective-permute-start(bf16[768,256]{1,0:T(8,128)(2,1)S(1)} %fusion.8.refs_0_), channel_id=1, source_target_pairs={{0,16},{16,0},{1,17},{17,1},{2,18},{18,2},{3,19},{19,3},{4,20},{20... | collective-permute-start | bytes 1179656 | tf_op jit(solution)/shard_map/ppermute | solution.py:365
  21.9 2.1 %copy-start.2 = (bf16[768,256]{1,0:T(8,128)(2,1)}, bf16[768,256]{1,0:T(8,128)(2,1)S(1)}, u32[]{:S(2)}) copy-start(bf16[768,256]{1,0:T(8,128)(2,1)S(1)} %collective-permute-done.6) | copy-start | bytes 1179652
  24.0 13.7 %collective-permute-start.8 = (bf16[768,256]{1,0:T(8,128)(2,1)S(1)}, bf16[768,256]{1,0:T(8,128)(2,1)}, u32[]{:S(2)}, u32[]{:S(2)}) collective-permute-start(bf16[768,256]{1,0:T(8,128)(2,1)S(1)} %fusion.8.refs_0_), channel_id=1, source_target_pairs={{0,12},{12,0},{1,13},{13,1},{2,14},{14,2},{3,15},{15,3},{16,28},{2... | collective-permute-start | bytes 1179656 | tf_op jit(solution)/shard_map/ppermute | solution.py:375
  28.4 10.2 %collective-permute-start.9 = (bf16[768,256]{1,0:T(8,128)(2,1)}, bf16[768,256]{1,0:T(8,128)(2,1)}, u32[]{:S(2)}, u32[]{:S(2)}) collective-permute-start(bf16[768,256]{1,0:T(8,128)(2,1)} %collective-permute-done.5.refs_1_), channel_id=1, source_target_pairs={{0,16},{16,0},{1,17},{17,1},{2,18},{18,2},{3,19},{19,3},{4,20},{20... | collective-permute-start | bytes 1179656 | tf_op jit(solution)/shard_map/ppermute | solution.py:365
  39.6 9.0 %collective-permute-start.10 = (bf16[768,256]{1,0:T(8,128)(2,1)S(1)}, bf16[768,256]{1,0:T(8,128)(2,1)S(1)}, u32[]{:S(2)}, u32[]{:S(2)}) collective-permute-start(bf16[768,256]{1,0:T(8,128)(2,1)S(1)} %broadcast_select_fusion.1.refs_3_), channel_id=1, source_target_pairs={{0,4},{4,0},{8,12},{12,8},{1,5},{5,1},{9,13},{13,9},{2,6},{6,2},{1... | collective-permute-start | bytes 1179656 | tf_op jit(solution)/shard_map/ppermute | solution.py:39
  40.5 8.4 %collective-permute-start.11 = (bf16[768,256]{1,0:T(8,128)(2,1)S(1)}, bf16[768,256]{1,0:T(8,128)(2,1)S(1)}, u32[]{:S(2)}, u32[]{:S(2)}) collective-permute-start(bf16[768,256]{1,0:T(8,128)(2,1)S(1)} %broadcast_select_fusion.1.refs_3_), channel_id=1, source_target_pairs={{0,16},{16,0},{1,17},{17,1},{2,18},{18,2},{3,19},{19,3},{4,20},{20... | collective-permute-start | bytes 1179656 | tf_op jit(solution)/shard_map/ppermute | solution.py:365
  42.0 11.9 %collective-permute-start = (bf16[880,1024]{1,0:T(8,128)(2,1)S(1)}, bf16[880,1024]{1,0:T(8,128)(2,1)S(1)}, u32[]{:S(2)}, u32[]{:S(2)}) collective-permute-start(bf16[880,1024]{1,0:T(8,128)(2,1)S(1)} %pad_maximum_fusion.refs_4_.refs_0_), channel_id=1, source_target_pairs={{0,1},{1,0},{2,3},{3,2},{4,5},{5,4},{6,7},{7,6},{8,9},{9,8},{10,11... | collective-permute-start | bytes 5406728 | tf_op jit(solution)/shard_map/ppermute | solution.py:421
  49.7 4.8 %collective-permute-start.12 = (bf16[880,1024]{1,0:T(8,128)(2,1)}, bf16[880,1024]{1,0:T(8,128)(2,1)S(1)}, u32[]{:S(2)}, u32[]{:S(2)}) collective-permute-start(bf16[880,1024]{1,0:T(8,128)(2,1)} %collective-permute-done.2.refs_6_.refs_2_), channel_id=1, source_target_pairs={{0,1},{1,0},{2,3},{3,2},{4,5},{5,4},{6,7},{7,6},{8,9},{9,8},{10,11... | collective-permute-start | bytes 5406728 | tf_op jit(solution)/shard_map/ppermute | solution.py:421
  49.7 4.2 %collective-permute-start.14 = (bf16[144,2048]{1,0:T(8,128)(2,1)S(1)}, bf16[144,2048]{1,0:T(8,128)(2,1)S(1)}, u32[]{:S(2)}, u32[]{:S(2)}) collective-permute-start(bf16[144,2048]{1,0:T(8,128)(2,1)S(1)} %slice_select_fusion.1.refs_8_), channel_id=1, source_target_pairs={{0,1},{1,0},{2,3},{3,2},{4,5},{5,4},{6,7},{7,6},{8,9},{9,8},{10,11... | collective-permute-start | bytes 1769480 | tf_op jit(solution)/shard_map/ppermute | solution.py:422
  50.2 17.5 %collective-permute-start.15 = (bf16[144,2048]{1,0:T(8,128)(2,1)S(1)}, bf16[144,2048]{1,0:T(8,128)(2,1)S(1)}, u32[]{:S(2)}, u32[]{:S(2)}) collective-permute-start(bf16[144,2048]{1,0:T(8,128)(2,1)S(1)} %slice_select_fusion.1.refs_8_), channel_id=1, source_target_pairs={{0,2},{2,0},{1,3},{3,1},{4,6},{6,4},{5,7},{7,5},{8,10},{10,8},{9,1... | collective-permute-start | bytes 1769480 | tf_op jit(solution)/shard_map/ppermute | solution.py:426
  51.8 10.7 %collective-permute-start.13 = (bf16[768,256]{1,0:T(8,128)(2,1)S(1)}, bf16[768,256]{1,0:T(8,128)(2,1)S(1)}, u32[]{:S(2)}, u32[]{:S(2)}) collective-permute-start(bf16[768,256]{1,0:T(8,128)(2,1)S(1)} %collective-permute-done.10.refs_2_), channel_id=1, source_target_pairs={{0,16},{16,0},{1,17},{17,1},{2,18},{18,2},{3,19},{19,3},{4,20},{20... | collective-permute-start | bytes 1179656 | tf_op jit(solution)/shard_map/ppermute | solution.py:365
  67.7 2.1 %collective-permute-start.16 = (bf16[144,2048]{1,0:T(8,128)(2,1)S(1)}, bf16[144,2048]{1,0:T(8,128)(2,1)S(1)}, u32[]{:S(2)}, u32[]{:S(2)}) collective-permute-start(bf16[144,2048]{1,0:T(8,128)(2,1)S(1)} %collective-permute-done.15.refs_8_), channel_id=1, source_target_pairs={{0,1},{1,0},{2,3},{3,2},{4,5},{5,4},{6,7},{7,6},{8,9},{9,8},{10,11... | collective-permute-start | bytes 1769480 | tf_op jit(solution)/shard_map/ppermute | solution.py:427
  67.8 2.0 %collective-permute-start.18 = (f32[8,256]{1,0:T(8,128)S(1)}, f32[8,256]{1,0:T(8,128)S(1)}, u32[]{:S(2)}, u32[]{:S(2)}) collective-permute-start(f32[8,256]{1,0:T(8,128)S(1)} %get-tuple-element.78.refs_11_), channel_id=1, source_target_pairs={{0,1},{1,0},{2,3},{3,2},{4,5},{5,4},{6,7},{7,6},{8,9},{9,8},{10,11... | collective-permute-start | bytes 24584 | tf_op jit(solution)/shard_map/ppermute | solution.py:429
  68.3 1.5 %collective-permute-start.17 = (f32[8,256]{1,0:T(8,128)S(1)}, f32[8,256]{1,0:T(8,128)S(1)}, u32[]{:S(2)}, u32[]{:S(2)}) collective-permute-start(f32[8,256]{1,0:T(8,128)S(1)} %get-tuple-element.77.refs_10_), channel_id=1, source_target_pairs={{0,1},{1,0},{2,3},{3,2},{4,5},{5,4},{6,7},{7,6},{8,9},{9,8},{10,11... | collective-permute-start | bytes 24584 | tf_op jit(solution)/shard_map/ppermute | solution.py:429
  72.9 9.3 %collective-permute-start.19 = (bf16[136,1024]{1,0:T(8,128)(2,1)S(1)}, bf16[136,1024]{1,0:T(8,128)(2,1)S(1)}, u32[]{:S(2)}, u32[]{:S(2)}) collective-permute-start(bf16[136,1024]{1,0:T(8,128)(2,1)S(1)} %get-tuple-element.83), channel_id=1, source_target_pairs={{0,4},{4,0},{8,12},{12,8},{1,5},{5,1},{9,13},{13,9},{2,6},{6,2},{1... | collective-permute-start | bytes 835592 | tf_op jit(solution)/shard_map/ppermute | solution.py:39
  74.5 11.7 %collective-permute-start.23 = (bf16[1024,256]{1,0:T(8,128)(2,1)S(1)}, bf16[1024,256]{1,0:T(8,128)(2,1)S(1)}, u32[]{:S(2)}, u32[]{:S(2)}) collective-permute-start(bf16[1024,256]{1,0:T(8,128)(2,1)S(1)} %get-tuple-element.86.refs_3_), channel_id=1, source_target_pairs={{0,1},{1,0},{2,3},{3,2},{4,5},{5,4},{6,7},{7,6},{8,9},{9,8},{10,11... | collective-permute-start | bytes 1572872 | tf_op jit(solution)/shard_map/ppermute | solution.py:430
  74.5 11.7 %collective-permute-start.22 = (bf16[1024,256]{1,0:T(8,128)(2,1)S(1)}, bf16[1024,256]{1,0:T(8,128)(2,1)S(1)}, u32[]{:S(2)}, u32[]{:S(2)}) collective-permute-start(bf16[1024,256]{1,0:T(8,128)(2,1)S(1)} %get-tuple-element.85.refs_2_), channel_id=1, source_target_pairs={{0,1},{1,0},{2,3},{3,2},{4,5},{5,4},{6,7},{7,6},{8,9},{9,8},{10,11... | collective-permute-start | bytes 1572872 | tf_op jit(solution)/shard_map/ppermute | solution.py:430
  78.3 9.3 %collective-permute-start.21 = (bf16[136,1024]{1,0:T(8,128)(2,1)S(1)}, bf16[136,1024]{1,0:T(8,128)(2,1)S(1)}, u32[]{:S(2)}, u32[]{:S(2)}) collective-permute-start(bf16[136,1024]{1,0:T(8,128)(2,1)S(1)} %get-tuple-element.84), channel_id=1, source_target_pairs={{0,4},{4,0},{8,12},{12,8},{1,5},{5,1},{9,13},{13,9},{2,6},{6,2},{1... | collective-permute-start | bytes 835592 | tf_op jit(solution)/shard_map/ppermute | solution.py:39
  82.2 13.4 %collective-permute-start.20 = (bf16[136,1024]{1,0:T(8,128)(2,1)S(1)}, bf16[136,1024]{1,0:T(8,128)(2,1)S(1)}, u32[]{:S(2)}, u32[]{:S(2)}) collective-permute-start(bf16[136,1024]{1,0:T(8,128)(2,1)S(1)} %shard_map.59), channel_id=1, source_target_pairs={{0,12},{4,8},{8,4},{12,0},{1,13},{5,9},{9,5},{13,1},{2,14},{6,10},... | collective-permute-start | bytes 835592 | tf_op jit(solution)/shard_map/ppermute | solution.py:39
  97.6 4.6 %collective-permute-start.24 = (bf16[128,256]{1,0:T(8,128)(2,1)S(1)}, bf16[128,256]{1,0:T(8,128)(2,1)S(1)}, u32[]{:S(2)}, u32[]{:S(2)}) collective-permute-start(bf16[128,256]{1,0:T(8,128)(2,1)S(1)} %get-tuple-element.88), channel_id=1, source_target_pairs={{0,4},{4,0},{8,12},{12,8},{1,5},{5,1},{9,13},{13,9},{2,6},{6,2},{1... | collective-permute-start | bytes 196616 | tf_op jit(solution)/shard_map/ppermute | solution.py:39
  99.1 5.9 %collective-permute-start.25 = (bf16[128,256]{1,0:T(8,128)(2,1)S(1)}, bf16[128,256]{1,0:T(8,128)(2,1)S(1)}, u32[]{:S(2)}, u32[]{:S(2)}) collective-permute-start(bf16[128,256]{1,0:T(8,128)(2,1)S(1)} %get-tuple-element.89), channel_id=1, source_target_pairs={{0,8},{4,12},{8,0},{12,4},{1,9},{5,13},{9,1},{13,5},{2,10},{6,14},... | collective-permute-start | bytes 196616 | tf_op jit(solution)/shard_map/ppermute | solution.py:39
  100.2 6.2 %collective-permute-start.26 = (bf16[128,256]{1,0:T(8,128)(2,1)S(1)}, bf16[128,256]{1,0:T(8,128)(2,1)S(1)}, u32[]{:S(2)}, u32[]{:S(2)}) collective-permute-start(bf16[128,256]{1,0:T(8,128)(2,1)S(1)} %get-tuple-element.90), channel_id=1, source_target_pairs={{0,12},{4,8},{8,4},{12,0},{1,13},{5,9},{9,5},{13,1},{2,14},{6,10},... | collective-permute-start | bytes 196616 | tf_op jit(solution)/shard_map/ppermute | solution.py:39
  108.3 2.0 %collective-permute-start.27 = (bf16[128,2048]{1,0:T(8,128)(2,1)S(1)}, bf16[128,2048]{1,0:T(8,128)(2,1)S(1)}, u32[]{:S(2)}, u32[]{:S(2)}) collective-permute-start(bf16[128,2048]{1,0:T(8,128)(2,1)S(1)} %convert_element_type.24), channel_id=1, source_target_pairs={{0,1},{1,0},{2,3},{3,2},{4,5},{5,4},{6,7},{7,6},{8,9},{9,8},{10,11... | collective-permute-start | bytes 1572872 | tf_op jit(solution)/shard_map/ppermute | solution.py:444
  110.4 8.4 %collective-permute-start.28 = (bf16[64,2048]{1,0:T(8,128)(2,1)S(1)}, bf16[64,2048]{1,0:T(8,128)(2,1)S(1)}, u32[]{:S(2)}, u32[]{:S(2)}) collective-permute-start(bf16[64,2048]{1,0:T(8,128)(2,1)S(1)} %fusion), channel_id=1, source_target_pairs={{0,2},{2,0},{1,3},{3,1},{4,6},{6,4},{5,7},{7,5},{8,10},{10,8},{9,1... | collective-permute-start | bytes 786440 | tf_op jit(solution)/shard_map/ppermute | solution.py:445

commit v9 on v8

--- a/solution.py
+++ b/solution.py
@@ -44,10 +44,12 @@
 
 
 def turn_kernel(levels, level_g, level_a, rows, where, *refs):
-    slots, pieces, later = refs[:levels], refs[levels : levels + 4], refs[levels + 4 : levels + 6]
-    basis_a, out_g, basis_g, sums, sems = refs[levels + 6 :]
+    slots, pieces, later = refs[:levels], list(refs[levels : levels + 4]), refs[levels + 4 : levels + 6]
+    basis_a, out_g, basis_g, sums, held, held_sem, sems = refs[levels + 6 :]
     (half, late), width = split(rows), basis_a.shape[0]
     part = basis_a.shape[1]
+    move = pltpu.make_async_copy(pieces[2], held, held_sem)
+    pieces[2] = held
     copies = []
     for i, (first, height, target) in enumerate(((level_g, level_a, basis_a), (0, level_g, basis_g))):
         for step, slot in enumerate(slots):
@@ -57,34 +59,41 @@
             )
             copy.start()
             copies.append(copy)
-    for copy in copies[:levels]:
-        copy.wait()
-    total_a = jnp.zeros((1, part), f32)
-    total_g = jnp.zeros((1, part), f32)
-    for piece in pieces:
-        block = jnp.dot(piece[:rows], basis_a[...], preferred_element_type=f32).astype(bf16)
-        total_a = total_a + jnp.sum(jnp.square(block.astype(f32)), axis=0, keepdims=True)
-    for copy in copies[levels:]:
-        copy.wait()
-    for i, piece in enumerate(pieces):
+    move.start()
+
+    def squares(x):
+        return jnp.sum(jnp.square(x.astype(f32)), axis=0, keepdims=True)
+
+    def turn_a(piece):
+        return squares(jnp.dot(piece[:rows], basis_a[...], preferred_element_type=f32).astype(bf16))
+
+    def turn_g(i):
         turned = sum(
             jnp.dot(
-                piece[pl.ds(rows + 16 + j * half, half)],
+                pieces[i][pl.ds(rows + 16 + j * half, half)],
                 basis_g[pl.ds(j * width, width)],
                 preferred_element_type=f32,
             )
             for j in range(2)
         ).astype(bf16)
         out_g[pl.ds(i * half, half)] = turned
-        total_g = total_g + jnp.sum(jnp.square(turned.astype(f32)), axis=0, keepdims=True)
+        return squares(turned)
+
+    for copy in copies[:levels]:
+        copy.wait()
+    total_a = sum(turn_a(pieces[i]) for i in (0, 1, 3))
+    for copy in copies[levels:]:
+        copy.wait()
+    total_g = sum(turn_g(i) for i in (0, 1, 3))
     for i, piece in enumerate(later):
         turned = jnp.dot(piece[...], basis_g[...], preferred_element_type=f32).astype(bf16)
         out_g[pl.ds(4 * half + i * late, late)] = turned
-        total_g = total_g + jnp.sum(jnp.square(turned.astype(f32)), axis=0, keepdims=True)
+        total_g = total_g + squares(turned)
+    move.wait()
     marks = sum(piece[rows : rows + 16, :part].astype(f32) for piece in pieces)
-    sums[0:1] = total_g
+    sums[0:1] = total_g + turn_g(2)
     sums[1:2] = marks[0:1] + marks[1:2]
-    sums[2:3] = total_a
+    sums[2:3] = total_a + turn_a(held)
     sums[3:8] = jnp.zeros((5, part), f32)
 
 
@@ -101,9 +110,13 @@
             shape((width_g, part), bf16),
             shape((8, part), f32),
         ),
-        in_specs=[SMEM] + [ANY] * levels + [VMEM] * 6,
+        in_specs=[SMEM] + [ANY] * levels + [VMEM] * 2 + [ANY] + [VMEM] * 3,
         out_specs=(VMEM,) * 4,
-        scratch_shapes=[pltpu.SemaphoreType.DMA((2 * levels,))],
+        scratch_shapes=[
+            pltpu.VMEM(pieces[2].shape, bf16),
+            pltpu.SemaphoreType.DMA,
+            pltpu.SemaphoreType.DMA((2 * levels,)),
+        ],
         compiler_params=params(MIDDLE),
         cost_estimate=cost(8 * rows * part * (width_a + width_g // 2), 8 * rows * (width_a + width_g // 2)),
     )(where, *slots, *pieces, *later)
@@ -315,7 +328,7 @@
 
 def result_kernel(levels, where, *refs):
     slots = refs[:levels]
-    one, two, sent, kept, mid, whole, sems = refs[levels:]
+    one, two, outs, (mid, whole, sems) = refs[levels], refs[levels + 1], refs[levels + 2 : -3], refs[-3:]
     chunk, height = slots[0].shape
     wide, part = one.shape
     copies = []
@@ -336,9 +349,8 @@
             for i, b in enumerate((one, two))
         )
     rows = height // 4
-    for i, (other, target) in enumerate(((3, sent), (1, sent), (2, kept), (0, kept))):
-        block = whole[pl.ds(pl.multiple_of((where[1] ^ other) * rows, rows), rows)]
-        target[pl.ds((i % 2) * rows, rows)] = block.astype(target.dtype)
+    for other, out in zip((3, 1, 2, 0), outs):
+        out[...] = whole[pl.ds(pl.multiple_of((where[1] ^ other) * rows, rows), rows)].astype(out.dtype)
 
 
 def result(where, slots, bases):
@@ -347,9 +359,9 @@
     wide, part = bases[0].shape
     return pl.pallas_call(
         functools.partial(result_kernel, levels),
-        out_shape=(shape((height // 2, wide), f32), shape((height // 2, wide), f32)),
+        out_shape=[shape((height // 4, wide), t) for t in (bf16, bf16, f32, f32)],
         in_specs=[SMEM] + [ANY] * levels + [VMEM] * 2,
-        out_specs=(VMEM, VMEM),
+        out_specs=[VMEM] * 4,
         scratch_shapes=[
             pltpu.VMEM((2 * part, height), bf16),
             pltpu.VMEM((height, wide), f32),
@@ -440,10 +452,10 @@
     mids = middle(where, own, own_extra, got, bases_a, levels)
     mids = [m if step == 0 else across(m, step, levels) for step, m in enumerate(mids)]
 
-    sent, kept = result(where, mids, bases_g)
-    sent = lax.ppermute(sent.astype(bf16), "core", SWAP).astype(f32)
-    last = lax.ppermute((kept[:rows_a] + sent[:rows_a]).astype(bf16), "chip", SWAP)
-    return (kept[rows_a:] + sent[rows_a:] + last.astype(f32)).astype(bf16)
+    *sent, far_kept, near_kept = result(where, mids, bases_g)
+    far_sent, near_sent = (lax.ppermute(x, "core", SWAP).astype(f32) for x in sent)
+    last = lax.ppermute((far_kept + far_sent).astype(bf16), "chip", SWAP)
+    return (near_kept + near_sent + last.astype(f32)).astype(bf16)
 
 
 def solution(mesh):

time: 120 us -> 119 us (level)
    ppermute x2 -> x3, waiting for transfers between devices: 9.74 us -> 8.87 us  [the longest x1 7.84 us: body(): last = lax.ppermute((far_kept + far_sent).astype(bf16), 'chip', SWAP)]
  transfers between devices with their start and end apart: 29 -> 30, of which waited for: 20 -> 20; matrix products, arithmetic and copies ran while one was open for 3% -> 3% of each run, Pallas kernels for 12% -> 11%
where the time goes in v9:
time: 119 us
  waiting for transfers between devices  57 us (48%)
  starting transfers between devices  33.7 us (28%)
  Pallas kernels  20 us (17%)
  other arithmetic  3.9 us (3%)
  local copies, waits for them, and re-layouts  3.1 us (3%)
    ppermute x8, waiting for transfers between devices, across(): return lax.ppermute(x, 'level', [(i, i ^ step) for i in range(levels)])  29.8 us
    ppermute x8, starting transfers between devices, across(): return lax.ppermute(x, 'level', [(i, i ^ step) for i in range(levels)])  13 us
    pallas_call x2, Pallas kernels, turn(): pl.pallas_call(functools.partial(turn_kernel, levels, level_g, level_a, r...  9.9 us
    ppermute x1, waiting for transfers between devices, body(): last = lax.ppermute((far_kept + far_sent).astype(bf16), 'chip', SWAP)  7.84 us
    ppermute x1, waiting for transfers between devices, gather_levels(): lax.ppermute(held, 'level', [(0, 3), (3, 0)])  7.8 us
    ppermute x4, waiting for transfers between devices, over(): return lax.ppermute(slot, 'group', SWAP)  6.38 us
    ppermute x4, starting transfers between devices, over(): return lax.ppermute(slot, 'group', SWAP)  6.06 us
    ppermute x1, starting transfers between devices, gather_levels(): lax.ppermute(held, 'level', [(0, 3), (3, 0)])  4.37 us
  transfers between devices with their start and end apart: 30, of which 20 were waited for; matrix products, arithmetic and copies ran while one was open for 3% of the time, Pallas kernels for 11%

profile of v9, /device:TPU:0, one launch (start us, length us, event | category | flops | bytes accessed | tf_op | source)
XLA Modules:
  0.0 118.8 jit_solution(1209633577298495144)
XLA Ops:
  0.0 0.9 constant_dynamic-slice_fusion.1
  0.9 1.0 constant_dynamic-slice_fusion.3
  2.4 2.6 %collective-permute-start.1 = (bf16[192,256]{1,0:T(8,128)(2,1)S(1)}, bf16[192,256]{1,0:T(8,128)(2,1)S(1)}, u32[]{:S(2)}, u32[]{:S(2)}) collective-permute-start(bf16[192,256]{1,0:T(8,128)(2,1)S(1)} %get-tuple-element.106), channel_id=1, source_target_pairs={{0,2},{2,0},{1,3},{3,1},{4,6},{6,4},{5,7},{7,5},{8,10},{10,8},{9,1... | collective-permute-start | bytes 294920 | tf_op jit(solution)/shard_map/ppermute | solution.py:413
  6.3 0.9 copy-done.1
  7.8 0.9 collective-permute-done.1
  8.7 1.9 %collective-permute-start.2 = (bf16[880,1024]{1,0:T(8,128)(2,1)S(1)}, bf16[880,1024]{1,0:T(8,128)(2,1)}, u32[]{:S(2)}, u32[]{:S(2)}) collective-permute-start(bf16[880,1024]{1,0:T(8,128)(2,1)S(1)} %pad_maximum_fusion.refs_4_.refs_0_), channel_id=1, source_target_pairs={{0,2},{2,0},{1,3},{3,1},{4,6},{6,4},{5,7},{7,5},{8,10},{10,8},{9,1... | collective-permute-start | bytes 5406728 | tf_op jit(solution)/shard_map/ppermute | solution.py:432
  10.8 1.6 %collective-permute-start.5 = (bf16[768,256]{1,0:T(8,128)(2,1)S(1)}, bf16[768,256]{1,0:T(8,128)(2,1)}, u32[]{:S(2)}, u32[]{:S(2)}) collective-permute-start(bf16[768,256]{1,0:T(8,128)(2,1)S(1)} %fusion.5.refs_0_), channel_id=1, source_target_pairs={{0,4},{4,0},{8,12},{12,8},{1,5},{5,1},{9,13},{13,9},{2,6},{6,2},{1... | collective-permute-start | bytes 1179656 | tf_op jit(solution)/shard_map/ppermute | solution.py:39
  12.5 0.7 collective-permute-start.6
  13.2 1.6 %collective-permute-start.7 = (bf16[768,256]{1,0:T(8,128)(2,1)S(1)}, bf16[768,256]{1,0:T(8,128)(2,1)S(1)}, u32[]{:S(2)}, u32[]{:S(2)}) collective-permute-start(bf16[768,256]{1,0:T(8,128)(2,1)S(1)} %fusion.5.refs_0_), channel_id=1, source_target_pairs={{0,16},{16,0},{1,17},{17,1},{2,18},{18,2},{3,19},{19,3},{4,20},{20... | collective-permute-start | bytes 1179656 | tf_op jit(solution)/shard_map/ppermute | solution.py:377
  14.7 1.2 slice_select_fusion.1.refs_8_
  15.9 6.0 %collective-permute-done.5.refs_1_ = bf16[768,256]{1,0:T(8,128)(2,1)} collective-permute-done((bf16[768,256]{1,0:T(8,128)(2,1)S(1)}, bf16[768,256]{1,0:T(8,128)(2,1)}, u32[]{:S(2)}, u32[]{:S(2)}) %collective-permute-start.5) | collective-permute-done | bytes 393248 | tf_op jit(solution)/shard_map/ppermute | solution.py:39
  21.9 2.1 %collective-permute-done.7.refs_0_ = bf16[768,256]{1,0:T(8,128)(2,1)S(1)} collective-permute-done((bf16[768,256]{1,0:T(8,128)(2,1)S(1)}, bf16[768,256]{1,0:T(8,128)(2,1)S(1)}, u32[]{:S(2)}, u32[]{:S(2)}) %collective-permute-start.7) | collective-permute-done | bytes 393248 | tf_op jit(solution)/shard_map/ppermute | solution.py:377
  24.0 4.4 %collective-permute-start.8 = (bf16[768,256]{1,0:T(8,128)(2,1)S(1)}, bf16[768,256]{1,0:T(8,128)(2,1)}, u32[]{:S(2)}, u32[]{:S(2)}) collective-permute-start(bf16[768,256]{1,0:T(8,128)(2,1)S(1)} %fusion.5.refs_0_), channel_id=1, source_target_pairs={{0,12},{12,0},{1,13},{13,1},{2,14},{14,2},{3,15},{15,3},{16,28},{2... | collective-permute-start | bytes 1179656 | tf_op jit(solution)/shard_map/ppermute | solution.py:387
  28.4 1.6 %collective-permute-start.9 = (bf16[768,256]{1,0:T(8,128)(2,1)}, bf16[768,256]{1,0:T(8,128)(2,1)}, u32[]{:S(2)}, u32[]{:S(2)}) collective-permute-start(bf16[768,256]{1,0:T(8,128)(2,1)} %collective-permute-done.5.refs_1_), channel_id=1, source_target_pairs={{0,16},{16,0},{1,17},{17,1},{2,18},{18,2},{3,19},{19,3},{4,20},{20... | collective-permute-start | bytes 1179656 | tf_op jit(solution)/shard_map/ppermute | solution.py:377
  29.9 7.8 %collective-permute-done.8 = bf16[768,256]{1,0:T(8,128)(2,1)} collective-permute-done((bf16[768,256]{1,0:T(8,128)(2,1)S(1)}, bf16[768,256]{1,0:T(8,128)(2,1)}, u32[]{:S(2)}, u32[]{:S(2)}) %collective-permute-start.8) | collective-permute-done | bytes 393248 | tf_op jit(solution)/shard_map/ppermute | solution.py:387
  37.7 0.8 collective-permute-done.9.refs_1_
  38.6 1.0 broadcast_select_fusion.1.refs_3_
  39.6 0.9 collective-permute-start.10
  40.5 1.5 %collective-permute-start.11 = (bf16[768,256]{1,0:T(8,128)(2,1)S(1)}, bf16[768,256]{1,0:T(8,128)(2,1)S(1)}, u32[]{:S(2)}, u32[]{:S(2)}) collective-permute-start(bf16[768,256]{1,0:T(8,128)(2,1)S(1)} %broadcast_select_fusion.1.refs_3_), channel_id=1, source_target_pairs={{0,16},{16,0},{1,17},{17,1},{2,18},{18,2},{3,19},{19,3},{4,20},{20... | collective-permute-start | bytes 1179656 | tf_op jit(solution)/shard_map/ppermute | solution.py:377
  42.0 6.5 %collective-permute-done.10.refs_2_ = bf16[768,256]{1,0:T(8,128)(2,1)S(1)} collective-permute-done((bf16[768,256]{1,0:T(8,128)(2,1)S(1)}, bf16[768,256]{1,0:T(8,128)(2,1)S(1)}, u32[]{:S(2)}, u32[]{:S(2)}) %collective-permute-start.10) | collective-permute-done | bytes 393248 | tf_op jit(solution)/shard_map/ppermute | solution.py:39
  49.0 0.7 collective-permute-done.2.refs_6_.refs_2_
  50.2 1.6 %collective-permute-start.15 = (bf16[144,2048]{1,0:T(8,128)(2,1)S(1)}, bf16[144,2048]{1,0:T(8,128)(2,1)S(1)}, u32[]{:S(2)}, u32[]{:S(2)}) collective-permute-start(bf16[144,2048]{1,0:T(8,128)(2,1)S(1)} %slice_select_fusion.1.refs_8_), channel_id=1, source_target_pairs={{0,2},{2,0},{1,3},{3,1},{4,6},{6,4},{5,7},{7,5},{8,10},{10,8},{9,1... | collective-permute-start | bytes 1769480 | tf_op jit(solution)/shard_map/ppermute | solution.py:438
  51.8 1.5 %collective-permute-start.13 = (bf16[768,256]{1,0:T(8,128)(2,1)S(1)}, bf16[768,256]{1,0:T(8,128)(2,1)S(1)}, u32[]{:S(2)}, u32[]{:S(2)}) collective-permute-start(bf16[768,256]{1,0:T(8,128)(2,1)S(1)} %collective-permute-done.10.refs_2_), channel_id=1, source_target_pairs={{0,16},{16,0},{1,17},{17,1},{2,18},{18,2},{3,19},{19,3},{4,20},{20... | collective-permute-start | bytes 1179656 | tf_op jit(solution)/shard_map/ppermute | solution.py:377
  53.3 0.6 collective-permute-done.14.refs_9_
  53.9 0.6 collective-permute-done.12.refs_7_.refs_3_
  54.5 5.0 %shard_map.55 = (bf16[1024,256]{1,0:T(8,128)(2,1)S(1)}, bf16[1248,256]{1,0:T(8,128)(2,1)S(1)}, bf16[2048,256]{1,0:T(8,128)(2,1)S(1)}, f32[8,256]{1,0:T(8,128)S(1)}) custom-call(s32[2]{0:T(128)S(1)} %pad_add_fusion.where, bf16[768,256]{1,0:T(8,128)(2,1)S(1)} %fusion.5.refs_0_, bf16[768,256]{1,0:T(8,128)(2,1)} %collective-permute-done.5.refs_1_, ...), custom_call_target="tpu_custom_call" | custom-call | flops 1610612736 | bytes 6291456 | tf_op jit(solution)/shard_map/pallas_call | solution.py:105
  59.5 3.1 %collective-permute-done.13.refs_2_ = bf16[768,256]{1,0:T(8,128)(2,1)S(1)} collective-permute-done((bf16[768,256]{1,0:T(8,128)(2,1)S(1)}, bf16[768,256]{1,0:T(8,128)(2,1)S(1)}, u32[]{:S(2)}, u32[]{:S(2)}) %collective-permute-start.13) | collective-permute-done | bytes 393248 | tf_op jit(solution)/shard_map/ppermute | solution.py:377
  62.5 5.0 %shard_map.56 = (bf16[1024,256]{1,0:T(8,128)(2,1)S(1)}, bf16[1248,256]{1,0:T(8,128)(2,1)S(1)}, bf16[2048,256]{1,0:T(8,128)(2,1)S(1)}, f32[8,256]{1,0:T(8,128)S(1)}) custom-call(s32[2]{0:T(128)S(1)} %pad_add_fusion.where, bf16[768,256]{1,0:T(8,128)(2,1)S(1)} %collective-permute-done.7.refs_0_, bf16[768,256]{1,0:T(8,128)(2,1)} %collective-permute-done.9.refs_1_, ...), custom_call_target="tpu_custom_call" | custom-call | flops 1610612736 | bytes 6291456 | tf_op jit(solution)/shard_map/pallas_call | solution.py:105
  68.2 1.4 %collective-permute-done.18.refs_13_ = f32[8,256]{1,0:T(8,128)S(1)} collective-permute-done((f32[8,256]{1,0:T(8,128)S(1)}, f32[8,256]{1,0:T(8,128)S(1)}, u32[]{:S(2)}, u32[]{:S(2)}) %collective-permute-start.18) | collective-permute-done | bytes 8224 | tf_op jit(solution)/shard_map/ppermute | solution.py:441
  69.6 3.0 %shard_map.57 = (bf16[136,1024]{1,0:T(8,128)(2,1)S(1)}, f32[8,1024]{1,0:T(8,128)S(1)}, bf16[1536,512]{1,0:T(8,128)(2,1)S(1)}) custom-call(s32[2]{0:T(128)S(1)} %pad_add_fusion.where, bf16[880,1024]{1,0:T(8,128)(2,1)S(1)} %pad_maximum_fusion.refs_4_.refs_0_, bf16[880,1024]{1,0:T(8,128)(2,1)S(1)} %collective-permute-done.refs_5_.refs_1_, ...), custom_call_target="tpu_custom_call" | custom-call | flops 402653184 | bytes 6291456 | tf_op jit(solution)/shard_map/pallas_call | solution.py:228
  72.6 1.6 %collective-permute-start.19 = (bf16[136,1024]{1,0:T(8,128)(2,1)S(1)}, bf16[136,1024]{1,0:T(8,128)(2,1)S(1)}, u32[]{:S(2)}, u32[]{:S(2)}) collective-permute-start(bf16[136,1024]{1,0:T(8,128)(2,1)S(1)} %get-tuple-element.85), channel_id=1, source_target_pairs={{0,4},{4,0},{8,12},{12,8},{1,5},{5,1},{9,13},{13,9},{2,6},{6,2},{1... | collective-permute-start | bytes 835592 | tf_op jit(solution)/shard_map/ppermute | solution.py:39
  74.7 3.3 %shard_map.58 = (f32[128,1024]{1,0:T(8,128)S(1)}, bf16[136,1024]{1,0:T(8,128)(2,1)S(1)}, f32[128,1024]{1,0:T(8,128)S(1)}) custom-call(s32[2]{0:T(128)S(1)} %pad_add_fusion.where, bf16[1536,512]{1,0:T(8,128)(2,1)S(1)} %get-tuple-element.81.right, f32[8,1024]{1,0:T(8,128)S(1)} %get-tuple-element.82.extra.own_extra, ...), custom_call_target="tpu_custom_call" | custom-call | flops 1207959552 | bytes 6291456 | tf_op jit(solution)/shard_map/pallas_call | solution.py:256
  78.0 0.6 collective-permute-start.21
  78.6 3.4 %collective-permute-done.19.got = bf16[136,1024]{1,0:T(8,128)(2,1)S(1)} collective-permute-done((bf16[136,1024]{1,0:T(8,128)(2,1)S(1)}, bf16[136,1024]{1,0:T(8,128)(2,1)S(1)}, u32[]{:S(2)}, u32[]{:S(2)}) %collective-permute-start.19) | collective-permute-done | bytes 278560 | tf_op jit(solution)/shard_map/ppermute | solution.py:39
  82.0 3.8 %collective-permute-start.20 = (bf16[136,1024]{1,0:T(8,128)(2,1)S(1)}, bf16[136,1024]{1,0:T(8,128)(2,1)S(1)}, u32[]{:S(2)}, u32[]{:S(2)}) collective-permute-start(bf16[136,1024]{1,0:T(8,128)(2,1)S(1)} %shard_map.59), channel_id=1, source_target_pairs={{0,12},{4,8},{8,4},{12,0},{1,13},{5,9},{9,5},{13,1},{2,14},{6,10},... | collective-permute-start | bytes 835592 | tf_op jit(solution)/shard_map/ppermute | solution.py:39
  85.9 1.5 %collective-permute-done.21.refs_1_ = bf16[136,1024]{1,0:T(8,128)(2,1)S(1)} collective-permute-done((bf16[136,1024]{1,0:T(8,128)(2,1)S(1)}, bf16[136,1024]{1,0:T(8,128)(2,1)S(1)}, u32[]{:S(2)}, u32[]{:S(2)}) %collective-permute-start.21) | collective-permute-done | bytes 278560 | tf_op jit(solution)/shard_map/ppermute | solution.py:39
  87.3 8.1 %collective-permute-done.20.refs_0_ = bf16[136,1024]{1,0:T(8,128)(2,1)S(1)} collective-permute-done((bf16[136,1024]{1,0:T(8,128)(2,1)S(1)}, bf16[136,1024]{1,0:T(8,128)(2,1)S(1)}, u32[]{:S(2)}, u32[]{:S(2)}) %collective-permute-start.20) | collective-permute-done | bytes 278560 | tf_op jit(solution)/shard_map/ppermute | solution.py:39
  95.4 1.9 %shard_map.60 = (bf16[128,256]{1,0:T(8,128)(2,1)S(1)}, bf16[128,256]{1,0:T(8,128)(2,1)S(1)}, bf16[128,256]{1,0:T(8,128)(2,1)S(1)}, bf16[128,256]{1,0:T(8,128)(2,1)S(1)}) custom-call(s32[2]{0:T(128)S(1)} %pad_add_fusion.where, f32[128,1024]{1,0:T(8,128)S(1)} %get-tuple-element.83.own, f32[8,1024]{1,0:T(8,128)S(1)} %get-tuple-element.82.extra.own_extra, ...), custom_call_target="tpu_custom_call" | custom-call | flops 805306368 | bytes 2097152 | tf_op jit(solution)/shard_map/pallas_call | solution.py:318
  97.3 1.5 %collective-permute-start.24 = (bf16[128,256]{1,0:T(8,128)(2,1)S(1)}, bf16[128,256]{1,0:T(8,128)(2,1)S(1)}, u32[]{:S(2)}, u32[]{:S(2)}) collective-permute-start(bf16[128,256]{1,0:T(8,128)(2,1)S(1)} %get-tuple-element.90), channel_id=1, source_target_pairs={{0,4},{4,0},{8,12},{12,8},{1,5},{5,1},{9,13},{13,9},{2,6},{6,2},{1... | collective-permute-start | bytes 196616 | tf_op jit(solution)/shard_map/ppermute | solution.py:39
  98.9 1.1 collective-permute-start.25
  100.0 1.8 %collective-permute-start.26 = (bf16[128,256]{1,0:T(8,128)(2,1)S(1)}, bf16[128,256]{1,0:T(8,128)(2,1)S(1)}, u32[]{:S(2)}, u32[]{:S(2)}) collective-permute-start(bf16[128,256]{1,0:T(8,128)(2,1)S(1)} %get-tuple-element.92), channel_id=1, source_target_pairs={{0,12},{4,8},{8,4},{12,0},{1,13},{5,9},{9,5},{13,1},{2,14},{6,10},... | collective-permute-start | bytes 196616 | tf_op jit(solution)/shard_map/ppermute | solution.py:39
  101.9 2.8 %collective-permute-done.25.refs_2_ = bf16[128,256]{1,0:T(8,128)(2,1)S(1)} collective-permute-done((bf16[128,256]{1,0:T(8,128)(2,1)S(1)}, bf16[128,256]{1,0:T(8,128)(2,1)S(1)}, u32[]{:S(2)}, u32[]{:S(2)}) %collective-permute-start.25) | collective-permute-done | bytes 65568 | tf_op jit(solution)/shard_map/ppermute | solution.py:39
  104.7 1.4 %collective-permute-done.26.refs_3_ = bf16[128,256]{1,0:T(8,128)(2,1)S(1)} collective-permute-done((bf16[128,256]{1,0:T(8,128)(2,1)S(1)}, bf16[128,256]{1,0:T(8,128)(2,1)S(1)}, u32[]{:S(2)}, u32[]{:S(2)}) %collective-permute-start.26) | collective-permute-done | bytes 65568 | tf_op jit(solution)/shard_map/ppermute | solution.py:39
  106.1 1.8 %shard_map.61 = (bf16[64,2048]{1,0:T(8,128)(2,1)S(1)}, bf16[64,2048]{1,0:T(8,128)(2,1)S(1)}, f32[64,2048]{1,0:T(8,128)S(1)}, f32[64,2048]{1,0:T(8,128)S(1)}) custom-call(s32[2]{0:T(128)S(1)} %pad_add_fusion.where, bf16[128,256]{1,0:T(8,128)(2,1)S(1)} %get-tuple-element.89.refs_0_, bf16[128,256]{1,0:T(8,128)(2,1)S(1)} %collective-permute-done.24.refs_1_, ...), custom_call_target="tpu_custom_call" | custom-call | flops 536870912 | bytes 2097152 | tf_op jit(solution)/shard_map/pallas_call | solution.py:360
  108.5 1.0 collective-permute-done.28
  109.6 0.6 collective-permute-start.29
  110.2 7.8 %collective-permute-done.29 = bf16[64,2048]{1,0:T(8,128)(2,1)S(1)} collective-permute-done((bf16[64,2048]{1,0:T(8,128)(2,1)S(1)}, bf16[64,2048]{1,0:T(8,128)(2,1)S(1)}, u32[]{:S(2)}, u32[]{:S(2)}) %collective-permute-start.29) | collective-permute-done | bytes 262176 | tf_op jit(solution)/shard_map/ppermute | solution.py:457
  118.0 0.8 add_convert_fusion
  (53 shorter events, 4.7 us)
Async XLA Ops:
  0.0 5.9 %copy-start = (bf16[384,2048]{1,0:T(8,128)(2,1)S(1)}, bf16[384,2048]{1,0:T(8,128)(2,1)}, u32[]{:S(2)}) copy-start(bf16[384,2048]{1,0:T(8,128)(2,1)} %param.6) | copy-start | bytes 4718596
  1.9 8.7 %collective-permute-start.3 = (bf16[192,256]{1,0:T(8,128)(2,1)S(1)}, bf16[192,256]{1,0:T(8,128)(2,1)S(1)}, u32[]{:S(2)}, u32[]{:S(2)}) collective-permute-start(bf16[192,256]{1,0:T(8,128)(2,1)S(1)} %get-tuple-element.107), channel_id=1, source_target_pairs={{0,1},{1,0},{2,3},{3,2},{4,5},{5,4},{6,7},{7,6},{8,9},{9,8},{10,11... | collective-permute-start | bytes 294920 | tf_op jit(solution)/shard_map/ppermute | solution.py:414
  2.4 6.2 %collective-permute-start.1 = (bf16[192,256]{1,0:T(8,128)(2,1)S(1)}, bf16[192,256]{1,0:T(8,128)(2,1)S(1)}, u32[]{:S(2)}, u32[]{:S(2)}) collective-permute-start(bf16[192,256]{1,0:T(8,128)(2,1)S(1)} %get-tuple-element.106), channel_id=1, source_target_pairs={{0,2},{2,0},{1,3},{3,1},{4,6},{6,4},{5,7},{7,5},{8,10},{10,8},{9,1... | collective-permute-start | bytes 294920 | tf_op jit(solution)/shard_map/ppermute | solution.py:413
  5.0 5.6 %collective-permute-start.4 = (bf16[192,256]{1,0:T(8,128)(2,1)S(1)}, bf16[192,256]{1,0:T(8,128)(2,1)S(1)}, u32[]{:S(2)}, u32[]{:S(2)}) collective-permute-start(bf16[192,256]{1,0:T(8,128)(2,1)S(1)} %get-tuple-element.108), channel_id=1, source_target_pairs={{0,3},{1,2},{2,1},{3,0},{4,7},{5,6},{6,5},{7,4},{8,11},{9,10},{10,... | collective-permute-start | bytes 294920 | tf_op jit(solution)/shard_map/ppermute | solution.py:411
  6.1 1.1 copy-start.1
  8.7 41.0 %collective-permute-start.2 = (bf16[880,1024]{1,0:T(8,128)(2,1)S(1)}, bf16[880,1024]{1,0:T(8,128)(2,1)}, u32[]{:S(2)}, u32[]{:S(2)}) collective-permute-start(bf16[880,1024]{1,0:T(8,128)(2,1)S(1)} %pad_maximum_fusion.refs_4_.refs_0_), channel_id=1, source_target_pairs={{0,2},{2,0},{1,3},{3,1},{4,6},{6,4},{5,7},{7,5},{8,10},{10,8},{9,1... | collective-permute-start | bytes 5406728 | tf_op jit(solution)/shard_map/ppermute | solution.py:432
  10.8 11.1 %collective-permute-start.5 = (bf16[768,256]{1,0:T(8,128)(2,1)S(1)}, bf16[768,256]{1,0:T(8,128)(2,1)}, u32[]{:S(2)}, u32[]{:S(2)}) collective-permute-start(bf16[768,256]{1,0:T(8,128)(2,1)S(1)} %fusion.5.refs_0_), channel_id=1, source_target_pairs={{0,4},{4,0},{8,12},{12,8},{1,5},{5,1},{9,13},{13,9},{2,6},{6,2},{1... | collective-permute-start | bytes 1179656 | tf_op jit(solution)/shard_map/ppermute | solution.py:39
  12.5 9.4 %collective-permute-start.6 = (bf16[768,256]{1,0:T(8,128)(2,1)S(1)}, bf16[768,256]{1,0:T(8,128)(2,1)S(1)}, u32[]{:S(2)}, u32[]{:S(2)}) collective-permute-start(bf16[768,256]{1,0:T(8,128)(2,1)S(1)} %fusion.5.refs_0_), channel_id=1, source_target_pairs={{4,8},{8,4},{5,9},{9,5},{6,10},{10,6},{7,11},{11,7},{20,24},{24,20... | collective-permute-start | bytes 1179656 | tf_op jit(solution)/shard_map/ppermute | solution.py:384
  13.2 10.8 %collective-permute-start.7 = (bf16[768,256]{1,0:T(8,128)(2,1)S(1)}, bf16[768,256]{1,0:T(8,128)(2,1)S(1)}, u32[]{:S(2)}, u32[]{:S(2)}) collective-permute-start(bf16[768,256]{1,0:T(8,128)(2,1)S(1)} %fusion.5.refs_0_), channel_id=1, source_target_pairs={{0,16},{16,0},{1,17},{17,1},{2,18},{18,2},{3,19},{19,3},{4,20},{20... | collective-permute-start | bytes 1179656 | tf_op jit(solution)/shard_map/ppermute | solution.py:377
  21.9 2.1 %copy-start.2 = (bf16[768,256]{1,0:T(8,128)(2,1)}, bf16[768,256]{1,0:T(8,128)(2,1)S(1)}, u32[]{:S(2)}) copy-start(bf16[768,256]{1,0:T(8,128)(2,1)S(1)} %collective-permute-done.6) | copy-start | bytes 1179652
  24.0 13.7 %collective-permute-start.8 = (bf16[768,256]{1,0:T(8,128)(2,1)S(1)}, bf16[768,256]{1,0:T(8,128)(2,1)}, u32[]{:S(2)}, u32[]{:S(2)}) collective-permute-start(bf16[768,256]{1,0:T(8,128)(2,1)S(1)} %fusion.5.refs_0_), channel_id=1, source_target_pairs={{0,12},{12,0},{1,13},{13,1},{2,14},{14,2},{3,15},{15,3},{16,28},{2... | collective-permute-start | bytes 1179656 | tf_op jit(solution)/shard_map/ppermute | solution.py:387
  28.4 10.2 %collective-permute-start.9 = (bf16[768,256]{1,0:T(8,128)(2,1)}, bf16[768,256]{1,0:T(8,128)(2,1)}, u32[]{:S(2)}, u32[]{:S(2)}) collective-permute-start(bf16[768,256]{1,0:T(8,128)(2,1)} %collective-permute-done.5.refs_1_), channel_id=1, source_target_pairs={{0,16},{16,0},{1,17},{17,1},{2,18},{18,2},{3,19},{19,3},{4,20},{20... | collective-permute-start | bytes 1179656 | tf_op jit(solution)/shard_map/ppermute | solution.py:377
  39.6 9.0 %collective-permute-start.10 = (bf16[768,256]{1,0:T(8,128)(2,1)S(1)}, bf16[768,256]{1,0:T(8,128)(2,1)S(1)}, u32[]{:S(2)}, u32[]{:S(2)}) collective-permute-start(bf16[768,256]{1,0:T(8,128)(2,1)S(1)} %broadcast_select_fusion.1.refs_3_), channel_id=1, source_target_pairs={{0,4},{4,0},{8,12},{12,8},{1,5},{5,1},{9,13},{13,9},{2,6},{6,2},{1... | collective-permute-start | bytes 1179656 | tf_op jit(solution)/shard_map/ppermute | solution.py:39
  40.5 8.4 %collective-permute-start.11 = (bf16[768,256]{1,0:T(8,128)(2,1)S(1)}, bf16[768,256]{1,0:T(8,128)(2,1)S(1)}, u32[]{:S(2)}, u32[]{:S(2)}) collective-permute-start(bf16[768,256]{1,0:T(8,128)(2,1)S(1)} %broadcast_select_fusion.1.refs_3_), channel_id=1, source_target_pairs={{0,16},{16,0},{1,17},{17,1},{2,18},{18,2},{3,19},{19,3},{4,20},{20... | collective-permute-start | bytes 1179656 | tf_op jit(solution)/shard_map/ppermute | solution.py:377
  42.0 11.9 %collective-permute-start = (bf16[880,1024]{1,0:T(8,128)(2,1)S(1)}, bf16[880,1024]{1,0:T(8,128)(2,1)S(1)}, u32[]{:S(2)}, u32[]{:S(2)}) collective-permute-start(bf16[880,1024]{1,0:T(8,128)(2,1)S(1)} %pad_maximum_fusion.refs_4_.refs_0_), channel_id=1, source_target_pairs={{0,1},{1,0},{2,3},{3,2},{4,5},{5,4},{6,7},{7,6},{8,9},{9,8},{10,11... | collective-permute-start | bytes 5406728 | tf_op jit(solution)/shard_map/ppermute | solution.py:433
  49.7 4.8 %collective-permute-start.12 = (bf16[880,1024]{1,0:T(8,128)(2,1)}, bf16[880,1024]{1,0:T(8,128)(2,1)S(1)}, u32[]{:S(2)}, u32[]{:S(2)}) collective-permute-start(bf16[880,1024]{1,0:T(8,128)(2,1)} %collective-permute-done.2.refs_6_.refs_2_), channel_id=1, source_target_pairs={{0,1},{1,0},{2,3},{3,2},{4,5},{5,4},{6,7},{7,6},{8,9},{9,8},{10,11... | collective-permute-start | bytes 5406728 | tf_op jit(solution)/shard_map/ppermute | solution.py:433
  49.7 4.2 %collective-permute-start.14 = (bf16[144,2048]{1,0:T(8,128)(2,1)S(1)}, bf16[144,2048]{1,0:T(8,128)(2,1)S(1)}, u32[]{:S(2)}, u32[]{:S(2)}) collective-permute-start(bf16[144,2048]{1,0:T(8,128)(2,1)S(1)} %slice_select_fusion.1.refs_8_), channel_id=1, source_target_pairs={{0,1},{1,0},{2,3},{3,2},{4,5},{5,4},{6,7},{7,6},{8,9},{9,8},{10,11... | collective-permute-start | bytes 1769480 | tf_op jit(solution)/shard_map/ppermute | solution.py:434
  50.2 17.3 %collective-permute-start.15 = (bf16[144,2048]{1,0:T(8,128)(2,1)S(1)}, bf16[144,2048]{1,0:T(8,128)(2,1)S(1)}, u32[]{:S(2)}, u32[]{:S(2)}) collective-permute-start(bf16[144,2048]{1,0:T(8,128)(2,1)S(1)} %slice_select_fusion.1.refs_8_), channel_id=1, source_target_pairs={{0,2},{2,0},{1,3},{3,1},{4,6},{6,4},{5,7},{7,5},{8,10},{10,8},{9,1... | collective-permute-start | bytes 1769480 | tf_op jit(solution)/shard_map/ppermute | solution.py:438
  51.8 10.7 %collective-permute-start.13 = (bf16[768,256]{1,0:T(8,128)(2,1)S(1)}, bf16[768,256]{1,0:T(8,128)(2,1)S(1)}, u32[]{:S(2)}, u32[]{:S(2)}) collective-permute-start(bf16[768,256]{1,0:T(8,128)(2,1)S(1)} %collective-permute-done.10.refs_2_), channel_id=1, source_target_pairs={{0,16},{16,0},{1,17},{17,1},{2,18},{18,2},{3,19},{19,3},{4,20},{20... | collective-permute-start | bytes 1179656 | tf_op jit(solution)/shard_map/ppermute | solution.py:377
  67.5 2.1 %collective-permute-start.16 = (bf16[144,2048]{1,0:T(8,128)(2,1)S(1)}, bf16[144,2048]{1,0:T(8,128)(2,1)S(1)}, u32[]{:S(2)}, u32[]{:S(2)}) collective-permute-start(bf16[144,2048]{1,0:T(8,128)(2,1)S(1)} %collective-permute-done.15.refs_8_), channel_id=1, source_target_pairs={{0,1},{1,0},{2,3},{3,2},{4,5},{5,4},{6,7},{7,6},{8,9},{9,8},{10,11... | collective-permute-start | bytes 1769480 | tf_op jit(solution)/shard_map/ppermute | solution.py:439
  67.6 2.0 %collective-permute-start.18 = (f32[8,256]{1,0:T(8,128)S(1)}, f32[8,256]{1,0:T(8,128)S(1)}, u32[]{:S(2)}, u32[]{:S(2)}) collective-permute-start(f32[8,256]{1,0:T(8,128)S(1)} %get-tuple-element.80.refs_11_), channel_id=1, source_target_pairs={{0,1},{1,0},{2,3},{3,2},{4,5},{5,4},{6,7},{7,6},{8,9},{9,8},{10,11... | collective-permute-start | bytes 24584 | tf_op jit(solution)/shard_map/ppermute | solution.py:441
  68.1 1.5 %collective-permute-start.17 = (f32[8,256]{1,0:T(8,128)S(1)}, f32[8,256]{1,0:T(8,128)S(1)}, u32[]{:S(2)}, u32[]{:S(2)}) collective-permute-start(f32[8,256]{1,0:T(8,128)S(1)} %get-tuple-element.79.refs_10_), channel_id=1, source_target_pairs={{0,1},{1,0},{2,3},{3,2},{4,5},{5,4},{6,7},{7,6},{8,9},{9,8},{10,11... | collective-permute-start | bytes 24584 | tf_op jit(solution)/shard_map/ppermute | solution.py:441
  72.6 9.4 %collective-permute-start.19 = (bf16[136,1024]{1,0:T(8,128)(2,1)S(1)}, bf16[136,1024]{1,0:T(8,128)(2,1)S(1)}, u32[]{:S(2)}, u32[]{:S(2)}) collective-permute-start(bf16[136,1024]{1,0:T(8,128)(2,1)S(1)} %get-tuple-element.85), channel_id=1, source_target_pairs={{0,4},{4,0},{8,12},{12,8},{1,5},{5,1},{9,13},{13,9},{2,6},{6,2},{1... | collective-permute-start | bytes 835592 | tf_op jit(solution)/shard_map/ppermute | solution.py:39
  74.2 11.7 %collective-permute-start.23 = (bf16[1024,256]{1,0:T(8,128)(2,1)S(1)}, bf16[1024,256]{1,0:T(8,128)(2,1)S(1)}, u32[]{:S(2)}, u32[]{:S(2)}) collective-permute-start(bf16[1024,256]{1,0:T(8,128)(2,1)S(1)} %get-tuple-element.88.refs_3_), channel_id=1, source_target_pairs={{0,1},{1,0},{2,3},{3,2},{4,5},{5,4},{6,7},{7,6},{8,9},{9,8},{10,11... | collective-permute-start | bytes 1572872 | tf_op jit(solution)/shard_map/ppermute | solution.py:442
  74.2 11.7 %collective-permute-start.22 = (bf16[1024,256]{1,0:T(8,128)(2,1)S(1)}, bf16[1024,256]{1,0:T(8,128)(2,1)S(1)}, u32[]{:S(2)}, u32[]{:S(2)}) collective-permute-start(bf16[1024,256]{1,0:T(8,128)(2,1)S(1)} %get-tuple-element.87.refs_2_), channel_id=1, source_target_pairs={{0,1},{1,0},{2,3},{3,2},{4,5},{5,4},{6,7},{7,6},{8,9},{9,8},{10,11... | collective-permute-start | bytes 1572872 | tf_op jit(solution)/shard_map/ppermute | solution.py:442
  78.0 9.3 %collective-permute-start.21 = (bf16[136,1024]{1,0:T(8,128)(2,1)S(1)}, bf16[136,1024]{1,0:T(8,128)(2,1)S(1)}, u32[]{:S(2)}, u32[]{:S(2)}) collective-permute-start(bf16[136,1024]{1,0:T(8,128)(2,1)S(1)} %get-tuple-element.86), channel_id=1, source_target_pairs={{0,4},{4,0},{8,12},{12,8},{1,5},{5,1},{9,13},{13,9},{2,6},{6,2},{1... | collective-permute-start | bytes 835592 | tf_op jit(solution)/shard_map/ppermute | solution.py:39
  82.0 13.4 %collective-permute-start.20 = (bf16[136,1024]{1,0:T(8,128)(2,1)S(1)}, bf16[136,1024]{1,0:T(8,128)(2,1)S(1)}, u32[]{:S(2)}, u32[]{:S(2)}) collective-permute-start(bf16[136,1024]{1,0:T(8,128)(2,1)S(1)} %shard_map.59), channel_id=1, source_target_pairs={{0,12},{4,8},{8,4},{12,0},{1,13},{5,9},{9,5},{13,1},{2,14},{6,10},... | collective-permute-start | bytes 835592 | tf_op jit(solution)/shard_map/ppermute | solution.py:39
  97.3 4.5 %collective-permute-start.24 = (bf16[128,256]{1,0:T(8,128)(2,1)S(1)}, bf16[128,256]{1,0:T(8,128)(2,1)S(1)}, u32[]{:S(2)}, u32[]{:S(2)}) collective-permute-start(bf16[128,256]{1,0:T(8,128)(2,1)S(1)} %get-tuple-element.90), channel_id=1, source_target_pairs={{0,4},{4,0},{8,12},{12,8},{1,5},{5,1},{9,13},{13,9},{2,6},{6,2},{1... | collective-permute-start | bytes 196616 | tf_op jit(solution)/shard_map/ppermute | solution.py:39
  98.9 5.9 %collective-permute-start.25 = (bf16[128,256]{1,0:T(8,128)(2,1)S(1)}, bf16[128,256]{1,0:T(8,128)(2,1)S(1)}, u32[]{:S(2)}, u32[]{:S(2)}) collective-permute-start(bf16[128,256]{1,0:T(8,128)(2,1)S(1)} %get-tuple-element.91), channel_id=1, source_target_pairs={{0,8},{4,12},{8,0},{12,4},{1,9},{5,13},{9,1},{13,5},{2,10},{6,14},... | collective-permute-start | bytes 196616 | tf_op jit(solution)/shard_map/ppermute | solution.py:39
  100.0 6.2 %collective-permute-start.26 = (bf16[128,256]{1,0:T(8,128)(2,1)S(1)}, bf16[128,256]{1,0:T(8,128)(2,1)S(1)}, u32[]{:S(2)}, u32[]{:S(2)}) collective-permute-start(bf16[128,256]{1,0:T(8,128)(2,1)S(1)} %get-tuple-element.92), channel_id=1, source_target_pairs={{0,12},{4,8},{8,4},{12,0},{1,13},{5,9},{9,5},{13,1},{2,14},{6,10},... | collective-permute-start | bytes 196616 | tf_op jit(solution)/shard_map/ppermute | solution.py:39
  108.0 1.6 %collective-permute-start.28 = (bf16[64,2048]{1,0:T(8,128)(2,1)S(1)}, bf16[64,2048]{1,0:T(8,128)(2,1)S(1)}, u32[]{:S(2)}, u32[]{:S(2)}) collective-permute-start(bf16[64,2048]{1,0:T(8,128)(2,1)S(1)} %get-tuple-element.96), channel_id=1, source_target_pairs={{0,1},{1,0},{2,3},{3,2},{4,5},{5,4},{6,7},{7,6},{8,9},{9,8},{10,11... | collective-permute-start | bytes 786440 | tf_op jit(solution)/shard_map/ppermute | solution.py:456
  108.0 2.1 %collective-permute-start.27 = (bf16[64,2048]{1,0:T(8,128)(2,1)S(1)}, bf16[64,2048]{1,0:T(8,128)(2,1)S(1)}, u32[]{:S(2)}, u32[]{:S(2)}) collective-permute-start(bf16[64,2048]{1,0:T(8,128)(2,1)S(1)} %get-tuple-element.94), channel_id=1, source_target_pairs={{0,1},{1,0},{2,3},{3,2},{4,5},{5,4},{6,7},{7,6},{8,9},{9,8},{10,11... | collective-permute-start | bytes 786440 | tf_op jit(solution)/shard_map/ppermute | solution.py:456
  109.6 8.4 %collective-permute-start.29 = (bf16[64,2048]{1,0:T(8,128)(2,1)S(1)}, bf16[64,2048]{1,0:T(8,128)(2,1)S(1)}, u32[]{:S(2)}, u32[]{:S(2)}) collective-permute-start(bf16[64,2048]{1,0:T(8,128)(2,1)S(1)} %add_convert_fusion.1), channel_id=1, source_target_pairs={{0,2},{2,0},{1,3},{3,1},{4,6},{6,4},{5,7},{7,5},{8,10},{10,8},{9,1... | collective-permute-start | bytes 786440 | tf_op jit(solution)/shard_map/ppermute | solution.py:457

commit v10 on v9

--- a/solution.py
+++ b/solution.py
@@ -127,10 +127,9 @@
     return high, (v - high.astype(f32)).astype(bf16)
 
 
-def turn_late(rows, acts, early, bases, pieces, sums, right, left, basis, held, sems, extra):
+def turn_late(rows, acts, early, bases, pieces, sums, right, moved, held, sems, extra):
     half, late = split(rows)
     part = bases[0].shape[1]
-    cols = 2 * part
     count = 0
 
     def copy(source, target):
@@ -140,9 +139,8 @@
         count += 1
         return made
 
-    first = [copy(b, basis.at[:, pl.ds(i * part, part)]) for i, b in enumerate(bases)]
-    first += [copy(p, held.at[pl.ds(i * late, late)]) for i, p in enumerate(pieces)]
-    rest = [copy(a.at[pl.ds(0, rows)], left.at[pl.ds(i * rows, rows)]) for i, a in enumerate(acts)]
+    first = [copy(p, held.at[pl.ds(i * late, late)]) for i, p in enumerate(pieces)]
+    rest = [copy(acts[2].at[pl.ds(0, rows)], moved)]
     for i in range(2):
         columns = pl.ds(i * part, part)
         for j in range(4):
@@ -150,19 +148,30 @@
         for j in range(2):
             source = early[i].at[pl.ds(4 * half + j * late, late)]
             rest.append(copy(source, right.at[pl.ds(j * rows + half, late), columns]))
-    for made in first:
-        made.wait()
-    block = jnp.dot(held[...], basis[...], preferred_element_type=f32).astype(bf16)
-    right[pl.ds(2 * rows + half, late)] = block[:late]
-    right[pl.ds(3 * rows + half, late)] = block[late:]
-    total = jnp.concatenate([sums[0][0:1], sums[1][0:1]], axis=1)
     extra[...] = jnp.zeros_like(extra)
-    extra[0:1, :cols] = total + jnp.sum(jnp.square(block.astype(f32)), axis=0, keepdims=True)
     for i in range(4):
         extra[1:2, pl.ds(i * part, part)] = sums[i][2:3]
         extra[2:3, pl.ds(i * part, part)] = sums[i][1:2]
+    for made in first:
+        made.wait()
+    for i, basis in enumerate(bases):
+        columns = pl.ds(i * part, part)
+        block = jnp.dot(held[...], basis[...], preferred_element_type=f32).astype(bf16)
+        right[pl.ds(2 * rows + half, late), columns] = block[:late]
+        right[pl.ds(3 * rows + half, late), columns] = block[late:]
+        extra[0:1, columns] = sums[i][0:1] + jnp.sum(jnp.square(block.astype(f32)), axis=0, keepdims=True)
     for made in rest:
         made.wait()
+    return acts[0], acts[1], moved, acts[3]
+
+
+def chunk_of(right, columns, acts, rows):
+    return sum(
+        lax.dot_general(
+            right[pl.ds(i * rows, rows), columns], a[:rows], (((0,), (0,)), ((), ())), preferred_element_type=f32
+        )
+        for i, a in enumerate(acts)
+    )
 
 
 def with_sums(block, sums):
@@ -173,22 +182,21 @@
 def cross_kernel(levels, rows, where, *refs):
     acts, early, bases, pieces, sums = refs[:4], refs[4:6], refs[6:8], refs[8:10], refs[10:14]
     own, extra, messages = refs[14], refs[15], refs[16 : 15 + levels]
-    right, left, basis, held, whole, sems = refs[15 + levels :]
+    right, moved, held, whole, sems = refs[15 + levels :]
     chunk = right.shape[1] // levels
-    turn_late(rows, acts, early, bases, pieces, sums, right, left, basis, held, sems, extra)
-    whole[...] = lax.dot_general(right[...], left[...], (((0,), (0,)), ((), ())), preferred_element_type=f32)
+    acts = turn_late(rows, acts, early, bases, pieces, sums, right, moved, held, sems, extra)
+    whole[...] = chunk_of(right, slice(None), acts, rows)
     own[...] = whole[pl.ds(pl.multiple_of(where[0] * chunk, chunk), chunk)]
     for step in range(1, levels):
         block = whole[pl.ds(pl.multiple_of((where[0] ^ step) * chunk, chunk), chunk)]
         messages[step - 1][...] = with_sums(block, extra)
 
 
-def scratch(rows, width, width_g, cols):
-    return [
-        pltpu.VMEM((4 * rows, width), bf16),
-        pltpu.VMEM((width_g, cols), bf16),
-        pltpu.VMEM((2 * split(rows)[1], width_g), bf16),
-    ]
+GIVEN = [SMEM] + [VMEM] * 2 + [ANY] + [VMEM] + [ANY] * 2 + [VMEM] * 2 + [ANY] * 2 + [VMEM] * 4
+
+
+def scratch(rows, width, width_g):
+    return [pltpu.VMEM((rows, width), bf16), pltpu.VMEM((2 * split(rows)[1], width_g), bf16)]
 
 
 def cross(where, acts, early, bases, pieces, sums, rows, levels):
@@ -200,11 +208,11 @@
         functools.partial(cross_kernel, levels, rows),
         out_shape=[shape((chunk, width), f32), shape((8, width), f32)]
         + [shape((chunk + 8, width), bf16)] * (levels - 1),
-        in_specs=[SMEM] + [ANY] * 10 + [VMEM] * 4,
+        in_specs=GIVEN,
         out_specs=[VMEM] * (1 + levels),
         scratch_shapes=[pltpu.VMEM((4 * rows, cols), bf16)]
-        + scratch(rows, width, width_g, cols)
-        + [pltpu.VMEM((cols, width), f32), pltpu.SemaphoreType.DMA((20,))],
+        + scratch(rows, width, width_g)
+        + [pltpu.VMEM((cols, width), f32), pltpu.SemaphoreType.DMA((15,))],
         compiler_params=params(LARGE),
         cost_estimate=cost(8 * rows * cols * width, 16 * rows * width),
     )(where, *acts, *early, *bases, *pieces, *sums)
@@ -212,12 +220,11 @@
 
 def far_kernel(levels, rows, where, *refs):
     acts, early, bases, pieces, sums = refs[:4], refs[4:6], refs[6:8], refs[8:10], refs[10:14]
-    message, extra, right, left, basis, held, sems = refs[14:]
+    message, extra, right, moved, held, sems = refs[14:]
     chunk = right.shape[1] // levels
-    turn_late(rows, acts, early, bases, pieces, sums, right, left, basis, held, sems, extra)
+    acts = turn_late(rows, acts, early, bases, pieces, sums, right, moved, held, sems, extra)
     columns = pl.ds(pl.multiple_of((where[0] ^ 2) * chunk, chunk), chunk)
-    block = lax.dot_general(right[:, columns], left[...], (((0,), (0,)), ((), ())), preferred_element_type=f32)
-    message[...] = with_sums(block, extra)
+    message[...] = with_sums(chunk_of(right, columns, acts, rows), extra)
 
 
 def far(where, acts, early, bases, pieces, sums, rows, levels):
@@ -228,9 +235,9 @@
     return pl.pallas_call(
         functools.partial(far_kernel, levels, rows),
         out_shape=(shape((chunk + 8, width), bf16), shape((8, width), f32), shape((4 * rows, cols), bf16)),
-        in_specs=[SMEM] + [ANY] * 10 + [VMEM] * 4,
+        in_specs=GIVEN,
         out_specs=(VMEM,) * 3,
-        scratch_shapes=scratch(rows, width, width_g, cols) + [pltpu.SemaphoreType.DMA((20,))],
+        scratch_shapes=scratch(rows, width, width_g) + [pltpu.SemaphoreType.DMA((15,))],
         compiler_params=params(LARGE),
         cost_estimate=cost(2 * rows * cols * width, 16 * rows * width),
     )(where, *acts, *early, *bases, *pieces, *sums)
@@ -241,12 +248,7 @@
     chunk = right.shape[1] // levels
     for step, target in ((0, own), (1, message), (3, kept)):
         columns = pl.ds(pl.multiple_of((where[0] ^ step) * chunk, chunk), chunk)
-        block = sum(
-            lax.dot_general(
-                right[pl.ds(i * rows, rows), columns], a[:rows], (((0,), (0,)), ((), ())), preferred_element_type=f32
-            )
-            for i, a in enumerate(acts)
-        )
+        block = chunk_of(right, columns, acts, rows)
         target[...] = with_sums(block, extra) if step == 1 else block
 
 
@@ -328,17 +330,11 @@
 
 def result_kernel(levels, where, *refs):
     slots = refs[:levels]
-    one, two, outs, (mid, whole, sems) = refs[levels], refs[levels + 1], refs[levels + 2 : -3], refs[-3:]
+    one, two, outs, (mid, whole) = refs[levels], refs[levels + 1], refs[levels + 2 : -2], refs[-2:]
     chunk, height = slots[0].shape
     wide, part = one.shape
-    copies = []
     for step, slot in enumerate(slots):
-        row = pl.multiple_of((where[0] ^ step) * chunk, chunk)
-        copy = pltpu.make_async_copy(slot, mid.at[pl.ds(row, chunk)], sems.at[step])
-        copy.start()
-        copies.append(copy)
-    for copy in copies:
-        copy.wait()
+        mid[pl.ds(pl.multiple_of((where[0] ^ step) * chunk, chunk), chunk)] = slot[...]
     quarter = wide // 4
     for j in range(4):
         columns = pl.ds(j * quarter, quarter)
@@ -360,12 +356,11 @@
     return pl.pallas_call(
         functools.partial(result_kernel, levels),
         out_shape=[shape((height // 4, wide), t) for t in (bf16, bf16, f32, f32)],
-        in_specs=[SMEM] + [ANY] * levels + [VMEM] * 2,
+        in_specs=[SMEM] + [VMEM] * (levels + 2),
         out_specs=[VMEM] * 4,
         scratch_shapes=[
             pltpu.VMEM((2 * part, height), bf16),
             pltpu.VMEM((height, wide), f32),
-            pltpu.SemaphoreType.DMA((levels,)),
         ],
         compiler_params=params(SMALL),
         cost_estimate=cost(4 * height * part * wide, 4 * wide * part),

time: 119 us -> 119 us (level)
  no operation moved by 1% of the time
where the time goes in v10:
time: 119 us; the launch traced here: 118 us
  waiting for transfers between devices  57.1 us (48%)
  starting transfers between devices  33.7 us (28%)
  Pallas kernels  19.5 us (16%)
  other arithmetic  3.9 us (3%)
  local copies, waits for them, and re-layouts  3.1 us (3%)
    ppermute x8, waiting for transfers between devices, across(): return lax.ppermute(x, 'level', [(i, i ^ step) for i in range(levels)])  29.8 us
    ppermute x8, starting transfers between devices, across(): return lax.ppermute(x, 'level', [(i, i ^ step) for i in range(levels)])  13 us
    pallas_call x2, Pallas kernels, turn(): pl.pallas_call(functools.partial(turn_kernel, levels, level_g, level_a, r...  9.9 us
    ppermute x1, waiting for transfers between devices, body(): last = lax.ppermute((far_kept + far_sent).astype(bf16), 'chip', SWAP)  7.83 us
    ppermute x1, waiting for transfers between devices, gather_levels(): lax.ppermute(held, 'level', [(0, 3), (3, 0)])  7.8 us
    ppermute x4, waiting for transfers between devices, over(): return lax.ppermute(slot, 'group', SWAP)  6.38 us
    ppermute x4, starting transfers between devices, over(): return lax.ppermute(slot, 'group', SWAP)  6.06 us
    ppermute x1, starting transfers between devices, gather_levels(): lax.ppermute(held, 'level', [(0, 3), (3, 0)])  4.37 us
  transfers between devices with their start and end apart: 30, of which 20 were waited for; matrix products, arithmetic and copies ran while one was open for 3% of the time, Pallas kernels for 11%

profile of v10, /device:TPU:0, one launch (start us, length us, event | category | flops | bytes accessed | tf_op | source)
XLA Modules:
  0.0 118.2 jit_solution(5955499580205632400)
XLA Ops:
  0.0 0.9 constant_dynamic-slice_fusion.1
  0.9 1.0 constant_dynamic-slice_fusion.3
  2.4 2.6 %collective-permute-start.1 = (bf16[192,256]{1,0:T(8,128)(2,1)S(1)}, bf16[192,256]{1,0:T(8,128)(2,1)S(1)}, u32[]{:S(2)}, u32[]{:S(2)}) collective-permute-start(bf16[192,256]{1,0:T(8,128)(2,1)S(1)} %get-tuple-element.106), channel_id=1, source_target_pairs={{0,2},{2,0},{1,3},{3,1},{4,6},{6,4},{5,7},{7,5},{8,10},{10,8},{9,1... | collective-permute-start | bytes 294920 | tf_op jit(solution)/shard_map/ppermute | solution.py:408
  6.3 0.9 copy-done.1
  7.8 0.9 collective-permute-done.1
  8.7 1.9 %collective-permute-start.2 = (bf16[880,1024]{1,0:T(8,128)(2,1)S(1)}, bf16[880,1024]{1,0:T(8,128)(2,1)}, u32[]{:S(2)}, u32[]{:S(2)}) collective-permute-start(bf16[880,1024]{1,0:T(8,128)(2,1)S(1)} %pad_maximum_fusion.refs_4_.refs_0_), channel_id=1, source_target_pairs={{0,2},{2,0},{1,3},{3,1},{4,6},{6,4},{5,7},{7,5},{8,10},{10,8},{9,1... | collective-permute-start | bytes 5406728 | tf_op jit(solution)/shard_map/ppermute | solution.py:427
  10.8 1.6 %collective-permute-start.5 = (bf16[768,256]{1,0:T(8,128)(2,1)S(1)}, bf16[768,256]{1,0:T(8,128)(2,1)}, u32[]{:S(2)}, u32[]{:S(2)}) collective-permute-start(bf16[768,256]{1,0:T(8,128)(2,1)S(1)} %fusion.5.refs_0_), channel_id=1, source_target_pairs={{0,4},{4,0},{8,12},{12,8},{1,5},{5,1},{9,13},{13,9},{2,6},{6,2},{1... | collective-permute-start | bytes 1179656 | tf_op jit(solution)/shard_map/ppermute | solution.py:39
  12.5 0.7 collective-permute-start.6
  13.2 1.6 %collective-permute-start.7 = (bf16[768,256]{1,0:T(8,128)(2,1)S(1)}, bf16[768,256]{1,0:T(8,128)(2,1)S(1)}, u32[]{:S(2)}, u32[]{:S(2)}) collective-permute-start(bf16[768,256]{1,0:T(8,128)(2,1)S(1)} %fusion.5.refs_0_), channel_id=1, source_target_pairs={{0,16},{16,0},{1,17},{17,1},{2,18},{18,2},{3,19},{19,3},{4,20},{20... | collective-permute-start | bytes 1179656 | tf_op jit(solution)/shard_map/ppermute | solution.py:372
  14.7 1.2 slice_select_fusion.1.refs_8_
  15.9 6.0 %collective-permute-done.5.refs_1_ = bf16[768,256]{1,0:T(8,128)(2,1)} collective-permute-done((bf16[768,256]{1,0:T(8,128)(2,1)S(1)}, bf16[768,256]{1,0:T(8,128)(2,1)}, u32[]{:S(2)}, u32[]{:S(2)}) %collective-permute-start.5) | collective-permute-done | bytes 393248 | tf_op jit(solution)/shard_map/ppermute | solution.py:39
  21.9 2.1 %collective-permute-done.7.refs_0_ = bf16[768,256]{1,0:T(8,128)(2,1)S(1)} collective-permute-done((bf16[768,256]{1,0:T(8,128)(2,1)S(1)}, bf16[768,256]{1,0:T(8,128)(2,1)S(1)}, u32[]{:S(2)}, u32[]{:S(2)}) %collective-permute-start.7) | collective-permute-done | bytes 393248 | tf_op jit(solution)/shard_map/ppermute | solution.py:372
  24.0 4.4 %collective-permute-start.8 = (bf16[768,256]{1,0:T(8,128)(2,1)S(1)}, bf16[768,256]{1,0:T(8,128)(2,1)}, u32[]{:S(2)}, u32[]{:S(2)}) collective-permute-start(bf16[768,256]{1,0:T(8,128)(2,1)S(1)} %fusion.5.refs_0_), channel_id=1, source_target_pairs={{0,12},{12,0},{1,13},{13,1},{2,14},{14,2},{3,15},{15,3},{16,28},{2... | collective-permute-start | bytes 1179656 | tf_op jit(solution)/shard_map/ppermute | solution.py:382
  28.4 1.6 %collective-permute-start.9 = (bf16[768,256]{1,0:T(8,128)(2,1)}, bf16[768,256]{1,0:T(8,128)(2,1)}, u32[]{:S(2)}, u32[]{:S(2)}) collective-permute-start(bf16[768,256]{1,0:T(8,128)(2,1)} %collective-permute-done.5.refs_1_), channel_id=1, source_target_pairs={{0,16},{16,0},{1,17},{17,1},{2,18},{18,2},{3,19},{19,3},{4,20},{20... | collective-permute-start | bytes 1179656 | tf_op jit(solution)/shard_map/ppermute | solution.py:372
  29.9 7.8 %collective-permute-done.8 = bf16[768,256]{1,0:T(8,128)(2,1)} collective-permute-done((bf16[768,256]{1,0:T(8,128)(2,1)S(1)}, bf16[768,256]{1,0:T(8,128)(2,1)}, u32[]{:S(2)}, u32[]{:S(2)}) %collective-permute-start.8) | collective-permute-done | bytes 393248 | tf_op jit(solution)/shard_map/ppermute | solution.py:382
  37.7 0.8 collective-permute-done.9.refs_1_
  38.6 1.0 broadcast_select_fusion.1.refs_3_
  39.6 0.9 collective-permute-start.10
  40.5 1.5 %collective-permute-start.11 = (bf16[768,256]{1,0:T(8,128)(2,1)S(1)}, bf16[768,256]{1,0:T(8,128)(2,1)S(1)}, u32[]{:S(2)}, u32[]{:S(2)}) collective-permute-start(bf16[768,256]{1,0:T(8,128)(2,1)S(1)} %broadcast_select_fusion.1.refs_3_), channel_id=1, source_target_pairs={{0,16},{16,0},{1,17},{17,1},{2,18},{18,2},{3,19},{19,3},{4,20},{20... | collective-permute-start | bytes 1179656 | tf_op jit(solution)/shard_map/ppermute | solution.py:372
  42.0 6.5 %collective-permute-done.10.refs_2_ = bf16[768,256]{1,0:T(8,128)(2,1)S(1)} collective-permute-done((bf16[768,256]{1,0:T(8,128)(2,1)S(1)}, bf16[768,256]{1,0:T(8,128)(2,1)S(1)}, u32[]{:S(2)}, u32[]{:S(2)}) %collective-permute-start.10) | collective-permute-done | bytes 393248 | tf_op jit(solution)/shard_map/ppermute | solution.py:39
  49.0 0.7 collective-permute-done.2.refs_6_.refs_2_
  50.2 1.6 %collective-permute-start.15 = (bf16[144,2048]{1,0:T(8,128)(2,1)S(1)}, bf16[144,2048]{1,0:T(8,128)(2,1)S(1)}, u32[]{:S(2)}, u32[]{:S(2)}) collective-permute-start(bf16[144,2048]{1,0:T(8,128)(2,1)S(1)} %slice_select_fusion.1.refs_8_), channel_id=1, source_target_pairs={{0,2},{2,0},{1,3},{3,1},{4,6},{6,4},{5,7},{7,5},{8,10},{10,8},{9,1... | collective-permute-start | bytes 1769480 | tf_op jit(solution)/shard_map/ppermute | solution.py:433
  51.8 1.5 %collective-permute-start.13 = (bf16[768,256]{1,0:T(8,128)(2,1)S(1)}, bf16[768,256]{1,0:T(8,128)(2,1)S(1)}, u32[]{:S(2)}, u32[]{:S(2)}) collective-permute-start(bf16[768,256]{1,0:T(8,128)(2,1)S(1)} %collective-permute-done.10.refs_2_), channel_id=1, source_target_pairs={{0,16},{16,0},{1,17},{17,1},{2,18},{18,2},{3,19},{19,3},{4,20},{20... | collective-permute-start | bytes 1179656 | tf_op jit(solution)/shard_map/ppermute | solution.py:372
  53.3 0.6 collective-permute-done.14.refs_9_
  53.9 0.6 collective-permute-done.12.refs_7_.refs_3_
  54.5 5.0 %shard_map.55 = (bf16[1024,256]{1,0:T(8,128)(2,1)S(1)}, bf16[1248,256]{1,0:T(8,128)(2,1)S(1)}, bf16[2048,256]{1,0:T(8,128)(2,1)S(1)}, f32[8,256]{1,0:T(8,128)S(1)}) custom-call(s32[2]{0:T(128)S(1)} %pad_add_fusion.where, bf16[768,256]{1,0:T(8,128)(2,1)S(1)} %fusion.5.refs_0_, bf16[768,256]{1,0:T(8,128)(2,1)} %collective-permute-done.5.refs_1_, ...), custom_call_target="tpu_custom_call" | custom-call | flops 1610612736 | bytes 6291456 | tf_op jit(solution)/shard_map/pallas_call | solution.py:105
  59.5 3.1 %collective-permute-done.13.refs_2_ = bf16[768,256]{1,0:T(8,128)(2,1)S(1)} collective-permute-done((bf16[768,256]{1,0:T(8,128)(2,1)S(1)}, bf16[768,256]{1,0:T(8,128)(2,1)S(1)}, u32[]{:S(2)}, u32[]{:S(2)}) %collective-permute-start.13) | collective-permute-done | bytes 393248 | tf_op jit(solution)/shard_map/ppermute | solution.py:372
  62.5 5.0 %shard_map.56 = (bf16[1024,256]{1,0:T(8,128)(2,1)S(1)}, bf16[1248,256]{1,0:T(8,128)(2,1)S(1)}, bf16[2048,256]{1,0:T(8,128)(2,1)S(1)}, f32[8,256]{1,0:T(8,128)S(1)}) custom-call(s32[2]{0:T(128)S(1)} %pad_add_fusion.where, bf16[768,256]{1,0:T(8,128)(2,1)S(1)} %collective-permute-done.7.refs_0_, bf16[768,256]{1,0:T(8,128)(2,1)} %collective-permute-done.9.refs_1_, ...), custom_call_target="tpu_custom_call" | custom-call | flops 1610612736 | bytes 6291456 | tf_op jit(solution)/shard_map/pallas_call | solution.py:105
  68.2 1.4 %collective-permute-done.18.refs_13_ = f32[8,256]{1,0:T(8,128)S(1)} collective-permute-done((f32[8,256]{1,0:T(8,128)S(1)}, f32[8,256]{1,0:T(8,128)S(1)}, u32[]{:S(2)}, u32[]{:S(2)}) %collective-permute-start.18) | collective-permute-done | bytes 8224 | tf_op jit(solution)/shard_map/ppermute | solution.py:436
  69.6 2.8 %shard_map.57 = (bf16[136,1024]{1,0:T(8,128)(2,1)S(1)}, f32[8,1024]{1,0:T(8,128)S(1)}, bf16[1536,512]{1,0:T(8,128)(2,1)S(1)}) custom-call(s32[2]{0:T(128)S(1)} %pad_add_fusion.where, bf16[880,1024]{1,0:T(8,128)(2,1)S(1)} %pad_maximum_fusion.refs_4_.refs_0_, bf16[880,1024]{1,0:T(8,128)(2,1)S(1)} %collective-permute-done.refs_5_.refs_1_, ...), custom_call_target="tpu_custom_call" | custom-call | flops 402653184 | bytes 6291456 | tf_op jit(solution)/shard_map/pallas_call | solution.py:235
  72.4 1.6 %collective-permute-start.19 = (bf16[136,1024]{1,0:T(8,128)(2,1)S(1)}, bf16[136,1024]{1,0:T(8,128)(2,1)S(1)}, u32[]{:S(2)}, u32[]{:S(2)}) collective-permute-start(bf16[136,1024]{1,0:T(8,128)(2,1)S(1)} %get-tuple-element.85), channel_id=1, source_target_pairs={{0,4},{4,0},{8,12},{12,8},{1,5},{5,1},{9,13},{13,9},{2,6},{6,2},{1... | collective-permute-start | bytes 835592 | tf_op jit(solution)/shard_map/ppermute | solution.py:39
  74.5 3.3 %shard_map.58 = (f32[128,1024]{1,0:T(8,128)S(1)}, bf16[136,1024]{1,0:T(8,128)(2,1)S(1)}, f32[128,1024]{1,0:T(8,128)S(1)}) custom-call(s32[2]{0:T(128)S(1)} %pad_add_fusion.where, bf16[1536,512]{1,0:T(8,128)(2,1)S(1)} %get-tuple-element.81.right, f32[8,1024]{1,0:T(8,128)S(1)} %get-tuple-element.82.extra.own_extra, ...), custom_call_target="tpu_custom_call" | custom-call | flops 1207959552 | bytes 6291456 | tf_op jit(solution)/shard_map/pallas_call | solution.py:258
  77.9 0.6 collective-permute-start.21
  78.4 3.4 %collective-permute-done.19.got = bf16[136,1024]{1,0:T(8,128)(2,1)S(1)} collective-permute-done((bf16[136,1024]{1,0:T(8,128)(2,1)S(1)}, bf16[136,1024]{1,0:T(8,128)(2,1)S(1)}, u32[]{:S(2)}, u32[]{:S(2)}) %collective-permute-start.19) | collective-permute-done | bytes 278560 | tf_op jit(solution)/shard_map/ppermute | solution.py:39
  81.9 3.8 %collective-permute-start.20 = (bf16[136,1024]{1,0:T(8,128)(2,1)S(1)}, bf16[136,1024]{1,0:T(8,128)(2,1)S(1)}, u32[]{:S(2)}, u32[]{:S(2)}) collective-permute-start(bf16[136,1024]{1,0:T(8,128)(2,1)S(1)} %shard_map.59), channel_id=1, source_target_pairs={{0,12},{4,8},{8,4},{12,0},{1,13},{5,9},{9,5},{13,1},{2,14},{6,10},... | collective-permute-start | bytes 835592 | tf_op jit(solution)/shard_map/ppermute | solution.py:39
  85.7 1.5 %collective-permute-done.21.refs_1_ = bf16[136,1024]{1,0:T(8,128)(2,1)S(1)} collective-permute-done((bf16[136,1024]{1,0:T(8,128)(2,1)S(1)}, bf16[136,1024]{1,0:T(8,128)(2,1)S(1)}, u32[]{:S(2)}, u32[]{:S(2)}) %collective-permute-start.21) | collective-permute-done | bytes 278560 | tf_op jit(solution)/shard_map/ppermute | solution.py:39
  87.2 8.0 %collective-permute-done.20.refs_0_ = bf16[136,1024]{1,0:T(8,128)(2,1)S(1)} collective-permute-done((bf16[136,1024]{1,0:T(8,128)(2,1)S(1)}, bf16[136,1024]{1,0:T(8,128)(2,1)S(1)}, u32[]{:S(2)}, u32[]{:S(2)}) %collective-permute-start.20) | collective-permute-done | bytes 278560 | tf_op jit(solution)/shard_map/ppermute | solution.py:39
  95.2 1.9 %shard_map.60 = (bf16[128,256]{1,0:T(8,128)(2,1)S(1)}, bf16[128,256]{1,0:T(8,128)(2,1)S(1)}, bf16[128,256]{1,0:T(8,128)(2,1)S(1)}, bf16[128,256]{1,0:T(8,128)(2,1)S(1)}) custom-call(s32[2]{0:T(128)S(1)} %pad_add_fusion.where, f32[128,1024]{1,0:T(8,128)S(1)} %get-tuple-element.83.own, f32[8,1024]{1,0:T(8,128)S(1)} %get-tuple-element.82.extra.own_extra, ...), custom_call_target="tpu_custom_call" | custom-call | flops 805306368 | bytes 2097152 | tf_op jit(solution)/shard_map/pallas_call | solution.py:320
  97.1 1.6 %collective-permute-start.24 = (bf16[128,256]{1,0:T(8,128)(2,1)S(1)}, bf16[128,256]{1,0:T(8,128)(2,1)S(1)}, u32[]{:S(2)}, u32[]{:S(2)}) collective-permute-start(bf16[128,256]{1,0:T(8,128)(2,1)S(1)} %get-tuple-element.90), channel_id=1, source_target_pairs={{0,4},{4,0},{8,12},{12,8},{1,5},{5,1},{9,13},{13,9},{2,6},{6,2},{1... | collective-permute-start | bytes 196616 | tf_op jit(solution)/shard_map/ppermute | solution.py:39
  98.7 1.1 collective-permute-start.25
  99.8 1.8 %collective-permute-start.26 = (bf16[128,256]{1,0:T(8,128)(2,1)S(1)}, bf16[128,256]{1,0:T(8,128)(2,1)S(1)}, u32[]{:S(2)}, u32[]{:S(2)}) collective-permute-start(bf16[128,256]{1,0:T(8,128)(2,1)S(1)} %get-tuple-element.92), channel_id=1, source_target_pairs={{0,12},{4,8},{8,4},{12,0},{1,13},{5,9},{9,5},{13,1},{2,14},{6,10},... | collective-permute-start | bytes 196616 | tf_op jit(solution)/shard_map/ppermute | solution.py:39
  101.7 2.9 %collective-permute-done.25.refs_2_ = bf16[128,256]{1,0:T(8,128)(2,1)S(1)} collective-permute-done((bf16[128,256]{1,0:T(8,128)(2,1)S(1)}, bf16[128,256]{1,0:T(8,128)(2,1)S(1)}, u32[]{:S(2)}, u32[]{:S(2)}) %collective-permute-start.25) | collective-permute-done | bytes 65568 | tf_op jit(solution)/shard_map/ppermute | solution.py:39
  104.6 1.3 %collective-permute-done.26.refs_3_ = bf16[128,256]{1,0:T(8,128)(2,1)S(1)} collective-permute-done((bf16[128,256]{1,0:T(8,128)(2,1)S(1)}, bf16[128,256]{1,0:T(8,128)(2,1)S(1)}, u32[]{:S(2)}, u32[]{:S(2)}) %collective-permute-start.26) | collective-permute-done | bytes 65568 | tf_op jit(solution)/shard_map/ppermute | solution.py:39
  105.9 1.4 %shard_map.61 = (bf16[64,2048]{1,0:T(8,128)(2,1)S(1)}, bf16[64,2048]{1,0:T(8,128)(2,1)S(1)}, f32[64,2048]{1,0:T(8,128)S(1)}, f32[64,2048]{1,0:T(8,128)S(1)}) custom-call(s32[2]{0:T(128)S(1)} %pad_add_fusion.where, bf16[128,256]{1,0:T(8,128)(2,1)S(1)} %get-tuple-element.89.refs_0_, bf16[128,256]{1,0:T(8,128)(2,1)S(1)} %collective-permute-done.24.refs_1_, ...), custom_call_target="tpu_custom_call" | custom-call | flops 536870912 | bytes 2097152 | tf_op jit(solution)/shard_map/pallas_call | solution.py:356
  108.0 1.0 collective-permute-done.28
  109.0 0.6 collective-permute-start.29
  109.6 7.8 %collective-permute-done.29 = bf16[64,2048]{1,0:T(8,128)(2,1)S(1)} collective-permute-done((bf16[64,2048]{1,0:T(8,128)(2,1)S(1)}, bf16[64,2048]{1,0:T(8,128)(2,1)S(1)}, u32[]{:S(2)}, u32[]{:S(2)}) %collective-permute-start.29) | collective-permute-done | bytes 262176 | tf_op jit(solution)/shard_map/ppermute | solution.py:452
  117.5 0.8 add_convert_fusion
  (53 shorter events, 4.7 us)
Async XLA Ops:
  0.0 5.9 %copy-start = (bf16[384,2048]{1,0:T(8,128)(2,1)S(1)}, bf16[384,2048]{1,0:T(8,128)(2,1)}, u32[]{:S(2)}) copy-start(bf16[384,2048]{1,0:T(8,128)(2,1)} %param.6) | copy-start | bytes 4718596
  1.9 8.7 %collective-permute-start.3 = (bf16[192,256]{1,0:T(8,128)(2,1)S(1)}, bf16[192,256]{1,0:T(8,128)(2,1)S(1)}, u32[]{:S(2)}, u32[]{:S(2)}) collective-permute-start(bf16[192,256]{1,0:T(8,128)(2,1)S(1)} %get-tuple-element.107), channel_id=1, source_target_pairs={{0,1},{1,0},{2,3},{3,2},{4,5},{5,4},{6,7},{7,6},{8,9},{9,8},{10,11... | collective-permute-start | bytes 294920 | tf_op jit(solution)/shard_map/ppermute | solution.py:409
  2.4 6.2 %collective-permute-start.1 = (bf16[192,256]{1,0:T(8,128)(2,1)S(1)}, bf16[192,256]{1,0:T(8,128)(2,1)S(1)}, u32[]{:S(2)}, u32[]{:S(2)}) collective-permute-start(bf16[192,256]{1,0:T(8,128)(2,1)S(1)} %get-tuple-element.106), channel_id=1, source_target_pairs={{0,2},{2,0},{1,3},{3,1},{4,6},{6,4},{5,7},{7,5},{8,10},{10,8},{9,1... | collective-permute-start | bytes 294920 | tf_op jit(solution)/shard_map/ppermute | solution.py:408
  5.0 5.6 %collective-permute-start.4 = (bf16[192,256]{1,0:T(8,128)(2,1)S(1)}, bf16[192,256]{1,0:T(8,128)(2,1)S(1)}, u32[]{:S(2)}, u32[]{:S(2)}) collective-permute-start(bf16[192,256]{1,0:T(8,128)(2,1)S(1)} %get-tuple-element.108), channel_id=1, source_target_pairs={{0,3},{1,2},{2,1},{3,0},{4,7},{5,6},{6,5},{7,4},{8,11},{9,10},{10,... | collective-permute-start | bytes 294920 | tf_op jit(solution)/shard_map/ppermute | solution.py:406
  6.1 1.1 copy-start.1
  8.7 41.0 %collective-permute-start.2 = (bf16[880,1024]{1,0:T(8,128)(2,1)S(1)}, bf16[880,1024]{1,0:T(8,128)(2,1)}, u32[]{:S(2)}, u32[]{:S(2)}) collective-permute-start(bf16[880,1024]{1,0:T(8,128)(2,1)S(1)} %pad_maximum_fusion.refs_4_.refs_0_), channel_id=1, source_target_pairs={{0,2},{2,0},{1,3},{3,1},{4,6},{6,4},{5,7},{7,5},{8,10},{10,8},{9,1... | collective-permute-start | bytes 5406728 | tf_op jit(solution)/shard_map/ppermute | solution.py:427
  10.8 11.1 %collective-permute-start.5 = (bf16[768,256]{1,0:T(8,128)(2,1)S(1)}, bf16[768,256]{1,0:T(8,128)(2,1)}, u32[]{:S(2)}, u32[]{:S(2)}) collective-permute-start(bf16[768,256]{1,0:T(8,128)(2,1)S(1)} %fusion.5.refs_0_), channel_id=1, source_target_pairs={{0,4},{4,0},{8,12},{12,8},{1,5},{5,1},{9,13},{13,9},{2,6},{6,2},{1... | collective-permute-start | bytes 1179656 | tf_op jit(solution)/shard_map/ppermute | solution.py:39
  12.5 9.4 %collective-permute-start.6 = (bf16[768,256]{1,0:T(8,128)(2,1)S(1)}, bf16[768,256]{1,0:T(8,128)(2,1)S(1)}, u32[]{:S(2)}, u32[]{:S(2)}) collective-permute-start(bf16[768,256]{1,0:T(8,128)(2,1)S(1)} %fusion.5.refs_0_), channel_id=1, source_target_pairs={{4,8},{8,4},{5,9},{9,5},{6,10},{10,6},{7,11},{11,7},{20,24},{24,20... | collective-permute-start | bytes 1179656 | tf_op jit(solution)/shard_map/ppermute | solution.py:379
  13.2 10.8 %collective-permute-start.7 = (bf16[768,256]{1,0:T(8,128)(2,1)S(1)}, bf16[768,256]{1,0:T(8,128)(2,1)S(1)}, u32[]{:S(2)}, u32[]{:S(2)}) collective-permute-start(bf16[768,256]{1,0:T(8,128)(2,1)S(1)} %fusion.5.refs_0_), channel_id=1, source_target_pairs={{0,16},{16,0},{1,17},{17,1},{2,18},{18,2},{3,19},{19,3},{4,20},{20... | collective-permute-start | bytes 1179656 | tf_op jit(solution)/shard_map/ppermute | solution.py:372
  21.9 2.1 %copy-start.2 = (bf16[768,256]{1,0:T(8,128)(2,1)}, bf16[768,256]{1,0:T(8,128)(2,1)S(1)}, u32[]{:S(2)}) copy-start(bf16[768,256]{1,0:T(8,128)(2,1)S(1)} %collective-permute-done.6) | copy-start | bytes 1179652
  24.0 13.7 %collective-permute-start.8 = (bf16[768,256]{1,0:T(8,128)(2,1)S(1)}, bf16[768,256]{1,0:T(8,128)(2,1)}, u32[]{:S(2)}, u32[]{:S(2)}) collective-permute-start(bf16[768,256]{1,0:T(8,128)(2,1)S(1)} %fusion.5.refs_0_), channel_id=1, source_target_pairs={{0,12},{12,0},{1,13},{13,1},{2,14},{14,2},{3,15},{15,3},{16,28},{2... | collective-permute-start | bytes 1179656 | tf_op jit(solution)/shard_map/ppermute | solution.py:382
  28.4 10.2 %collective-permute-start.9 = (bf16[768,256]{1,0:T(8,128)(2,1)}, bf16[768,256]{1,0:T(8,128)(2,1)}, u32[]{:S(2)}, u32[]{:S(2)}) collective-permute-start(bf16[768,256]{1,0:T(8,128)(2,1)} %collective-permute-done.5.refs_1_), channel_id=1, source_target_pairs={{0,16},{16,0},{1,17},{17,1},{2,18},{18,2},{3,19},{19,3},{4,20},{20... | collective-permute-start | bytes 1179656 | tf_op jit(solution)/shard_map/ppermute | solution.py:372
  39.6 9.0 %collective-permute-start.10 = (bf16[768,256]{1,0:T(8,128)(2,1)S(1)}, bf16[768,256]{1,0:T(8,128)(2,1)S(1)}, u32[]{:S(2)}, u32[]{:S(2)}) collective-permute-start(bf16[768,256]{1,0:T(8,128)(2,1)S(1)} %broadcast_select_fusion.1.refs_3_), channel_id=1, source_target_pairs={{0,4},{4,0},{8,12},{12,8},{1,5},{5,1},{9,13},{13,9},{2,6},{6,2},{1... | collective-permute-start | bytes 1179656 | tf_op jit(solution)/shard_map/ppermute | solution.py:39
  40.5 8.4 %collective-permute-start.11 = (bf16[768,256]{1,0:T(8,128)(2,1)S(1)}, bf16[768,256]{1,0:T(8,128)(2,1)S(1)}, u32[]{:S(2)}, u32[]{:S(2)}) collective-permute-start(bf16[768,256]{1,0:T(8,128)(2,1)S(1)} %broadcast_select_fusion.1.refs_3_), channel_id=1, source_target_pairs={{0,16},{16,0},{1,17},{17,1},{2,18},{18,2},{3,19},{19,3},{4,20},{20... | collective-permute-start | bytes 1179656 | tf_op jit(solution)/shard_map/ppermute | solution.py:372
  42.0 11.9 %collective-permute-start = (bf16[880,1024]{1,0:T(8,128)(2,1)S(1)}, bf16[880,1024]{1,0:T(8,128)(2,1)S(1)}, u32[]{:S(2)}, u32[]{:S(2)}) collective-permute-start(bf16[880,1024]{1,0:T(8,128)(2,1)S(1)} %pad_maximum_fusion.refs_4_.refs_0_), channel_id=1, source_target_pairs={{0,1},{1,0},{2,3},{3,2},{4,5},{5,4},{6,7},{7,6},{8,9},{9,8},{10,11... | collective-permute-start | bytes 5406728 | tf_op jit(solution)/shard_map/ppermute | solution.py:428
  49.7 4.8 %collective-permute-start.12 = (bf16[880,1024]{1,0:T(8,128)(2,1)}, bf16[880,1024]{1,0:T(8,128)(2,1)S(1)}, u32[]{:S(2)}, u32[]{:S(2)}) collective-permute-start(bf16[880,1024]{1,0:T(8,128)(2,1)} %collective-permute-done.2.refs_6_.refs_2_), channel_id=1, source_target_pairs={{0,1},{1,0},{2,3},{3,2},{4,5},{5,4},{6,7},{7,6},{8,9},{9,8},{10,11... | collective-permute-start | bytes 5406728 | tf_op jit(solution)/shard_map/ppermute | solution.py:428
  49.7 4.2 %collective-permute-start.14 = (bf16[144,2048]{1,0:T(8,128)(2,1)S(1)}, bf16[144,2048]{1,0:T(8,128)(2,1)S(1)}, u32[]{:S(2)}, u32[]{:S(2)}) collective-permute-start(bf16[144,2048]{1,0:T(8,128)(2,1)S(1)} %slice_select_fusion.1.refs_8_), channel_id=1, source_target_pairs={{0,1},{1,0},{2,3},{3,2},{4,5},{5,4},{6,7},{7,6},{8,9},{9,8},{10,11... | collective-permute-start | bytes 1769480 | tf_op jit(solution)/shard_map/ppermute | solution.py:429
  50.2 17.3 %collective-permute-start.15 = (bf16[144,2048]{1,0:T(8,128)(2,1)S(1)}, bf16[144,2048]{1,0:T(8,128)(2,1)S(1)}, u32[]{:S(2)}, u32[]{:S(2)}) collective-permute-start(bf16[144,2048]{1,0:T(8,128)(2,1)S(1)} %slice_select_fusion.1.refs_8_), channel_id=1, source_target_pairs={{0,2},{2,0},{1,3},{3,1},{4,6},{6,4},{5,7},{7,5},{8,10},{10,8},{9,1... | collective-permute-start | bytes 1769480 | tf_op jit(solution)/shard_map/ppermute | solution.py:433
  51.8 10.7 %collective-permute-start.13 = (bf16[768,256]{1,0:T(8,128)(2,1)S(1)}, bf16[768,256]{1,0:T(8,128)(2,1)S(1)}, u32[]{:S(2)}, u32[]{:S(2)}) collective-permute-start(bf16[768,256]{1,0:T(8,128)(2,1)S(1)} %collective-permute-done.10.refs_2_), channel_id=1, source_target_pairs={{0,16},{16,0},{1,17},{17,1},{2,18},{18,2},{3,19},{19,3},{4,20},{20... | collective-permute-start | bytes 1179656 | tf_op jit(solution)/shard_map/ppermute | solution.py:372
  67.5 2.1 %collective-permute-start.16 = (bf16[144,2048]{1,0:T(8,128)(2,1)S(1)}, bf16[144,2048]{1,0:T(8,128)(2,1)S(1)}, u32[]{:S(2)}, u32[]{:S(2)}) collective-permute-start(bf16[144,2048]{1,0:T(8,128)(2,1)S(1)} %collective-permute-done.15.refs_8_), channel_id=1, source_target_pairs={{0,1},{1,0},{2,3},{3,2},{4,5},{5,4},{6,7},{7,6},{8,9},{9,8},{10,11... | collective-permute-start | bytes 1769480 | tf_op jit(solution)/shard_map/ppermute | solution.py:434
  67.6 2.0 %collective-permute-start.18 = (f32[8,256]{1,0:T(8,128)S(1)}, f32[8,256]{1,0:T(8,128)S(1)}, u32[]{:S(2)}, u32[]{:S(2)}) collective-permute-start(f32[8,256]{1,0:T(8,128)S(1)} %get-tuple-element.80.refs_11_), channel_id=1, source_target_pairs={{0,1},{1,0},{2,3},{3,2},{4,5},{5,4},{6,7},{7,6},{8,9},{9,8},{10,11... | collective-permute-start | bytes 24584 | tf_op jit(solution)/shard_map/ppermute | solution.py:436
  68.1 1.5 %collective-permute-start.17 = (f32[8,256]{1,0:T(8,128)S(1)}, f32[8,256]{1,0:T(8,128)S(1)}, u32[]{:S(2)}, u32[]{:S(2)}) collective-permute-start(f32[8,256]{1,0:T(8,128)S(1)} %get-tuple-element.79.refs_10_), channel_id=1, source_target_pairs={{0,1},{1,0},{2,3},{3,2},{4,5},{5,4},{6,7},{7,6},{8,9},{9,8},{10,11... | collective-permute-start | bytes 24584 | tf_op jit(solution)/shard_map/ppermute | solution.py:436
  72.4 9.4 %collective-permute-start.19 = (bf16[136,1024]{1,0:T(8,128)(2,1)S(1)}, bf16[136,1024]{1,0:T(8,128)(2,1)S(1)}, u32[]{:S(2)}, u32[]{:S(2)}) collective-permute-start(bf16[136,1024]{1,0:T(8,128)(2,1)S(1)} %get-tuple-element.85), channel_id=1, source_target_pairs={{0,4},{4,0},{8,12},{12,8},{1,5},{5,1},{9,13},{13,9},{2,6},{6,2},{1... | collective-permute-start | bytes 835592 | tf_op jit(solution)/shard_map/ppermute | solution.py:39
  74.0 11.6 %collective-permute-start.23 = (bf16[1024,256]{1,0:T(8,128)(2,1)S(1)}, bf16[1024,256]{1,0:T(8,128)(2,1)S(1)}, u32[]{:S(2)}, u32[]{:S(2)}) collective-permute-start(bf16[1024,256]{1,0:T(8,128)(2,1)S(1)} %get-tuple-element.88.refs_3_), channel_id=1, source_target_pairs={{0,1},{1,0},{2,3},{3,2},{4,5},{5,4},{6,7},{7,6},{8,9},{9,8},{10,11... | collective-permute-start | bytes 1572872 | tf_op jit(solution)/shard_map/ppermute | solution.py:437
  74.0 11.6 %collective-permute-start.22 = (bf16[1024,256]{1,0:T(8,128)(2,1)S(1)}, bf16[1024,256]{1,0:T(8,128)(2,1)S(1)}, u32[]{:S(2)}, u32[]{:S(2)}) collective-permute-start(bf16[1024,256]{1,0:T(8,128)(2,1)S(1)} %get-tuple-element.87.refs_2_), channel_id=1, source_target_pairs={{0,1},{1,0},{2,3},{3,2},{4,5},{5,4},{6,7},{7,6},{8,9},{9,8},{10,11... | collective-permute-start | bytes 1572872 | tf_op jit(solution)/shard_map/ppermute | solution.py:437
  77.9 9.3 %collective-permute-start.21 = (bf16[136,1024]{1,0:T(8,128)(2,1)S(1)}, bf16[136,1024]{1,0:T(8,128)(2,1)S(1)}, u32[]{:S(2)}, u32[]{:S(2)}) collective-permute-start(bf16[136,1024]{1,0:T(8,128)(2,1)S(1)} %get-tuple-element.86), channel_id=1, source_target_pairs={{0,4},{4,0},{8,12},{12,8},{1,5},{5,1},{9,13},{13,9},{2,6},{6,2},{1... | collective-permute-start | bytes 835592 | tf_op jit(solution)/shard_map/ppermute | solution.py:39
  81.9 13.3 %collective-permute-start.20 = (bf16[136,1024]{1,0:T(8,128)(2,1)S(1)}, bf16[136,1024]{1,0:T(8,128)(2,1)S(1)}, u32[]{:S(2)}, u32[]{:S(2)}) collective-permute-start(bf16[136,1024]{1,0:T(8,128)(2,1)S(1)} %shard_map.59), channel_id=1, source_target_pairs={{0,12},{4,8},{8,4},{12,0},{1,13},{5,9},{9,5},{13,1},{2,14},{6,10},... | collective-permute-start | bytes 835592 | tf_op jit(solution)/shard_map/ppermute | solution.py:39
  97.1 4.6 %collective-permute-start.24 = (bf16[128,256]{1,0:T(8,128)(2,1)S(1)}, bf16[128,256]{1,0:T(8,128)(2,1)S(1)}, u32[]{:S(2)}, u32[]{:S(2)}) collective-permute-start(bf16[128,256]{1,0:T(8,128)(2,1)S(1)} %get-tuple-element.90), channel_id=1, source_target_pairs={{0,4},{4,0},{8,12},{12,8},{1,5},{5,1},{9,13},{13,9},{2,6},{6,2},{1... | collective-permute-start | bytes 196616 | tf_op jit(solution)/shard_map/ppermute | solution.py:39
  98.7 5.9 %collective-permute-start.25 = (bf16[128,256]{1,0:T(8,128)(2,1)S(1)}, bf16[128,256]{1,0:T(8,128)(2,1)S(1)}, u32[]{:S(2)}, u32[]{:S(2)}) collective-permute-start(bf16[128,256]{1,0:T(8,128)(2,1)S(1)} %get-tuple-element.91), channel_id=1, source_target_pairs={{0,8},{4,12},{8,0},{12,4},{1,9},{5,13},{9,1},{13,5},{2,10},{6,14},... | collective-permute-start | bytes 196616 | tf_op jit(solution)/shard_map/ppermute | solution.py:39
  99.8 6.2 %collective-permute-start.26 = (bf16[128,256]{1,0:T(8,128)(2,1)S(1)}, bf16[128,256]{1,0:T(8,128)(2,1)S(1)}, u32[]{:S(2)}, u32[]{:S(2)}) collective-permute-start(bf16[128,256]{1,0:T(8,128)(2,1)S(1)} %get-tuple-element.92), channel_id=1, source_target_pairs={{0,12},{4,8},{8,4},{12,0},{1,13},{5,9},{9,5},{13,1},{2,14},{6,10},... | collective-permute-start | bytes 196616 | tf_op jit(solution)/shard_map/ppermute | solution.py:39
  107.4 1.6 %collective-permute-start.28 = (bf16[64,2048]{1,0:T(8,128)(2,1)S(1)}, bf16[64,2048]{1,0:T(8,128)(2,1)S(1)}, u32[]{:S(2)}, u32[]{:S(2)}) collective-permute-start(bf16[64,2048]{1,0:T(8,128)(2,1)S(1)} %get-tuple-element.96), channel_id=1, source_target_pairs={{0,1},{1,0},{2,3},{3,2},{4,5},{5,4},{6,7},{7,6},{8,9},{9,8},{10,11... | collective-permute-start | bytes 786440 | tf_op jit(solution)/shard_map/ppermute | solution.py:451
  107.5 2.2 %collective-permute-start.27 = (bf16[64,2048]{1,0:T(8,128)(2,1)S(1)}, bf16[64,2048]{1,0:T(8,128)(2,1)S(1)}, u32[]{:S(2)}, u32[]{:S(2)}) collective-permute-start(bf16[64,2048]{1,0:T(8,128)(2,1)S(1)} %get-tuple-element.94), channel_id=1, source_target_pairs={{0,1},{1,0},{2,3},{3,2},{4,5},{5,4},{6,7},{7,6},{8,9},{9,8},{10,11... | collective-permute-start | bytes 786440 | tf_op jit(solution)/shard_map/ppermute | solution.py:451
  109.0 8.4 %collective-permute-start.29 = (bf16[64,2048]{1,0:T(8,128)(2,1)S(1)}, bf16[64,2048]{1,0:T(8,128)(2,1)S(1)}, u32[]{:S(2)}, u32[]{:S(2)}) collective-permute-start(bf16[64,2048]{1,0:T(8,128)(2,1)S(1)} %add_convert_fusion.1), channel_id=1, source_target_pairs={{0,2},{2,0},{1,3},{3,1},{4,6},{6,4},{5,7},{7,5},{8,10},{10,8},{9,1... | collective-permute-start | bytes 786440 | tf_op jit(solution)/shard_map/ppermute | solution.py:452

commit v11 on v10

--- a/solution.py
+++ b/solution.py
@@ -127,7 +127,30 @@
     return high, (v - high.astype(f32)).astype(bf16)
 
 
-def turn_late(rows, acts, early, bases, pieces, sums, right, moved, held, sems, extra):
+def turn_other_kernel(rows, one, two, out, sums):
+    part = one.shape[1]
+    sums[...] = jnp.zeros_like(sums)
+    for i, basis in enumerate((one, two)):
+        columns = pl.ds(i * part, part)
+        turned = jnp.dot(rows[...], basis[...], preferred_element_type=f32).astype(bf16)
+        out[:, columns] = turned
+        sums[0:1, columns] = jnp.sum(jnp.square(turned.astype(f32)), axis=0, keepdims=True)
+
+
+def turn_other(rows, bases):
+    height, width = rows.shape
+    part = bases[0].shape[1]
+    return pl.pallas_call(
+        turn_other_kernel,
+        out_shape=(shape((height, 2 * part), bf16), shape((8, 2 * part), f32)),
+        in_specs=[VMEM] * 3,
+        out_specs=(VMEM, VMEM),
+        compiler_params=params(SMALL),
+        cost_estimate=cost(4 * height * part * width, 2 * height * width),
+    )(rows, *bases)
+
+
+def turn_late(rows, acts, early, bases, pieces, sums, right, moved, sems, extra):
     half, late = split(rows)
     part = bases[0].shape[1]
     count = 0
@@ -139,8 +162,8 @@
         count += 1
         return made
 
-    first = [copy(p, held.at[pl.ds(i * late, late)]) for i, p in enumerate(pieces)]
-    rest = [copy(acts[2].at[pl.ds(0, rows)], moved)]
+    last, other, other_sums = pieces
+    rest = [copy(acts[2].at[pl.ds(0, rows)], moved), copy(other, right.at[pl.ds(2 * rows + half, late)])]
     for i in range(2):
         columns = pl.ds(i * part, part)
         for j in range(4):
@@ -152,14 +175,12 @@
     for i in range(4):
         extra[1:2, pl.ds(i * part, part)] = sums[i][2:3]
         extra[2:3, pl.ds(i * part, part)] = sums[i][1:2]
-    for made in first:
-        made.wait()
     for i, basis in enumerate(bases):
         columns = pl.ds(i * part, part)
-        block = jnp.dot(held[...], basis[...], preferred_element_type=f32).astype(bf16)
-        right[pl.ds(2 * rows + half, late), columns] = block[:late]
-        right[pl.ds(3 * rows + half, late), columns] = block[late:]
-        extra[0:1, columns] = sums[i][0:1] + jnp.sum(jnp.square(block.astype(f32)), axis=0, keepdims=True)
+        block = jnp.dot(last[...], basis[...], preferred_element_type=f32).astype(bf16)
+        right[pl.ds(3 * rows + half, late), columns] = block
+        total = sums[i][0:1] + other_sums[0:1, columns]
+        extra[0:1, columns] = total + jnp.sum(jnp.square(block.astype(f32)), axis=0, keepdims=True)
     for made in rest:
         made.wait()
     return acts[0], acts[1], moved, acts[3]
@@ -180,11 +201,11 @@
 
 
 def cross_kernel(levels, rows, where, *refs):
-    acts, early, bases, pieces, sums = refs[:4], refs[4:6], refs[6:8], refs[8:10], refs[10:14]
-    own, extra, messages = refs[14], refs[15], refs[16 : 15 + levels]
-    right, moved, held, whole, sems = refs[15 + levels :]
+    acts, early, bases, pieces, sums = refs[:4], refs[4:6], refs[6:8], refs[8:11], refs[11:15]
+    own, extra, messages = refs[15], refs[16], refs[17 : 16 + levels]
+    right, moved, whole, sems = refs[16 + levels :]
     chunk = right.shape[1] // levels
-    acts = turn_late(rows, acts, early, bases, pieces, sums, right, moved, held, sems, extra)
+    acts = turn_late(rows, acts, early, bases, pieces, sums, right, moved, sems, extra)
     whole[...] = chunk_of(right, slice(None), acts, rows)
     own[...] = whole[pl.ds(pl.multiple_of(where[0] * chunk, chunk), chunk)]
     for step in range(1, levels):
@@ -192,15 +213,11 @@
         messages[step - 1][...] = with_sums(block, extra)
 
 
-GIVEN = [SMEM] + [VMEM] * 2 + [ANY] + [VMEM] + [ANY] * 2 + [VMEM] * 2 + [ANY] * 2 + [VMEM] * 4
-
-
-def scratch(rows, width, width_g):
-    return [pltpu.VMEM((rows, width), bf16), pltpu.VMEM((2 * split(rows)[1], width_g), bf16)]
+GIVEN = [SMEM] + [VMEM] * 2 + [ANY] + [VMEM] + [ANY] * 2 + [VMEM] * 3 + [ANY] + [VMEM] * 5
 
 
 def cross(where, acts, early, bases, pieces, sums, rows, levels):
-    width_g, part = bases[0].shape
+    part = bases[0].shape[1]
     width = acts[0].shape[1]
     cols = 2 * part
     chunk = cols // levels
@@ -210,25 +227,28 @@
         + [shape((chunk + 8, width), bf16)] * (levels - 1),
         in_specs=GIVEN,
         out_specs=[VMEM] * (1 + levels),
-        scratch_shapes=[pltpu.VMEM((4 * rows, cols), bf16)]
-        + scratch(rows, width, width_g)
-        + [pltpu.VMEM((cols, width), f32), pltpu.SemaphoreType.DMA((15,))],
+        scratch_shapes=[
+            pltpu.VMEM((4 * rows, cols), bf16),
+            pltpu.VMEM((rows, width), bf16),
+            pltpu.VMEM((cols, width), f32),
+            pltpu.SemaphoreType.DMA((14,)),
+        ],
         compiler_params=params(LARGE),
         cost_estimate=cost(8 * rows * cols * width, 16 * rows * width),
     )(where, *acts, *early, *bases, *pieces, *sums)
 
 
 def far_kernel(levels, rows, where, *refs):
-    acts, early, bases, pieces, sums = refs[:4], refs[4:6], refs[6:8], refs[8:10], refs[10:14]
-    message, extra, right, moved, held, sems = refs[14:]
+    acts, early, bases, pieces, sums = refs[:4], refs[4:6], refs[6:8], refs[8:11], refs[11:15]
+    message, extra, right, moved, sems = refs[15:]
     chunk = right.shape[1] // levels
-    acts = turn_late(rows, acts, early, bases, pieces, sums, right, moved, held, sems, extra)
+    acts = turn_late(rows, acts, early, bases, pieces, sums, right, moved, sems, extra)
     columns = pl.ds(pl.multiple_of((where[0] ^ 2) * chunk, chunk), chunk)
     message[...] = with_sums(chunk_of(right, columns, acts, rows), extra)
 
 
 def far(where, acts, early, bases, pieces, sums, rows, levels):
-    width_g, part = bases[0].shape
+    part = bases[0].shape[1]
     width = acts[0].shape[1]
     cols = 2 * part
     chunk = cols // levels
@@ -237,7 +257,7 @@
         out_shape=(shape((chunk + 8, width), bf16), shape((8, width), f32), shape((4 * rows, cols), bf16)),
         in_specs=GIVEN,
         out_specs=(VMEM,) * 3,
-        scratch_shapes=scratch(rows, width, width_g) + [pltpu.SemaphoreType.DMA((15,))],
+        scratch_shapes=[pltpu.VMEM((rows, width), bf16), pltpu.SemaphoreType.DMA((14,))],
         compiler_params=params(LARGE),
         cost_estimate=cost(2 * rows * cols * width, 16 * rows * width),
     )(where, *acts, *early, *bases, *pieces, *sums)
@@ -428,12 +448,13 @@
     early = [early, lax.ppermute(early, "core", SWAP), far_rows, lax.ppermute(far_rows, "core", SWAP)]
     later = [late, lax.ppermute(late, "core", SWAP)]
     first = turn(where, slots, early, later, rows, level_g, level_a)
-    others[2], first = together((others[2], first))
+    first_sums = lax.ppermute(first[3], "core", SWAP)
+    others[2], first, first_sums = together((others[2], first, first_sums))
     second = turn(where, others, early, later, rows, level_g, level_a)
     far_rows, second = together((lax.ppermute(late, "chip", SWAP), second))
-    late = [far_rows, lax.ppermute(far_rows, "core", SWAP)]
     bases_a, turned_g, bases_g, sums = zip(first, second)
-    sums += tuple(lax.ppermute(t, "core", SWAP) for t in sums)
+    late = [lax.ppermute(far_rows, "core", SWAP), *turn_other(far_rows, bases_g)]
+    sums += (first_sums, lax.ppermute(sums[1], "core", SWAP))
     bases_a += tuple(lax.ppermute(t, "core", SWAP) for t in bases_a)
 
     if levels == 4:

time: 119 us -> 118 us (level)
  transfers between devices with their start and end apart: 30 -> 30, of which waited for: 20 -> 20; matrix products, arithmetic and copies ran while one was open for 3% -> 3% of each run, Pallas kernels for 11% -> 12%
where the time goes in v11:
time: 118 us
  waiting for transfers between devices  56.4 us (48%)
  starting transfers between devices  33.9 us (29%)
  Pallas kernels  19.7 us (17%)
  other arithmetic  3.9 us (3%)
  local copies, waits for them, and re-layouts  3.1 us (3%)
    ppermute x8, waiting for transfers between devices, across(): return lax.ppermute(x, 'level', [(i, i ^ step) for i in range(levels)])  29.8 us
    ppermute x8, starting transfers between devices, across(): return lax.ppermute(x, 'level', [(i, i ^ step) for i in range(levels)])  13 us
    pallas_call x2, Pallas kernels, turn(): pl.pallas_call(functools.partial(turn_kernel, levels, level_g, level_a, r...  9.89 us
    ppermute x1, waiting for transfers between devices, body(): last = lax.ppermute((far_kept + far_sent).astype(bf16), 'chip', SWAP)  7.83 us
    ppermute x1, waiting for transfers between devices, gather_levels(): lax.ppermute(held, 'level', [(0, 3), (3, 0)])  7.8 us
    ppermute x4, waiting for transfers between devices, over(): return lax.ppermute(slot, 'group', SWAP)  6.19 us
    ppermute x4, starting transfers between devices, over(): return lax.ppermute(slot, 'group', SWAP)  6.06 us
    ppermute x1, starting transfers between devices, gather_levels(): lax.ppermute(held, 'level', [(0, 3), (3, 0)])  4.37 us
  transfers between devices with their start and end apart: 30, of which 20 were waited for; matrix products, arithmetic and copies ran while one was open for 3% of the time, Pallas kernels for 12%

profile of v11, /device:TPU:0, one launch (start us, length us, event | category | flops | bytes accessed | tf_op | source)
XLA Modules:
  0.0 118.0 jit_solution(15943754346239035635)
XLA Ops:
  0.0 0.9 constant_dynamic-slice_fusion.1
  0.9 1.0 constant_dynamic-slice_fusion.3
  2.4 2.6 %collective-permute-start.1 = (bf16[192,256]{1,0:T(8,128)(2,1)S(1)}, bf16[192,256]{1,0:T(8,128)(2,1)S(1)}, u32[]{:S(2)}, u32[]{:S(2)}) collective-permute-start(bf16[192,256]{1,0:T(8,128)(2,1)S(1)} %get-tuple-element.112), channel_id=1, source_target_pairs={{0,2},{2,0},{1,3},{3,1},{4,6},{6,4},{5,7},{7,5},{8,10},{10,8},{9,1... | collective-permute-start | bytes 294920 | tf_op jit(solution)/shard_map/ppermute | solution.py:428
  6.3 0.9 copy-done.1
  7.8 0.9 collective-permute-done.1
  8.7 1.9 %collective-permute-start.2 = (bf16[880,1024]{1,0:T(8,128)(2,1)S(1)}, bf16[880,1024]{1,0:T(8,128)(2,1)}, u32[]{:S(2)}, u32[]{:S(2)}) collective-permute-start(bf16[880,1024]{1,0:T(8,128)(2,1)S(1)} %pad_maximum_fusion.refs_4_.refs_0_), channel_id=1, source_target_pairs={{0,2},{2,0},{1,3},{3,1},{4,6},{6,4},{5,7},{7,5},{8,10},{10,8},{9,1... | collective-permute-start | bytes 5406728 | tf_op jit(solution)/shard_map/ppermute | solution.py:447
  10.8 1.6 %collective-permute-start.5 = (bf16[768,256]{1,0:T(8,128)(2,1)S(1)}, bf16[768,256]{1,0:T(8,128)(2,1)}, u32[]{:S(2)}, u32[]{:S(2)}) collective-permute-start(bf16[768,256]{1,0:T(8,128)(2,1)S(1)} %fusion.5.refs_0_), channel_id=1, source_target_pairs={{0,4},{4,0},{8,12},{12,8},{1,5},{5,1},{9,13},{13,9},{2,6},{6,2},{1... | collective-permute-start | bytes 1179656 | tf_op jit(solution)/shard_map/ppermute | solution.py:39
  12.5 0.7 collective-permute-start.6
  13.2 1.6 %collective-permute-start.7 = (bf16[768,256]{1,0:T(8,128)(2,1)S(1)}, bf16[768,256]{1,0:T(8,128)(2,1)S(1)}, u32[]{:S(2)}, u32[]{:S(2)}) collective-permute-start(bf16[768,256]{1,0:T(8,128)(2,1)S(1)} %fusion.5.refs_0_), channel_id=1, source_target_pairs={{0,16},{16,0},{1,17},{17,1},{2,18},{18,2},{3,19},{19,3},{4,20},{20... | collective-permute-start | bytes 1179656 | tf_op jit(solution)/shard_map/ppermute | solution.py:392
  14.7 1.2 slice_select_fusion.1.refs_8_
  15.9 6.0 %collective-permute-done.5.refs_1_ = bf16[768,256]{1,0:T(8,128)(2,1)} collective-permute-done((bf16[768,256]{1,0:T(8,128)(2,1)S(1)}, bf16[768,256]{1,0:T(8,128)(2,1)}, u32[]{:S(2)}, u32[]{:S(2)}) %collective-permute-start.5) | collective-permute-done | bytes 393248 | tf_op jit(solution)/shard_map/ppermute | solution.py:39
  21.9 2.1 %collective-permute-done.7.refs_0_ = bf16[768,256]{1,0:T(8,128)(2,1)S(1)} collective-permute-done((bf16[768,256]{1,0:T(8,128)(2,1)S(1)}, bf16[768,256]{1,0:T(8,128)(2,1)S(1)}, u32[]{:S(2)}, u32[]{:S(2)}) %collective-permute-start.7) | collective-permute-done | bytes 393248 | tf_op jit(solution)/shard_map/ppermute | solution.py:392
  24.0 4.4 %collective-permute-start.8 = (bf16[768,256]{1,0:T(8,128)(2,1)S(1)}, bf16[768,256]{1,0:T(8,128)(2,1)}, u32[]{:S(2)}, u32[]{:S(2)}) collective-permute-start(bf16[768,256]{1,0:T(8,128)(2,1)S(1)} %fusion.5.refs_0_), channel_id=1, source_target_pairs={{0,12},{12,0},{1,13},{13,1},{2,14},{14,2},{3,15},{15,3},{16,28},{2... | collective-permute-start | bytes 1179656 | tf_op jit(solution)/shard_map/ppermute | solution.py:402
  28.4 1.6 %collective-permute-start.9 = (bf16[768,256]{1,0:T(8,128)(2,1)}, bf16[768,256]{1,0:T(8,128)(2,1)}, u32[]{:S(2)}, u32[]{:S(2)}) collective-permute-start(bf16[768,256]{1,0:T(8,128)(2,1)} %collective-permute-done.5.refs_1_), channel_id=1, source_target_pairs={{0,16},{16,0},{1,17},{17,1},{2,18},{18,2},{3,19},{19,3},{4,20},{20... | collective-permute-start | bytes 1179656 | tf_op jit(solution)/shard_map/ppermute | solution.py:392
  29.9 7.8 %collective-permute-done.8 = bf16[768,256]{1,0:T(8,128)(2,1)} collective-permute-done((bf16[768,256]{1,0:T(8,128)(2,1)S(1)}, bf16[768,256]{1,0:T(8,128)(2,1)}, u32[]{:S(2)}, u32[]{:S(2)}) %collective-permute-start.8) | collective-permute-done | bytes 393248 | tf_op jit(solution)/shard_map/ppermute | solution.py:402
  37.7 0.8 collective-permute-done.9.refs_1_
  38.6 1.0 broadcast_select_fusion.1.refs_3_
  39.6 0.9 collective-permute-start.10
  40.5 1.5 %collective-permute-start.11 = (bf16[768,256]{1,0:T(8,128)(2,1)S(1)}, bf16[768,256]{1,0:T(8,128)(2,1)S(1)}, u32[]{:S(2)}, u32[]{:S(2)}) collective-permute-start(bf16[768,256]{1,0:T(8,128)(2,1)S(1)} %broadcast_select_fusion.1.refs_3_), channel_id=1, source_target_pairs={{0,16},{16,0},{1,17},{17,1},{2,18},{18,2},{3,19},{19,3},{4,20},{20... | collective-permute-start | bytes 1179656 | tf_op jit(solution)/shard_map/ppermute | solution.py:392
  42.0 6.5 %collective-permute-done.10.refs_2_ = bf16[768,256]{1,0:T(8,128)(2,1)S(1)} collective-permute-done((bf16[768,256]{1,0:T(8,128)(2,1)S(1)}, bf16[768,256]{1,0:T(8,128)(2,1)S(1)}, u32[]{:S(2)}, u32[]{:S(2)}) %collective-permute-start.10) | collective-permute-done | bytes 393248 | tf_op jit(solution)/shard_map/ppermute | solution.py:39
  49.0 0.7 collective-permute-done.2.refs_6_.refs_2_
  50.2 1.6 %collective-permute-start.16 = (bf16[144,2048]{1,0:T(8,128)(2,1)S(1)}, bf16[144,2048]{1,0:T(8,128)(2,1)S(1)}, u32[]{:S(2)}, u32[]{:S(2)}) collective-permute-start(bf16[144,2048]{1,0:T(8,128)(2,1)S(1)} %slice_select_fusion.1.refs_8_), channel_id=1, source_target_pairs={{0,2},{2,0},{1,3},{3,1},{4,6},{6,4},{5,7},{7,5},{8,10},{10,8},{9,1... | collective-permute-start | bytes 1769480 | tf_op jit(solution)/shard_map/ppermute | solution.py:454
  51.8 1.5 %collective-permute-start.13 = (bf16[768,256]{1,0:T(8,128)(2,1)S(1)}, bf16[768,256]{1,0:T(8,128)(2,1)S(1)}, u32[]{:S(2)}, u32[]{:S(2)}) collective-permute-start(bf16[768,256]{1,0:T(8,128)(2,1)S(1)} %collective-permute-done.10.refs_2_), channel_id=1, source_target_pairs={{0,16},{16,0},{1,17},{17,1},{2,18},{18,2},{3,19},{19,3},{4,20},{20... | collective-permute-start | bytes 1179656 | tf_op jit(solution)/shard_map/ppermute | solution.py:392
  53.3 0.6 collective-permute-done.14.refs_9_
  53.9 0.6 collective-permute-done.12.refs_7_.refs_3_
  54.5 5.0 %shard_map.55 = (bf16[1024,256]{1,0:T(8,128)(2,1)S(1)}, bf16[1248,256]{1,0:T(8,128)(2,1)S(1)}, bf16[2048,256]{1,0:T(8,128)(2,1)S(1)}, f32[8,256]{1,0:T(8,128)S(1)}) custom-call(s32[2]{0:T(128)S(1)} %pad_add_fusion.where, bf16[768,256]{1,0:T(8,128)(2,1)S(1)} %fusion.5.refs_0_, bf16[768,256]{1,0:T(8,128)(2,1)} %collective-permute-done.5.refs_1_, ...), custom_call_target="tpu_custom_call" | custom-call | flops 1610612736 | bytes 6291456 | tf_op jit(solution)/shard_map/pallas_call | solution.py:105
  59.6 2.9 %collective-permute-done.13.refs_2_ = bf16[768,256]{1,0:T(8,128)(2,1)S(1)} collective-permute-done((bf16[768,256]{1,0:T(8,128)(2,1)S(1)}, bf16[768,256]{1,0:T(8,128)(2,1)S(1)}, u32[]{:S(2)}, u32[]{:S(2)}) %collective-permute-start.13) | collective-permute-done | bytes 393248 | tf_op jit(solution)/shard_map/ppermute | solution.py:392
  62.5 4.9 %shard_map.56 = (bf16[1024,256]{1,0:T(8,128)(2,1)S(1)}, bf16[1248,256]{1,0:T(8,128)(2,1)S(1)}, bf16[2048,256]{1,0:T(8,128)(2,1)S(1)}, f32[8,256]{1,0:T(8,128)S(1)}) custom-call(s32[2]{0:T(128)S(1)} %pad_add_fusion.where, bf16[768,256]{1,0:T(8,128)(2,1)S(1)} %collective-permute-done.7.refs_0_, bf16[768,256]{1,0:T(8,128)(2,1)} %collective-permute-done.9.refs_1_, ...), custom_call_target="tpu_custom_call" | custom-call | flops 1610612736 | bytes 6291456 | tf_op jit(solution)/shard_map/pallas_call | solution.py:105
  68.6 1.0 collective-permute-done.18.refs_14_
  69.6 2.6 %shard_map.58 = (bf16[136,1024]{1,0:T(8,128)(2,1)S(1)}, f32[8,1024]{1,0:T(8,128)S(1)}, bf16[1536,512]{1,0:T(8,128)(2,1)S(1)}) custom-call(s32[2]{0:T(128)S(1)} %pad_add_fusion.where, bf16[880,1024]{1,0:T(8,128)(2,1)S(1)} %pad_maximum_fusion.refs_4_.refs_0_, bf16[880,1024]{1,0:T(8,128)(2,1)S(1)} %collective-permute-done.refs_5_.refs_1_, ...), custom_call_target="tpu_custom_call" | custom-call | flops 402653184 | bytes 6291456 | tf_op jit(solution)/shard_map/pallas_call | solution.py:255
  72.2 1.6 %collective-permute-start.19 = (bf16[136,1024]{1,0:T(8,128)(2,1)S(1)}, bf16[136,1024]{1,0:T(8,128)(2,1)S(1)}, u32[]{:S(2)}, u32[]{:S(2)}) collective-permute-start(bf16[136,1024]{1,0:T(8,128)(2,1)S(1)} %get-tuple-element.91), channel_id=1, source_target_pairs={{0,4},{4,0},{8,12},{12,8},{1,5},{5,1},{9,13},{13,9},{2,6},{6,2},{1... | collective-permute-start | bytes 835592 | tf_op jit(solution)/shard_map/ppermute | solution.py:39
  74.3 3.3 %shard_map.59 = (f32[128,1024]{1,0:T(8,128)S(1)}, bf16[136,1024]{1,0:T(8,128)(2,1)S(1)}, f32[128,1024]{1,0:T(8,128)S(1)}) custom-call(s32[2]{0:T(128)S(1)} %pad_add_fusion.where, bf16[1536,512]{1,0:T(8,128)(2,1)S(1)} %get-tuple-element.87.right, f32[8,1024]{1,0:T(8,128)S(1)} %get-tuple-element.88.extra.own_extra, ...), custom_call_target="tpu_custom_call" | custom-call | flops 1207959552 | bytes 6291456 | tf_op jit(solution)/shard_map/pallas_call | solution.py:278
  77.6 0.5 collective-permute-start.21
  78.2 3.4 %collective-permute-done.19.got = bf16[136,1024]{1,0:T(8,128)(2,1)S(1)} collective-permute-done((bf16[136,1024]{1,0:T(8,128)(2,1)S(1)}, bf16[136,1024]{1,0:T(8,128)(2,1)S(1)}, u32[]{:S(2)}, u32[]{:S(2)}) %collective-permute-start.19) | collective-permute-done | bytes 278560 | tf_op jit(solution)/shard_map/ppermute | solution.py:39
  81.6 3.8 %collective-permute-start.20 = (bf16[136,1024]{1,0:T(8,128)(2,1)S(1)}, bf16[136,1024]{1,0:T(8,128)(2,1)S(1)}, u32[]{:S(2)}, u32[]{:S(2)}) collective-permute-start(bf16[136,1024]{1,0:T(8,128)(2,1)S(1)} %shard_map.60), channel_id=1, source_target_pairs={{0,12},{4,8},{8,4},{12,0},{1,13},{5,9},{9,5},{13,1},{2,14},{6,10},... | collective-permute-start | bytes 835592 | tf_op jit(solution)/shard_map/ppermute | solution.py:39
  85.4 1.5 %collective-permute-done.21.refs_1_ = bf16[136,1024]{1,0:T(8,128)(2,1)S(1)} collective-permute-done((bf16[136,1024]{1,0:T(8,128)(2,1)S(1)}, bf16[136,1024]{1,0:T(8,128)(2,1)S(1)}, u32[]{:S(2)}, u32[]{:S(2)}) %collective-permute-start.21) | collective-permute-done | bytes 278560 | tf_op jit(solution)/shard_map/ppermute | solution.py:39
  86.9 8.1 %collective-permute-done.20.refs_0_ = bf16[136,1024]{1,0:T(8,128)(2,1)S(1)} collective-permute-done((bf16[136,1024]{1,0:T(8,128)(2,1)S(1)}, bf16[136,1024]{1,0:T(8,128)(2,1)S(1)}, u32[]{:S(2)}, u32[]{:S(2)}) %collective-permute-start.20) | collective-permute-done | bytes 278560 | tf_op jit(solution)/shard_map/ppermute | solution.py:39
  95.0 1.9 %shard_map.61 = (bf16[128,256]{1,0:T(8,128)(2,1)S(1)}, bf16[128,256]{1,0:T(8,128)(2,1)S(1)}, bf16[128,256]{1,0:T(8,128)(2,1)S(1)}, bf16[128,256]{1,0:T(8,128)(2,1)S(1)}) custom-call(s32[2]{0:T(128)S(1)} %pad_add_fusion.where, f32[128,1024]{1,0:T(8,128)S(1)} %get-tuple-element.89.own, f32[8,1024]{1,0:T(8,128)S(1)} %get-tuple-element.88.extra.own_extra, ...), custom_call_target="tpu_custom_call" | custom-call | flops 805306368 | bytes 2097152 | tf_op jit(solution)/shard_map/pallas_call | solution.py:340
  96.9 1.5 %collective-permute-start.24 = (bf16[128,256]{1,0:T(8,128)(2,1)S(1)}, bf16[128,256]{1,0:T(8,128)(2,1)S(1)}, u32[]{:S(2)}, u32[]{:S(2)}) collective-permute-start(bf16[128,256]{1,0:T(8,128)(2,1)S(1)} %get-tuple-element.96), channel_id=1, source_target_pairs={{0,4},{4,0},{8,12},{12,8},{1,5},{5,1},{9,13},{13,9},{2,6},{6,2},{1... | collective-permute-start | bytes 196616 | tf_op jit(solution)/shard_map/ppermute | solution.py:39
  98.4 1.1 collective-permute-start.25
  99.5 1.8 %collective-permute-start.26 = (bf16[128,256]{1,0:T(8,128)(2,1)S(1)}, bf16[128,256]{1,0:T(8,128)(2,1)S(1)}, u32[]{:S(2)}, u32[]{:S(2)}) collective-permute-start(bf16[128,256]{1,0:T(8,128)(2,1)S(1)} %get-tuple-element.98), channel_id=1, source_target_pairs={{0,12},{4,8},{8,4},{12,0},{1,13},{5,9},{9,5},{13,1},{2,14},{6,10},... | collective-permute-start | bytes 196616 | tf_op jit(solution)/shard_map/ppermute | solution.py:39
  101.5 2.9 %collective-permute-done.25.refs_2_ = bf16[128,256]{1,0:T(8,128)(2,1)S(1)} collective-permute-done((bf16[128,256]{1,0:T(8,128)(2,1)S(1)}, bf16[128,256]{1,0:T(8,128)(2,1)S(1)}, u32[]{:S(2)}, u32[]{:S(2)}) %collective-permute-start.25) | collective-permute-done | bytes 65568 | tf_op jit(solution)/shard_map/ppermute | solution.py:39
  104.3 1.4 %collective-permute-done.26.refs_3_ = bf16[128,256]{1,0:T(8,128)(2,1)S(1)} collective-permute-done((bf16[128,256]{1,0:T(8,128)(2,1)S(1)}, bf16[128,256]{1,0:T(8,128)(2,1)S(1)}, u32[]{:S(2)}, u32[]{:S(2)}) %collective-permute-start.26) | collective-permute-done | bytes 65568 | tf_op jit(solution)/shard_map/ppermute | solution.py:39
  105.7 1.4 %shard_map.62 = (bf16[64,2048]{1,0:T(8,128)(2,1)S(1)}, bf16[64,2048]{1,0:T(8,128)(2,1)S(1)}, f32[64,2048]{1,0:T(8,128)S(1)}, f32[64,2048]{1,0:T(8,128)S(1)}) custom-call(s32[2]{0:T(128)S(1)} %pad_add_fusion.where, bf16[128,256]{1,0:T(8,128)(2,1)S(1)} %get-tuple-element.95.refs_0_, bf16[128,256]{1,0:T(8,128)(2,1)S(1)} %collective-permute-done.24.refs_1_, ...), custom_call_target="tpu_custom_call" | custom-call | flops 536870912 | bytes 2097152 | tf_op jit(solution)/shard_map/pallas_call | solution.py:376
  107.7 1.0 collective-permute-done.28
  108.8 0.6 collective-permute-start.29
  109.4 7.8 %collective-permute-done.29 = bf16[64,2048]{1,0:T(8,128)(2,1)S(1)} collective-permute-done((bf16[64,2048]{1,0:T(8,128)(2,1)S(1)}, bf16[64,2048]{1,0:T(8,128)(2,1)S(1)}, u32[]{:S(2)}, u32[]{:S(2)}) %collective-permute-start.29) | collective-permute-done | bytes 262176 | tf_op jit(solution)/shard_map/ppermute | solution.py:473
  117.2 0.8 add_convert_fusion
  (54 shorter events, 5.4 us)
Async XLA Ops:
  0.0 5.9 %copy-start = (bf16[384,2048]{1,0:T(8,128)(2,1)S(1)}, bf16[384,2048]{1,0:T(8,128)(2,1)}, u32[]{:S(2)}) copy-start(bf16[384,2048]{1,0:T(8,128)(2,1)} %param.6) | copy-start | bytes 4718596
  1.9 8.7 %collective-permute-start.3 = (bf16[192,256]{1,0:T(8,128)(2,1)S(1)}, bf16[192,256]{1,0:T(8,128)(2,1)S(1)}, u32[]{:S(2)}, u32[]{:S(2)}) collective-permute-start(bf16[192,256]{1,0:T(8,128)(2,1)S(1)} %get-tuple-element.113), channel_id=1, source_target_pairs={{0,1},{1,0},{2,3},{3,2},{4,5},{5,4},{6,7},{7,6},{8,9},{9,8},{10,11... | collective-permute-start | bytes 294920 | tf_op jit(solution)/shard_map/ppermute | solution.py:429
  2.4 6.2 %collective-permute-start.1 = (bf16[192,256]{1,0:T(8,128)(2,1)S(1)}, bf16[192,256]{1,0:T(8,128)(2,1)S(1)}, u32[]{:S(2)}, u32[]{:S(2)}) collective-permute-start(bf16[192,256]{1,0:T(8,128)(2,1)S(1)} %get-tuple-element.112), channel_id=1, source_target_pairs={{0,2},{2,0},{1,3},{3,1},{4,6},{6,4},{5,7},{7,5},{8,10},{10,8},{9,1... | collective-permute-start | bytes 294920 | tf_op jit(solution)/shard_map/ppermute | solution.py:428
  5.0 5.6 %collective-permute-start.4 = (bf16[192,256]{1,0:T(8,128)(2,1)S(1)}, bf16[192,256]{1,0:T(8,128)(2,1)S(1)}, u32[]{:S(2)}, u32[]{:S(2)}) collective-permute-start(bf16[192,256]{1,0:T(8,128)(2,1)S(1)} %get-tuple-element.114), channel_id=1, source_target_pairs={{0,3},{1,2},{2,1},{3,0},{4,7},{5,6},{6,5},{7,4},{8,11},{9,10},{10,... | collective-permute-start | bytes 294920 | tf_op jit(solution)/shard_map/ppermute | solution.py:426
  6.1 1.1 copy-start.1
  8.7 41.0 %collective-permute-start.2 = (bf16[880,1024]{1,0:T(8,128)(2,1)S(1)}, bf16[880,1024]{1,0:T(8,128)(2,1)}, u32[]{:S(2)}, u32[]{:S(2)}) collective-permute-start(bf16[880,1024]{1,0:T(8,128)(2,1)S(1)} %pad_maximum_fusion.refs_4_.refs_0_), channel_id=1, source_target_pairs={{0,2},{2,0},{1,3},{3,1},{4,6},{6,4},{5,7},{7,5},{8,10},{10,8},{9,1... | collective-permute-start | bytes 5406728 | tf_op jit(solution)/shard_map/ppermute | solution.py:447
  10.8 11.1 %collective-permute-start.5 = (bf16[768,256]{1,0:T(8,128)(2,1)S(1)}, bf16[768,256]{1,0:T(8,128)(2,1)}, u32[]{:S(2)}, u32[]{:S(2)}) collective-permute-start(bf16[768,256]{1,0:T(8,128)(2,1)S(1)} %fusion.5.refs_0_), channel_id=1, source_target_pairs={{0,4},{4,0},{8,12},{12,8},{1,5},{5,1},{9,13},{13,9},{2,6},{6,2},{1... | collective-permute-start | bytes 1179656 | tf_op jit(solution)/shard_map/ppermute | solution.py:39
  12.5 9.4 %collective-permute-start.6 = (bf16[768,256]{1,0:T(8,128)(2,1)S(1)}, bf16[768,256]{1,0:T(8,128)(2,1)S(1)}, u32[]{:S(2)}, u32[]{:S(2)}) collective-permute-start(bf16[768,256]{1,0:T(8,128)(2,1)S(1)} %fusion.5.refs_0_), channel_id=1, source_target_pairs={{4,8},{8,4},{5,9},{9,5},{6,10},{10,6},{7,11},{11,7},{20,24},{24,20... | collective-permute-start | bytes 1179656 | tf_op jit(solution)/shard_map/ppermute | solution.py:399
  13.2 10.8 %collective-permute-start.7 = (bf16[768,256]{1,0:T(8,128)(2,1)S(1)}, bf16[768,256]{1,0:T(8,128)(2,1)S(1)}, u32[]{:S(2)}, u32[]{:S(2)}) collective-permute-start(bf16[768,256]{1,0:T(8,128)(2,1)S(1)} %fusion.5.refs_0_), channel_id=1, source_target_pairs={{0,16},{16,0},{1,17},{17,1},{2,18},{18,2},{3,19},{19,3},{4,20},{20... | collective-permute-start | bytes 1179656 | tf_op jit(solution)/shard_map/ppermute | solution.py:392
  21.9 2.1 %copy-start.2 = (bf16[768,256]{1,0:T(8,128)(2,1)}, bf16[768,256]{1,0:T(8,128)(2,1)S(1)}, u32[]{:S(2)}) copy-start(bf16[768,256]{1,0:T(8,128)(2,1)S(1)} %collective-permute-done.6) | copy-start | bytes 1179652
  24.0 13.7 %collective-permute-start.8 = (bf16[768,256]{1,0:T(8,128)(2,1)S(1)}, bf16[768,256]{1,0:T(8,128)(2,1)}, u32[]{:S(2)}, u32[]{:S(2)}) collective-permute-start(bf16[768,256]{1,0:T(8,128)(2,1)S(1)} %fusion.5.refs_0_), channel_id=1, source_target_pairs={{0,12},{12,0},{1,13},{13,1},{2,14},{14,2},{3,15},{15,3},{16,28},{2... | collective-permute-start | bytes 1179656 | tf_op jit(solution)/shard_map/ppermute | solution.py:402
  28.4 10.2 %collective-permute-start.9 = (bf16[768,256]{1,0:T(8,128)(2,1)}, bf16[768,256]{1,0:T(8,128)(2,1)}, u32[]{:S(2)}, u32[]{:S(2)}) collective-permute-start(bf16[768,256]{1,0:T(8,128)(2,1)} %collective-permute-done.5.refs_1_), channel_id=1, source_target_pairs={{0,16},{16,0},{1,17},{17,1},{2,18},{18,2},{3,19},{19,3},{4,20},{20... | collective-permute-start | bytes 1179656 | tf_op jit(solution)/shard_map/ppermute | solution.py:392
  39.6 9.0 %collective-permute-start.10 = (bf16[768,256]{1,0:T(8,128)(2,1)S(1)}, bf16[768,256]{1,0:T(8,128)(2,1)S(1)}, u32[]{:S(2)}, u32[]{:S(2)}) collective-permute-start(bf16[768,256]{1,0:T(8,128)(2,1)S(1)} %broadcast_select_fusion.1.refs_3_), channel_id=1, source_target_pairs={{0,4},{4,0},{8,12},{12,8},{1,5},{5,1},{9,13},{13,9},{2,6},{6,2},{1... | collective-permute-start | bytes 1179656 | tf_op jit(solution)/shard_map/ppermute | solution.py:39
  40.5 8.4 %collective-permute-start.11 = (bf16[768,256]{1,0:T(8,128)(2,1)S(1)}, bf16[768,256]{1,0:T(8,128)(2,1)S(1)}, u32[]{:S(2)}, u32[]{:S(2)}) collective-permute-start(bf16[768,256]{1,0:T(8,128)(2,1)S(1)} %broadcast_select_fusion.1.refs_3_), channel_id=1, source_target_pairs={{0,16},{16,0},{1,17},{17,1},{2,18},{18,2},{3,19},{19,3},{4,20},{20... | collective-permute-start | bytes 1179656 | tf_op jit(solution)/shard_map/ppermute | solution.py:392
  42.0 11.9 %collective-permute-start = (bf16[880,1024]{1,0:T(8,128)(2,1)S(1)}, bf16[880,1024]{1,0:T(8,128)(2,1)S(1)}, u32[]{:S(2)}, u32[]{:S(2)}) collective-permute-start(bf16[880,1024]{1,0:T(8,128)(2,1)S(1)} %pad_maximum_fusion.refs_4_.refs_0_), channel_id=1, source_target_pairs={{0,1},{1,0},{2,3},{3,2},{4,5},{5,4},{6,7},{7,6},{8,9},{9,8},{10,11... | collective-permute-start | bytes 5406728 | tf_op jit(solution)/shard_map/ppermute | solution.py:448
  49.7 4.8 %collective-permute-start.12 = (bf16[880,1024]{1,0:T(8,128)(2,1)}, bf16[880,1024]{1,0:T(8,128)(2,1)S(1)}, u32[]{:S(2)}, u32[]{:S(2)}) collective-permute-start(bf16[880,1024]{1,0:T(8,128)(2,1)} %collective-permute-done.2.refs_6_.refs_2_), channel_id=1, source_target_pairs={{0,1},{1,0},{2,3},{3,2},{4,5},{5,4},{6,7},{7,6},{8,9},{9,8},{10,11... | collective-permute-start | bytes 5406728 | tf_op jit(solution)/shard_map/ppermute | solution.py:448
  49.7 4.2 %collective-permute-start.14 = (bf16[144,2048]{1,0:T(8,128)(2,1)S(1)}, bf16[144,2048]{1,0:T(8,128)(2,1)S(1)}, u32[]{:S(2)}, u32[]{:S(2)}) collective-permute-start(bf16[144,2048]{1,0:T(8,128)(2,1)S(1)} %slice_select_fusion.1.refs_8_), channel_id=1, source_target_pairs={{0,1},{1,0},{2,3},{3,2},{4,5},{5,4},{6,7},{7,6},{8,9},{9,8},{10,11... | collective-permute-start | bytes 1769480 | tf_op jit(solution)/shard_map/ppermute | solution.py:449
  50.2 17.3 %collective-permute-start.16 = (bf16[144,2048]{1,0:T(8,128)(2,1)S(1)}, bf16[144,2048]{1,0:T(8,128)(2,1)S(1)}, u32[]{:S(2)}, u32[]{:S(2)}) collective-permute-start(bf16[144,2048]{1,0:T(8,128)(2,1)S(1)} %slice_select_fusion.1.refs_8_), channel_id=1, source_target_pairs={{0,2},{2,0},{1,3},{3,1},{4,6},{6,4},{5,7},{7,5},{8,10},{10,8},{9,1... | collective-permute-start | bytes 1769480 | tf_op jit(solution)/shard_map/ppermute | solution.py:454
  51.8 10.7 %collective-permute-start.13 = (bf16[768,256]{1,0:T(8,128)(2,1)S(1)}, bf16[768,256]{1,0:T(8,128)(2,1)S(1)}, u32[]{:S(2)}, u32[]{:S(2)}) collective-permute-start(bf16[768,256]{1,0:T(8,128)(2,1)S(1)} %collective-permute-done.10.refs_2_), channel_id=1, source_target_pairs={{0,16},{16,0},{1,17},{17,1},{2,18},{18,2},{3,19},{19,3},{4,20},{20... | collective-permute-start | bytes 1179656 | tf_op jit(solution)/shard_map/ppermute | solution.py:392
  59.5 3.1 %collective-permute-start.15 = (f32[8,256]{1,0:T(8,128)S(1)}, f32[8,256]{1,0:T(8,128)S(1)}, u32[]{:S(2)}, u32[]{:S(2)}) collective-permute-start(f32[8,256]{1,0:T(8,128)S(1)} %get-tuple-element.84.refs_11_), channel_id=1, source_target_pairs={{0,1},{1,0},{2,3},{3,2},{4,5},{5,4},{6,7},{7,6},{8,9},{9,8},{10,11... | collective-permute-start | bytes 24584 | tf_op jit(solution)/shard_map/ppermute | solution.py:451
  67.5 2.1 %collective-permute-start.17 = (bf16[144,2048]{1,0:T(8,128)(2,1)S(1)}, bf16[144,2048]{1,0:T(8,128)(2,1)S(1)}, u32[]{:S(2)}, u32[]{:S(2)}) collective-permute-start(bf16[144,2048]{1,0:T(8,128)(2,1)S(1)} %collective-permute-done.16.rows), channel_id=1, source_target_pairs={{0,1},{1,0},{2,3},{3,2},{4,5},{5,4},{6,7},{7,6},{8,9},{9,8},{10,11... | collective-permute-start | bytes 1769480 | tf_op jit(solution)/shard_map/ppermute | solution.py:456
  67.6 2.0 %collective-permute-start.18 = (f32[8,256]{1,0:T(8,128)S(1)}, f32[8,256]{1,0:T(8,128)S(1)}, u32[]{:S(2)}, u32[]{:S(2)}) collective-permute-start(f32[8,256]{1,0:T(8,128)S(1)} %get-tuple-element.85.refs_12_), channel_id=1, source_target_pairs={{0,1},{1,0},{2,3},{3,2},{4,5},{5,4},{6,7},{7,6},{8,9},{9,8},{10,11... | collective-permute-start | bytes 24584 | tf_op jit(solution)/shard_map/ppermute | solution.py:457
  72.2 9.4 %collective-permute-start.19 = (bf16[136,1024]{1,0:T(8,128)(2,1)S(1)}, bf16[136,1024]{1,0:T(8,128)(2,1)S(1)}, u32[]{:S(2)}, u32[]{:S(2)}) collective-permute-start(bf16[136,1024]{1,0:T(8,128)(2,1)S(1)} %get-tuple-element.91), channel_id=1, source_target_pairs={{0,4},{4,0},{8,12},{12,8},{1,5},{5,1},{9,13},{13,9},{2,6},{6,2},{1... | collective-permute-start | bytes 835592 | tf_op jit(solution)/shard_map/ppermute | solution.py:39
  73.8 11.6 %collective-permute-start.23 = (bf16[1024,256]{1,0:T(8,128)(2,1)S(1)}, bf16[1024,256]{1,0:T(8,128)(2,1)S(1)}, u32[]{:S(2)}, u32[]{:S(2)}) collective-permute-start(bf16[1024,256]{1,0:T(8,128)(2,1)S(1)} %get-tuple-element.94.refs_3_), channel_id=1, source_target_pairs={{0,1},{1,0},{2,3},{3,2},{4,5},{5,4},{6,7},{7,6},{8,9},{9,8},{10,11... | collective-permute-start | bytes 1572872 | tf_op jit(solution)/shard_map/ppermute | solution.py:458
  73.8 11.6 %collective-permute-start.22 = (bf16[1024,256]{1,0:T(8,128)(2,1)S(1)}, bf16[1024,256]{1,0:T(8,128)(2,1)S(1)}, u32[]{:S(2)}, u32[]{:S(2)}) collective-permute-start(bf16[1024,256]{1,0:T(8,128)(2,1)S(1)} %get-tuple-element.93.refs_2_), channel_id=1, source_target_pairs={{0,1},{1,0},{2,3},{3,2},{4,5},{5,4},{6,7},{7,6},{8,9},{9,8},{10,11... | collective-permute-start | bytes 1572872 | tf_op jit(solution)/shard_map/ppermute | solution.py:458
  77.6 9.3 %collective-permute-start.21 = (bf16[136,1024]{1,0:T(8,128)(2,1)S(1)}, bf16[136,1024]{1,0:T(8,128)(2,1)S(1)}, u32[]{:S(2)}, u32[]{:S(2)}) collective-permute-start(bf16[136,1024]{1,0:T(8,128)(2,1)S(1)} %get-tuple-element.92), channel_id=1, source_target_pairs={{0,4},{4,0},{8,12},{12,8},{1,5},{5,1},{9,13},{13,9},{2,6},{6,2},{1... | collective-permute-start | bytes 835592 | tf_op jit(solution)/shard_map/ppermute | solution.py:39
  81.6 13.4 %collective-permute-start.20 = (bf16[136,1024]{1,0:T(8,128)(2,1)S(1)}, bf16[136,1024]{1,0:T(8,128)(2,1)S(1)}, u32[]{:S(2)}, u32[]{:S(2)}) collective-permute-start(bf16[136,1024]{1,0:T(8,128)(2,1)S(1)} %shard_map.60), channel_id=1, source_target_pairs={{0,12},{4,8},{8,4},{12,0},{1,13},{5,9},{9,5},{13,1},{2,14},{6,10},... | collective-permute-start | bytes 835592 | tf_op jit(solution)/shard_map/ppermute | solution.py:39
  96.9 4.6 %collective-permute-start.24 = (bf16[128,256]{1,0:T(8,128)(2,1)S(1)}, bf16[128,256]{1,0:T(8,128)(2,1)S(1)}, u32[]{:S(2)}, u32[]{:S(2)}) collective-permute-start(bf16[128,256]{1,0:T(8,128)(2,1)S(1)} %get-tuple-element.96), channel_id=1, source_target_pairs={{0,4},{4,0},{8,12},{12,8},{1,5},{5,1},{9,13},{13,9},{2,6},{6,2},{1... | collective-permute-start | bytes 196616 | tf_op jit(solution)/shard_map/ppermute | solution.py:39
  98.4 5.9 %collective-permute-start.25 = (bf16[128,256]{1,0:T(8,128)(2,1)S(1)}, bf16[128,256]{1,0:T(8,128)(2,1)S(1)}, u32[]{:S(2)}, u32[]{:S(2)}) collective-permute-start(bf16[128,256]{1,0:T(8,128)(2,1)S(1)} %get-tuple-element.97), channel_id=1, source_target_pairs={{0,8},{4,12},{8,0},{12,4},{1,9},{5,13},{9,1},{13,5},{2,10},{6,14},... | collective-permute-start | bytes 196616 | tf_op jit(solution)/shard_map/ppermute | solution.py:39
  99.5 6.2 %collective-permute-start.26 = (bf16[128,256]{1,0:T(8,128)(2,1)S(1)}, bf16[128,256]{1,0:T(8,128)(2,1)S(1)}, u32[]{:S(2)}, u32[]{:S(2)}) collective-permute-start(bf16[128,256]{1,0:T(8,128)(2,1)S(1)} %get-tuple-element.98), channel_id=1, source_target_pairs={{0,12},{4,8},{8,4},{12,0},{1,13},{5,9},{9,5},{13,1},{2,14},{6,10},... | collective-permute-start | bytes 196616 | tf_op jit(solution)/shard_map/ppermute | solution.py:39
  107.1 1.6 %collective-permute-start.28 = (bf16[64,2048]{1,0:T(8,128)(2,1)S(1)}, bf16[64,2048]{1,0:T(8,128)(2,1)S(1)}, u32[]{:S(2)}, u32[]{:S(2)}) collective-permute-start(bf16[64,2048]{1,0:T(8,128)(2,1)S(1)} %get-tuple-element.102), channel_id=1, source_target_pairs={{0,1},{1,0},{2,3},{3,2},{4,5},{5,4},{6,7},{7,6},{8,9},{9,8},{10,11... | collective-permute-start | bytes 786440 | tf_op jit(solution)/shard_map/ppermute | solution.py:472
  107.2 2.2 %collective-permute-start.27 = (bf16[64,2048]{1,0:T(8,128)(2,1)S(1)}, bf16[64,2048]{1,0:T(8,128)(2,1)S(1)}, u32[]{:S(2)}, u32[]{:S(2)}) collective-permute-start(bf16[64,2048]{1,0:T(8,128)(2,1)S(1)} %get-tuple-element.100), channel_id=1, source_target_pairs={{0,1},{1,0},{2,3},{3,2},{4,5},{5,4},{6,7},{7,6},{8,9},{9,8},{10,11... | collective-permute-start | bytes 786440 | tf_op jit(solution)/shard_map/ppermute | solution.py:472
  108.8 8.4 %collective-permute-start.29 = (bf16[64,2048]{1,0:T(8,128)(2,1)S(1)}, bf16[64,2048]{1,0:T(8,128)(2,1)S(1)}, u32[]{:S(2)}, u32[]{:S(2)}) collective-permute-start(bf16[64,2048]{1,0:T(8,128)(2,1)S(1)} %add_convert_fusion.1), channel_id=1, source_target_pairs={{0,2},{2,0},{1,3},{3,1},{4,6},{6,4},{5,7},{7,5},{8,10},{10,8},{9,1... | collective-permute-start | bytes 786440 | tf_op jit(solution)/shard_map/ppermute | solution.py:473

commit v12 on v11

--- a/solution.py
+++ b/solution.py
@@ -238,51 +238,115 @@
     )(where, *acts, *early, *bases, *pieces, *sums)
 
 
-def far_kernel(levels, rows, where, *refs):
-    acts, early, bases, pieces, sums = refs[:4], refs[4:6], refs[6:8], refs[8:11], refs[11:15]
-    message, extra, right, moved, sems = refs[15:]
+def ready_kernel(levels, rows, where, *refs):
+    acts, early, bases, other = refs[:4], refs[4:6], refs[6:8], refs[8]
+    right, partial, sums, moved, sems = refs[9:]
+    half, late = split(rows)
+    part = bases[0].shape[1]
     chunk = right.shape[1] // levels
-    acts = turn_late(rows, acts, early, bases, pieces, sums, right, moved, sems, extra)
+    pairs = [(acts[2].at[pl.ds(0, rows)], moved)]
+    for i in range(2):
+        columns = pl.ds(i * part, part)
+        for j in range(4):
+            pairs.append((early[i].at[pl.ds(j * half, half)], right.at[pl.ds(j * rows, half), columns]))
+        for j in range(2):
+            source = early[i].at[pl.ds(4 * half + j * late, late)]
+            pairs.append((source, right.at[pl.ds(j * rows + half, late), columns]))
+    copies = [pltpu.make_async_copy(a, b, sems.at[n]) for n, (a, b) in enumerate(pairs)]
+    for copy in copies:
+        copy.start()
+    sums[...] = jnp.zeros_like(sums)
+    right[pl.ds(3 * rows + half, late)] = jnp.zeros((late, 2 * part), bf16)
+    for i, basis in enumerate(bases):
+        columns = pl.ds(i * part, part)
+        turned = jnp.dot(other[...], basis[...], preferred_element_type=f32).astype(bf16)
+        right[pl.ds(2 * rows + half, late), columns] = turned
+        sums[0:1, columns] = jnp.sum(jnp.square(turned.astype(f32)), axis=0, keepdims=True)
+    for copy in copies:
+        copy.wait()
     columns = pl.ds(pl.multiple_of((where[0] ^ 2) * chunk, chunk), chunk)
-    message[...] = with_sums(chunk_of(right, columns, acts, rows), extra)
-
-
-def far(where, acts, early, bases, pieces, sums, rows, levels):
+    partial[...] = chunk_of(right, columns, (acts[0], acts[1], moved, acts[3]), rows)
+
+
+def ready(where, acts, early, bases, other, rows, levels):
     part = bases[0].shape[1]
     width = acts[0].shape[1]
     cols = 2 * part
-    chunk = cols // levels
-    return pl.pallas_call(
-        functools.partial(far_kernel, levels, rows),
-        out_shape=(shape((chunk + 8, width), bf16), shape((8, width), f32), shape((4 * rows, cols), bf16)),
-        in_specs=GIVEN,
+    return pl.pallas_call(
+        functools.partial(ready_kernel, levels, rows),
+        out_shape=(
+            shape((4 * rows, cols), bf16),
+            shape((cols // levels, width), f32),
+            shape((8, cols), f32),
+        ),
+        in_specs=[SMEM] + [VMEM] * 2 + [ANY] + [VMEM] + [ANY] * 2 + [VMEM] * 3,
         out_specs=(VMEM,) * 3,
-        scratch_shapes=[pltpu.VMEM((rows, width), bf16), pltpu.SemaphoreType.DMA((14,))],
+        scratch_shapes=[pltpu.VMEM((rows, width), bf16), pltpu.SemaphoreType.DMA((13,))],
         compiler_params=params(LARGE),
         cost_estimate=cost(2 * rows * cols * width, 16 * rows * width),
-    )(where, *acts, *early, *bases, *pieces, *sums)
-
-
-def near_kernel(levels, rows, where, right, extra, *refs):
+    )(where, *acts, *early, *bases, other)
+
+
+def last_chunk(block, columns, piece, rows):
+    half, late = split(rows)
+    return lax.dot_general(
+        block[:, columns], piece[pl.ds(half, late)], (((0,), (0,)), ((), ())), preferred_element_type=f32
+    )
+
+
+def far_kernel(levels, rows, where, *refs):
+    piece, last, bases, partial, other_sums, sums = refs[0], refs[1], refs[2:4], refs[4], refs[5], refs[6:10]
+    message, extra, block = refs[10:]
+    part = bases[0].shape[1]
+    chunk = 2 * part // levels
+    extra[...] = jnp.zeros_like(extra)
+    for i in range(4):
+        extra[1:2, pl.ds(i * part, part)] = sums[i][2:3]
+        extra[2:3, pl.ds(i * part, part)] = sums[i][1:2]
+    for i, basis in enumerate(bases):
+        columns = pl.ds(i * part, part)
+        turned = jnp.dot(last[...], basis[...], preferred_element_type=f32).astype(bf16)
+        block[:, columns] = turned
+        total = sums[i][0:1] + other_sums[0:1, columns]
+        extra[0:1, columns] = total + jnp.sum(jnp.square(turned.astype(f32)), axis=0, keepdims=True)
+    columns = pl.ds(pl.multiple_of((where[0] ^ 2) * chunk, chunk), chunk)
+    message[...] = with_sums(partial[...] + last_chunk(block, columns, piece, rows), extra)
+
+
+def far(where, piece, last, bases, partial, other_sums, sums, rows, levels):
+    part = bases[0].shape[1]
+    width = piece.shape[1]
+    chunk = 2 * part // levels
+    return pl.pallas_call(
+        functools.partial(far_kernel, levels, rows),
+        out_shape=(shape((chunk + 8, width), bf16), shape((8, width), f32), shape((last.shape[0], 2 * part), bf16)),
+        in_specs=[SMEM] + [VMEM] * 10,
+        out_specs=(VMEM,) * 3,
+        compiler_params=params(LARGE),
+        cost_estimate=cost(rows * part * width, 4 * rows * width),
+    )(where, piece, last, *bases, partial, other_sums, *sums)
+
+
+def near_kernel(levels, rows, where, right, block, extra, *refs):
     acts, own, message, kept = refs[:4], refs[4], refs[5], refs[6]
     chunk = right.shape[1] // levels
     for step, target in ((0, own), (1, message), (3, kept)):
         columns = pl.ds(pl.multiple_of((where[0] ^ step) * chunk, chunk), chunk)
-        block = chunk_of(right, columns, acts, rows)
-        target[...] = with_sums(block, extra) if step == 1 else block
-
-
-def near(where, right, extra, acts, rows, levels):
+        total = chunk_of(right, columns, acts, rows) + last_chunk(block, columns, acts[3], rows)
+        target[...] = with_sums(total, extra) if step == 1 else total
+
+
+def near(where, right, block, extra, acts, rows, levels):
     width = acts[0].shape[1]
     chunk = right.shape[1] // levels
     return pl.pallas_call(
         functools.partial(near_kernel, levels, rows),
         out_shape=(shape((chunk, width), f32), shape((chunk + 8, width), bf16), shape((chunk, width), f32)),
-        in_specs=[SMEM] + [VMEM] * 6,
+        in_specs=[SMEM] + [VMEM] * 7,
         out_specs=(VMEM,) * 3,
         compiler_params=params(LARGE),
         cost_estimate=cost(24 * rows * chunk * width, 16 * rows * width),
-    )(where, right, extra, *acts)
+    )(where, right, block, extra, *acts)
 
 
 def add_kernel(kept, extra, got, out):
@@ -453,16 +517,18 @@
     second = turn(where, others, early, later, rows, level_g, level_a)
     far_rows, second = together((lax.ppermute(late, "chip", SWAP), second))
     bases_a, turned_g, bases_g, sums = zip(first, second)
-    late = [lax.ppermute(far_rows, "core", SWAP), *turn_other(far_rows, bases_g)]
+    last = lax.ppermute(far_rows, "core", SWAP)
     sums += (first_sums, lax.ppermute(sums[1], "core", SWAP))
     bases_a += tuple(lax.ppermute(t, "core", SWAP) for t in bases_a)
 
     if levels == 4:
-        message, own_extra, right = far(where, early, turned_g, bases_g, late, sums, rows, levels)
+        right, partial, other_sums = ready(where, early, turned_g, bases_g, far_rows, rows, levels)
+        message, own_extra, block = far(where, early[3], last, bases_g, partial, other_sums, sums, rows, levels)
         message = across(message, 1, levels)
-        own, beside, kept = near(where, right, own_extra, early, rows, levels)
+        own, beside, kept = near(where, right, block, own_extra, early, rows, levels)
         got = [across(add(kept, own_extra, message), 3, levels), across(beside, 1, levels)]
     else:
+        late = [last, *turn_other(far_rows, bases_g)]
         own, own_extra, *messages = cross(where, early, turned_g, bases_g, late, sums, rows, levels)
         got = [across(m, step + 1, levels) for step, m in enumerate(messages)]
     mids = middle(where, own, own_extra, got, bases_a, levels)

time: 118 us -> 118 us (level)
  waiting for transfers between devices: 56.4 us -> 54.7 us
    pallas_call x1, Pallas kernels: 0.5 us -> 2.56 us  [ready(): pl.pallas_call(functools.partial(ready_kernel, levels, rows), out_shape=(...]
    pallas_call x1, Pallas kernels: 2.58 us -> 1.31 us  [far(): pl.pallas_call(functools.partial(far_kernel, levels, rows), out_shape=(sh...]
  transfers between devices with their start and end apart: 30 -> 30, of which waited for: 20 -> 18; matrix products, arithmetic and copies ran while one was open for 3% -> 3% of each run, Pallas kernels for 12% -> 14%
where the time goes in v12:
time: 118 us
  waiting for transfers between devices  54.7 us (46%)
  starting transfers between devices  34.2 us (29%)
  Pallas kernels  20.7 us (18%)
  other arithmetic  3.9 us (3%)
  local copies, waits for them, and re-layouts  3.1 us (3%)
    ppermute x8, waiting for transfers between devices, across(): return lax.ppermute(x, 'level', [(i, i ^ step) for i in range(levels)])  29.1 us
    ppermute x8, starting transfers between devices, across(): return lax.ppermute(x, 'level', [(i, i ^ step) for i in range(levels)])  13.4 us
    pallas_call x2, Pallas kernels, turn(): pl.pallas_call(functools.partial(turn_kernel, levels, level_g, level_a, r...  9.89 us
    ppermute x1, waiting for transfers between devices, body(): last = lax.ppermute((far_kept + far_sent).astype(bf16), 'chip', SWAP)  7.85 us
    ppermute x1, waiting for transfers between devices, gather_levels(): lax.ppermute(held, 'level', [(0, 3), (3, 0)])  7.8 us
    ppermute x4, waiting for transfers between devices, over(): return lax.ppermute(slot, 'group', SWAP)  6.19 us
    ppermute x4, starting transfers between devices, over(): return lax.ppermute(slot, 'group', SWAP)  6.06 us
    ppermute x1, starting transfers between devices, gather_levels(): lax.ppermute(held, 'level', [(0, 3), (3, 0)])  4.37 us
  transfers between devices with their start and end apart: 30, of which 18 were waited for; matrix products, arithmetic and copies ran while one was open for 3% of the time, Pallas kernels for 14%

profile of v12, /device:TPU:0, one launch (start us, length us, event | category | flops | bytes accessed | tf_op | source)
XLA Modules:
  0.0 117.7 jit_solution(5652978246021029733)
XLA Ops:
  0.0 0.9 constant_dynamic-slice_fusion.1
  0.9 1.0 constant_dynamic-slice_fusion.3
  2.4 2.6 %collective-permute-start.1 = (bf16[192,256]{1,0:T(8,128)(2,1)S(1)}, bf16[192,256]{1,0:T(8,128)(2,1)S(1)}, u32[]{:S(2)}, u32[]{:S(2)}) collective-permute-start(bf16[192,256]{1,0:T(8,128)(2,1)S(1)} %get-tuple-element.114), channel_id=1, source_target_pairs={{0,2},{2,0},{1,3},{3,1},{4,6},{6,4},{5,7},{7,5},{8,10},{10,8},{9,1... | collective-permute-start | bytes 294920 | tf_op jit(solution)/shard_map/ppermute | solution.py:492
  6.3 0.9 copy-done.1
  7.8 0.9 collective-permute-done.1
  8.7 1.9 %collective-permute-start.2 = (bf16[880,1024]{1,0:T(8,128)(2,1)S(1)}, bf16[880,1024]{1,0:T(8,128)(2,1)}, u32[]{:S(2)}, u32[]{:S(2)}) collective-permute-start(bf16[880,1024]{1,0:T(8,128)(2,1)S(1)} %pad_maximum_fusion.refs_4_.refs_0_), channel_id=1, source_target_pairs={{0,2},{2,0},{1,3},{3,1},{4,6},{6,4},{5,7},{7,5},{8,10},{10,8},{9,1... | collective-permute-start | bytes 5406728 | tf_op jit(solution)/shard_map/ppermute | solution.py:511
  10.8 1.6 %collective-permute-start.5 = (bf16[768,256]{1,0:T(8,128)(2,1)S(1)}, bf16[768,256]{1,0:T(8,128)(2,1)}, u32[]{:S(2)}, u32[]{:S(2)}) collective-permute-start(bf16[768,256]{1,0:T(8,128)(2,1)S(1)} %fusion.5.refs_0_), channel_id=1, source_target_pairs={{0,4},{4,0},{8,12},{12,8},{1,5},{5,1},{9,13},{13,9},{2,6},{6,2},{1... | collective-permute-start | bytes 1179656 | tf_op jit(solution)/shard_map/ppermute | solution.py:39
  12.5 0.7 collective-permute-start.6
  13.2 1.6 %collective-permute-start.7 = (bf16[768,256]{1,0:T(8,128)(2,1)S(1)}, bf16[768,256]{1,0:T(8,128)(2,1)S(1)}, u32[]{:S(2)}, u32[]{:S(2)}) collective-permute-start(bf16[768,256]{1,0:T(8,128)(2,1)S(1)} %fusion.5.refs_0_), channel_id=1, source_target_pairs={{0,16},{16,0},{1,17},{17,1},{2,18},{18,2},{3,19},{19,3},{4,20},{20... | collective-permute-start | bytes 1179656 | tf_op jit(solution)/shard_map/ppermute | solution.py:456
  14.7 1.2 slice_select_fusion.1.refs_8_
  15.9 6.0 %collective-permute-done.5.refs_1_ = bf16[768,256]{1,0:T(8,128)(2,1)} collective-permute-done((bf16[768,256]{1,0:T(8,128)(2,1)S(1)}, bf16[768,256]{1,0:T(8,128)(2,1)}, u32[]{:S(2)}, u32[]{:S(2)}) %collective-permute-start.5) | collective-permute-done | bytes 393248 | tf_op jit(solution)/shard_map/ppermute | solution.py:39
  21.9 2.1 %collective-permute-done.7.refs_0_ = bf16[768,256]{1,0:T(8,128)(2,1)S(1)} collective-permute-done((bf16[768,256]{1,0:T(8,128)(2,1)S(1)}, bf16[768,256]{1,0:T(8,128)(2,1)S(1)}, u32[]{:S(2)}, u32[]{:S(2)}) %collective-permute-start.7) | collective-permute-done | bytes 393248 | tf_op jit(solution)/shard_map/ppermute | solution.py:456
  24.0 4.4 %collective-permute-start.8 = (bf16[768,256]{1,0:T(8,128)(2,1)S(1)}, bf16[768,256]{1,0:T(8,128)(2,1)}, u32[]{:S(2)}, u32[]{:S(2)}) collective-permute-start(bf16[768,256]{1,0:T(8,128)(2,1)S(1)} %fusion.5.refs_0_), channel_id=1, source_target_pairs={{0,12},{12,0},{1,13},{13,1},{2,14},{14,2},{3,15},{15,3},{16,28},{2... | collective-permute-start | bytes 1179656 | tf_op jit(solution)/shard_map/ppermute | solution.py:466
  28.4 1.6 %collective-permute-start.9 = (bf16[768,256]{1,0:T(8,128)(2,1)}, bf16[768,256]{1,0:T(8,128)(2,1)}, u32[]{:S(2)}, u32[]{:S(2)}) collective-permute-start(bf16[768,256]{1,0:T(8,128)(2,1)} %collective-permute-done.5.refs_1_), channel_id=1, source_target_pairs={{0,16},{16,0},{1,17},{17,1},{2,18},{18,2},{3,19},{19,3},{4,20},{20... | collective-permute-start | bytes 1179656 | tf_op jit(solution)/shard_map/ppermute | solution.py:456
  29.9 7.8 %collective-permute-done.8 = bf16[768,256]{1,0:T(8,128)(2,1)} collective-permute-done((bf16[768,256]{1,0:T(8,128)(2,1)S(1)}, bf16[768,256]{1,0:T(8,128)(2,1)}, u32[]{:S(2)}, u32[]{:S(2)}) %collective-permute-start.8) | collective-permute-done | bytes 393248 | tf_op jit(solution)/shard_map/ppermute | solution.py:466
  37.7 0.8 collective-permute-done.9.refs_1_
  38.6 1.0 broadcast_select_fusion.1.refs_3_
  39.6 0.9 collective-permute-start.10
  40.5 1.5 %collective-permute-start.11 = (bf16[768,256]{1,0:T(8,128)(2,1)S(1)}, bf16[768,256]{1,0:T(8,128)(2,1)S(1)}, u32[]{:S(2)}, u32[]{:S(2)}) collective-permute-start(bf16[768,256]{1,0:T(8,128)(2,1)S(1)} %broadcast_select_fusion.1.refs_3_), channel_id=1, source_target_pairs={{0,16},{16,0},{1,17},{17,1},{2,18},{18,2},{3,19},{19,3},{4,20},{20... | collective-permute-start | bytes 1179656 | tf_op jit(solution)/shard_map/ppermute | solution.py:456
  42.0 6.5 %collective-permute-done.10.refs_2_ = bf16[768,256]{1,0:T(8,128)(2,1)S(1)} collective-permute-done((bf16[768,256]{1,0:T(8,128)(2,1)S(1)}, bf16[768,256]{1,0:T(8,128)(2,1)S(1)}, u32[]{:S(2)}, u32[]{:S(2)}) %collective-permute-start.10) | collective-permute-done | bytes 393248 | tf_op jit(solution)/shard_map/ppermute | solution.py:39
  49.0 0.7 collective-permute-done.2.refs_6_.refs_2_
  50.2 1.6 %collective-permute-start.16 = (bf16[144,2048]{1,0:T(8,128)(2,1)S(1)}, bf16[144,2048]{1,0:T(8,128)(2,1)S(1)}, u32[]{:S(2)}, u32[]{:S(2)}) collective-permute-start(bf16[144,2048]{1,0:T(8,128)(2,1)S(1)} %slice_select_fusion.1.refs_8_), channel_id=1, source_target_pairs={{0,2},{2,0},{1,3},{3,1},{4,6},{6,4},{5,7},{7,5},{8,10},{10,8},{9,1... | collective-permute-start | bytes 1769480 | tf_op jit(solution)/shard_map/ppermute | solution.py:518
  51.8 1.5 %collective-permute-start.13 = (bf16[768,256]{1,0:T(8,128)(2,1)S(1)}, bf16[768,256]{1,0:T(8,128)(2,1)S(1)}, u32[]{:S(2)}, u32[]{:S(2)}) collective-permute-start(bf16[768,256]{1,0:T(8,128)(2,1)S(1)} %collective-permute-done.10.refs_2_), channel_id=1, source_target_pairs={{0,16},{16,0},{1,17},{17,1},{2,18},{18,2},{3,19},{19,3},{4,20},{20... | collective-permute-start | bytes 1179656 | tf_op jit(solution)/shard_map/ppermute | solution.py:456
  53.3 0.6 collective-permute-done.14.refs_9_
  53.9 0.6 collective-permute-done.12.refs_7_.refs_3_.refs_0_
  54.5 5.0 %shard_map.55 = (bf16[1024,256]{1,0:T(8,128)(2,1)S(1)}, bf16[1248,256]{1,0:T(8,128)(2,1)S(1)}, bf16[2048,256]{1,0:T(8,128)(2,1)S(1)}, f32[8,256]{1,0:T(8,128)S(1)}) custom-call(s32[2]{0:T(128)S(1)} %pad_add_fusion.where, bf16[768,256]{1,0:T(8,128)(2,1)S(1)} %fusion.5.refs_0_, bf16[768,256]{1,0:T(8,128)(2,1)} %collective-permute-done.5.refs_1_, ...), custom_call_target="tpu_custom_call" | custom-call | flops 1610612736 | bytes 6291456 | tf_op jit(solution)/shard_map/pallas_call | solution.py:105
  59.6 2.9 %collective-permute-done.13.refs_2_ = bf16[768,256]{1,0:T(8,128)(2,1)S(1)} collective-permute-done((bf16[768,256]{1,0:T(8,128)(2,1)S(1)}, bf16[768,256]{1,0:T(8,128)(2,1)S(1)}, u32[]{:S(2)}, u32[]{:S(2)}) %collective-permute-start.13) | collective-permute-done | bytes 393248 | tf_op jit(solution)/shard_map/ppermute | solution.py:456
  62.5 4.9 %shard_map.56 = (bf16[1024,256]{1,0:T(8,128)(2,1)S(1)}, bf16[1248,256]{1,0:T(8,128)(2,1)S(1)}, bf16[2048,256]{1,0:T(8,128)(2,1)S(1)}, f32[8,256]{1,0:T(8,128)S(1)}) custom-call(s32[2]{0:T(128)S(1)} %pad_add_fusion.where, bf16[768,256]{1,0:T(8,128)(2,1)S(1)} %collective-permute-done.7.refs_0_, bf16[768,256]{1,0:T(8,128)(2,1)} %collective-permute-done.9.refs_1_, ...), custom_call_target="tpu_custom_call" | custom-call | flops 1610612736 | bytes 6291456 | tf_op jit(solution)/shard_map/pallas_call | solution.py:105
  68.1 2.6 %shard_map.57 = (bf16[1536,512]{1,0:T(8,128)(2,1)S(1)}, f32[128,1024]{1,0:T(8,128)S(1)}, f32[8,512]{1,0:T(8,128)S(1)}) custom-call(s32[2]{0:T(128)S(1)} %pad_add_fusion.where, bf16[880,1024]{1,0:T(8,128)(2,1)S(1)} %pad_maximum_fusion.refs_4_.refs_0_, bf16[880,1024]{1,0:T(8,128)(2,1)S(1)} %collective-permute-done.refs_5_.refs_1_, ...), custom_call_target="tpu_custom_call" | custom-call | flops 402653184 | bytes 6291456 | tf_op jit(solution)/shard_map/pallas_call | solution.py:275
  70.7 1.3 %shard_map.58 = (bf16[136,1024]{1,0:T(8,128)(2,1)S(1)}, f32[8,1024]{1,0:T(8,128)S(1)}, bf16[144,512]{1,0:T(8,128)(2,1)S(1)}) custom-call(s32[2]{0:T(128)S(1)} %pad_add_fusion.where, bf16[880,1024]{1,0:T(8,128)(2,1)S(1)} %collective-permute-done.12.refs_7_.refs_3_.refs_0_, bf16[144,2048]{1,0:T(8,128)(2,1)S(1)} %collective-permute-done.17.refs_1_, ...), custom_call_target="tpu_custom_call" | custom-call | flops 100663296 | bytes 1572864 | tf_op jit(solution)/shard_map/pallas_call | solution.py:320
  72.0 1.6 %collective-permute-start.19 = (bf16[136,1024]{1,0:T(8,128)(2,1)S(1)}, bf16[136,1024]{1,0:T(8,128)(2,1)S(1)}, u32[]{:S(2)}, u32[]{:S(2)}) collective-permute-start(bf16[136,1024]{1,0:T(8,128)(2,1)S(1)} %get-tuple-element.93), channel_id=1, source_target_pairs={{0,4},{4,0},{8,12},{12,8},{1,5},{5,1},{9,13},{13,9},{2,6},{6,2},{1... | collective-permute-start | bytes 835592 | tf_op jit(solution)/shard_map/ppermute | solution.py:39
  74.1 3.5 %shard_map.59 = (f32[128,1024]{1,0:T(8,128)S(1)}, bf16[136,1024]{1,0:T(8,128)(2,1)S(1)}, f32[128,1024]{1,0:T(8,128)S(1)}) custom-call(s32[2]{0:T(128)S(1)} %pad_add_fusion.where, bf16[1536,512]{1,0:T(8,128)(2,1)S(1)} %get-tuple-element.83.right, bf16[144,512]{1,0:T(8,128)(2,1)S(1)} %get-tuple-element.89.block, ...), custom_call_target="tpu_custom_call" | custom-call | flops 1207959552 | bytes 6291456 | tf_op jit(solution)/shard_map/pallas_call | solution.py:342
  77.6 0.5 collective-permute-start.21
  78.2 2.8 %collective-permute-done.19.got = bf16[136,1024]{1,0:T(8,128)(2,1)S(1)} collective-permute-done((bf16[136,1024]{1,0:T(8,128)(2,1)S(1)}, bf16[136,1024]{1,0:T(8,128)(2,1)S(1)}, u32[]{:S(2)}, u32[]{:S(2)}) %collective-permute-start.19) | collective-permute-done | bytes 278560 | tf_op jit(solution)/shard_map/ppermute | solution.py:39
  81.1 4.2 %collective-permute-start.20 = (bf16[136,1024]{1,0:T(8,128)(2,1)S(1)}, bf16[136,1024]{1,0:T(8,128)(2,1)S(1)}, u32[]{:S(2)}, u32[]{:S(2)}) collective-permute-start(bf16[136,1024]{1,0:T(8,128)(2,1)S(1)} %shard_map.60), channel_id=1, source_target_pairs={{0,12},{4,8},{8,4},{12,0},{1,13},{5,9},{9,5},{13,1},{2,14},{6,10},... | collective-permute-start | bytes 835592 | tf_op jit(solution)/shard_map/ppermute | solution.py:39
  85.3 1.4 %collective-permute-done.21.refs_1_ = bf16[136,1024]{1,0:T(8,128)(2,1)S(1)} collective-permute-done((bf16[136,1024]{1,0:T(8,128)(2,1)S(1)}, bf16[136,1024]{1,0:T(8,128)(2,1)S(1)}, u32[]{:S(2)}, u32[]{:S(2)}) %collective-permute-start.21) | collective-permute-done | bytes 278560 | tf_op jit(solution)/shard_map/ppermute | solution.py:39
  86.7 8.1 %collective-permute-done.20.refs_0_ = bf16[136,1024]{1,0:T(8,128)(2,1)S(1)} collective-permute-done((bf16[136,1024]{1,0:T(8,128)(2,1)S(1)}, bf16[136,1024]{1,0:T(8,128)(2,1)S(1)}, u32[]{:S(2)}, u32[]{:S(2)}) %collective-permute-start.20) | collective-permute-done | bytes 278560 | tf_op jit(solution)/shard_map/ppermute | solution.py:39
  94.7 1.9 %shard_map.61 = (bf16[128,256]{1,0:T(8,128)(2,1)S(1)}, bf16[128,256]{1,0:T(8,128)(2,1)S(1)}, bf16[128,256]{1,0:T(8,128)(2,1)S(1)}, bf16[128,256]{1,0:T(8,128)(2,1)S(1)}) custom-call(s32[2]{0:T(128)S(1)} %pad_add_fusion.where, f32[128,1024]{1,0:T(8,128)S(1)} %get-tuple-element.91.own, f32[8,1024]{1,0:T(8,128)S(1)} %get-tuple-element.90.extra.own_extra, ...), custom_call_target="tpu_custom_call" | custom-call | flops 805306368 | bytes 2097152 | tf_op jit(solution)/shard_map/pallas_call | solution.py:404
  96.7 1.5 %collective-permute-start.24 = (bf16[128,256]{1,0:T(8,128)(2,1)S(1)}, bf16[128,256]{1,0:T(8,128)(2,1)S(1)}, u32[]{:S(2)}, u32[]{:S(2)}) collective-permute-start(bf16[128,256]{1,0:T(8,128)(2,1)S(1)} %get-tuple-element.98), channel_id=1, source_target_pairs={{0,4},{4,0},{8,12},{12,8},{1,5},{5,1},{9,13},{13,9},{2,6},{6,2},{1... | collective-permute-start | bytes 196616 | tf_op jit(solution)/shard_map/ppermute | solution.py:39
  98.1 1.1 collective-permute-start.25
  99.2 1.9 %collective-permute-start.26 = (bf16[128,256]{1,0:T(8,128)(2,1)S(1)}, bf16[128,256]{1,0:T(8,128)(2,1)S(1)}, u32[]{:S(2)}, u32[]{:S(2)}) collective-permute-start(bf16[128,256]{1,0:T(8,128)(2,1)S(1)} %get-tuple-element.100), channel_id=1, source_target_pairs={{0,12},{4,8},{8,4},{12,0},{1,13},{5,9},{9,5},{13,1},{2,14},{6,10},... | collective-permute-start | bytes 196616 | tf_op jit(solution)/shard_map/ppermute | solution.py:39
  101.1 2.9 %collective-permute-done.25.refs_2_ = bf16[128,256]{1,0:T(8,128)(2,1)S(1)} collective-permute-done((bf16[128,256]{1,0:T(8,128)(2,1)S(1)}, bf16[128,256]{1,0:T(8,128)(2,1)S(1)}, u32[]{:S(2)}, u32[]{:S(2)}) %collective-permute-start.25) | collective-permute-done | bytes 65568 | tf_op jit(solution)/shard_map/ppermute | solution.py:39
  104.0 1.3 %collective-permute-done.26.refs_3_ = bf16[128,256]{1,0:T(8,128)(2,1)S(1)} collective-permute-done((bf16[128,256]{1,0:T(8,128)(2,1)S(1)}, bf16[128,256]{1,0:T(8,128)(2,1)S(1)}, u32[]{:S(2)}, u32[]{:S(2)}) %collective-permute-start.26) | collective-permute-done | bytes 65568 | tf_op jit(solution)/shard_map/ppermute | solution.py:39
  105.4 1.4 %shard_map.62 = (bf16[64,2048]{1,0:T(8,128)(2,1)S(1)}, bf16[64,2048]{1,0:T(8,128)(2,1)S(1)}, f32[64,2048]{1,0:T(8,128)S(1)}, f32[64,2048]{1,0:T(8,128)S(1)}) custom-call(s32[2]{0:T(128)S(1)} %pad_add_fusion.where, bf16[128,256]{1,0:T(8,128)(2,1)S(1)} %get-tuple-element.97.refs_0_, bf16[128,256]{1,0:T(8,128)(2,1)S(1)} %collective-permute-done.24.refs_1_, ...), custom_call_target="tpu_custom_call" | custom-call | flops 536870912 | bytes 2097152 | tf_op jit(solution)/shard_map/pallas_call | solution.py:440
  107.4 1.0 collective-permute-done.28
  108.5 0.6 collective-permute-start.29
  109.0 7.9 %collective-permute-done.29 = bf16[64,2048]{1,0:T(8,128)(2,1)S(1)} collective-permute-done((bf16[64,2048]{1,0:T(8,128)(2,1)S(1)}, bf16[64,2048]{1,0:T(8,128)(2,1)S(1)}, u32[]{:S(2)}, u32[]{:S(2)}) %collective-permute-start.29) | collective-permute-done | bytes 262176 | tf_op jit(solution)/shard_map/ppermute | solution.py:539
  116.9 0.8 add_convert_fusion
  (54 shorter events, 4.8 us)
Async XLA Ops:
  0.0 5.9 %copy-start = (bf16[384,2048]{1,0:T(8,128)(2,1)S(1)}, bf16[384,2048]{1,0:T(8,128)(2,1)}, u32[]{:S(2)}) copy-start(bf16[384,2048]{1,0:T(8,128)(2,1)} %param.6) | copy-start | bytes 4718596
  1.9 8.7 %collective-permute-start.3 = (bf16[192,256]{1,0:T(8,128)(2,1)S(1)}, bf16[192,256]{1,0:T(8,128)(2,1)S(1)}, u32[]{:S(2)}, u32[]{:S(2)}) collective-permute-start(bf16[192,256]{1,0:T(8,128)(2,1)S(1)} %get-tuple-element.115), channel_id=1, source_target_pairs={{0,1},{1,0},{2,3},{3,2},{4,5},{5,4},{6,7},{7,6},{8,9},{9,8},{10,11... | collective-permute-start | bytes 294920 | tf_op jit(solution)/shard_map/ppermute | solution.py:493
  2.4 6.2 %collective-permute-start.1 = (bf16[192,256]{1,0:T(8,128)(2,1)S(1)}, bf16[192,256]{1,0:T(8,128)(2,1)S(1)}, u32[]{:S(2)}, u32[]{:S(2)}) collective-permute-start(bf16[192,256]{1,0:T(8,128)(2,1)S(1)} %get-tuple-element.114), channel_id=1, source_target_pairs={{0,2},{2,0},{1,3},{3,1},{4,6},{6,4},{5,7},{7,5},{8,10},{10,8},{9,1... | collective-permute-start | bytes 294920 | tf_op jit(solution)/shard_map/ppermute | solution.py:492
  5.0 5.6 %collective-permute-start.4 = (bf16[192,256]{1,0:T(8,128)(2,1)S(1)}, bf16[192,256]{1,0:T(8,128)(2,1)S(1)}, u32[]{:S(2)}, u32[]{:S(2)}) collective-permute-start(bf16[192,256]{1,0:T(8,128)(2,1)S(1)} %get-tuple-element.116), channel_id=1, source_target_pairs={{0,3},{1,2},{2,1},{3,0},{4,7},{5,6},{6,5},{7,4},{8,11},{9,10},{10,... | collective-permute-start | bytes 294920 | tf_op jit(solution)/shard_map/ppermute | solution.py:490
  6.1 1.1 copy-start.1
  8.7 41.0 %collective-permute-start.2 = (bf16[880,1024]{1,0:T(8,128)(2,1)S(1)}, bf16[880,1024]{1,0:T(8,128)(2,1)}, u32[]{:S(2)}, u32[]{:S(2)}) collective-permute-start(bf16[880,1024]{1,0:T(8,128)(2,1)S(1)} %pad_maximum_fusion.refs_4_.refs_0_), channel_id=1, source_target_pairs={{0,2},{2,0},{1,3},{3,1},{4,6},{6,4},{5,7},{7,5},{8,10},{10,8},{9,1... | collective-permute-start | bytes 5406728 | tf_op jit(solution)/shard_map/ppermute | solution.py:511
  10.8 11.1 %collective-permute-start.5 = (bf16[768,256]{1,0:T(8,128)(2,1)S(1)}, bf16[768,256]{1,0:T(8,128)(2,1)}, u32[]{:S(2)}, u32[]{:S(2)}) collective-permute-start(bf16[768,256]{1,0:T(8,128)(2,1)S(1)} %fusion.5.refs_0_), channel_id=1, source_target_pairs={{0,4},{4,0},{8,12},{12,8},{1,5},{5,1},{9,13},{13,9},{2,6},{6,2},{1... | collective-permute-start | bytes 1179656 | tf_op jit(solution)/shard_map/ppermute | solution.py:39
  12.5 9.4 %collective-permute-start.6 = (bf16[768,256]{1,0:T(8,128)(2,1)S(1)}, bf16[768,256]{1,0:T(8,128)(2,1)S(1)}, u32[]{:S(2)}, u32[]{:S(2)}) collective-permute-start(bf16[768,256]{1,0:T(8,128)(2,1)S(1)} %fusion.5.refs_0_), channel_id=1, source_target_pairs={{4,8},{8,4},{5,9},{9,5},{6,10},{10,6},{7,11},{11,7},{20,24},{24,20... | collective-permute-start | bytes 1179656 | tf_op jit(solution)/shard_map/ppermute | solution.py:463
  13.2 10.8 %collective-permute-start.7 = (bf16[768,256]{1,0:T(8,128)(2,1)S(1)}, bf16[768,256]{1,0:T(8,128)(2,1)S(1)}, u32[]{:S(2)}, u32[]{:S(2)}) collective-permute-start(bf16[768,256]{1,0:T(8,128)(2,1)S(1)} %fusion.5.refs_0_), channel_id=1, source_target_pairs={{0,16},{16,0},{1,17},{17,1},{2,18},{18,2},{3,19},{19,3},{4,20},{20... | collective-permute-start | bytes 1179656 | tf_op jit(solution)/shard_map/ppermute | solution.py:456
  21.9 2.1 %copy-start.2 = (bf16[768,256]{1,0:T(8,128)(2,1)}, bf16[768,256]{1,0:T(8,128)(2,1)S(1)}, u32[]{:S(2)}) copy-start(bf16[768,256]{1,0:T(8,128)(2,1)S(1)} %collective-permute-done.6) | copy-start | bytes 1179652
  24.0 13.7 %collective-permute-start.8 = (bf16[768,256]{1,0:T(8,128)(2,1)S(1)}, bf16[768,256]{1,0:T(8,128)(2,1)}, u32[]{:S(2)}, u32[]{:S(2)}) collective-permute-start(bf16[768,256]{1,0:T(8,128)(2,1)S(1)} %fusion.5.refs_0_), channel_id=1, source_target_pairs={{0,12},{12,0},{1,13},{13,1},{2,14},{14,2},{3,15},{15,3},{16,28},{2... | collective-permute-start | bytes 1179656 | tf_op jit(solution)/shard_map/ppermute | solution.py:466
  28.4 10.2 %collective-permute-start.9 = (bf16[768,256]{1,0:T(8,128)(2,1)}, bf16[768,256]{1,0:T(8,128)(2,1)}, u32[]{:S(2)}, u32[]{:S(2)}) collective-permute-start(bf16[768,256]{1,0:T(8,128)(2,1)} %collective-permute-done.5.refs_1_), channel_id=1, source_target_pairs={{0,16},{16,0},{1,17},{17,1},{2,18},{18,2},{3,19},{19,3},{4,20},{20... | collective-permute-start | bytes 1179656 | tf_op jit(solution)/shard_map/ppermute | solution.py:456
  39.6 9.0 %collective-permute-start.10 = (bf16[768,256]{1,0:T(8,128)(2,1)S(1)}, bf16[768,256]{1,0:T(8,128)(2,1)S(1)}, u32[]{:S(2)}, u32[]{:S(2)}) collective-permute-start(bf16[768,256]{1,0:T(8,128)(2,1)S(1)} %broadcast_select_fusion.1.refs_3_), channel_id=1, source_target_pairs={{0,4},{4,0},{8,12},{12,8},{1,5},{5,1},{9,13},{13,9},{2,6},{6,2},{1... | collective-permute-start | bytes 1179656 | tf_op jit(solution)/shard_map/ppermute | solution.py:39
  40.5 8.4 %collective-permute-start.11 = (bf16[768,256]{1,0:T(8,128)(2,1)S(1)}, bf16[768,256]{1,0:T(8,128)(2,1)S(1)}, u32[]{:S(2)}, u32[]{:S(2)}) collective-permute-start(bf16[768,256]{1,0:T(8,128)(2,1)S(1)} %broadcast_select_fusion.1.refs_3_), channel_id=1, source_target_pairs={{0,16},{16,0},{1,17},{17,1},{2,18},{18,2},{3,19},{19,3},{4,20},{20... | collective-permute-start | bytes 1179656 | tf_op jit(solution)/shard_map/ppermute | solution.py:456
  42.0 11.9 %collective-permute-start = (bf16[880,1024]{1,0:T(8,128)(2,1)S(1)}, bf16[880,1024]{1,0:T(8,128)(2,1)S(1)}, u32[]{:S(2)}, u32[]{:S(2)}) collective-permute-start(bf16[880,1024]{1,0:T(8,128)(2,1)S(1)} %pad_maximum_fusion.refs_4_.refs_0_), channel_id=1, source_target_pairs={{0,1},{1,0},{2,3},{3,2},{4,5},{5,4},{6,7},{7,6},{8,9},{9,8},{10,11... | collective-permute-start | bytes 5406728 | tf_op jit(solution)/shard_map/ppermute | solution.py:512
  49.7 4.8 %collective-permute-start.12 = (bf16[880,1024]{1,0:T(8,128)(2,1)}, bf16[880,1024]{1,0:T(8,128)(2,1)S(1)}, u32[]{:S(2)}, u32[]{:S(2)}) collective-permute-start(bf16[880,1024]{1,0:T(8,128)(2,1)} %collective-permute-done.2.refs_6_.refs_2_), channel_id=1, source_target_pairs={{0,1},{1,0},{2,3},{3,2},{4,5},{5,4},{6,7},{7,6},{8,9},{9,8},{10,11... | collective-permute-start | bytes 5406728 | tf_op jit(solution)/shard_map/ppermute | solution.py:512
  49.7 4.2 %collective-permute-start.14 = (bf16[144,2048]{1,0:T(8,128)(2,1)S(1)}, bf16[144,2048]{1,0:T(8,128)(2,1)S(1)}, u32[]{:S(2)}, u32[]{:S(2)}) collective-permute-start(bf16[144,2048]{1,0:T(8,128)(2,1)S(1)} %slice_select_fusion.1.refs_8_), channel_id=1, source_target_pairs={{0,1},{1,0},{2,3},{3,2},{4,5},{5,4},{6,7},{7,6},{8,9},{9,8},{10,11... | collective-permute-start | bytes 1769480 | tf_op jit(solution)/shard_map/ppermute | solution.py:513
  50.2 17.3 %collective-permute-start.16 = (bf16[144,2048]{1,0:T(8,128)(2,1)S(1)}, bf16[144,2048]{1,0:T(8,128)(2,1)S(1)}, u32[]{:S(2)}, u32[]{:S(2)}) collective-permute-start(bf16[144,2048]{1,0:T(8,128)(2,1)S(1)} %slice_select_fusion.1.refs_8_), channel_id=1, source_target_pairs={{0,2},{2,0},{1,3},{3,1},{4,6},{6,4},{5,7},{7,5},{8,10},{10,8},{9,1... | collective-permute-start | bytes 1769480 | tf_op jit(solution)/shard_map/ppermute | solution.py:518
  51.8 10.7 %collective-permute-start.13 = (bf16[768,256]{1,0:T(8,128)(2,1)S(1)}, bf16[768,256]{1,0:T(8,128)(2,1)S(1)}, u32[]{:S(2)}, u32[]{:S(2)}) collective-permute-start(bf16[768,256]{1,0:T(8,128)(2,1)S(1)} %collective-permute-done.10.refs_2_), channel_id=1, source_target_pairs={{0,16},{16,0},{1,17},{17,1},{2,18},{18,2},{3,19},{19,3},{4,20},{20... | collective-permute-start | bytes 1179656 | tf_op jit(solution)/shard_map/ppermute | solution.py:456
  59.5 3.1 %collective-permute-start.15 = (f32[8,256]{1,0:T(8,128)S(1)}, f32[8,256]{1,0:T(8,128)S(1)}, u32[]{:S(2)}, u32[]{:S(2)}) collective-permute-start(f32[8,256]{1,0:T(8,128)S(1)} %get-tuple-element.86.refs_6_), channel_id=1, source_target_pairs={{0,1},{1,0},{2,3},{3,2},{4,5},{5,4},{6,7},{7,6},{8,9},{9,8},{10,11... | collective-permute-start | bytes 24584 | tf_op jit(solution)/shard_map/ppermute | solution.py:515
  67.5 3.2 %collective-permute-start.17 = (bf16[144,2048]{1,0:T(8,128)(2,1)S(1)}, bf16[144,2048]{1,0:T(8,128)(2,1)S(1)}, u32[]{:S(2)}, u32[]{:S(2)}) collective-permute-start(bf16[144,2048]{1,0:T(8,128)(2,1)S(1)} %collective-permute-done.16.refs_8_), channel_id=1, source_target_pairs={{0,1},{1,0},{2,3},{3,2},{4,5},{5,4},{6,7},{7,6},{8,9},{9,8},{10,11... | collective-permute-start | bytes 1769480 | tf_op jit(solution)/shard_map/ppermute | solution.py:520
  67.6 3.1 %collective-permute-start.18 = (f32[8,256]{1,0:T(8,128)S(1)}, f32[8,256]{1,0:T(8,128)S(1)}, u32[]{:S(2)}, u32[]{:S(2)}) collective-permute-start(f32[8,256]{1,0:T(8,128)S(1)} %get-tuple-element.87.refs_7_), channel_id=1, source_target_pairs={{0,1},{1,0},{2,3},{3,2},{4,5},{5,4},{6,7},{7,6},{8,9},{9,8},{10,11... | collective-permute-start | bytes 24584 | tf_op jit(solution)/shard_map/ppermute | solution.py:521
  72.0 9.0 %collective-permute-start.19 = (bf16[136,1024]{1,0:T(8,128)(2,1)S(1)}, bf16[136,1024]{1,0:T(8,128)(2,1)S(1)}, u32[]{:S(2)}, u32[]{:S(2)}) collective-permute-start(bf16[136,1024]{1,0:T(8,128)(2,1)S(1)} %get-tuple-element.93), channel_id=1, source_target_pairs={{0,4},{4,0},{8,12},{12,8},{1,5},{5,1},{9,13},{13,9},{2,6},{6,2},{1... | collective-permute-start | bytes 835592 | tf_op jit(solution)/shard_map/ppermute | solution.py:39
  73.6 11.7 %collective-permute-start.23 = (bf16[1024,256]{1,0:T(8,128)(2,1)S(1)}, bf16[1024,256]{1,0:T(8,128)(2,1)S(1)}, u32[]{:S(2)}, u32[]{:S(2)}) collective-permute-start(bf16[1024,256]{1,0:T(8,128)(2,1)S(1)} %get-tuple-element.96.refs_3_), channel_id=1, source_target_pairs={{0,1},{1,0},{2,3},{3,2},{4,5},{5,4},{6,7},{7,6},{8,9},{9,8},{10,11... | collective-permute-start | bytes 1572872 | tf_op jit(solution)/shard_map/ppermute | solution.py:522
  73.6 11.7 %collective-permute-start.22 = (bf16[1024,256]{1,0:T(8,128)(2,1)S(1)}, bf16[1024,256]{1,0:T(8,128)(2,1)S(1)}, u32[]{:S(2)}, u32[]{:S(2)}) collective-permute-start(bf16[1024,256]{1,0:T(8,128)(2,1)S(1)} %get-tuple-element.95.refs_2_), channel_id=1, source_target_pairs={{0,1},{1,0},{2,3},{3,2},{4,5},{5,4},{6,7},{7,6},{8,9},{9,8},{10,11... | collective-permute-start | bytes 1572872 | tf_op jit(solution)/shard_map/ppermute | solution.py:522
  77.6 9.0 %collective-permute-start.21 = (bf16[136,1024]{1,0:T(8,128)(2,1)S(1)}, bf16[136,1024]{1,0:T(8,128)(2,1)S(1)}, u32[]{:S(2)}, u32[]{:S(2)}) collective-permute-start(bf16[136,1024]{1,0:T(8,128)(2,1)S(1)} %get-tuple-element.94), channel_id=1, source_target_pairs={{0,4},{4,0},{8,12},{12,8},{1,5},{5,1},{9,13},{13,9},{2,6},{6,2},{1... | collective-permute-start | bytes 835592 | tf_op jit(solution)/shard_map/ppermute | solution.py:39
  81.1 13.6 %collective-permute-start.20 = (bf16[136,1024]{1,0:T(8,128)(2,1)S(1)}, bf16[136,1024]{1,0:T(8,128)(2,1)S(1)}, u32[]{:S(2)}, u32[]{:S(2)}) collective-permute-start(bf16[136,1024]{1,0:T(8,128)(2,1)S(1)} %shard_map.60), channel_id=1, source_target_pairs={{0,12},{4,8},{8,4},{12,0},{1,13},{5,9},{9,5},{13,1},{2,14},{6,10},... | collective-permute-start | bytes 835592 | tf_op jit(solution)/shard_map/ppermute | solution.py:39
  96.7 4.5 %collective-permute-start.24 = (bf16[128,256]{1,0:T(8,128)(2,1)S(1)}, bf16[128,256]{1,0:T(8,128)(2,1)S(1)}, u32[]{:S(2)}, u32[]{:S(2)}) collective-permute-start(bf16[128,256]{1,0:T(8,128)(2,1)S(1)} %get-tuple-element.98), channel_id=1, source_target_pairs={{0,4},{4,0},{8,12},{12,8},{1,5},{5,1},{9,13},{13,9},{2,6},{6,2},{1... | collective-permute-start | bytes 196616 | tf_op jit(solution)/shard_map/ppermute | solution.py:39
  98.1 5.9 %collective-permute-start.25 = (bf16[128,256]{1,0:T(8,128)(2,1)S(1)}, bf16[128,256]{1,0:T(8,128)(2,1)S(1)}, u32[]{:S(2)}, u32[]{:S(2)}) collective-permute-start(bf16[128,256]{1,0:T(8,128)(2,1)S(1)} %get-tuple-element.99), channel_id=1, source_target_pairs={{0,8},{4,12},{8,0},{12,4},{1,9},{5,13},{9,1},{13,5},{2,10},{6,14},... | collective-permute-start | bytes 196616 | tf_op jit(solution)/shard_map/ppermute | solution.py:39
  99.2 6.2 %collective-permute-start.26 = (bf16[128,256]{1,0:T(8,128)(2,1)S(1)}, bf16[128,256]{1,0:T(8,128)(2,1)S(1)}, u32[]{:S(2)}, u32[]{:S(2)}) collective-permute-start(bf16[128,256]{1,0:T(8,128)(2,1)S(1)} %get-tuple-element.100), channel_id=1, source_target_pairs={{0,12},{4,8},{8,4},{12,0},{1,13},{5,9},{9,5},{13,1},{2,14},{6,10},... | collective-permute-start | bytes 196616 | tf_op jit(solution)/shard_map/ppermute | solution.py:39
  106.8 1.6 %collective-permute-start.28 = (bf16[64,2048]{1,0:T(8,128)(2,1)S(1)}, bf16[64,2048]{1,0:T(8,128)(2,1)S(1)}, u32[]{:S(2)}, u32[]{:S(2)}) collective-permute-start(bf16[64,2048]{1,0:T(8,128)(2,1)S(1)} %get-tuple-element.104), channel_id=1, source_target_pairs={{0,1},{1,0},{2,3},{3,2},{4,5},{5,4},{6,7},{7,6},{8,9},{9,8},{10,11... | collective-permute-start | bytes 786440 | tf_op jit(solution)/shard_map/ppermute | solution.py:538
  106.9 2.1 %collective-permute-start.27 = (bf16[64,2048]{1,0:T(8,128)(2,1)S(1)}, bf16[64,2048]{1,0:T(8,128)(2,1)S(1)}, u32[]{:S(2)}, u32[]{:S(2)}) collective-permute-start(bf16[64,2048]{1,0:T(8,128)(2,1)S(1)} %get-tuple-element.102), channel_id=1, source_target_pairs={{0,1},{1,0},{2,3},{3,2},{4,5},{5,4},{6,7},{7,6},{8,9},{9,8},{10,11... | collective-permute-start | bytes 786440 | tf_op jit(solution)/shard_map/ppermute | solution.py:538
  108.5 8.4 %collective-permute-start.29 = (bf16[64,2048]{1,0:T(8,128)(2,1)S(1)}, bf16[64,2048]{1,0:T(8,128)(2,1)S(1)}, u32[]{:S(2)}, u32[]{:S(2)}) collective-permute-start(bf16[64,2048]{1,0:T(8,128)(2,1)S(1)} %add_convert_fusion.1), channel_id=1, source_target_pairs={{0,2},{2,0},{1,3},{3,1},{4,6},{6,4},{5,7},{7,5},{8,10},{10,8},{9,1... | collective-permute-start | bytes 786440 | tf_op jit(solution)/shard_map/ppermute | solution.py:539

commit v13 on v12

--- a/solution.py
+++ b/solution.py
@@ -262,10 +262,12 @@
         turned = jnp.dot(other[...], basis[...], preferred_element_type=f32).astype(bf16)
         right[pl.ds(2 * rows + half, late), columns] = turned
         sums[0:1, columns] = jnp.sum(jnp.square(turned.astype(f32)), axis=0, keepdims=True)
-    for copy in copies:
+    for copy in copies[1:]:
         copy.wait()
     columns = pl.ds(pl.multiple_of((where[0] ^ 2) * chunk, chunk), chunk)
-    partial[...] = chunk_of(right, columns, (acts[0], acts[1], moved, acts[3]), rows)
+    total = chunk_of(right, columns, acts[:2], rows)
+    copies[0].wait()
+    partial[...] = total + chunk_of(right.at[pl.ds(2 * rows, 2 * rows)], columns, (moved, acts[3]), rows)
 
 
 def ready(where, acts, early, bases, other, rows, levels):

time: 118 us -> 118 us (level)
  transfers between devices with their start and end apart: 30 -> 30, of which waited for: 18 -> 18; matrix products, arithmetic and copies ran while one was open for 3% -> 3% of each run, Pallas kernels for 14% -> 13%
where the time goes in v13:
time: 118 us; the launch traced here: 117 us
  waiting for transfers between devices  54.7 us (46%)
  starting transfers between devices  34.2 us (29%)
  Pallas kernels  20.4 us (17%)
  other arithmetic  3.9 us (3%)
  local copies, waits for them, and re-layouts  3.1 us (3%)
    ppermute x8, waiting for transfers between devices, across(): return lax.ppermute(x, 'level', [(i, i ^ step) for i in range(levels)])  29.1 us
    ppermute x8, starting transfers between devices, across(): return lax.ppermute(x, 'level', [(i, i ^ step) for i in range(levels)])  13.4 us
    pallas_call x2, Pallas kernels, turn(): pl.pallas_call(functools.partial(turn_kernel, levels, level_g, level_a, r...  9.89 us
    ppermute x1, waiting for transfers between devices, body(): last = lax.ppermute((far_kept + far_sent).astype(bf16), 'chip', SWAP)  7.85 us
    ppermute x1, waiting for transfers between devices, gather_levels(): lax.ppermute(held, 'level', [(0, 3), (3, 0)])  7.8 us
    ppermute x4, waiting for transfers between devices, over(): return lax.ppermute(slot, 'group', SWAP)  6.19 us
    ppermute x4, starting transfers between devices, over(): return lax.ppermute(slot, 'group', SWAP)  6.06 us
    ppermute x1, starting transfers between devices, gather_levels(): lax.ppermute(held, 'level', [(0, 3), (3, 0)])  4.37 us
  transfers between devices with their start and end apart: 30, of which 18 were waited for; matrix products, arithmetic and copies ran while one was open for 3% of the time, Pallas kernels for 13%

profile of v13, /device:TPU:0, one launch (start us, length us, event | category | flops | bytes accessed | tf_op | source)
XLA Modules:
  0.0 117.4 jit_solution(1955758790091548264)
XLA Ops:
  0.0 0.9 constant_dynamic-slice_fusion.1
  0.9 1.0 constant_dynamic-slice_fusion.3
  2.4 2.6 %collective-permute-start.1 = (bf16[192,256]{1,0:T(8,128)(2,1)S(1)}, bf16[192,256]{1,0:T(8,128)(2,1)S(1)}, u32[]{:S(2)}, u32[]{:S(2)}) collective-permute-start(bf16[192,256]{1,0:T(8,128)(2,1)S(1)} %get-tuple-element.114), channel_id=1, source_target_pairs={{0,2},{2,0},{1,3},{3,1},{4,6},{6,4},{5,7},{7,5},{8,10},{10,8},{9,1... | collective-permute-start | bytes 294920 | tf_op jit(solution)/shard_map/ppermute | solution.py:494
  6.3 0.9 copy-done.1
  7.8 0.9 collective-permute-done.1
  8.7 1.9 %collective-permute-start.2 = (bf16[880,1024]{1,0:T(8,128)(2,1)S(1)}, bf16[880,1024]{1,0:T(8,128)(2,1)}, u32[]{:S(2)}, u32[]{:S(2)}) collective-permute-start(bf16[880,1024]{1,0:T(8,128)(2,1)S(1)} %pad_maximum_fusion.refs_4_.refs_0_), channel_id=1, source_target_pairs={{0,2},{2,0},{1,3},{3,1},{4,6},{6,4},{5,7},{7,5},{8,10},{10,8},{9,1... | collective-permute-start | bytes 5406728 | tf_op jit(solution)/shard_map/ppermute | solution.py:513
  10.8 1.6 %collective-permute-start.5 = (bf16[768,256]{1,0:T(8,128)(2,1)S(1)}, bf16[768,256]{1,0:T(8,128)(2,1)}, u32[]{:S(2)}, u32[]{:S(2)}) collective-permute-start(bf16[768,256]{1,0:T(8,128)(2,1)S(1)} %fusion.5.refs_0_), channel_id=1, source_target_pairs={{0,4},{4,0},{8,12},{12,8},{1,5},{5,1},{9,13},{13,9},{2,6},{6,2},{1... | collective-permute-start | bytes 1179656 | tf_op jit(solution)/shard_map/ppermute | solution.py:39
  12.5 0.7 collective-permute-start.6
  13.2 1.6 %collective-permute-start.7 = (bf16[768,256]{1,0:T(8,128)(2,1)S(1)}, bf16[768,256]{1,0:T(8,128)(2,1)S(1)}, u32[]{:S(2)}, u32[]{:S(2)}) collective-permute-start(bf16[768,256]{1,0:T(8,128)(2,1)S(1)} %fusion.5.refs_0_), channel_id=1, source_target_pairs={{0,16},{16,0},{1,17},{17,1},{2,18},{18,2},{3,19},{19,3},{4,20},{20... | collective-permute-start | bytes 1179656 | tf_op jit(solution)/shard_map/ppermute | solution.py:458
  14.7 1.2 slice_select_fusion.1.refs_8_
  15.9 6.0 %collective-permute-done.5.refs_1_ = bf16[768,256]{1,0:T(8,128)(2,1)} collective-permute-done((bf16[768,256]{1,0:T(8,128)(2,1)S(1)}, bf16[768,256]{1,0:T(8,128)(2,1)}, u32[]{:S(2)}, u32[]{:S(2)}) %collective-permute-start.5) | collective-permute-done | bytes 393248 | tf_op jit(solution)/shard_map/ppermute | solution.py:39
  21.9 2.1 %collective-permute-done.7.refs_0_ = bf16[768,256]{1,0:T(8,128)(2,1)S(1)} collective-permute-done((bf16[768,256]{1,0:T(8,128)(2,1)S(1)}, bf16[768,256]{1,0:T(8,128)(2,1)S(1)}, u32[]{:S(2)}, u32[]{:S(2)}) %collective-permute-start.7) | collective-permute-done | bytes 393248 | tf_op jit(solution)/shard_map/ppermute | solution.py:458
  24.0 4.4 %collective-permute-start.8 = (bf16[768,256]{1,0:T(8,128)(2,1)S(1)}, bf16[768,256]{1,0:T(8,128)(2,1)}, u32[]{:S(2)}, u32[]{:S(2)}) collective-permute-start(bf16[768,256]{1,0:T(8,128)(2,1)S(1)} %fusion.5.refs_0_), channel_id=1, source_target_pairs={{0,12},{12,0},{1,13},{13,1},{2,14},{14,2},{3,15},{15,3},{16,28},{2... | collective-permute-start | bytes 1179656 | tf_op jit(solution)/shard_map/ppermute | solution.py:468
  28.4 1.6 %collective-permute-start.9 = (bf16[768,256]{1,0:T(8,128)(2,1)}, bf16[768,256]{1,0:T(8,128)(2,1)}, u32[]{:S(2)}, u32[]{:S(2)}) collective-permute-start(bf16[768,256]{1,0:T(8,128)(2,1)} %collective-permute-done.5.refs_1_), channel_id=1, source_target_pairs={{0,16},{16,0},{1,17},{17,1},{2,18},{18,2},{3,19},{19,3},{4,20},{20... | collective-permute-start | bytes 1179656 | tf_op jit(solution)/shard_map/ppermute | solution.py:458
  29.9 7.8 %collective-permute-done.8 = bf16[768,256]{1,0:T(8,128)(2,1)} collective-permute-done((bf16[768,256]{1,0:T(8,128)(2,1)S(1)}, bf16[768,256]{1,0:T(8,128)(2,1)}, u32[]{:S(2)}, u32[]{:S(2)}) %collective-permute-start.8) | collective-permute-done | bytes 393248 | tf_op jit(solution)/shard_map/ppermute | solution.py:468
  37.7 0.8 collective-permute-done.9.refs_1_
  38.6 1.0 broadcast_select_fusion.1.refs_3_
  39.6 0.9 collective-permute-start.10
  40.5 1.5 %collective-permute-start.11 = (bf16[768,256]{1,0:T(8,128)(2,1)S(1)}, bf16[768,256]{1,0:T(8,128)(2,1)S(1)}, u32[]{:S(2)}, u32[]{:S(2)}) collective-permute-start(bf16[768,256]{1,0:T(8,128)(2,1)S(1)} %broadcast_select_fusion.1.refs_3_), channel_id=1, source_target_pairs={{0,16},{16,0},{1,17},{17,1},{2,18},{18,2},{3,19},{19,3},{4,20},{20... | collective-permute-start | bytes 1179656 | tf_op jit(solution)/shard_map/ppermute | solution.py:458
  42.0 6.5 %collective-permute-done.10.refs_2_ = bf16[768,256]{1,0:T(8,128)(2,1)S(1)} collective-permute-done((bf16[768,256]{1,0:T(8,128)(2,1)S(1)}, bf16[768,256]{1,0:T(8,128)(2,1)S(1)}, u32[]{:S(2)}, u32[]{:S(2)}) %collective-permute-start.10) | collective-permute-done | bytes 393248 | tf_op jit(solution)/shard_map/ppermute | solution.py:39
  49.0 0.7 collective-permute-done.2.refs_6_.refs_2_
  50.2 1.6 %collective-permute-start.16 = (bf16[144,2048]{1,0:T(8,128)(2,1)S(1)}, bf16[144,2048]{1,0:T(8,128)(2,1)S(1)}, u32[]{:S(2)}, u32[]{:S(2)}) collective-permute-start(bf16[144,2048]{1,0:T(8,128)(2,1)S(1)} %slice_select_fusion.1.refs_8_), channel_id=1, source_target_pairs={{0,2},{2,0},{1,3},{3,1},{4,6},{6,4},{5,7},{7,5},{8,10},{10,8},{9,1... | collective-permute-start | bytes 1769480 | tf_op jit(solution)/shard_map/ppermute | solution.py:520
  51.8 1.5 %collective-permute-start.13 = (bf16[768,256]{1,0:T(8,128)(2,1)S(1)}, bf16[768,256]{1,0:T(8,128)(2,1)S(1)}, u32[]{:S(2)}, u32[]{:S(2)}) collective-permute-start(bf16[768,256]{1,0:T(8,128)(2,1)S(1)} %collective-permute-done.10.refs_2_), channel_id=1, source_target_pairs={{0,16},{16,0},{1,17},{17,1},{2,18},{18,2},{3,19},{19,3},{4,20},{20... | collective-permute-start | bytes 1179656 | tf_op jit(solution)/shard_map/ppermute | solution.py:458
  53.3 0.6 collective-permute-done.14.refs_9_
  53.9 0.6 collective-permute-done.12.refs_7_.refs_3_.refs_0_
  54.5 5.0 %shard_map.55 = (bf16[1024,256]{1,0:T(8,128)(2,1)S(1)}, bf16[1248,256]{1,0:T(8,128)(2,1)S(1)}, bf16[2048,256]{1,0:T(8,128)(2,1)S(1)}, f32[8,256]{1,0:T(8,128)S(1)}) custom-call(s32[2]{0:T(128)S(1)} %pad_add_fusion.where, bf16[768,256]{1,0:T(8,128)(2,1)S(1)} %fusion.5.refs_0_, bf16[768,256]{1,0:T(8,128)(2,1)} %collective-permute-done.5.refs_1_, ...), custom_call_target="tpu_custom_call" | custom-call | flops 1610612736 | bytes 6291456 | tf_op jit(solution)/shard_map/pallas_call | solution.py:105
  59.6 2.9 %collective-permute-done.13.refs_2_ = bf16[768,256]{1,0:T(8,128)(2,1)S(1)} collective-permute-done((bf16[768,256]{1,0:T(8,128)(2,1)S(1)}, bf16[768,256]{1,0:T(8,128)(2,1)S(1)}, u32[]{:S(2)}, u32[]{:S(2)}) %collective-permute-start.13) | collective-permute-done | bytes 393248 | tf_op jit(solution)/shard_map/ppermute | solution.py:458
  62.5 4.9 %shard_map.56 = (bf16[1024,256]{1,0:T(8,128)(2,1)S(1)}, bf16[1248,256]{1,0:T(8,128)(2,1)S(1)}, bf16[2048,256]{1,0:T(8,128)(2,1)S(1)}, f32[8,256]{1,0:T(8,128)S(1)}) custom-call(s32[2]{0:T(128)S(1)} %pad_add_fusion.where, bf16[768,256]{1,0:T(8,128)(2,1)S(1)} %collective-permute-done.7.refs_0_, bf16[768,256]{1,0:T(8,128)(2,1)} %collective-permute-done.9.refs_1_, ...), custom_call_target="tpu_custom_call" | custom-call | flops 1610612736 | bytes 6291456 | tf_op jit(solution)/shard_map/pallas_call | solution.py:105
  68.1 2.3 %shard_map.57 = (bf16[1536,512]{1,0:T(8,128)(2,1)S(1)}, f32[128,1024]{1,0:T(8,128)S(1)}, f32[8,512]{1,0:T(8,128)S(1)}) custom-call(s32[2]{0:T(128)S(1)} %pad_add_fusion.where, bf16[880,1024]{1,0:T(8,128)(2,1)S(1)} %pad_maximum_fusion.refs_4_.refs_0_, bf16[880,1024]{1,0:T(8,128)(2,1)S(1)} %collective-permute-done.refs_5_.refs_1_, ...), custom_call_target="tpu_custom_call" | custom-call | flops 402653184 | bytes 6291456 | tf_op jit(solution)/shard_map/pallas_call | solution.py:277
  70.4 1.3 %shard_map.58 = (bf16[136,1024]{1,0:T(8,128)(2,1)S(1)}, f32[8,1024]{1,0:T(8,128)S(1)}, bf16[144,512]{1,0:T(8,128)(2,1)S(1)}) custom-call(s32[2]{0:T(128)S(1)} %pad_add_fusion.where, bf16[880,1024]{1,0:T(8,128)(2,1)S(1)} %collective-permute-done.12.refs_7_.refs_3_.refs_0_, bf16[144,2048]{1,0:T(8,128)(2,1)S(1)} %collective-permute-done.17.refs_1_, ...), custom_call_target="tpu_custom_call" | custom-call | flops 100663296 | bytes 1572864 | tf_op jit(solution)/shard_map/pallas_call | solution.py:322
  71.7 1.6 %collective-permute-start.19 = (bf16[136,1024]{1,0:T(8,128)(2,1)S(1)}, bf16[136,1024]{1,0:T(8,128)(2,1)S(1)}, u32[]{:S(2)}, u32[]{:S(2)}) collective-permute-start(bf16[136,1024]{1,0:T(8,128)(2,1)S(1)} %get-tuple-element.93), channel_id=1, source_target_pairs={{0,4},{4,0},{8,12},{12,8},{1,5},{5,1},{9,13},{13,9},{2,6},{6,2},{1... | collective-permute-start | bytes 835592 | tf_op jit(solution)/shard_map/ppermute | solution.py:39
  73.8 3.5 %shard_map.59 = (f32[128,1024]{1,0:T(8,128)S(1)}, bf16[136,1024]{1,0:T(8,128)(2,1)S(1)}, f32[128,1024]{1,0:T(8,128)S(1)}) custom-call(s32[2]{0:T(128)S(1)} %pad_add_fusion.where, bf16[1536,512]{1,0:T(8,128)(2,1)S(1)} %get-tuple-element.83.right, bf16[144,512]{1,0:T(8,128)(2,1)S(1)} %get-tuple-element.89.block, ...), custom_call_target="tpu_custom_call" | custom-call | flops 1207959552 | bytes 6291456 | tf_op jit(solution)/shard_map/pallas_call | solution.py:344
  77.3 0.5 collective-permute-start.21
  77.9 2.8 %collective-permute-done.19.got = bf16[136,1024]{1,0:T(8,128)(2,1)S(1)} collective-permute-done((bf16[136,1024]{1,0:T(8,128)(2,1)S(1)}, bf16[136,1024]{1,0:T(8,128)(2,1)S(1)}, u32[]{:S(2)}, u32[]{:S(2)}) %collective-permute-start.19) | collective-permute-done | bytes 278560 | tf_op jit(solution)/shard_map/ppermute | solution.py:39
  80.8 4.2 %collective-permute-start.20 = (bf16[136,1024]{1,0:T(8,128)(2,1)S(1)}, bf16[136,1024]{1,0:T(8,128)(2,1)S(1)}, u32[]{:S(2)}, u32[]{:S(2)}) collective-permute-start(bf16[136,1024]{1,0:T(8,128)(2,1)S(1)} %shard_map.60), channel_id=1, source_target_pairs={{0,12},{4,8},{8,4},{12,0},{1,13},{5,9},{9,5},{13,1},{2,14},{6,10},... | collective-permute-start | bytes 835592 | tf_op jit(solution)/shard_map/ppermute | solution.py:39
  85.0 1.4 %collective-permute-done.21.refs_1_ = bf16[136,1024]{1,0:T(8,128)(2,1)S(1)} collective-permute-done((bf16[136,1024]{1,0:T(8,128)(2,1)S(1)}, bf16[136,1024]{1,0:T(8,128)(2,1)S(1)}, u32[]{:S(2)}, u32[]{:S(2)}) %collective-permute-start.21) | collective-permute-done | bytes 278560 | tf_op jit(solution)/shard_map/ppermute | solution.py:39
  86.4 8.1 %collective-permute-done.20.refs_0_ = bf16[136,1024]{1,0:T(8,128)(2,1)S(1)} collective-permute-done((bf16[136,1024]{1,0:T(8,128)(2,1)S(1)}, bf16[136,1024]{1,0:T(8,128)(2,1)S(1)}, u32[]{:S(2)}, u32[]{:S(2)}) %collective-permute-start.20) | collective-permute-done | bytes 278560 | tf_op jit(solution)/shard_map/ppermute | solution.py:39
  94.4 1.9 %shard_map.61 = (bf16[128,256]{1,0:T(8,128)(2,1)S(1)}, bf16[128,256]{1,0:T(8,128)(2,1)S(1)}, bf16[128,256]{1,0:T(8,128)(2,1)S(1)}, bf16[128,256]{1,0:T(8,128)(2,1)S(1)}) custom-call(s32[2]{0:T(128)S(1)} %pad_add_fusion.where, f32[128,1024]{1,0:T(8,128)S(1)} %get-tuple-element.91.own, f32[8,1024]{1,0:T(8,128)S(1)} %get-tuple-element.90.extra.own_extra, ...), custom_call_target="tpu_custom_call" | custom-call | flops 805306368 | bytes 2097152 | tf_op jit(solution)/shard_map/pallas_call | solution.py:406
  96.4 1.5 %collective-permute-start.24 = (bf16[128,256]{1,0:T(8,128)(2,1)S(1)}, bf16[128,256]{1,0:T(8,128)(2,1)S(1)}, u32[]{:S(2)}, u32[]{:S(2)}) collective-permute-start(bf16[128,256]{1,0:T(8,128)(2,1)S(1)} %get-tuple-element.98), channel_id=1, source_target_pairs={{0,4},{4,0},{8,12},{12,8},{1,5},{5,1},{9,13},{13,9},{2,6},{6,2},{1... | collective-permute-start | bytes 196616 | tf_op jit(solution)/shard_map/ppermute | solution.py:39
  97.8 1.1 collective-permute-start.25
  98.9 1.9 %collective-permute-start.26 = (bf16[128,256]{1,0:T(8,128)(2,1)S(1)}, bf16[128,256]{1,0:T(8,128)(2,1)S(1)}, u32[]{:S(2)}, u32[]{:S(2)}) collective-permute-start(bf16[128,256]{1,0:T(8,128)(2,1)S(1)} %get-tuple-element.100), channel_id=1, source_target_pairs={{0,12},{4,8},{8,4},{12,0},{1,13},{5,9},{9,5},{13,1},{2,14},{6,10},... | collective-permute-start | bytes 196616 | tf_op jit(solution)/shard_map/ppermute | solution.py:39
  100.8 2.9 %collective-permute-done.25.refs_2_ = bf16[128,256]{1,0:T(8,128)(2,1)S(1)} collective-permute-done((bf16[128,256]{1,0:T(8,128)(2,1)S(1)}, bf16[128,256]{1,0:T(8,128)(2,1)S(1)}, u32[]{:S(2)}, u32[]{:S(2)}) %collective-permute-start.25) | collective-permute-done | bytes 65568 | tf_op jit(solution)/shard_map/ppermute | solution.py:39
  103.7 1.3 %collective-permute-done.26.refs_3_ = bf16[128,256]{1,0:T(8,128)(2,1)S(1)} collective-permute-done((bf16[128,256]{1,0:T(8,128)(2,1)S(1)}, bf16[128,256]{1,0:T(8,128)(2,1)S(1)}, u32[]{:S(2)}, u32[]{:S(2)}) %collective-permute-start.26) | collective-permute-done | bytes 65568 | tf_op jit(solution)/shard_map/ppermute | solution.py:39
  105.1 1.4 %shard_map.62 = (bf16[64,2048]{1,0:T(8,128)(2,1)S(1)}, bf16[64,2048]{1,0:T(8,128)(2,1)S(1)}, f32[64,2048]{1,0:T(8,128)S(1)}, f32[64,2048]{1,0:T(8,128)S(1)}) custom-call(s32[2]{0:T(128)S(1)} %pad_add_fusion.where, bf16[128,256]{1,0:T(8,128)(2,1)S(1)} %get-tuple-element.97.refs_0_, bf16[128,256]{1,0:T(8,128)(2,1)S(1)} %collective-permute-done.24.refs_1_, ...), custom_call_target="tpu_custom_call" | custom-call | flops 536870912 | bytes 2097152 | tf_op jit(solution)/shard_map/pallas_call | solution.py:442
  107.1 1.0 collective-permute-done.28
  108.2 0.6 collective-permute-start.29
  108.7 7.9 %collective-permute-done.29 = bf16[64,2048]{1,0:T(8,128)(2,1)S(1)} collective-permute-done((bf16[64,2048]{1,0:T(8,128)(2,1)S(1)}, bf16[64,2048]{1,0:T(8,128)(2,1)S(1)}, u32[]{:S(2)}, u32[]{:S(2)}) %collective-permute-start.29) | collective-permute-done | bytes 262176 | tf_op jit(solution)/shard_map/ppermute | solution.py:541
  116.6 0.8 add_convert_fusion
  (54 shorter events, 4.8 us)
Async XLA Ops:
  0.0 5.9 %copy-start = (bf16[384,2048]{1,0:T(8,128)(2,1)S(1)}, bf16[384,2048]{1,0:T(8,128)(2,1)}, u32[]{:S(2)}) copy-start(bf16[384,2048]{1,0:T(8,128)(2,1)} %param.6) | copy-start | bytes 4718596
  1.9 8.7 %collective-permute-start.3 = (bf16[192,256]{1,0:T(8,128)(2,1)S(1)}, bf16[192,256]{1,0:T(8,128)(2,1)S(1)}, u32[]{:S(2)}, u32[]{:S(2)}) collective-permute-start(bf16[192,256]{1,0:T(8,128)(2,1)S(1)} %get-tuple-element.115), channel_id=1, source_target_pairs={{0,1},{1,0},{2,3},{3,2},{4,5},{5,4},{6,7},{7,6},{8,9},{9,8},{10,11... | collective-permute-start | bytes 294920 | tf_op jit(solution)/shard_map/ppermute | solution.py:495
  2.4 6.2 %collective-permute-start.1 = (bf16[192,256]{1,0:T(8,128)(2,1)S(1)}, bf16[192,256]{1,0:T(8,128)(2,1)S(1)}, u32[]{:S(2)}, u32[]{:S(2)}) collective-permute-start(bf16[192,256]{1,0:T(8,128)(2,1)S(1)} %get-tuple-element.114), channel_id=1, source_target_pairs={{0,2},{2,0},{1,3},{3,1},{4,6},{6,4},{5,7},{7,5},{8,10},{10,8},{9,1... | collective-permute-start | bytes 294920 | tf_op jit(solution)/shard_map/ppermute | solution.py:494
  5.0 5.6 %collective-permute-start.4 = (bf16[192,256]{1,0:T(8,128)(2,1)S(1)}, bf16[192,256]{1,0:T(8,128)(2,1)S(1)}, u32[]{:S(2)}, u32[]{:S(2)}) collective-permute-start(bf16[192,256]{1,0:T(8,128)(2,1)S(1)} %get-tuple-element.116), channel_id=1, source_target_pairs={{0,3},{1,2},{2,1},{3,0},{4,7},{5,6},{6,5},{7,4},{8,11},{9,10},{10,... | collective-permute-start | bytes 294920 | tf_op jit(solution)/shard_map/ppermute | solution.py:492
  6.1 1.1 copy-start.1
  8.7 41.0 %collective-permute-start.2 = (bf16[880,1024]{1,0:T(8,128)(2,1)S(1)}, bf16[880,1024]{1,0:T(8,128)(2,1)}, u32[]{:S(2)}, u32[]{:S(2)}) collective-permute-start(bf16[880,1024]{1,0:T(8,128)(2,1)S(1)} %pad_maximum_fusion.refs_4_.refs_0_), channel_id=1, source_target_pairs={{0,2},{2,0},{1,3},{3,1},{4,6},{6,4},{5,7},{7,5},{8,10},{10,8},{9,1... | collective-permute-start | bytes 5406728 | tf_op jit(solution)/shard_map/ppermute | solution.py:513
  10.8 11.1 %collective-permute-start.5 = (bf16[768,256]{1,0:T(8,128)(2,1)S(1)}, bf16[768,256]{1,0:T(8,128)(2,1)}, u32[]{:S(2)}, u32[]{:S(2)}) collective-permute-start(bf16[768,256]{1,0:T(8,128)(2,1)S(1)} %fusion.5.refs_0_), channel_id=1, source_target_pairs={{0,4},{4,0},{8,12},{12,8},{1,5},{5,1},{9,13},{13,9},{2,6},{6,2},{1... | collective-permute-start | bytes 1179656 | tf_op jit(solution)/shard_map/ppermute | solution.py:39
  12.5 9.4 %collective-permute-start.6 = (bf16[768,256]{1,0:T(8,128)(2,1)S(1)}, bf16[768,256]{1,0:T(8,128)(2,1)S(1)}, u32[]{:S(2)}, u32[]{:S(2)}) collective-permute-start(bf16[768,256]{1,0:T(8,128)(2,1)S(1)} %fusion.5.refs_0_), channel_id=1, source_target_pairs={{4,8},{8,4},{5,9},{9,5},{6,10},{10,6},{7,11},{11,7},{20,24},{24,20... | collective-permute-start | bytes 1179656 | tf_op jit(solution)/shard_map/ppermute | solution.py:465
  13.2 10.8 %collective-permute-start.7 = (bf16[768,256]{1,0:T(8,128)(2,1)S(1)}, bf16[768,256]{1,0:T(8,128)(2,1)S(1)}, u32[]{:S(2)}, u32[]{:S(2)}) collective-permute-start(bf16[768,256]{1,0:T(8,128)(2,1)S(1)} %fusion.5.refs_0_), channel_id=1, source_target_pairs={{0,16},{16,0},{1,17},{17,1},{2,18},{18,2},{3,19},{19,3},{4,20},{20... | collective-permute-start | bytes 1179656 | tf_op jit(solution)/shard_map/ppermute | solution.py:458
  21.9 2.1 %copy-start.2 = (bf16[768,256]{1,0:T(8,128)(2,1)}, bf16[768,256]{1,0:T(8,128)(2,1)S(1)}, u32[]{:S(2)}) copy-start(bf16[768,256]{1,0:T(8,128)(2,1)S(1)} %collective-permute-done.6) | copy-start | bytes 1179652
  24.0 13.7 %collective-permute-start.8 = (bf16[768,256]{1,0:T(8,128)(2,1)S(1)}, bf16[768,256]{1,0:T(8,128)(2,1)}, u32[]{:S(2)}, u32[]{:S(2)}) collective-permute-start(bf16[768,256]{1,0:T(8,128)(2,1)S(1)} %fusion.5.refs_0_), channel_id=1, source_target_pairs={{0,12},{12,0},{1,13},{13,1},{2,14},{14,2},{3,15},{15,3},{16,28},{2... | collective-permute-start | bytes 1179656 | tf_op jit(solution)/shard_map/ppermute | solution.py:468
  28.4 10.2 %collective-permute-start.9 = (bf16[768,256]{1,0:T(8,128)(2,1)}, bf16[768,256]{1,0:T(8,128)(2,1)}, u32[]{:S(2)}, u32[]{:S(2)}) collective-permute-start(bf16[768,256]{1,0:T(8,128)(2,1)} %collective-permute-done.5.refs_1_), channel_id=1, source_target_pairs={{0,16},{16,0},{1,17},{17,1},{2,18},{18,2},{3,19},{19,3},{4,20},{20... | collective-permute-start | bytes 1179656 | tf_op jit(solution)/shard_map/ppermute | solution.py:458
  39.6 9.0 %collective-permute-start.10 = (bf16[768,256]{1,0:T(8,128)(2,1)S(1)}, bf16[768,256]{1,0:T(8,128)(2,1)S(1)}, u32[]{:S(2)}, u32[]{:S(2)}) collective-permute-start(bf16[768,256]{1,0:T(8,128)(2,1)S(1)} %broadcast_select_fusion.1.refs_3_), channel_id=1, source_target_pairs={{0,4},{4,0},{8,12},{12,8},{1,5},{5,1},{9,13},{13,9},{2,6},{6,2},{1... | collective-permute-start | bytes 1179656 | tf_op jit(solution)/shard_map/ppermute | solution.py:39
  40.5 8.4 %collective-permute-start.11 = (bf16[768,256]{1,0:T(8,128)(2,1)S(1)}, bf16[768,256]{1,0:T(8,128)(2,1)S(1)}, u32[]{:S(2)}, u32[]{:S(2)}) collective-permute-start(bf16[768,256]{1,0:T(8,128)(2,1)S(1)} %broadcast_select_fusion.1.refs_3_), channel_id=1, source_target_pairs={{0,16},{16,0},{1,17},{17,1},{2,18},{18,2},{3,19},{19,3},{4,20},{20... | collective-permute-start | bytes 1179656 | tf_op jit(solution)/shard_map/ppermute | solution.py:458
  42.0 11.9 %collective-permute-start = (bf16[880,1024]{1,0:T(8,128)(2,1)S(1)}, bf16[880,1024]{1,0:T(8,128)(2,1)S(1)}, u32[]{:S(2)}, u32[]{:S(2)}) collective-permute-start(bf16[880,1024]{1,0:T(8,128)(2,1)S(1)} %pad_maximum_fusion.refs_4_.refs_0_), channel_id=1, source_target_pairs={{0,1},{1,0},{2,3},{3,2},{4,5},{5,4},{6,7},{7,6},{8,9},{9,8},{10,11... | collective-permute-start | bytes 5406728 | tf_op jit(solution)/shard_map/ppermute | solution.py:514
  49.7 4.8 %collective-permute-start.12 = (bf16[880,1024]{1,0:T(8,128)(2,1)}, bf16[880,1024]{1,0:T(8,128)(2,1)S(1)}, u32[]{:S(2)}, u32[]{:S(2)}) collective-permute-start(bf16[880,1024]{1,0:T(8,128)(2,1)} %collective-permute-done.2.refs_6_.refs_2_), channel_id=1, source_target_pairs={{0,1},{1,0},{2,3},{3,2},{4,5},{5,4},{6,7},{7,6},{8,9},{9,8},{10,11... | collective-permute-start | bytes 5406728 | tf_op jit(solution)/shard_map/ppermute | solution.py:514
  49.7 4.2 %collective-permute-start.14 = (bf16[144,2048]{1,0:T(8,128)(2,1)S(1)}, bf16[144,2048]{1,0:T(8,128)(2,1)S(1)}, u32[]{:S(2)}, u32[]{:S(2)}) collective-permute-start(bf16[144,2048]{1,0:T(8,128)(2,1)S(1)} %slice_select_fusion.1.refs_8_), channel_id=1, source_target_pairs={{0,1},{1,0},{2,3},{3,2},{4,5},{5,4},{6,7},{7,6},{8,9},{9,8},{10,11... | collective-permute-start | bytes 1769480 | tf_op jit(solution)/shard_map/ppermute | solution.py:515
  50.2 17.3 %collective-permute-start.16 = (bf16[144,2048]{1,0:T(8,128)(2,1)S(1)}, bf16[144,2048]{1,0:T(8,128)(2,1)S(1)}, u32[]{:S(2)}, u32[]{:S(2)}) collective-permute-start(bf16[144,2048]{1,0:T(8,128)(2,1)S(1)} %slice_select_fusion.1.refs_8_), channel_id=1, source_target_pairs={{0,2},{2,0},{1,3},{3,1},{4,6},{6,4},{5,7},{7,5},{8,10},{10,8},{9,1... | collective-permute-start | bytes 1769480 | tf_op jit(solution)/shard_map/ppermute | solution.py:520
  51.8 10.7 %collective-permute-start.13 = (bf16[768,256]{1,0:T(8,128)(2,1)S(1)}, bf16[768,256]{1,0:T(8,128)(2,1)S(1)}, u32[]{:S(2)}, u32[]{:S(2)}) collective-permute-start(bf16[768,256]{1,0:T(8,128)(2,1)S(1)} %collective-permute-done.10.refs_2_), channel_id=1, source_target_pairs={{0,16},{16,0},{1,17},{17,1},{2,18},{18,2},{3,19},{19,3},{4,20},{20... | collective-permute-start | bytes 1179656 | tf_op jit(solution)/shard_map/ppermute | solution.py:458
  59.5 3.1 %collective-permute-start.15 = (f32[8,256]{1,0:T(8,128)S(1)}, f32[8,256]{1,0:T(8,128)S(1)}, u32[]{:S(2)}, u32[]{:S(2)}) collective-permute-start(f32[8,256]{1,0:T(8,128)S(1)} %get-tuple-element.86.refs_6_), channel_id=1, source_target_pairs={{0,1},{1,0},{2,3},{3,2},{4,5},{5,4},{6,7},{7,6},{8,9},{9,8},{10,11... | collective-permute-start | bytes 24584 | tf_op jit(solution)/shard_map/ppermute | solution.py:517
  67.5 2.9 %collective-permute-start.17 = (bf16[144,2048]{1,0:T(8,128)(2,1)S(1)}, bf16[144,2048]{1,0:T(8,128)(2,1)S(1)}, u32[]{:S(2)}, u32[]{:S(2)}) collective-permute-start(bf16[144,2048]{1,0:T(8,128)(2,1)S(1)} %collective-permute-done.16.refs_8_), channel_id=1, source_target_pairs={{0,1},{1,0},{2,3},{3,2},{4,5},{5,4},{6,7},{7,6},{8,9},{9,8},{10,11... | collective-permute-start | bytes 1769480 | tf_op jit(solution)/shard_map/ppermute | solution.py:522
  67.6 2.8 %collective-permute-start.18 = (f32[8,256]{1,0:T(8,128)S(1)}, f32[8,256]{1,0:T(8,128)S(1)}, u32[]{:S(2)}, u32[]{:S(2)}) collective-permute-start(f32[8,256]{1,0:T(8,128)S(1)} %get-tuple-element.87.refs_7_), channel_id=1, source_target_pairs={{0,1},{1,0},{2,3},{3,2},{4,5},{5,4},{6,7},{7,6},{8,9},{9,8},{10,11... | collective-permute-start | bytes 24584 | tf_op jit(solution)/shard_map/ppermute | solution.py:523
  71.7 9.0 %collective-permute-start.19 = (bf16[136,1024]{1,0:T(8,128)(2,1)S(1)}, bf16[136,1024]{1,0:T(8,128)(2,1)S(1)}, u32[]{:S(2)}, u32[]{:S(2)}) collective-permute-start(bf16[136,1024]{1,0:T(8,128)(2,1)S(1)} %get-tuple-element.93), channel_id=1, source_target_pairs={{0,4},{4,0},{8,12},{12,8},{1,5},{5,1},{9,13},{13,9},{2,6},{6,2},{1... | collective-permute-start | bytes 835592 | tf_op jit(solution)/shard_map/ppermute | solution.py:39
  73.3 11.7 %collective-permute-start.23 = (bf16[1024,256]{1,0:T(8,128)(2,1)S(1)}, bf16[1024,256]{1,0:T(8,128)(2,1)S(1)}, u32[]{:S(2)}, u32[]{:S(2)}) collective-permute-start(bf16[1024,256]{1,0:T(8,128)(2,1)S(1)} %get-tuple-element.96.refs_3_), channel_id=1, source_target_pairs={{0,1},{1,0},{2,3},{3,2},{4,5},{5,4},{6,7},{7,6},{8,9},{9,8},{10,11... | collective-permute-start | bytes 1572872 | tf_op jit(solution)/shard_map/ppermute | solution.py:524
  73.3 11.7 %collective-permute-start.22 = (bf16[1024,256]{1,0:T(8,128)(2,1)S(1)}, bf16[1024,256]{1,0:T(8,128)(2,1)S(1)}, u32[]{:S(2)}, u32[]{:S(2)}) collective-permute-start(bf16[1024,256]{1,0:T(8,128)(2,1)S(1)} %get-tuple-element.95.refs_2_), channel_id=1, source_target_pairs={{0,1},{1,0},{2,3},{3,2},{4,5},{5,4},{6,7},{7,6},{8,9},{9,8},{10,11... | collective-permute-start | bytes 1572872 | tf_op jit(solution)/shard_map/ppermute | solution.py:524
  77.3 9.0 %collective-permute-start.21 = (bf16[136,1024]{1,0:T(8,128)(2,1)S(1)}, bf16[136,1024]{1,0:T(8,128)(2,1)S(1)}, u32[]{:S(2)}, u32[]{:S(2)}) collective-permute-start(bf16[136,1024]{1,0:T(8,128)(2,1)S(1)} %get-tuple-element.94), channel_id=1, source_target_pairs={{0,4},{4,0},{8,12},{12,8},{1,5},{5,1},{9,13},{13,9},{2,6},{6,2},{1... | collective-permute-start | bytes 835592 | tf_op jit(solution)/shard_map/ppermute | solution.py:39
  80.8 13.6 %collective-permute-start.20 = (bf16[136,1024]{1,0:T(8,128)(2,1)S(1)}, bf16[136,1024]{1,0:T(8,128)(2,1)S(1)}, u32[]{:S(2)}, u32[]{:S(2)}) collective-permute-start(bf16[136,1024]{1,0:T(8,128)(2,1)S(1)} %shard_map.60), channel_id=1, source_target_pairs={{0,12},{4,8},{8,4},{12,0},{1,13},{5,9},{9,5},{13,1},{2,14},{6,10},... | collective-permute-start | bytes 835592 | tf_op jit(solution)/shard_map/ppermute | solution.py:39
  96.4 4.5 %collective-permute-start.24 = (bf16[128,256]{1,0:T(8,128)(2,1)S(1)}, bf16[128,256]{1,0:T(8,128)(2,1)S(1)}, u32[]{:S(2)}, u32[]{:S(2)}) collective-permute-start(bf16[128,256]{1,0:T(8,128)(2,1)S(1)} %get-tuple-element.98), channel_id=1, source_target_pairs={{0,4},{4,0},{8,12},{12,8},{1,5},{5,1},{9,13},{13,9},{2,6},{6,2},{1... | collective-permute-start | bytes 196616 | tf_op jit(solution)/shard_map/ppermute | solution.py:39
  97.8 5.9 %collective-permute-start.25 = (bf16[128,256]{1,0:T(8,128)(2,1)S(1)}, bf16[128,256]{1,0:T(8,128)(2,1)S(1)}, u32[]{:S(2)}, u32[]{:S(2)}) collective-permute-start(bf16[128,256]{1,0:T(8,128)(2,1)S(1)} %get-tuple-element.99), channel_id=1, source_target_pairs={{0,8},{4,12},{8,0},{12,4},{1,9},{5,13},{9,1},{13,5},{2,10},{6,14},... | collective-permute-start | bytes 196616 | tf_op jit(solution)/shard_map/ppermute | solution.py:39
  98.9 6.2 %collective-permute-start.26 = (bf16[128,256]{1,0:T(8,128)(2,1)S(1)}, bf16[128,256]{1,0:T(8,128)(2,1)S(1)}, u32[]{:S(2)}, u32[]{:S(2)}) collective-permute-start(bf16[128,256]{1,0:T(8,128)(2,1)S(1)} %get-tuple-element.100), channel_id=1, source_target_pairs={{0,12},{4,8},{8,4},{12,0},{1,13},{5,9},{9,5},{13,1},{2,14},{6,10},... | collective-permute-start | bytes 196616 | tf_op jit(solution)/shard_map/ppermute | solution.py:39
  106.5 1.6 %collective-permute-start.28 = (bf16[64,2048]{1,0:T(8,128)(2,1)S(1)}, bf16[64,2048]{1,0:T(8,128)(2,1)S(1)}, u32[]{:S(2)}, u32[]{:S(2)}) collective-permute-start(bf16[64,2048]{1,0:T(8,128)(2,1)S(1)} %get-tuple-element.104), channel_id=1, source_target_pairs={{0,1},{1,0},{2,3},{3,2},{4,5},{5,4},{6,7},{7,6},{8,9},{9,8},{10,11... | collective-permute-start | bytes 786440 | tf_op jit(solution)/shard_map/ppermute | solution.py:540
  106.6 2.1 %collective-permute-start.27 = (bf16[64,2048]{1,0:T(8,128)(2,1)S(1)}, bf16[64,2048]{1,0:T(8,128)(2,1)S(1)}, u32[]{:S(2)}, u32[]{:S(2)}) collective-permute-start(bf16[64,2048]{1,0:T(8,128)(2,1)S(1)} %get-tuple-element.102), channel_id=1, source_target_pairs={{0,1},{1,0},{2,3},{3,2},{4,5},{5,4},{6,7},{7,6},{8,9},{9,8},{10,11... | collective-permute-start | bytes 786440 | tf_op jit(solution)/shard_map/ppermute | solution.py:540
  108.2 8.4 %collective-permute-start.29 = (bf16[64,2048]{1,0:T(8,128)(2,1)S(1)}, bf16[64,2048]{1,0:T(8,128)(2,1)S(1)}, u32[]{:S(2)}, u32[]{:S(2)}) collective-permute-start(bf16[64,2048]{1,0:T(8,128)(2,1)S(1)} %add_convert_fusion.1), channel_id=1, source_target_pairs={{0,2},{2,0},{1,3},{3,1},{4,6},{6,4},{5,7},{7,5},{8,10},{10,8},{9,1... | collective-permute-start | bytes 786440 | tf_op jit(solution)/shard_map/ppermute | solution.py:541
